TPU v7x, 32 devices: a whole 2x2x4 slice. The times are simulated.
32 devices in a mesh: dp: 4 (over x, core), seq: 4 (over z), tensor: 2 (over y).
Axes of the slice: x: 2, y: 2, z: 4, core: 2. Of those that a mesh axis runs over, the one named last changes fastest.
Arguments:
- source: bfloat16 [4, 2048, 768], P('dp', 'seq'), may hold values from -6 to 6
- target: bfloat16 [4, 2048, 768], P('dp', 'seq'), may hold values from -6 to 6
- source_segments: int32 [4, 2048], P('dp'), may hold values from 0 to 3, never falling along the last dimension, each value on 1 to 1537 neighbouring positions
- target_segments: int32 [4, 2048], P('dp'), may hold values from 0 to 3, never falling along the last dimension, each value on 1 to 1537 neighbouring positions
- enc_qkv: bfloat16 [3, 768, 768], P(None, None, 'tensor'), may hold values from -0.21875 to 0.21875
- enc_qv_bias: bfloat16 [2, 768], P(None, 'tensor'), may hold values from -3 to 3
- enc_proj: bfloat16 [768, 768], P('tensor'), may hold values from -1.5 to 1.5
- enc_ff_in: bfloat16 [768, 3072], P(None, 'tensor'), may hold values from -0.21875 to 0.21875
- enc_ff_in_bias: bfloat16 [3072], P('tensor'), may hold values from -3 to 3
- enc_ff_out: bfloat16 [3072, 768], P('tensor'), may hold values from -0.109375 to 0.109375
- enc_bias: bfloat16 [2, 768], replicated, may hold values from -2 to 2
- enc_gains: bfloat16 [2, 768], replicated, may hold values from 0.5 to 1.5
- enc_shifts: bfloat16 [2, 768], replicated, may hold values from -2 to 2
- dec_self: bfloat16 [3, 768, 768], P(None, None, 'tensor'), may hold values from -0.21875 to 0.21875
- dec_self_bias: bfloat16 [2, 768], P(None, 'tensor'), may hold values from -3 to 3
- dec_self_proj: bfloat16 [768, 768], P('tensor'), may hold values from -1.5 to 1.5
- dec_cross: bfloat16 [3, 768, 768], P(None, None, 'tensor'), may hold values from -0.21875 to 0.21875
- dec_cross_bias: bfloat16 [2, 768], P(None, 'tensor'), may hold values from -3 to 3
- dec_cross_proj: bfloat16 [768, 768], P('tensor'), may hold values from -1.5 to 1.5
- dec_ff_in: bfloat16 [768, 3072], P(None, 'tensor'), may hold values from -0.21875 to 0.21875
- dec_ff_in_bias: bfloat16 [3072], P('tensor'), may hold values from -3 to 3
- dec_ff_out: bfloat16 [3072, 768], P('tensor'), may hold values from -0.109375 to 0.109375
- dec_bias: bfloat16 [3, 768], replicated, may hold values from -2 to 2
- dec_gains: bfloat16 [3, 768], replicated, may hold values from 0.5 to 1.5
- dec_shifts: bfloat16 [3, 768], replicated, may hold values from -2 to 2
- enc_cotangent: bfloat16 [4, 2048, 768], P('dp', 'seq'), may hold values from -6 to 6
- dec_cotangent: bfloat16 [4, 2048, 768], P('dp', 'seq'), may hold values from -6 to 6
Outputs:
- enc_output: bfloat16 [4, 2048, 768], P('dp', 'seq')
- dec_output: bfloat16 [4, 2048, 768], P('dp', 'seq')
- grad_source: float32 [4, 2048, 768], P('dp', 'seq')
- grad_target: float32 [4, 2048, 768], P('dp', 'seq')
- grad_enc_qkv: float32 [3, 768, 768], P(None, ('dp', 'seq'), 'tensor')
- grad_enc_qv_bias: float32 [2, 768], P(None, 'tensor')
- grad_enc_proj: float32 [768, 768], P('tensor', ('dp', 'seq'))
- grad_enc_ff_in: float32 [768, 3072], P(('dp', 'seq'), 'tensor')
- grad_enc_ff_in_bias: float32 [3072], P('tensor')
- grad_enc_ff_out: float32 [3072, 768], P('tensor', ('dp', 'seq'))
- grad_enc_bias: float32 [2, 768], replicated
- grad_enc_gains: float32 [2, 768], replicated
- grad_enc_shifts: float32 [2, 768], replicated
- grad_dec_self: float32 [3, 768, 768], P(None, ('dp', 'seq'), 'tensor')
- grad_dec_self_bias: float32 [2, 768], P(None, 'tensor')
- grad_dec_self_proj: float32 [768, 768], P('tensor', ('dp', 'seq'))
- grad_dec_cross: float32 [3, 768, 768], P(None, ('dp', 'seq'), 'tensor')
- grad_dec_cross_bias: float32 [2, 768], P(None, 'tensor')
- grad_dec_cross_proj: float32 [768, 768], P('tensor', ('dp', 'seq'))
- grad_dec_ff_in: float32 [768, 3072], P(('dp', 'seq'), 'tensor')
- grad_dec_ff_in_bias: float32 [3072], P('tensor')
- grad_dec_ff_out: float32 [3072, 768], P('tensor', ('dp', 'seq'))
- grad_dec_bias: float32 [3, 768], replicated
- grad_dec_gains: float32 [3, 768], replicated
- grad_dec_shifts: float32 [3, 768], replicated
Inputs may be any that keep to these rules, and one draw needn't show every extreme that they name: `source_segments`: each row holds 4 documents in order, each of one position or more; one of them has exactly 1537 positions. `target_segments`: each row holds 4 documents in order, each of one position or more; one of them has exactly 1537 positions.
All inputs are finite; a program needn't handle non-finite values.
Results may differ from a plain program's by a relative error of at most 0.025.
Values may be sent and summed in bfloat16 or wider, within the bound.
A program may use at most 256 MiB of HBM per device.

v0:
```python
import jax
import jax.numpy as jnp
from jax import lax
from jax.sharding import PartitionSpec as P

HEAD_DIM = 64


EPS = 1e-05


def dot_plain(left, right):
    return jnp.dot(left, right, preferred_element_type=jnp.float32)


def dot_last(left, right):
    return lax.dot_general(
        left, right, (((1,), (1,)), ((), ())), preferred_element_type=jnp.float32
    )


def dot_first(left, right):
    return lax.dot_general(
        left, right, (((0,), (0,)), ((), ())), preferred_element_type=jnp.float32
    )


def column_sum(value):
    return jnp.sum(value.astype(jnp.float32), axis=0)


def norm_forward(hidden, gain, shift):
    centered = hidden - jnp.mean(hidden, axis=-1, keepdims=True)
    spread = jnp.mean(centered * centered, axis=-1, keepdims=True)
    factor = lax.rsqrt(spread + EPS)
    normed = centered * factor
    return (normed * gain.astype(jnp.float32) + shift.astype(jnp.float32), (normed, factor))


def norm_backward(grad, saved, gain):
    normed, factor = saved
    scaled = grad * gain.astype(jnp.float32)
    centered = scaled - jnp.mean(scaled, axis=-1, keepdims=True)
    grad_hidden = factor * (centered - normed * jnp.mean(scaled * normed, axis=-1, keepdims=True))
    return (grad_hidden, jnp.sum(grad * normed, axis=0), jnp.sum(grad, axis=0))


def split_heads(value):
    return value.reshape(value.shape[0], value.shape[1] // HEAD_DIM, HEAD_DIM)


def key_mask(query_seg, query_pos, key_seg, key_pos, causal):
    allowed = query_seg[:, None] == key_seg[None, :]
    if causal:
        allowed = allowed & (key_pos[None, :] <= query_pos[:, None])
    return allowed


def scores_of(query_heads, block_keys, allowed):
    raw = jnp.einsum("qhd,khd->hqk", query_heads, block_keys, preferred_element_type=jnp.float32)
    return jnp.where(allowed[None], raw * HEAD_DIM ** (-0.5), -jnp.inf)


def over_blocks(length, step_fn, carry):
    width = 512
    number = length // width
    return lax.fori_loop(
        0, number, lambda index, state: step_fn(index * width, width, state), carry
    )


def tensor_sum(value):
    return lax.psum(value, "tensor")


def tensor_grad(value):
    return lax.psum(value, "tensor")


def attend(queries, keys, values, query_seg, key_seg, query_start, causal):
    count = queries.shape[0]
    heads = queries.shape[1] // HEAD_DIM
    query_heads = split_heads(queries)
    query_pos = query_start + jnp.arange(count, dtype=jnp.int32)
    start_state = (
        jnp.full((heads, count), -1e30, jnp.float32),
        jnp.zeros((heads, count), jnp.float32),
        jnp.zeros((heads, count, HEAD_DIM), jnp.float32),
    )
    key_piece = split_heads(lax.all_gather(keys, "seq", axis=0, tiled=True))
    value_piece = split_heads(lax.all_gather(values, "seq", axis=0, tiled=True))

    def fold_one_block(offset, width, state):
        best, total, summed = state
        block_keys = lax.dynamic_slice_in_dim(key_piece, offset, width, 0)
        block_values = lax.dynamic_slice_in_dim(value_piece, offset, width, 0)
        key_pos = offset + jnp.arange(width, dtype=jnp.int32)
        block_seg = lax.dynamic_slice_in_dim(key_seg, offset, width, 0)
        scores = scores_of(
            query_heads, block_keys, key_mask(query_seg, query_pos, block_seg, key_pos, causal)
        )
        newest = jnp.maximum(best, jnp.max(scores, axis=2))
        weights = jnp.exp(scores - newest[:, :, None])
        factor = jnp.exp(best - newest)
        total = total * factor + jnp.sum(weights, axis=2)
        update = jnp.einsum(
            "hqk,khd->hqd",
            weights.astype(jnp.bfloat16),
            block_values,
            preferred_element_type=jnp.float32,
        )
        return (newest, total, summed * factor[:, :, None] + update)

    best, total, summed = over_blocks(key_piece.shape[0], fold_one_block, start_state)
    output = jnp.transpose(summed / total[:, :, None], (1, 0, 2)).reshape(count, heads * HEAD_DIM)
    return (output, best + jnp.log(total), None)


def attend_back(
    queries, keys, values, grad_out, output, lse, query_seg, key_seg, query_start, causal
):
    all_keys, all_values = (
        lax.all_gather(keys, "seq", axis=0, tiled=True),
        lax.all_gather(values, "seq", axis=0, tiled=True),
    )
    count = queries.shape[0]
    heads = queries.shape[1] // HEAD_DIM
    length = all_keys.shape[0]
    width = heads * HEAD_DIM
    query_heads = split_heads(queries)
    grad_heads = split_heads(grad_out)
    query_pos = query_start + jnp.arange(count, dtype=jnp.int32)
    delta = jnp.sum(grad_heads.astype(jnp.float32) * split_heads(output), axis=2).T
    key_heads = split_heads(all_keys)
    value_heads = split_heads(all_values)

    def attend_one_block(offset, span, state):
        grad_query, grad_keys, grad_values = state
        block_keys = lax.dynamic_slice_in_dim(key_heads, offset, span, 0)
        block_values = lax.dynamic_slice_in_dim(value_heads, offset, span, 0)
        key_pos = offset + jnp.arange(span, dtype=jnp.int32)
        block_seg = lax.dynamic_slice_in_dim(key_seg, offset, span, 0)
        scores = scores_of(
            query_heads, block_keys, key_mask(query_seg, query_pos, block_seg, key_pos, causal)
        )
        probs = jnp.exp(scores - lse[:, :, None])
        grad_v = jnp.einsum(
            "hqk,qhd->khd",
            probs.astype(jnp.bfloat16),
            grad_heads,
            preferred_element_type=jnp.float32,
        )
        grad_probs = jnp.einsum(
            "qhd,khd->hqk", grad_heads, block_values, preferred_element_type=jnp.float32
        )
        grad_raw = (probs * (grad_probs - delta[:, :, None]) * HEAD_DIM ** (-0.5)).astype(
            jnp.bfloat16
        )
        grad_query = grad_query + jnp.einsum(
            "hqk,khd->hqd", grad_raw, block_keys, preferred_element_type=jnp.float32
        )
        grad_k = jnp.einsum(
            "hqk,qhd->khd", grad_raw, query_heads, preferred_element_type=jnp.float32
        )
        grad_keys = lax.dynamic_update_slice_in_dim(grad_keys, grad_k, offset, 0)
        grad_values = lax.dynamic_update_slice_in_dim(grad_values, grad_v, offset, 0)
        return (grad_query, grad_keys, grad_values)

    start_state = (
        jnp.zeros((heads, count, HEAD_DIM), jnp.float32),
        jnp.zeros((length, heads, HEAD_DIM), jnp.float32),
        jnp.zeros((length, heads, HEAD_DIM), jnp.float32),
    )
    grad_query, grad_keys, grad_values = over_blocks(length, attend_one_block, start_state)
    own_k, own_v = (
        lax.psum_scatter(grad_keys.reshape(length, width), "seq", scatter_dimension=0, tiled=True),
        lax.psum_scatter(
            grad_values.reshape(length, width), "seq", scatter_dimension=0, tiled=True
        ),
    )
    grad_q = jnp.transpose(grad_query, (1, 0, 2)).reshape(count, width).astype(jnp.bfloat16)
    return (grad_q, own_k.astype(jnp.bfloat16), own_v.astype(jnp.bfloat16))


def attention_forward(
    query_in, key_in, qkv, qv_bias, out_weight, out_bias, query_seg, key_seg, query_start, causal
):
    queries = (dot_plain(query_in, qkv[0]) + qv_bias[0].astype(jnp.float32)).astype(jnp.bfloat16)
    keys = dot_plain(key_in, qkv[1]).astype(jnp.bfloat16)
    values = (dot_plain(key_in, qkv[2]) + qv_bias[1].astype(jnp.float32)).astype(jnp.bfloat16)
    output, lse, gathered = attend(queries, keys, values, query_seg, key_seg, query_start, causal)
    mixed = output.astype(jnp.bfloat16)
    branch = tensor_sum(dot_plain(mixed, out_weight)) + out_bias.astype(jnp.float32)
    return (branch, (queries, keys, values, gathered, output, lse, mixed))


def attention_backward(
    grad_branch, saved, query_in, key_in, qkv, out_weight, query_seg, key_seg, query_start, causal
):
    queries, keys, values, gathered, output, lse, mixed = saved
    grad_mixed = dot_last(grad_branch, out_weight).astype(jnp.bfloat16)
    grad_out_weight = dot_first(mixed, grad_branch)
    grad_q, grad_k, grad_v = attend_back(
        queries, keys, values, grad_mixed, output, lse, query_seg, key_seg, query_start, causal
    )
    grad_query_in = dot_last(grad_q, qkv[0])
    grad_key_in = dot_last(grad_k, qkv[1]) + dot_last(grad_v, qkv[2])
    grad_qkv = jnp.stack(
        [dot_first(query_in, grad_q), dot_first(key_in, grad_k), dot_first(key_in, grad_v)]
    )
    grad_bias = jnp.stack([column_sum(grad_q), column_sum(grad_v)])
    return (grad_query_in, grad_key_in, grad_qkv, grad_bias, grad_out_weight)


def feed_forward(x_in, w_in, b_in, w_out, b_out):
    hidden = dot_plain(x_in, w_in) + b_in.astype(jnp.float32)
    active = jax.nn.gelu(hidden, approximate=False).astype(jnp.bfloat16)
    branch = tensor_sum(dot_plain(active, w_out)) + b_out.astype(jnp.float32)
    return (branch, (hidden, active))


def feed_backward(grad_branch, saved, x_in, w_in, w_out):
    hidden, active = saved
    grad_active = dot_last(grad_branch, w_out)
    slope = jax.vjp(lambda value: jax.nn.gelu(value, approximate=False), hidden)[1](grad_active)[0]
    grad_hidden = slope.astype(jnp.bfloat16)
    grad_in = dot_last(grad_hidden, w_in)
    return (
        grad_in,
        dot_first(x_in, grad_hidden),
        column_sum(grad_hidden),
        dot_first(active, grad_branch),
    )


def shards(
    source,
    target,
    source_segments,
    target_segments,
    enc_qkv,
    enc_qv_bias,
    enc_proj,
    enc_ff_in,
    enc_ff_in_bias,
    enc_ff_out,
    enc_bias,
    enc_gains,
    enc_shifts,
    dec_self,
    dec_self_bias,
    dec_self_proj,
    dec_cross,
    dec_cross_bias,
    dec_cross_proj,
    dec_ff_in,
    dec_ff_in_bias,
    dec_ff_out,
    dec_bias,
    dec_gains,
    dec_shifts,
    enc_cotangent,
    dec_cotangent,
):
    count = source.shape[1]
    first_row = lax.axis_index("seq") * count
    source_keys = source_segments[0]
    target_keys = target_segments[0]
    source_own = lax.dynamic_slice_in_dim(source_keys, first_row, count, 0)
    target_own = lax.dynamic_slice_in_dim(target_keys, first_row, count, 0)
    source_low = source[0]
    target_low = target[0]
    branch, enc_attn = attention_forward(
        source_low,
        source_low,
        enc_qkv,
        enc_qv_bias,
        enc_proj,
        enc_bias[0],
        source_own,
        source_keys,
        first_row,
        False,
    )
    first, enc_norm_one = norm_forward(
        source_low.astype(jnp.float32) + branch, enc_gains[0], enc_shifts[0]
    )
    first_low = first.astype(jnp.bfloat16)
    branch, enc_feed = feed_forward(first_low, enc_ff_in, enc_ff_in_bias, enc_ff_out, enc_bias[1])
    encoded, enc_norm_two = norm_forward(first + branch, enc_gains[1], enc_shifts[1])
    encoded_low = encoded.astype(jnp.bfloat16)
    branch, self_attn = attention_forward(
        target_low,
        target_low,
        dec_self,
        dec_self_bias,
        dec_self_proj,
        dec_bias[0],
        target_own,
        target_keys,
        first_row,
        True,
    )
    second, dec_norm_one = norm_forward(
        target_low.astype(jnp.float32) + branch, dec_gains[0], dec_shifts[0]
    )
    second_low = second.astype(jnp.bfloat16)
    branch, cross_attn = attention_forward(
        second_low,
        encoded_low,
        dec_cross,
        dec_cross_bias,
        dec_cross_proj,
        dec_bias[1],
        target_own,
        source_keys,
        first_row,
        False,
    )
    third, dec_norm_two = norm_forward(second + branch, dec_gains[1], dec_shifts[1])
    third_low = third.astype(jnp.bfloat16)
    branch, dec_feed = feed_forward(third_low, dec_ff_in, dec_ff_in_bias, dec_ff_out, dec_bias[2])
    decoded, dec_norm_three = norm_forward(third + branch, dec_gains[2], dec_shifts[2])
    grad_hidden, dec_gain_three, dec_shift_three = norm_backward(
        dec_cotangent[0].astype(jnp.float32), dec_norm_three, dec_gains[2]
    )
    grad_branch = grad_hidden.astype(jnp.bfloat16)
    feed_in, dec_w_in, dec_b_in, dec_w_out = feed_backward(
        grad_branch, dec_feed, third_low, dec_ff_in, dec_ff_out
    )
    dec_bias_three = column_sum(grad_branch)
    grad_third = grad_hidden + tensor_grad(feed_in)
    grad_hidden, dec_gain_two, dec_shift_two = norm_backward(grad_third, dec_norm_two, dec_gains[1])
    grad_branch = grad_hidden.astype(jnp.bfloat16)
    query_part, key_part, cross_qkv, cross_bias, cross_proj = attention_backward(
        grad_branch,
        cross_attn,
        second_low,
        encoded_low,
        dec_cross,
        dec_cross_proj,
        target_own,
        source_keys,
        first_row,
        False,
    )
    dec_bias_two = column_sum(grad_branch)
    query_total, key_total = tensor_grad((query_part, key_part))
    grad_second = grad_hidden + query_total
    grad_hidden, dec_gain_one, dec_shift_one = norm_backward(
        grad_second, dec_norm_one, dec_gains[0]
    )
    grad_branch = grad_hidden.astype(jnp.bfloat16)
    query_part, key_part, self_qkv, self_bias, self_proj = attention_backward(
        grad_branch,
        self_attn,
        target_low,
        target_low,
        dec_self,
        dec_self_proj,
        target_own,
        target_keys,
        first_row,
        True,
    )
    dec_bias_one = column_sum(grad_branch)
    grad_target = grad_hidden + tensor_grad(query_part + key_part)
    grad_hidden, enc_gain_two, enc_shift_two = norm_backward(
        enc_cotangent[0].astype(jnp.float32) + key_total, enc_norm_two, enc_gains[1]
    )
    grad_branch = grad_hidden.astype(jnp.bfloat16)
    feed_in, enc_w_in, enc_b_in, enc_w_out = feed_backward(
        grad_branch, enc_feed, first_low, enc_ff_in, enc_ff_out
    )
    enc_bias_two = column_sum(grad_branch)
    grad_first = grad_hidden + tensor_grad(feed_in)
    grad_hidden, enc_gain_one, enc_shift_one = norm_backward(grad_first, enc_norm_one, enc_gains[0])
    grad_branch = grad_hidden.astype(jnp.bfloat16)
    query_part, key_part, enc_qkv_grad, enc_bias_grad, enc_proj_grad = attention_backward(
        grad_branch,
        enc_attn,
        source_low,
        source_low,
        enc_qkv,
        enc_proj,
        source_own,
        source_keys,
        first_row,
        False,
    )
    enc_bias_one = column_sum(grad_branch)
    grad_source = grad_hidden + tensor_grad(query_part + key_part)
    matrices = (
        enc_qkv_grad,
        enc_proj_grad,
        enc_w_in,
        enc_w_out,
        self_qkv,
        self_proj,
        cross_qkv,
        cross_proj,
        dec_w_in,
        dec_w_out,
    )
    reduced = (
        lax.psum_scatter(matrices[0], ("dp", "seq"), scatter_dimension=1, tiled=True),
        lax.psum_scatter(matrices[1], ("dp", "seq"), scatter_dimension=1, tiled=True),
        lax.psum_scatter(matrices[2], ("dp", "seq"), scatter_dimension=0, tiled=True),
        lax.psum_scatter(matrices[3], ("dp", "seq"), scatter_dimension=1, tiled=True),
        lax.psum_scatter(matrices[4], ("dp", "seq"), scatter_dimension=1, tiled=True),
        lax.psum_scatter(matrices[5], ("dp", "seq"), scatter_dimension=1, tiled=True),
        lax.psum_scatter(matrices[6], ("dp", "seq"), scatter_dimension=1, tiled=True),
        lax.psum_scatter(matrices[7], ("dp", "seq"), scatter_dimension=1, tiled=True),
        lax.psum_scatter(matrices[8], ("dp", "seq"), scatter_dimension=0, tiled=True),
        lax.psum_scatter(matrices[9], ("dp", "seq"), scatter_dimension=1, tiled=True),
    )
    small = lax.psum(
        (
            enc_bias_grad,
            enc_b_in,
            jnp.stack([enc_bias_one, enc_bias_two]),
            jnp.stack([enc_gain_one, enc_gain_two]),
            jnp.stack([enc_shift_one, enc_shift_two]),
            self_bias,
            cross_bias,
            dec_b_in,
            jnp.stack([dec_bias_one, dec_bias_two, dec_bias_three]),
            jnp.stack([dec_gain_one, dec_gain_two, dec_gain_three]),
            jnp.stack([dec_shift_one, dec_shift_two, dec_shift_three]),
        ),
        ("dp", "seq"),
    )
    return (
        encoded_low[None],
        decoded.astype(jnp.bfloat16)[None],
        grad_source[None],
        grad_target[None],
        reduced[0],
        small[0],
        reduced[1],
        reduced[2],
        small[1],
        reduced[3],
        small[2],
        small[3],
        small[4],
        reduced[4],
        small[5],
        reduced[5],
        reduced[6],
        small[6],
        reduced[7],
        reduced[8],
        small[7],
        reduced[9],
        small[8],
        small[9],
        small[10],
    )


def solution(mesh):
    return jax.shard_map(
        shards,
        mesh=mesh,
        in_specs=(
            P("dp", "seq", None),
            P("dp", "seq", None),
            P("dp", None),
            P("dp", None),
            P(None, None, "tensor"),
            P(None, "tensor"),
            P("tensor", None),
            P(None, "tensor"),
            P("tensor"),
            P("tensor", None),
            P(),
            P(),
            P(),
            P(None, None, "tensor"),
            P(None, "tensor"),
            P("tensor", None),
            P(None, None, "tensor"),
            P(None, "tensor"),
            P("tensor", None),
            P(None, "tensor"),
            P("tensor"),
            P("tensor", None),
            P(),
            P(),
            P(),
            P("dp", "seq", None),
            P("dp", "seq", None),
        ),
        out_specs=(
            P("dp", "seq", None),
            P("dp", "seq", None),
            P("dp", "seq", None),
            P("dp", "seq", None),
            P(None, ("dp", "seq"), "tensor"),
            P(None, "tensor"),
            P("tensor", ("dp", "seq")),
            P(("dp", "seq"), "tensor"),
            P("tensor"),
            P("tensor", ("dp", "seq")),
            P(),
            P(),
            P(),
            P(None, ("dp", "seq"), "tensor"),
            P(None, "tensor"),
            P("tensor", ("dp", "seq")),
            P(None, ("dp", "seq"), "tensor"),
            P(None, "tensor"),
            P("tensor", ("dp", "seq")),
            P(("dp", "seq"), "tensor"),
            P("tensor"),
            P("tensor", ("dp", "seq")),
            P(),
            P(),
            P(),
        ),
        check_vma=False,
    )
```

profile of v0, /device:TPU:1, one launch (start us, length us, event | category | flops | bytes accessed | tf_op | source)
XLA Modules:
  0.0 2342.5 jit_solution(13201029112002647510)
XLA Ops:
  22.6 27.4 %all-gather.9.cloned.1.call-done = bf16[2048,384]{1,0:T(8,128)(2,1)} async-done(((bf16[512,384]{1,0:T(8,128)(2,1)}), bf16[2048,384]{1,0:T(8,128)(2,1)}) %all-gather.9.cloned.1.call-update) | async-done | bytes 1572880 | tf_op jit(solution)/shard_map/all_gather | solution.py:91
  52.6 35.6 %all-gather.7.cloned.1.call-done = bf16[2048,384]{1,0:T(8,128)(2,1)} async-done(((bf16[512,384]{1,0:T(8,128)(2,1)}), bf16[2048,384]{1,0:T(8,128)(2,1)}) %all-gather.7.cloned.1.call-update) | async-done | bytes 1572880 | tf_op jit(solution)/shard_map/all_gather | solution.py:90
  90.7 55.0 %while.108 = (s32[]{:T(128)}, f32[6,512]{1,0:T(8,128)S(1)}, f32[6,512]{1,0:T(8,128)S(1)}, f32[6,512,64]{1,2,0:T(8,128)}, s32[512]{0:T(512)S(1)}, /*index=5*/s32[...) while((s32[]{:T(128)}, f32[6,512]{1,0:T(8,128)S(1)}, ...), condition=%wide.region_3.4_spmd.clone, body=%wide.region_0.3_spmd.clone.sunk | while | flops 420822016 | bytes 48046300 | solution.py:67
  165.7 55.3 %while.109 = (s32[]{:T(128)}, f32[6,512]{1,0:T(8,128)S(1)}, f32[6,512]{1,0:T(8,128)S(1)}, f32[6,512,64]{1,2,0:T(8,128)}, s32[512]{0:T(512)S(1)}, /*index=5*/s32[...) while((s32[]{:T(128)}, f32[6,512]{1,0:T(8,128)S(1)}, ...), condition=%wide.region_13.14_spmd.clone, body=%wide.region_10.13_spmd.clone.sunk | while | flops 421347328 | bytes 48054508 | solution.py:67
  228.5 9.4 multiply_convert_fusion.1
  242.4 85.1 %all-reduce.36.cloned.1.call-done = (f32[512,768]{1,0:T(8,128)}, f32[512,768]{1,0:T(8,128)}) async-done(((f32[512,768]{1,0:T(8,128)}, f32[512,768]{1,0:T(8,128)}), (f32[512,768]{1,0:T(8,128)}, f32[512,768]{1,0:T(8,128)})) %all-reduce.36.cloned.1.call-update) | async-done | bytes 3145744 | tf_op jit(solution)/shard_map/psum | solution.py:73
  342.9 30.0 %all-gather.17.cloned.1.call-done = bf16[2048,384]{1,0:T(8,128)(2,1)} async-done(((bf16[512,384]{1,0:T(8,128)(2,1)}), bf16[2048,384]{1,0:T(8,128)(2,1)}) %all-gather.17.cloned.1.call-update) | async-done | bytes 1572880 | tf_op jit(solution)/shard_map/all_gather | solution.py:91
  375.5 35.5 %all-gather.15.cloned.1.call-done = bf16[2048,384]{1,0:T(8,128)(2,1)} async-done(((bf16[512,384]{1,0:T(8,128)(2,1)}), bf16[2048,384]{1,0:T(8,128)(2,1)}) %all-gather.15.cloned.1.call-update) | async-done | bytes 1572880 | tf_op jit(solution)/shard_map/all_gather | solution.py:90
  413.6 54.5 %while.110 = (s32[]{:T(128)}, f32[6,512]{1,0:T(8,128)S(1)}, f32[6,512]{1,0:T(8,128)S(1)}, f32[6,512,64]{1,2,0:T(8,128)}, s32[512]{0:T(512)S(1)}, /*index=5*/s32[...) while((s32[]{:T(128)}, f32[6,512]{1,0:T(8,128)S(1)}, ...), condition=%wide.region_20.21_spmd.clone, body=%wide.region_17.20_spmd.clone.sunk | while | flops 420822016 | bytes 48046300 | solution.py:67
  473.1 50.5 %all-reduce.20.cloned.1.call-done = f32[512,768]{1,0:T(8,128)} async-done(((f32[512,768]{1,0:T(8,128)}), f32[512,768]{1,0:T(8,128)}) %all-reduce.20.cloned.1.call-update) | async-done | bytes 1572880 | tf_op jit(solution)/shard_map/psum | solution.py:73
  539.8 51.4 %all-reduce.22.cloned.1.call-done = f32[512,768]{1,0:T(8,128)} async-done(((f32[512,768]{1,0:T(8,128)}), f32[512,768]{1,0:T(8,128)}) %all-reduce.22.cloned.1.call-update) | async-done | bytes 1572880 | tf_op jit(solution)/shard_map/psum | solution.py:73
  605.2 51.5 %all-reduce.24.cloned.1.call-done = f32[512,768]{1,0:T(8,128)} async-done(((f32[512,768]{1,0:T(8,128)}), f32[512,768]{1,0:T(8,128)}) %all-reduce.24.cloned.1.call-update) | async-done | bytes 1572880 | tf_op jit(solution)/shard_map/psum | solution.py:77
  667.1 67.4 %while.111 = (s32[]{:T(128)}, f32[6,512,64]{1,2,0:T(8,128)S(1)}, f32[2048,6,64]{0,2,1:T(8,128)}, f32[2048,6,64]{0,2,1:T(8,128)}, s32[512]{0:T(512)S(1)}, /*index...) while((s32[]{:T(128)}, f32[6,512,64]{1,2,0:T(8,128)S(1)}, ...), condition=%wide.region_34.35_spmd.clone, body=%wide.region_33.34_spmd.clone.sunk | while | flops 1024589824 | bytes 72790296 | solution.py:67
  735.3 59.5 %reduce-scatter.15.cloned.1.call-done = f32[512,384]{0,1:T(8,128)} async-done(((f32[2048,384]{0,1:T(8,128)}), f32[512,384]{0,1:T(8,128)}) %reduce-scatter.15.cloned.1.call-update) | async-done | bytes 786448 | tf_op jit(solution)/shard_map/reduce_scatter | solution.py:176
  796.7 60.8 %reduce-scatter.17.cloned.1.call-done = f32[512,384]{0,1:T(8,128)} async-done(((f32[2048,384]{0,1:T(8,128)}), f32[512,384]{0,1:T(8,128)}) %reduce-scatter.17.cloned.1.call-update) | async-done | bytes 786448 | tf_op jit(solution)/shard_map/reduce_scatter | solution.py:177
  865.2 47.2 %all-reduce.26.cloned.1.call-done = f32[512,768]{1,0:T(8,128)} async-done(((f32[512,768]{1,0:T(8,128)}), f32[512,768]{1,0:T(8,128)}) %all-reduce.26.cloned.1.call-update) | async-done | bytes 1572880 | tf_op jit(solution)/shard_map/psum | solution.py:77
  928.0 85.4 %all-reduce.34.cloned.1.call-done = (f32[512,768]{1,0:T(8,128)}, f32[512,768]{1,0:T(8,128)}) async-done(((f32[512,768]{1,0:T(8,128)}, f32[512,768]{1,0:T(8,128)}), (f32[512,768]{1,0:T(8,128)}, f32[512,768]{1,0:T(8,128)})) %all-reduce.34.cloned.1.call-update) | async-done | bytes 3145744 | tf_op jit(solution)/shard_map/psum | solution.py:77
  1023.8 79.3 %while.113 = (s32[]{:T(128)}, f32[6,512,64]{1,2,0:T(8,128)}, f32[2048,6,64]{0,2,1:T(8,128)}, f32[2048,6,64]{0,2,1:T(8,128)}, s32[512]{0:T(512)S(1)}, /*index=5*/...) while((s32[]{:T(128)}, f32[6,512,64]{1,2,0:T(8,128)}, ...), condition=%wide.region_54.55_spmd.clone, body=%wide.region_53.54_spmd.clone.sunk | while | flops 1025115136 | bytes 72798512 | solution.py:67
  1113.8 72.1 %while.112 = (s32[]{:T(128)}, f32[6,512,64]{1,2,0:T(8,128)S(1)}, f32[2048,6,64]{0,2,1:T(8,128)}, f32[2048,6,64]{0,2,1:T(8,128)}, s32[512]{0:T(512)S(1)}, /*index...) while((s32[]{:T(128)}, f32[6,512,64]{1,2,0:T(8,128)S(1)}, ...), condition=%wide.region_45.46_spmd.clone, body=%wide.region_44.45_spmd.clone.sunk | while | flops 1024589824 | bytes 72790296 | solution.py:67
  1197.4 48.7 %reduce-scatter.19.cloned.1.call-done = f32[512,384]{0,1:T(8,128)} async-done(((f32[2048,384]{0,1:T(8,128)}), f32[512,384]{0,1:T(8,128)}) %reduce-scatter.19.cloned.1.call-update) | async-done | bytes 786448 | tf_op jit(solution)/shard_map/reduce_scatter | solution.py:176
  1249.2 59.5 %reduce-scatter.25.cloned.1.call-done = f32[512,384]{0,1:T(8,128)} async-done(((f32[2048,384]{0,1:T(8,128)}), f32[512,384]{0,1:T(8,128)}) %reduce-scatter.25.cloned.1.call-update) | async-done | bytes 786448 | tf_op jit(solution)/shard_map/reduce_scatter | solution.py:177
  1312.8 58.7 %reduce-scatter.21.cloned.1.call-done = f32[512,384]{0,1:T(8,128)} async-done(((f32[2048,384]{0,1:T(8,128)}), f32[512,384]{0,1:T(8,128)}) %reduce-scatter.21.cloned.1.call-update) | async-done | bytes 786448 | tf_op jit(solution)/shard_map/reduce_scatter | solution.py:177
  1466.0 184.5 %all-reduce.30.cloned.1.call-done = (f32[3,768,384]{2,0,1:T(4,128)}, f32[3,768,384]{2,0,1:T(4,128)}) async-done(((f32[3,768,384]{2,0,1:T(4,128)}, f32[3,768,384]{2,0,1:T(4,128)}), (f32[3,768,384]{2,0,1:T(4,128)}, f32[3,768,384]{2,0,1:T(4,128)})) %all-reduce.30.cloned.1.call-update) | async-done | bytes 7077904
  1654.0 57.6 %reduce-scatter.37.cloned.1.call-done = f32[384,48]{0,1:T(8,128)} async-done(((f32[384,768]{0,1:T(8,128)}), f32[384,48]{0,1:T(8,128)}) %reduce-scatter.37.cloned.1.call-update) | async-done | bytes 73744 | tf_op jit(solution)/shard_map/reduce_scatter | solution.py:413
  1711.6 80.4 %reduce-scatter.39.cloned.1.call-done = f32[48,1536]{1,0:T(8,128)} async-done(((f32[768,1536]{1,0:T(8,128)}), f32[48,1536]{1,0:T(8,128)}) %reduce-scatter.39.cloned.1.call-update) | async-done | bytes 294928 | tf_op jit(solution)/shard_map/reduce_scatter | solution.py:414
  1792.0 78.9 %reduce-scatter.41.cloned.1.call-done = f32[1536,48]{0,1:T(8,128)} async-done(((f32[1536,768]{0,1:T(8,128)}), f32[1536,48]{0,1:T(8,128)}) %reduce-scatter.41.cloned.1.call-update) | async-done | bytes 294928 | tf_op jit(solution)/shard_map/reduce_scatter | solution.py:415
  1870.9 71.8 %reduce-scatter.35.cloned.1.call-done = f32[3,48,384]{2,1,0:T(8,128)} async-done(((f32[3,768,384]{2,1,0:T(8,128)}), f32[3,48,384]{2,1,0:T(8,128)}) %reduce-scatter.35.cloned.1.call-update) | async-done | bytes 221200 | tf_op jit(solution)/shard_map/reduce_scatter | solution.py:412
  1942.7 60.9 %reduce-scatter.33.cloned.1.call-done = f32[384,48]{0,1:T(8,128)} async-done(((f32[384,768]{0,1:T(8,128)}), f32[384,48]{0,1:T(8,128)}) %reduce-scatter.33.cloned.1.call-update) | async-done | bytes 73744 | tf_op jit(solution)/shard_map/reduce_scatter | solution.py:411
  2003.6 61.6 %reduce-scatter.27.cloned.1.call-done = f32[384,48]{0,1:T(8,128)} async-done(((f32[384,768]{0,1:T(8,128)}), f32[384,48]{0,1:T(8,128)}) %reduce-scatter.27.cloned.1.call-update) | async-done | bytes 73744 | tf_op jit(solution)/shard_map/reduce_scatter | solution.py:407
  2065.2 80.3 %reduce-scatter.29.cloned.1.call-done = f32[48,1536]{1,0:T(8,128)} async-done(((f32[768,1536]{1,0:T(8,128)}), f32[48,1536]{1,0:T(8,128)}) %reduce-scatter.29.cloned.1.call-update) | async-done | bytes 294928 | tf_op jit(solution)/shard_map/reduce_scatter | solution.py:408
  2145.5 79.1 %reduce-scatter.31.cloned.1.call-done = f32[1536,48]{0,1:T(8,128)} async-done(((f32[1536,768]{0,1:T(8,128)}), f32[1536,48]{0,1:T(8,128)}) %reduce-scatter.31.cloned.1.call-update) | async-done | bytes 294928 | tf_op jit(solution)/shard_map/reduce_scatter | solution.py:409
  2224.6 96.7 %all-reduce.28.cloned.1.call-done = (f32[2,384]{1,0:T(2,128)}, f32[1536]{0:T(1024)}, f32[2,768]{1,0:T(2,128)}, f32[2,768]{1,0:T(2,128)}, f32[2,768]{1,0:T(2,128)...) async-done(((f32[2,384]{1,0:T(2,128)}, f32[1536]{0:T(1024)}, ...) | async-done | bytes 67600 | tf_op jit(solution)/shard_map/psum | solution.py:417
  (808 shorter events, 676.4 us)
Async XLA Ops:
  7.2 42.8 %all-gather.9.cloned.1.call-start = ((), (), s32[]{:S(2)}) async-start(), calls=%async_computation.15 | async-start | bytes 1966080 | tf_op jit(solution)/shard_map/all_gather | solution.py:91
  10.8 77.3 %all-gather.7.cloned.1.call-start = ((), (), s32[]{:S(2)}) async-start(), calls=%async_computation.14 | async-start | bytes 1966080 | tf_op jit(solution)/shard_map/all_gather | solution.py:90
  13.5 137.6 %all-gather.13.cloned.1.call-start = ((), (), s32[]{:S(2)}) async-start(), calls=%async_computation.18 | async-start | bytes 1966080 | tf_op jit(solution)/shard_map/all_gather | solution.py:91
  16.1 147.1 %all-gather.11.cloned.1.call-start = ((), (), s32[]{:S(2)}) async-start(), calls=%async_computation.17 | async-start | bytes 1966080 | tf_op jit(solution)/shard_map/all_gather | solution.py:90
  18.5 207.5 %all-reduce.18.cloned.1.call-start = ((), (), s32[]{:S(2)}) async-start(), calls=%async_computation.16 | async-start | bytes 3145728 | tf_op jit(solution)/shard_map/psum | solution.py:73
  150.7 176.7 %all-reduce.36.cloned.1.call-start = ((), (), s32[]{:S(2)}) async-start(), calls=%async_computation.43 | async-start | bytes 6291456 | tf_op jit(solution)/shard_map/psum | solution.py:73
  241.6 131.2 %all-gather.17.cloned.1.call-start = ((), (), s32[]{:S(2)}) async-start(), calls=%async_computation.20 | async-start | bytes 1966080 | tf_op jit(solution)/shard_map/all_gather | solution.py:91
  335.7 75.3 %all-gather.15.cloned.1.call-start = ((), (), s32[]{:S(2)}) async-start(), calls=%async_computation.19 | async-start | bytes 1966080 | tf_op jit(solution)/shard_map/all_gather | solution.py:90
  338.2 185.4 %all-reduce.20.cloned.1.call-start = ((), (), s32[]{:S(2)}) async-start(), calls=%async_computation.21 | async-start | bytes 3145728 | tf_op jit(solution)/shard_map/psum | solution.py:73
  338.9 677.8 %copy-start.87 = (f32[768]{0:T(1024)}, f32[768]{0:T(1024)S(1)}, u32[]{:S(2)}) copy-start(f32[768]{0:T(1024)S(1)} %get-tuple-element.1751) | copy-start | bytes 9220
  473.0 118.2 %all-reduce.22.cloned.1.call-start = ((), (), s32[]{:S(2)}) async-start(), calls=%async_computation.22 | async-start | bytes 3145728 | tf_op jit(solution)/shard_map/psum | solution.py:73
  539.6 117.2 %all-reduce.24.cloned.1.call-start = ((), (), s32[]{:S(2)}) async-start(), calls=%async_computation.23 | async-start | bytes 3145728 | tf_op jit(solution)/shard_map/psum | solution.py:77
  605.1 189.7 %reduce-scatter.15.cloned.1.call-start = ((), (), s32[]{:S(2)}) async-start(), calls=%async_computation.24 | async-start | bytes 3932160 | tf_op jit(solution)/shard_map/reduce_scatter | solution.py:176
  734.5 123.0 %reduce-scatter.17.cloned.1.call-start = ((), (), s32[]{:S(2)}) async-start(), calls=%async_computation.25 | async-start | bytes 3932160 | tf_op jit(solution)/shard_map/reduce_scatter | solution.py:177
  735.3 177.1 %all-reduce.26.cloned.1.call-start = ((), (), s32[]{:S(2)}) async-start(), calls=%async_computation.26 | async-start | bytes 3145728 | tf_op jit(solution)/shard_map/psum | solution.py:77
  860.6 152.8 %all-reduce.34.cloned.1.call-start = ((), (), s32[]{:S(2)}) async-start(), calls=%async_computation.42 | async-start | bytes 6291456 | tf_op jit(solution)/shard_map/psum | solution.py:77
  927.3 267.1 %reduce-scatter.23.cloned.1.call-start = ((), (), s32[]{:S(2)}) async-start(), calls=%async_computation.29 | async-start | bytes 3932160 | tf_op jit(solution)/shard_map/reduce_scatter | solution.py:176
  1109.4 136.7 %reduce-scatter.19.cloned.1.call-start = ((), (), s32[]{:S(2)}) async-start(), calls=%async_computation.27 | async-start | bytes 3932160 | tf_op jit(solution)/shard_map/reduce_scatter | solution.py:176
  1185.9 122.8 %reduce-scatter.25.cloned.1.call-start = ((), (), s32[]{:S(2)}) async-start(), calls=%async_computation.30 | async-start | bytes 3932160 | tf_op jit(solution)/shard_map/reduce_scatter | solution.py:177
  1186.4 185.0 %reduce-scatter.21.cloned.1.call-start = ((), (), s32[]{:S(2)}) async-start(), calls=%async_computation.28 | async-start | bytes 3932160 | tf_op jit(solution)/shard_map/reduce_scatter | solution.py:177
  1187.2 274.6 %all-reduce.32.cloned.1.call-start = ((), (), s32[]{:S(2)}) async-start(), calls=%async_computation.41 | async-start | bytes 6291456 | tf_op jit(solution)/shard_map/psum | solution.py:77
  1375.5 275.0 %all-reduce.30.cloned.1.call-start = ((), (), s32[]{:S(2)}) async-start(), calls=%async_computation.40 | async-start | bytes 18874368
  1400.8 310.8 %reduce-scatter.37.cloned.1.call-start = ((), (), s32[]{:S(2)}) async-start(), calls=%async_computation.36 | async-start | bytes 1253376 | tf_op jit(solution)/shard_map/reduce_scatter | solution.py:413
  1404.8 387.2 %reduce-scatter.39.cloned.1.call-start = ((), (), s32[]{:S(2)}) async-start(), calls=%async_computation.37 | async-start | bytes 5013504 | tf_op jit(solution)/shard_map/reduce_scatter | solution.py:414
  1410.6 460.3 %reduce-scatter.41.cloned.1.call-start = ((), (), s32[]{:S(2)}) async-start(), calls=%async_computation.38 | async-start | bytes 5013504 | tf_op jit(solution)/shard_map/reduce_scatter | solution.py:415
  1416.3 526.4 %reduce-scatter.35.cloned.1.call-start = ((), (), s32[]{:S(2)}) async-start(), calls=%async_computation.35 | async-start | bytes 3760128 | tf_op jit(solution)/shard_map/reduce_scatter | solution.py:412
  1423.4 580.2 %reduce-scatter.33.cloned.1.call-start = ((), (), s32[]{:S(2)}) async-start(), calls=%async_computation.34 | async-start | bytes 1253376 | tf_op jit(solution)/shard_map/reduce_scatter | solution.py:411
  1427.6 637.5 %reduce-scatter.27.cloned.1.call-start = ((), (), s32[]{:S(2)}) async-start(), calls=%async_computation.31 | async-start | bytes 1253376 | tf_op jit(solution)/shard_map/reduce_scatter | solution.py:407
  1431.0 714.5 %reduce-scatter.29.cloned.1.call-start = ((), (), s32[]{:S(2)}) async-start(), calls=%async_computation.32 | async-start | bytes 5013504 | tf_op jit(solution)/shard_map/reduce_scatter | solution.py:408
  1436.3 788.3 %reduce-scatter.31.cloned.1.call-start = ((), (), s32[]{:S(2)}) async-start(), calls=%async_computation.33 | async-start | bytes 5013504 | tf_op jit(solution)/shard_map/reduce_scatter | solution.py:409
  1442.8 878.4 %all-reduce.28.cloned.1.call-start = ((), (), s32[]{:S(2)}) async-start(), calls=%async_computation.39 | async-start | bytes 161792 | tf_op jit(solution)/shard_map/psum | solution.py:417
  1464.7 870.7 %copy-start.1 = (bf16[768,1536]{1,0:T(8,128)(2,1)S(1)}, bf16[768,1536]{1,0:T(8,128)(2,1)}, u32[]{:S(2)}) copy-start(bf16[768,1536]{1,0:T(8,128)(2,1)} %param.58) | copy-start | bytes 7077892
  (179 other events, 5626.5 us)
Sparse Core Ops, SparseCore 0:
  10.9 39.0 all-gather.8
  52.1 35.9 all-gather.6
  89.7 35.9 all-gather.12
  127.1 35.9 all-gather.10
  165.2 50.4 all-reduce.17
  241.8 85.6 all-reduce.35
  335.8 36.9 all-gather.16
  375.0 35.9 all-gather.14
  473.1 50.4 all-reduce.19
  539.7 51.4 all-reduce.21
  605.2 51.4 all-reduce.23
  734.6 60.0 reduce-scatter.14
  797.2 60.2 reduce-scatter.16
  860.7 51.6 all-reduce.25
  927.4 85.9 all-reduce.33
  1109.6 60.0 reduce-scatter.22
  1186.0 60.0 reduce-scatter.18
  1248.4 60.2 reduce-scatter.24
  1311.1 60.2 reduce-scatter.20
  1375.6 86.1 all-reduce.31
  1465.5 184.9 all-reduce.29
  1655.2 56.3 reduce-scatter.36
  1716.5 75.4 reduce-scatter.38
  1796.3 74.5 reduce-scatter.40
  1875.8 66.8 reduce-scatter.34
  1947.2 56.3 reduce-scatter.32
  2008.1 57.0 reduce-scatter.26
  2070.1 75.3 reduce-scatter.28
  2150.0 74.5 reduce-scatter.30
  2232.5 88.6 all-reduce.27
where the time goes:
time: 2350 us; the launch traced here: 2340 us
  waiting for transfers between devices  1660 us (71%)
  matrix products  432 us (18%)
  other arithmetic  119 us (5%)
  local copies, waits for them, and re-layouts  112 us (5%)
    psum x4, waiting for transfers between devices, tensor_grad(): return lax.psum(value, 'tensor')  192 us
    psum x4, waiting for transfers between devices, tensor_sum(): return lax.psum(value, 'tensor')  187 us
    unnamed x31, waiting for transfers between devices  187 us
    reduce_scatter x3, waiting for transfers between devices, attend_back(): lax.psum_scatter(grad_values.reshape(length, width), 'seq', scatter_dimen...  179 us
    reduce_scatter x3, waiting for transfers between devices, attend_back(): lax.psum_scatter(grad_keys.reshape(length, width), 'seq', scatter_dimensi...  108 us
    psum x1, waiting for transfers between devices, shards(): lax.psum((enc_bias_grad, enc_b_in, jnp.stack([enc_bias_one, enc_bias_two]...  96.7 us
    all_gather x3, waiting for transfers between devices, attend(): key_piece = split_heads(lax.all_gather(keys, 'seq', axis=0, tiled=True))  80.4 us
    reduce_scatter x1, waiting for transfers between devices, shards(): lax.psum_scatter(matrices[8], ('dp', 'seq'), scatter_dimension=0, tiled=T...  80.4 us
  transfers between devices with their start and end apart: 30, of which 27 were waited for; matrix products, arithmetic and copies ran while one was open for 13% of the time, Pallas kernels for 0%

commit v1 on v0

v1 whole, which is shorter than its diff:
```python
import functools

import jax
import jax.numpy as jnp
from jax import lax
from jax.experimental import pallas as pl
from jax.experimental.pallas import tpu as pltpu
from jax.sharding import PartitionSpec as P

HEAD_DIM = 64
EPS = 1e-05
NEG = -1e30
BF16 = jnp.bfloat16
F32 = jnp.float32
NT = (((1,), (1,)), ((), ()))
TN = (((0,), (0,)), ((), ()))
KEY_BLOCK = 512


def dot_plain(left, right):
    return jnp.dot(left, right, preferred_element_type=F32)


def dot_last(left, right):
    return lax.dot_general(left, right, NT, preferred_element_type=F32)


def dot_first(left, right):
    return lax.dot_general(left, right, TN, preferred_element_type=F32)


def column_sum(value):
    return jnp.sum(value.astype(F32), axis=0)


def rounded(value):
    return lax.reduce_precision(value, 8, 7)


def norm_forward(hidden, gain, shift):
    centered = hidden - jnp.mean(hidden, axis=-1, keepdims=True)
    spread = jnp.mean(centered * centered, axis=-1, keepdims=True)
    factor = lax.rsqrt(spread + EPS)
    normed = centered * factor
    return (normed * gain.astype(F32) + shift.astype(F32), (normed, factor))


def norm_backward(grad, saved, gain):
    normed, factor = saved
    scaled = grad * gain.astype(F32)
    centered = scaled - jnp.mean(scaled, axis=-1, keepdims=True)
    grad_hidden = factor * (centered - normed * jnp.mean(scaled * normed, axis=-1, keepdims=True))
    return (grad_hidden, jnp.sum(grad * normed, axis=0), jnp.sum(grad, axis=0))


def head_columns(head):
    return slice(head // 2 * 128, head // 2 * 128 + 128)


def head_rows(head):
    return slice(head * HEAD_DIM, (head + 1) * HEAD_DIM)


def own_lanes(shape, head):
    lanes = lax.broadcasted_iota(jnp.int32, shape, 1)
    return lanes >= HEAD_DIM if head % 2 else lanes < HEAD_DIM


def allowed_in(index, block, base, low_ref, high_ref, count):
    part = block // 2
    place = lax.broadcasted_iota(jnp.int32, (block, count), 0)
    place = place + jnp.where(place < part, base[2 * index], base[2 * index + 1] - part)
    return (place >= low_ref[...]) & (place < high_ref[...])


def over_blocks(flags, length, block, body, skipped):
    @pl.loop(0, length // block)
    def _(index):
        flag = flags[index]
        rows = pl.ds(pl.multiple_of(index * block, block), block)

        @pl.when(flag == 0)
        def _():
            skipped(rows)

        @pl.when(flag == 1)
        def _():
            body(index, rows, True)

        @pl.when(flag == 2)
        def _():
            body(index, rows, False)


def forward_kernel(
    block, flags, base, q_ref, kv_ref, low_ref, high_ref, out_ref, lse_ref, masked_q, acc, top
):
    count, width = q_ref.shape
    heads = width // HEAD_DIM
    for head in range(heads):
        pair = q_ref[:, head_columns(head)]
        masked_q[head] = jnp.where(own_lanes(pair.shape, head), pair, jnp.zeros_like(pair))
    acc[...] = jnp.zeros_like(acc)
    top[...] = jnp.full_like(top, NEG)

    def body(index, rows, partial):
        if partial:
            allowed = allowed_in(index, block, base, low_ref, high_ref, count)
        for head in range(heads):
            cols = head_columns(head)
            scores = lax.dot_general(
                kv_ref[rows, cols], masked_q[head], NT, preferred_element_type=F32
            )
            if partial:
                scores = jnp.where(allowed, scores, NEG)
            old = top[head : head + 1, :]
            new = jnp.maximum(old, jnp.max(scores, axis=0, keepdims=True))
            weights = jnp.exp(scores - new).astype(BF16)
            vals = kv_ref[rows, width + cols.start : width + cols.stop]
            vals = jnp.where(own_lanes(vals.shape, head), vals, jnp.ones_like(vals))
            acc[head] = acc[head] * jnp.exp(old - new) + lax.dot_general(
                vals, weights, TN, preferred_element_type=F32
            )
            top[head : head + 1, :] = new

    over_blocks(flags, kv_ref.shape[0], block, body, lambda rows: None)
    lse_ref[...] = jnp.zeros_like(lse_ref)
    for head in range(heads):
        first = head % 2 * HEAD_DIM
        total = acc[head, HEAD_DIM - first : HEAD_DIM - first + 1, :]
        out_ref[head_rows(head), :] = acc[head, first : first + HEAD_DIM, :] / total
        lse_ref[head : head + 1, :] = top[head : head + 1, :] + jnp.log(total)


def backward_kernel(
    block,
    flags,
    base,
    q_ref,
    kv_ref,
    do_ref,
    dot_ref,
    out_ref,
    lse_ref,
    low_ref,
    high_ref,
    dq_ref,
    dkv_ref,
    masked_q,
    masked_do,
    delta,
    dq,
):
    count, width = q_ref.shape
    heads = width // HEAD_DIM
    for head in range(heads):
        pair = q_ref[:, head_columns(head)]
        keep = own_lanes(pair.shape, head)
        masked_q[head] = jnp.where(keep, pair, jnp.zeros_like(pair))
        pair = do_ref[:, head_columns(head)]
        masked_do[head] = jnp.where(keep, pair, jnp.zeros_like(pair))
        part = head_rows(head)
        delta[head : head + 1, :] = jnp.sum(
            dot_ref[part, :].astype(F32) * out_ref[part, :], axis=0, keepdims=True
        )
    dq[...] = jnp.zeros_like(dq)

    def body(index, rows, partial):
        if partial:
            allowed = allowed_in(index, block, base, low_ref, high_ref, count)
        for pair in range(heads // 2):
            cols = head_columns(2 * pair)
            later = slice(width + cols.start, width + cols.stop)
            keys, vals = kv_ref[rows, cols], kv_ref[rows, later]
            dk = dv = 0.0
            for head in (2 * pair, 2 * pair + 1):
                scores = lax.dot_general(keys, masked_q[head], NT, preferred_element_type=F32)
                probs = jnp.exp(scores - lse_ref[head : head + 1, :])
                if partial:
                    probs = jnp.where(allowed, probs, 0.0)
                dprobs = lax.dot_general(vals, masked_do[head], NT, preferred_element_type=F32)
                draw = (probs * (dprobs - delta[head : head + 1, :])).astype(BF16)
                probs = probs.astype(BF16)
                dv = dv + jnp.dot(probs, masked_do[head], preferred_element_type=F32)
                dk = dk + jnp.dot(draw, masked_q[head], preferred_element_type=F32)
                first = head % 2 * HEAD_DIM
                both = lax.dot_general(keys, draw, TN, preferred_element_type=F32)
                dq[head_rows(head), :] += both[first : first + HEAD_DIM]
            dkv_ref[rows, cols] = dk.astype(BF16)
            dkv_ref[rows, later] = dv.astype(BF16)

    def skipped(rows):
        dkv_ref[rows, :] = jnp.zeros((block, 2 * width), BF16)

    over_blocks(flags, kv_ref.shape[0], block, body, skipped)
    dq_ref[...] = (dq[...] * HEAD_DIM ** (-0.5)).astype(BF16)


SCALARS = pl.BlockSpec(memory_space=pltpu.SMEM)
VECTORS = pl.BlockSpec(memory_space=pltpu.VMEM)


def kernel_call(kernel, inputs, scalars, shapes, scratch, work, limit):
    length, count, width = work
    product = 2 * length * count * width
    return pl.pallas_call(
        kernel,
        out_shape=shapes,
        in_specs=[SCALARS] * scalars + [VECTORS] * (len(inputs) - scalars),
        out_specs=(VECTORS,) * len(shapes),
        scratch_shapes=scratch,
        compiler_params=pltpu.CompilerParams(vmem_limit_bytes=limit),
        cost_estimate=pl.CostEstimate(
            flops=5 * product, bytes_accessed=8 * length * width, transcendentals=0
        ),
    )(*inputs)


def attend(queries, kv, mask):
    count, width = queries.shape
    heads = width // HEAD_DIM
    flags, base, low, high = mask
    return kernel_call(
        functools.partial(forward_kernel, KEY_BLOCK),
        (flags, base, queries, kv, low, high),
        2,
        (jax.ShapeDtypeStruct((width, count), F32), jax.ShapeDtypeStruct((8, count), F32)),
        [
            pltpu.VMEM((heads, count, 128), BF16),
            pltpu.VMEM((heads, 128, count), F32),
            pltpu.VMEM((8, count), F32),
        ],
        (kv.shape[0], count, width),
        40 << 20,
    )


def attend_back(queries, kv, grad_out, grad_out_t, output, lse, mask):
    count, width = queries.shape
    heads = width // HEAD_DIM
    flags, base, low, high = mask
    return kernel_call(
        functools.partial(backward_kernel, KEY_BLOCK),
        (flags, base, queries, kv, grad_out, grad_out_t, output, lse, low, high),
        2,
        (
            jax.ShapeDtypeStruct((width, count), BF16),
            jax.ShapeDtypeStruct(kv.shape, BF16),
        ),
        [
            pltpu.VMEM((heads, count, 128), BF16),
            pltpu.VMEM((heads, count, 128), BF16),
            pltpu.VMEM((8, count), F32),
            pltpu.VMEM((width, count), F32),
        ],
        (kv.shape[0], count, width),
        48 << 20,
    )


class Places:
    def __init__(self, pairs, ring):
        self.pairs, self.ring = pairs, ring
        self.d = lax.axis_index("dp")
        self.x, self.core = self.d // 2, self.d % 2
        self.y, self.z = lax.axis_index("tensor"), lax.axis_index("seq")

    def swap_core(self, value):
        return lax.ppermute(value, "dp", [(i, i ^ 1) for i in range(self.pairs)])

    def swap_y(self, value):
        return lax.ppermute(value, "tensor", [(0, 1), (1, 0)])

    def swap_x(self, value, bit):
        return lax.ppermute(value, "dp", [(i, i ^ (2 << bit)) for i in range(self.pairs)])

    def swap_z(self, value, bit):
        return lax.ppermute(value, "seq", [(i, i ^ (1 << bit)) for i in range(self.ring)])

    def from_z(self, value, step):
        return lax.ppermute(value, "seq", [((i + step) % self.ring, i) for i in range(self.ring)])

    def to_z(self, value, step):
        return lax.ppermute(value, "seq", [(i, (i + step) % self.ring) for i in range(self.ring)])

    def permute(self, value, source_of):
        moves = []
        for d in range(self.pairs):
            for y in range(2):
                source = source_of(d, y)
                if source is not None:
                    moves.append((source[0] * 2 + source[1], d * 2 + y))
        return lax.ppermute(value, ("dp", "tensor"), moves)

    def fetch_weight(self, value):
        return self.permute(value, lambda d, y: (d + 1, y) if d % 2 == 0 else (d - 1, 1 - y))

    def core_sum(self, partial):
        low = rounded(partial)
        return low + self.swap_core(low.astype(BF16)).astype(F32)

    def own_pair(self, rows):
        return jnp.where(self.core == self.y, rows, self.swap_core(rows))

    def hand_out(self, rows):
        other = self.permute(rows, lambda d, y: (d, 1 - y) if d % 2 != y else None)
        return jnp.where(self.core == self.y, rows, other)

    def gather_rows(self, own):
        part = own.shape[0] // 2
        half = lax.dynamic_slice_in_dim(own, self.core * part, part, 0)
        pieces = [own]
        for step in range(1, self.ring):
            mine = self.from_z(half, step)
            pieces += [mine, self.swap_core(mine)]
        return jnp.concatenate(pieces, axis=0)

    def bases(self, count):
        part = count // 2
        places = [self.z * count, self.z * count + part]
        for step in range(1, self.ring):
            shard = (self.z + step) % self.ring * count
            places += [shard + self.core * part, shard + (1 - self.core) * part]
        return jnp.stack(places).astype(jnp.int32)

    def return_rows(self, piece_of, count):
        part = count // 2
        total = None
        for step in list(range(1, self.ring)) + [0]:
            piece = rounded(piece_of(step))
            if step == 0:
                mine = lax.dynamic_slice_in_dim(piece, self.core * part, part, 0)
                others = lax.dynamic_slice_in_dim(piece, (1 - self.core) * part, part, 0)
            else:
                mine, others = piece[:part], piece[part:]
            both = mine + self.swap_core(others.astype(BF16)).astype(F32)
            if step:
                both = self.to_z(both.astype(BF16), step).astype(F32)
            total = both if total is None else total + both
        total = rounded(total)
        other = self.swap_core(total.astype(BF16)).astype(F32)
        return jnp.where(
            self.core == 0,
            jnp.concatenate([total, other]),
            jnp.concatenate([other, total]),
        )

    def scatter(self, grad, x_first):
        rows, columns = grad.shape
        owners = self.pairs // 2
        grad = grad.reshape(owners, 2, self.ring, rows // (self.pairs * self.ring), columns)
        for stage in "xyz" if x_first else "yxz":
            if stage == "y":
                kept = lax.dynamic_index_in_dim(grad, self.core, grad.ndim - 4, False)
                sent = lax.dynamic_index_in_dim(grad, 1 - self.core, grad.ndim - 4, False)
                first = self.permute(
                    sent, lambda d, y: (d + 1, 1 - y) if d % 2 == 0 else (d - 1, y)
                )
                second = self.permute(kept, lambda d, y: (d, 1 - y) if d % 2 else None)
                kept = jnp.where(self.core == 0, kept, second)
                grad = (kept.astype(F32) + first.astype(F32)).astype(BF16)
            else:
                axis = 0 if stage == "x" else grad.ndim - 3
                place, swap = (self.x, self.swap_x) if stage == "x" else (self.z, self.swap_z)
                size, bit = grad.shape[axis], 0
                while size > 1:
                    shape = grad.shape[:axis] + (size // 2, 2) + grad.shape[axis + 1 :]
                    grad = grad.reshape(shape)
                    mine = (place >> bit) & 1
                    kept = lax.dynamic_index_in_dim(grad, mine, axis + 1, False)
                    sent = lax.dynamic_index_in_dim(grad, 1 - mine, axis + 1, False)
                    grad = kept.astype(F32) + swap(sent, bit).astype(F32)
                    size, bit = size // 2, bit + 1
                    if stage == "x" or size > 1:
                        grad = grad.astype(BF16)
                grad = lax.squeeze(grad, (axis,))
        return grad.astype(F32)

    def all_sum(self, whole, halves):
        both = jnp.concatenate([whole, halves])
        for bit in range((self.pairs // 2).bit_length() - 1):
            both = both + self.swap_x(both, bit)
        for bit in range(self.ring.bit_length() - 1):
            both = both + self.swap_z(both, bit)
        whole, halves = both[: whole.shape[0]], both[whole.shape[0] :]
        whole = whole + self.swap_y(whole)
        whole = (whole + self.swap_core(whole)) * 0.5
        first = self.permute(halves, lambda d, y: (d + 1, 1 - y) if d % 2 == 0 else (d - 1, y))
        second = self.swap_y(halves)
        halves = jnp.where(self.core == 0, halves, second) + first
        return whole, halves


def mask_of(query_seg, key_seg, first_row, base, causal, count):
    low = jnp.sum(key_seg[None, :] < query_seg[:, None], axis=1, dtype=jnp.int32)
    high = jnp.sum(key_seg[None, :] <= query_seg[:, None], axis=1, dtype=jnp.int32)
    if causal:
        high = jnp.minimum(high, first_row + jnp.arange(count, dtype=jnp.int32) + 1)
    part = count // 2
    active = (jnp.min(low) < base + part) & (jnp.max(high) > base)
    full = (jnp.max(low) <= base) & (jnp.min(high) >= base + part)
    per = KEY_BLOCK // part
    active = jnp.any(active.reshape(-1, per), axis=1)
    full = jnp.all(full.reshape(-1, per), axis=1)
    flags = active.astype(jnp.int32) + full.astype(jnp.int32)
    return (flags, base, low[None], high[None])


def attention_forward(place, query_in, key_in, weights, out_weight, out_bias, mask):
    w_q, w_kv, b_q, b_kv = weights
    scale = HEAD_DIM ** (-0.5)
    queries = ((dot_plain(query_in, w_q) + b_q).astype(BF16) * scale).astype(BF16)
    kv = (dot_plain(key_in, w_kv) + b_kv).astype(BF16)
    output, lse = attend(queries, kv, mask)
    mixed = output.astype(BF16)
    branch = place.core_sum(dot_first(mixed, out_weight)) + out_bias.astype(F32)
    return (branch, (queries, kv, output, lse, mixed))


def attention_backward(grad_branch, saved, query_in, key_in, weights, out_weight, mask):
    queries, kv, output, lse, mixed = saved
    w_q, w_kv = weights[:2]
    count, width = queries.shape
    grad_mixed = dot_last(grad_branch, out_weight).astype(BF16)
    grad_mixed_t = dot_last(out_weight, grad_branch).astype(BF16)
    grad_q, grad_kv = attend_back(queries, kv, grad_mixed, grad_mixed_t, output, lse, mask)
    grad_query_in = dot_general_q(grad_q, w_q)

    def grad_key_in(step):
        return dot_last(grad_kv[step * count : (step + 1) * count], w_kv)

    grad_qkv = jnp.concatenate(
        [
            lax.dot_general(query_in, grad_q, (((0,), (1,)), ((), ())), preferred_element_type=F32),
            dot_first(key_in, grad_kv),
        ],
        axis=1,
    ).astype(BF16)
    grad_out = lax.dot_general(
        grad_branch, mixed, (((0,), (1,)), ((), ())), preferred_element_type=F32
    ).astype(BF16)
    grad_bias = jnp.concatenate(
        [jnp.sum(grad_q.astype(F32), axis=1), column_sum(grad_kv[:, width:])]
    )
    return (grad_query_in, grad_key_in, grad_qkv, grad_out, grad_bias)


def dot_general_q(grad_q, w_q):
    return lax.dot_general(grad_q, w_q, (((0,), (1,)), ((), ())), preferred_element_type=F32)


def feed_forward(place, x_in, w_in, b_in, w_out, b_out):
    hidden = dot_plain(x_in, w_in) + b_in.astype(F32)
    active = jax.nn.gelu(hidden, approximate=False).astype(BF16)
    branch = place.core_sum(dot_plain(active, w_out)) + b_out.astype(F32)
    return (branch, (hidden, active))


def feed_backward(place, grad_branch, saved, x_in, w_in, w_out):
    hidden, active = saved
    grad_active = dot_last(grad_branch, w_out)
    slope = jax.vjp(lambda value: jax.nn.gelu(value, approximate=False), hidden)[1](grad_active)[0]
    grad_hidden = slope.astype(BF16)
    grad_in = place.core_sum(dot_last(grad_hidden, w_in))
    return (
        grad_in,
        dot_first(x_in, grad_hidden).astype(BF16),
        column_sum(grad_hidden),
        dot_first(grad_branch, active).astype(BF16),
    )


def shards(
    source,
    target,
    source_segments,
    target_segments,
    enc_qkv,
    enc_qv_bias,
    enc_proj,
    enc_ff_in,
    enc_ff_in_bias,
    enc_ff_out,
    enc_bias,
    enc_gains,
    enc_shifts,
    dec_self,
    dec_self_bias,
    dec_self_proj,
    dec_cross,
    dec_cross_bias,
    dec_cross_proj,
    dec_ff_in,
    dec_ff_in_bias,
    dec_ff_out,
    dec_bias,
    dec_gains,
    dec_shifts,
    enc_cotangent,
    dec_cotangent,
):
    count = source.shape[1]
    model = source.shape[2]
    place = Places(lax.axis_size("dp"), lax.axis_size("seq"))
    first_row = place.z * count

    xs = place.own_pair(source[0])
    x_all = place.gather_rows(xs)
    enc_qkv = place.fetch_weight(enc_qkv)
    vectors = place.fetch_weight(
        jnp.concatenate(
            [
                enc_qv_bias.reshape(-1),
                dec_self_bias.reshape(-1),
                dec_cross_bias.reshape(-1),
                enc_ff_in_bias,
                dec_ff_in_bias,
            ]
        )
    )
    ts = place.own_pair(target[0])
    t_all = place.gather_rows(ts)
    segments = place.own_pair(jnp.concatenate([source_segments, target_segments]))
    dec_self = place.fetch_weight(dec_self)
    enc_proj = place.fetch_weight(enc_proj)
    enc_ff_in = place.fetch_weight(enc_ff_in)
    enc_ff_out = place.fetch_weight(enc_ff_out)
    dec_self_proj = place.fetch_weight(dec_self_proj)
    dec_cross = place.fetch_weight(dec_cross)
    dec_cross_proj = place.fetch_weight(dec_cross_proj)
    dec_ff_in = place.fetch_weight(dec_ff_in)
    dec_ff_out = place.fetch_weight(dec_ff_out)
    enc_cot = place.own_pair(enc_cotangent[0])
    dec_cot = place.own_pair(dec_cotangent[0])

    width = enc_qkv.shape[2]
    hidden_units = enc_ff_in.shape[1]
    marks = [0, 2 * width, 4 * width, 6 * width, 6 * width + hidden_units, 6 * width + 2 * hidden_units]
    enc_qv_bias, dec_self_bias, dec_cross_bias, enc_ff_in_bias, dec_ff_in_bias = (
        vectors[a:b] for a, b in zip(marks[:-1], marks[1:])
    )

    def prepared(qkv, bias):
        bias = bias.astype(F32)
        b_kv = jnp.concatenate([jnp.zeros((width,), F32), bias[width:]])
        return (qkv[0], jnp.concatenate([qkv[1], qkv[2]], axis=1), bias[:width], b_kv)

    enc_w = prepared(enc_qkv, enc_qv_bias)
    self_w = prepared(dec_self, dec_self_bias)
    cross_w = prepared(dec_cross, dec_cross_bias)

    source_keys, target_keys = segments[0], segments[1]
    source_own = lax.dynamic_slice_in_dim(source_keys, first_row, count, 0)
    target_own = lax.dynamic_slice_in_dim(target_keys, first_row, count, 0)
    base = place.bases(count)
    enc_mask = mask_of(source_own, source_keys, first_row, base, False, count)
    self_mask = mask_of(target_own, target_keys, first_row, base, True, count)
    cross_mask = mask_of(target_own, source_keys, first_row, base, False, count)

    branch, enc_attn = attention_forward(place, xs, x_all, enc_w, enc_proj, enc_bias[0], enc_mask)
    first, enc_norm_one = norm_forward(xs.astype(F32) + branch, enc_gains[0], enc_shifts[0])
    first_low = first.astype(BF16)
    branch, enc_feed = feed_forward(
        place, first_low, enc_ff_in, enc_ff_in_bias, enc_ff_out, enc_bias[1]
    )
    encoded, enc_norm_two = norm_forward(first + branch, enc_gains[1], enc_shifts[1])
    encoded_low = encoded.astype(BF16)
    e_all = place.gather_rows(encoded_low)

    branch, self_attn = attention_forward(
        place, ts, t_all, self_w, dec_self_proj, dec_bias[0], self_mask
    )
    second, dec_norm_one = norm_forward(ts.astype(F32) + branch, dec_gains[0], dec_shifts[0])
    second_low = second.astype(BF16)
    branch, cross_attn = attention_forward(
        place, second_low, e_all, cross_w, dec_cross_proj, dec_bias[1], cross_mask
    )
    third, dec_norm_two = norm_forward(second + branch, dec_gains[1], dec_shifts[1])
    third_low = third.astype(BF16)
    branch, dec_feed = feed_forward(
        place, third_low, dec_ff_in, dec_ff_in_bias, dec_ff_out, dec_bias[2]
    )
    decoded, dec_norm_three = norm_forward(third + branch, dec_gains[2], dec_shifts[2])

    grad_hidden, dec_gain_three, dec_shift_three = norm_backward(
        dec_cot.astype(F32), dec_norm_three, dec_gains[2]
    )
    grad_branch = grad_hidden.astype(BF16)
    feed_in, dec_w_in, dec_b_in, dec_w_out = feed_backward(
        place, grad_branch, dec_feed, third_low, dec_ff_in, dec_ff_out
    )
    dec_ff_grad = place.scatter(jnp.concatenate([dec_w_in, dec_w_out], axis=1), False)
    dec_bias_three = column_sum(grad_branch)
    grad_third = grad_hidden + feed_in
    grad_hidden, dec_gain_two, dec_shift_two = norm_backward(grad_third, dec_norm_two, dec_gains[1])
    grad_branch = grad_hidden.astype(BF16)
    query_part, key_part, cross_qkv, cross_proj, cross_bias = attention_backward(
        grad_branch, cross_attn, second_low, e_all, cross_w, dec_cross_proj, cross_mask
    )
    cross_grad = place.scatter(jnp.concatenate([cross_qkv, cross_proj], axis=1), True)
    dec_bias_two = column_sum(grad_branch)
    key_total = place.return_rows(key_part, count)
    grad_second = grad_hidden + place.core_sum(query_part)
    grad_hidden, dec_gain_one, dec_shift_one = norm_backward(
        grad_second, dec_norm_one, dec_gains[0]
    )
    grad_branch = grad_hidden.astype(BF16)
    query_part, key_part, self_qkv, self_proj, self_bias = attention_backward(
        grad_branch, self_attn, ts, t_all, self_w, dec_self_proj, self_mask
    )
    self_grad = place.scatter(jnp.concatenate([self_qkv, self_proj], axis=1), True)
    dec_bias_one = column_sum(grad_branch)

    def self_part(step, query_part=query_part, key_part=key_part):
        return key_part(step) if step else key_part(step) + query_part

    grad_target = grad_hidden + place.return_rows(self_part, count)
    grad_hidden, enc_gain_two, enc_shift_two = norm_backward(
        enc_cot.astype(F32) + key_total, enc_norm_two, enc_gains[1]
    )
    grad_branch = grad_hidden.astype(BF16)
    feed_in, enc_w_in, enc_b_in, enc_w_out = feed_backward(
        place, grad_branch, enc_feed, first_low, enc_ff_in, enc_ff_out
    )
    enc_ff_grad = place.scatter(jnp.concatenate([enc_w_in, enc_w_out], axis=1), True)
    enc_bias_two = column_sum(grad_branch)
    grad_first = grad_hidden + feed_in
    grad_hidden, enc_gain_one, enc_shift_one = norm_backward(grad_first, enc_norm_one, enc_gains[0])
    grad_branch = grad_hidden.astype(BF16)
    query_part, key_part, enc_qkv_grad, enc_proj_grad, enc_bias_grad = attention_backward(
        grad_branch, enc_attn, xs, x_all, enc_w, enc_proj, enc_mask
    )
    enc_grad = place.scatter(jnp.concatenate([enc_qkv_grad, enc_proj_grad], axis=1), False)
    enc_bias_one = column_sum(grad_branch)

    def enc_part(step, query_part=query_part, key_part=key_part):
        return key_part(step) if step else key_part(step) + query_part

    grad_source = grad_hidden + place.return_rows(enc_part, count)

    def attention_grads(grad):
        qkv = grad[:, : 3 * width].reshape(-1, 3, width).transpose(1, 0, 2)
        return (qkv, grad[:, 3 * width :].T)

    def feed_grads(grad):
        return (grad[:, :hidden_units], grad[:, hidden_units:].T)

    out_enc_qkv, out_enc_proj = attention_grads(enc_grad)
    out_self, out_self_proj = attention_grads(self_grad)
    out_cross, out_cross_proj = attention_grads(cross_grad)
    out_enc_in, out_enc_out = feed_grads(enc_ff_grad)
    out_dec_in, out_dec_out = feed_grads(dec_ff_grad)
    whole, halves = place.all_sum(
        jnp.concatenate(
            [
                enc_bias_one,
                enc_bias_two,
                enc_gain_one,
                enc_gain_two,
                enc_shift_one,
                enc_shift_two,
                dec_bias_one,
                dec_bias_two,
                dec_bias_three,
                dec_gain_one,
                dec_gain_two,
                dec_gain_three,
                dec_shift_one,
                dec_shift_two,
                dec_shift_three,
            ]
        ),
        jnp.concatenate([enc_bias_grad, self_bias, cross_bias, enc_b_in, dec_b_in]),
    )
    whole = whole.reshape(15, model)
    small = [halves[a:b] for a, b in zip(marks[:-1], marks[1:])]
    return (
        place.hand_out(encoded_low)[None],
        place.hand_out(decoded.astype(BF16))[None],
        place.hand_out(rounded(grad_source).astype(BF16)).astype(F32)[None],
        place.hand_out(rounded(grad_target).astype(BF16)).astype(F32)[None],
        out_enc_qkv,
        small[0].reshape(2, width),
        out_enc_proj,
        out_enc_in,
        small[3],
        out_enc_out,
        whole[0:2],
        whole[2:4],
        whole[4:6],
        out_self,
        small[1].reshape(2, width),
        out_self_proj,
        out_cross,
        small[2].reshape(2, width),
        out_cross_proj,
        out_dec_in,
        small[4],
        out_dec_out,
        whole[6:9],
        whole[9:12],
        whole[12:15],
    )


def solution(mesh):
    return jax.shard_map(
        shards,
        mesh=mesh,
        in_specs=(
            P("dp", "seq", None),
            P("dp", "seq", None),
            P("dp", None),
            P("dp", None),
            P(None, None, "tensor"),
            P(None, "tensor"),
            P("tensor", None),
            P(None, "tensor"),
            P("tensor"),
            P("tensor", None),
            P(),
            P(),
            P(),
            P(None, None, "tensor"),
            P(None, "tensor"),
            P("tensor", None),
            P(None, None, "tensor"),
            P(None, "tensor"),
            P("tensor", None),
            P(None, "tensor"),
            P("tensor"),
            P("tensor", None),
            P(),
            P(),
            P(),
            P("dp", "seq", None),
            P("dp", "seq", None),
        ),
        out_specs=(
            P("dp", "seq", None),
            P("dp", "seq", None),
            P("dp", "seq", None),
            P("dp", "seq", None),
            P(None, ("dp", "seq"), "tensor"),
            P(None, "tensor"),
            P("tensor", ("dp", "seq")),
            P(("dp", "seq"), "tensor"),
            P("tensor"),
            P("tensor", ("dp", "seq")),
            P(),
            P(),
            P(),
            P(None, ("dp", "seq"), "tensor"),
            P(None, "tensor"),
            P("tensor", ("dp", "seq")),
            P(None, ("dp", "seq"), "tensor"),
            P(None, "tensor"),
            P("tensor", ("dp", "seq")),
            P(("dp", "seq"), "tensor"),
            P("tensor"),
            P("tensor", ("dp", "seq")),
            P(),
            P(),
            P(),
        ),
        check_vma=False,
    )
```

time: 2350 us -> 848 us (0.36)
  waiting for transfers between devices: 1660 us -> 311 us
  matrix products: 432 us -> 101 us
  starting transfers between devices: 3.48 us -> 137 us
  Pallas kernels: 0 us -> 84.3 us
  other arithmetic: 119 us -> 88.7 us
    reduce_scatter x14 -> x0, waiting for transfers between devices: 858 us -> none  [the longest x3 179 us: attend_back(): lax.psum_scatter(grad_values.reshape(length, width), 'seq', scatter_dimen...]
    psum x9 -> x0, waiting for transfers between devices: 475 us -> none  [the longest x4 192 us: tensor_grad(): return lax.psum(value, 'tensor')]
    dot_general x132 -> x48, matrix products: 432 us -> 101 us  [the longest x10 41.5 us: dot_plain(): return jnp.dot(left, right, preferred_element_type=F32)]
    ppermute x0 -> x102, waiting for transfers between devices: none -> 311 us  [the longest x26 142 us: permute(): return lax.ppermute(value, ('dp', 'tensor'), moves)]
    unnamed x31 -> x0, waiting for transfers between devices: 187 us -> none
    all_gather x6 -> x0, waiting for transfers between devices: 138 us -> none  [the longest x3 80.4 us: attend(): key_piece = split_heads(lax.all_gather(keys, 'seq', axis=0, tiled=True))]
    ppermute x0 -> x102, starting transfers between devices: none -> 137 us  [the longest x26 36.2 us: permute(): return lax.ppermute(value, ('dp', 'tensor'), moves)]
    pallas_call x0 -> x6, Pallas kernels: none -> 84.3 us  [kernel_call(): pl.pallas_call(kernel, out_shape=shapes, in_specs=[SCALARS] * scalars + [...]
  transfers between devices with their start and end apart: 30 -> 102, of which waited for: 27 -> 32; matrix products, arithmetic and copies ran while one was open for 13% -> 33% of each run, Pallas kernels for 0% -> 10%
where the time goes in v1:
time: 848 us; the launch traced here: 837 us
  waiting for transfers between devices  311 us (37%)
  starting transfers between devices  137 us (16%)
  local copies, waits for them, and re-layouts  111 us (13%)
  matrix products  101 us (12%)
  other arithmetic  88.7 us (10%)
  Pallas kernels  84.3 us (10%)
    ppermute x26, waiting for transfers between devices, permute(): return lax.ppermute(value, ('dp', 'tensor'), moves)  142 us
    pallas_call x6, Pallas kernels, kernel_call(): pl.pallas_call(kernel, out_shape=shapes, in_specs=[SCALARS] * scalars + [...  84.3 us
    ppermute x9, waiting for transfers between devices, from_z(): lax.ppermute(value, 'seq', [((i + step) % self.ring, i) for i in range(se...  67.4 us
    ppermute x12, waiting for transfers between devices, swap_z(): lax.ppermute(value, 'seq', [(i, i ^ 1 << bit) for i in range(self.ring)])  66.7 us
    unnamed x286, local copies, waits for them, and re-layouts  55.8 us
    dot_general x10, matrix products, dot_plain(): return jnp.dot(left, right, preferred_element_type=F32)  41.5 us
    ppermute x26, starting transfers between devices, permute(): return lax.ppermute(value, ('dp', 'tensor'), moves)  36.2 us
    ppermute x9, starting transfers between devices, from_z(): lax.ppermute(value, 'seq', [((i + step) % self.ring, i) for i in range(se...  34.4 us
  transfers between devices with their start and end apart: 102, of which 32 were waited for; matrix products, arithmetic and copies ran while one was open for 33% of the time, Pallas kernels for 10%

profile of v1, /device:TPU:1, one launch (start us, length us, event | category | flops | bytes accessed | tf_op | source)
XLA Modules:
  0.0 836.9 jit_solution(7118868050364530560)
XLA Ops:
  13.8 10.2 %collective-permute-done.3 = bf16[5376]{0:T(1024)(128)(2,1)S(1)} collective-permute-done((bf16[5376]{0:T(1024)(128)(2,1)S(1)}, bf16[5376]{0:T(1024)(128)(2,1)S(1)}, u32[]{:S(2)}, u32[]{:S(2)}) %collective-permute-start.3) | collective-permute-done | bytes 10784 | tf_op jit(solution)/shard_map/ppermute | solution.py:293
  31.5 7.8 compare_and_fusion.3
  57.0 15.9 %collective-permute-done.6 = bf16[256,768]{1,0:T(8,128)(2,1)} collective-permute-done((bf16[256,768]{1,0:T(8,128)(2,1)}, bf16[256,768]{1,0:T(8,128)(2,1)}, u32[]{:S(2)}, u32[]{:S(2)}) %collective-permute-start.6) | collective-permute-done | bytes 393248 | tf_op jit(solution)/shard_map/ppermute | solution.py:281
  75.5 17.6 %collective-permute-start.8 = (bf16[256,768]{1,0:T(8,128)(2,1)}, bf16[256,768]{1,0:T(8,128)(2,1)S(1)}, u32[]{:S(2)}, u32[]{:S(2)}) collective-permute-start(bf16[256,768]{1,0:T(8,128)(2,1)} %constant_dynamic-slice_fusion.10), channel_id=1, source_target_pairs={{6,0},{0,2},{2,4},{4,6},{7,1},{1,3},{3,5},{5,7},{14,8},{8,10},{10,... | collective-permute-start | bytes 1179656 | tf_op jit(solution)/shard_map/ppermute | solution.py:281
  93.9 12.6 %collective-permute-done.20 = bf16[256,768]{1,0:T(8,128)(2,1)S(1)} collective-permute-done((bf16[256,768]{1,0:T(8,128)(2,1)S(1)}, bf16[256,768]{1,0:T(8,128)(2,1)S(1)}, u32[]{:S(2)}, u32[]{:S(2)}) %collective-permute-start.20) | collective-permute-done | bytes 393248 | tf_op jit(solution)/shard_map/ppermute | solution.py:281
  111.8 6.6 collective-permute-done.22
  133.5 14.8 %shard_map.450 = (f32[384,512]{1,0:T(8,128)S(1)}, f32[8,512]{1,0:T(8,128)S(1)}) custom-call(s32[4]{0:T(128)S(1)} %convert_add_fusion.10.flags, s32[8]{0:T(128)S(1)} %stack.35.base, bf16[512,384]{1,0:T(8,128)(2,1)S(1)} %fusion.37.q_ref, bf16[2048,768]{1,0:T(8,128)(2,1)S(1)} %add_convert_fusion.2.kv_ref, s32[1,512]{1,0:T(1,128)S(1)} %bitcast.208, ...), custom_call_target="tpu_custom_call" | custom-call | flops 4026531840 | bytes 6291456 | tf_op jit(solution)/shard_map/pallas_call | solution.py:206
  149.8 63.2 %collective-permute-done.17 = bf16[3,768,384]{2,1,0:T(8,128)(2,1)S(1)} collective-permute-done((bf16[3,768,384]{2,1,0:T(8,128)(2,1)S(1)}, bf16[3,768,384]{2,1,0:T(8,128)(2,1)S(1)}, u32[]{:S(2)}, u32[]{:S(2)}) %collective-permute-start.17) | collective-permute-done | bytes 1769504 | tf_op jit(solution)/shard_map/ppermute | solution.py:293
  224.3 11.3 %multiply_convert_fusion.1 = (bf16[512,1536]{1,0:T(8,128)(2,1)S(1)}, f32[512,1536]{1,0:T(8,128)}, f32[512,1536]{1,0:T(8,128)}) fusion(f32[1536]{0:T(1024)S(1)} %get-tuple-element.237, bf16[768,1536]{1,0:T(8,128)(2,1)} %collective-permute-done.12, f32[512,768]{1,0:T(8,128)S(1)} %get-tuple-element.196, f32[768]{0:T(1024)S(1)} %get-tuple-element.139, ...), kind=kOutput, calls=%fused_computation.44 | convolution fusion | flops 1261830144 | bytes 11812864 | tf_op jit(solution)/shard_map/dot_general | solution.py:21
  243.4 9.9 %collective-permute-start.27 = (bf16[256,768]{1,0:T(8,128)(2,1)S(1)}, bf16[256,768]{1,0:T(8,128)(2,1)S(1)}, u32[]{:S(2)}, u32[]{:S(2)}) collective-permute-start(bf16[256,768]{1,0:T(8,128)(2,1)S(1)} %constant_dynamic-slice_fusion.7), channel_id=1, source_target_pairs={{2,0},{4,2},{6,4},{0,6},{3,1},{5,3},{7,5},{1,7},{10,8},{12,10},{14... | collective-permute-start | bytes 1179656 | tf_op jit(solution)/shard_map/ppermute | solution.py:281
  254.2 7.6 collective-permute-done.27
  263.7 19.5 %collective-permute-done.29 = bf16[256,768]{1,0:T(8,128)(2,1)S(1)} collective-permute-done((bf16[256,768]{1,0:T(8,128)(2,1)S(1)}, bf16[256,768]{1,0:T(8,128)(2,1)S(1)}, u32[]{:S(2)}, u32[]{:S(2)}) %collective-permute-start.29) | collective-permute-done | bytes 393248 | tf_op jit(solution)/shard_map/ppermute | solution.py:281
  289.2 14.8 %shard_map.452 = (f32[384,512]{1,0:T(8,128)S(1)}, f32[8,512]{1,0:T(8,128)S(1)}) custom-call(s32[4]{0:T(128)S(1)} %convert_add_fusion.8.flags, s32[8]{0:T(128)S(1)} %stack.35.base, bf16[512,384]{1,0:T(8,128)(2,1)S(1)} %fusion.35.q_ref, bf16[2048,768]{1,0:T(8,128)(2,1)S(1)} %add_convert_fusion.kv_ref, s32[1,512]{1,0:T(1,128)S(1)} %bitcast.216, ...), custom_call_target="tpu_custom_call" | custom-call | flops 4026531840 | bytes 6291456 | tf_op jit(solution)/shard_map/pallas_call | solution.py:206
  308.2 12.0 %multiply_convert_fusion = (bf16[512,1536]{1,0:T(8,128)(2,1)S(1)}, f32[512,1536]{1,0:T(8,128)}, f32[512,1536]{1,0:T(8,128)}) fusion(f32[1536]{0:T(1024)S(1)} %get-tuple-element.236, bf16[768,1536]{1,0:T(8,128)(2,1)} %collective-permute-done.35, f32[512,768]{1,0:T(8,128)S(1)} %get-tuple-element.184, f32[768]{0:T(1024)S(1)} %get-tuple-element.132, ...), kind=kOutput, calls=%fused_computation.31 | convolution fusion | flops 1261830144 | bytes 11812864 | tf_op jit(solution)/shard_map/dot_general | solution.py:21
  320.2 22.2 %collective-permute-done.36 = bf16[1536,768]{1,0:T(8,128)(2,1)S(1)} collective-permute-done((bf16[1536,768]{1,0:T(8,128)(2,1)S(1)}, bf16[1536,768]{1,0:T(8,128)(2,1)S(1)}, u32[]{:S(2)}, u32[]{:S(2)}) %collective-permute-start.36) | collective-permute-done | bytes 2359328 | tf_op jit(solution)/shard_map/ppermute | solution.py:293
  373.1 21.4 %shard_map.453 = (bf16[384,512]{1,0:T(8,128)(2,1)S(1)}, bf16[2048,768]{1,0:T(8,128)(2,1)S(1)}) custom-call(s32[4]{0:T(128)S(1)} %convert_add_fusion.8.flags, s32[8]{0:T(128)S(1)} %stack.35.base, bf16[512,384]{1,0:T(8,128)(2,1)S(1)} %fusion.35.q_ref, bf16[2048,768]{1,0:T(8,128)(2,1)} %copy-done.25, bf16[512,384]{1,0:T(8,128)(2,1)S(1)} %copy.74.do_ref, ...), custom_call_target="tpu_custom_call" | custom-call | flops 4026531840 | bytes 6291456 | tf_op jit(solution)/shard_map/pallas_call | solution.py:206
  431.1 7.4 shard_map.455
  461.6 7.3 collective-permute-start.97
  500.9 10.4 %collective-permute-start.64 = (bf16[256,768]{1,0:T(8,128)(2,1)S(1)}, bf16[256,768]{1,0:T(8,128)(2,1)S(1)}, u32[]{:S(2)}, u32[]{:S(2)}) collective-permute-start(bf16[256,768]{1,0:T(8,128)(2,1)S(1)} %copy-done.95), channel_id=1, source_target_pairs={{0,4},{2,6},{4,0},{6,2},{1,5},{3,7},{5,1},{7,3},{8,12},{10,14},{12... | collective-permute-start | bytes 1179656 | tf_op jit(solution)/shard_map/ppermute | solution.py:284
  511.3 8.7 %collective-permute-done.98 = bf16[2,4,48,3072]{3,2,1,0:T(8,128)(2,1)S(1)} collective-permute-done((bf16[2,4,48,3072]{3,2,1,0:T(8,128)(2,1)S(1)}, bf16[2,4,48,3072]{3,2,1,0:T(8,128)(2,1)S(1)}, u32[]{:S(2)}, u32[]{:S(2)}) %collective-permute-start.98) | collective-permute-done | bytes 2359328 | tf_op jit(solution)/shard_map/ppermute | solution.py:293
  520.0 13.5 %collective-permute-start.66 = (bf16[256,768]{1,0:T(8,128)(2,1)S(1)}, bf16[256,768]{1,0:T(8,128)(2,1)S(1)}, u32[]{:S(2)}, u32[]{:S(2)}) collective-permute-start(bf16[256,768]{1,0:T(8,128)(2,1)S(1)} %fusion.40), channel_id=1, source_target_pairs={{0,6},{2,0},{4,2},{6,4},{1,7},{3,1},{5,3},{7,5},{8,14},{10,8},{12,... | collective-permute-start | bytes 1179656 | tf_op jit(solution)/shard_map/ppermute | solution.py:284
  562.4 21.5 %shard_map.454 = (bf16[384,512]{1,0:T(8,128)(2,1)S(1)}, bf16[2048,768]{1,0:T(8,128)(2,1)S(1)}) custom-call(s32[4]{0:T(128)S(1)} %copy-done.16, s32[8]{0:T(128)S(1)} %stack.35.base, bf16[512,384]{1,0:T(8,128)(2,1)S(1)} %copy-done.20, bf16[2048,768]{1,0:T(8,128)(2,1)} %copy-done.23, bf16[512,384]{1,0:T(8,128)(2,1)S(1)} %copy.76.do_ref, ...), custom_call_target="tpu_custom_call" | custom-call | flops 4026531840 | bytes 6291456 | tf_op jit(solution)/shard_map/pallas_call | solution.py:206
  657.8 7.3 collective-permute-done.96
  688.4 14.2 %collective-permute-done.69 = bf16[512,768]{1,0:T(8,128)(2,1)S(1)} collective-permute-done((bf16[512,768]{1,0:T(8,128)(2,1)S(1)}, bf16[512,768]{1,0:T(8,128)(2,1)S(1)}, u32[]{:S(2)}, u32[]{:S(2)}) %collective-permute-start.69) | collective-permute-done | bytes 786464 | tf_op jit(solution)/shard_map/ppermute | solution.py:293
  703.9 14.0 %collective-permute-done.90 = bf16[2,48,1536]{2,1,0:T(8,128)(2,1)S(1)} collective-permute-done((bf16[2,48,1536]{2,1,0:T(8,128)(2,1)S(1)}, bf16[2,48,1536]{2,1,0:T(8,128)(2,1)S(1)}, u32[]{:S(2)}, u32[]{:S(2)}) %collective-permute-start.90) | collective-permute-done | bytes 294944 | tf_op jit(solution)/shard_map/ppermute | solution.py:278
  722.6 6.2 collective-permute-done.56
  729.8 12.7 %collective-permute-done.91 = bf16[1,48,1536]{2,1,0:T(8,128)(2,1)S(1)} collective-permute-done((bf16[1,48,1536]{2,1,0:T(8,128)(2,1)S(1)}, bf16[1,48,1536]{2,1,0:T(8,128)(2,1)S(1)}, u32[]{:S(2)}, u32[]{:S(2)}) %collective-permute-start.91) | collective-permute-done | bytes 147488 | tf_op jit(solution)/shard_map/ppermute | solution.py:278
  758.2 15.2 %collective-permute-done.80 = bf16[1,2,4,48,3072]{4,3,2,1,0:T(8,128)(2,1)} collective-permute-done((bf16[1,2,4,48,3072]{4,3,2,1,0:T(8,128)(2,1)}, bf16[1,2,4,48,3072]{4,3,2,1,0:T(8,128)(2,1)}, u32[]{:S(2)}, u32[]{:S(2)}) %collective-permute-start.80) | collective-permute-done | bytes 2359328 | tf_op jit(solution)/shard_map/ppermute | solution.py:275
  788.1 6.0 collective-permute-done.81
  794.1 10.5 %collective-permute-done.82 = bf16[4,48,3072]{2,1,0:T(8,128)(2,1)S(1)} collective-permute-done((bf16[4,48,3072]{2,1,0:T(8,128)(2,1)S(1)}, bf16[4,48,3072]{2,1,0:T(8,128)(2,1)S(1)}, u32[]{:S(2)}, u32[]{:S(2)}) %collective-permute-start.82) | collective-permute-done | bytes 1179680 | tf_op jit(solution)/shard_map/ppermute | solution.py:293
  807.3 14.2 %collective-permute-done.83 = bf16[2,48,3072]{2,1,0:T(8,128)(2,1)S(1)} collective-permute-done((bf16[2,48,3072]{2,1,0:T(8,128)(2,1)S(1)}, bf16[2,48,3072]{2,1,0:T(8,128)(2,1)S(1)}, u32[]{:S(2)}, u32[]{:S(2)}) %collective-permute-start.83) | collective-permute-done | bytes 589856 | tf_op jit(solution)/shard_map/ppermute | solution.py:278
  823.2 12.5 %collective-permute-done.84 = bf16[1,48,3072]{2,1,0:T(8,128)(2,1)S(1)} collective-permute-done((bf16[1,48,3072]{2,1,0:T(8,128)(2,1)S(1)}, bf16[1,48,3072]{2,1,0:T(8,128)(2,1)S(1)}, u32[]{:S(2)}, u32[]{:S(2)}) %collective-permute-start.84) | collective-permute-done | bytes 294944 | tf_op jit(solution)/shard_map/ppermute | solution.py:278
  (736 shorter events, 384.0 us)
Async XLA Ops:
  0.7 39.5 %collective-permute-start = (bf16[512,768]{1,0:T(8,128)(2,1)}, bf16[512,768]{1,0:T(8,128)(2,1)S(1)}, u32[]{:S(2)}, u32[]{:S(2)}) collective-permute-start(bf16[512,768]{1,0:T(8,128)(2,1)} %bitcast.240), channel_id=1, source_target_pairs={{0,8},{8,0},{16,24},{24,16},{1,9},{9,1},{17,25},{25,17},{2,10},{10... | collective-permute-start | bytes 2359304 | tf_op jit(solution)/shard_map/ppermute | solution.py:269
  0.8 125.1 %collective-permute-start.2 = (bf16[3,768,384]{2,1,0:T(8,128)(2,1)}, bf16[3,768,384]{2,1,0:T(8,128)(2,1)}, u32[]{:S(2)}, u32[]{:S(2)}) collective-permute-start(bf16[3,768,384]{2,1,0:T(8,128)(2,1)} %param.31), channel_id=1, source_target_pairs={{8,0},{9,1},{1,8},{0,9},{24,16},{25,17},{17,24},{16,25},{10,2},{11... | collective-permute-start | bytes 5308424 | tf_op jit(solution)/shard_map/ppermute | solution.py:293
  9.1 38.0 %collective-permute-start.16 = (bf16[512,768]{1,0:T(8,128)(2,1)}, bf16[512,768]{1,0:T(8,128)(2,1)S(1)}, u32[]{:S(2)}, u32[]{:S(2)}) collective-permute-start(bf16[512,768]{1,0:T(8,128)(2,1)} %bitcast.241), channel_id=1, source_target_pairs={{0,8},{8,0},{16,24},{24,16},{1,9},{9,1},{17,25},{25,17},{2,10},{10... | collective-permute-start | bytes 2359304 | tf_op jit(solution)/shard_map/ppermute | solution.py:269
  48.9 57.6 %collective-permute-start.20 = (bf16[256,768]{1,0:T(8,128)(2,1)S(1)}, bf16[256,768]{1,0:T(8,128)(2,1)S(1)}, u32[]{:S(2)}, u32[]{:S(2)}) collective-permute-start(bf16[256,768]{1,0:T(8,128)(2,1)S(1)} %constant_dynamic-slice_fusion.8), channel_id=1, source_target_pairs={{4,0},{6,2},{0,4},{2,6},{5,1},{7,3},{1,5},{3,7},{12,8},{14,10},{8,... | collective-permute-start | bytes 1179656 | tf_op jit(solution)/shard_map/ppermute | solution.py:281
  56.2 50.3 %collective-permute-start.5 = (bf16[256,768]{1,0:T(8,128)(2,1)}, bf16[256,768]{1,0:T(8,128)(2,1)S(1)}, u32[]{:S(2)}, u32[]{:S(2)}) collective-permute-start(bf16[256,768]{1,0:T(8,128)(2,1)} %collective-permute-done.4), channel_id=1, source_target_pairs={{0,8},{8,0},{16,24},{24,16},{1,9},{9,1},{17,25},{25,17},{2,10},{10... | collective-permute-start | bytes 1179656 | tf_op jit(solution)/shard_map/ppermute | solution.py:269
  121.5 102.2 %collective-permute-start.12 = (bf16[768,1536]{1,0:T(8,128)(2,1)S(1)}, bf16[768,1536]{1,0:T(8,128)(2,1)}, u32[]{:S(2)}, u32[]{:S(2)}) collective-permute-start(bf16[768,1536]{1,0:T(8,128)(2,1)S(1)} %copy-done.102), channel_id=1, source_target_pairs={{8,0},{9,1},{1,8},{0,9},{24,16},{25,17},{17,24},{16,25},{10,2},{11... | collective-permute-start | bytes 7077896 | tf_op jit(solution)/shard_map/ppermute | solution.py:293
  123.6 112.0 %collective-permute-start.13 = (bf16[1536,768]{1,0:T(8,128)(2,1)S(1)}, bf16[1536,768]{1,0:T(8,128)(2,1)}, u32[]{:S(2)}, u32[]{:S(2)}) collective-permute-start(bf16[1536,768]{1,0:T(8,128)(2,1)S(1)} %copy-done.103), channel_id=1, source_target_pairs={{8,0},{9,1},{1,8},{0,9},{24,16},{25,17},{17,24},{16,25},{10,2},{11... | collective-permute-start | bytes 7077896 | tf_op jit(solution)/shard_map/ppermute | solution.py:293
  124.6 114.9 %collective-permute-start.26 = (bf16[3,768,384]{2,1,0:T(8,128)(2,1)}, bf16[3,768,384]{2,1,0:T(8,128)(2,1)S(1)}, u32[]{:S(2)}, u32[]{:S(2)}) collective-permute-start(bf16[3,768,384]{2,1,0:T(8,128)(2,1)} %param.43), channel_id=1, source_target_pairs={{8,0},{9,1},{1,8},{0,9},{24,16},{25,17},{17,24},{16,25},{10,2},{11... | collective-permute-start | bytes 5308424 | tf_op jit(solution)/shard_map/ppermute | solution.py:293
  125.9 87.1 %collective-permute-start.17 = (bf16[3,768,384]{2,1,0:T(8,128)(2,1)S(1)}, bf16[3,768,384]{2,1,0:T(8,128)(2,1)S(1)}, u32[]{:S(2)}, u32[]{:S(2)}) collective-permute-start(bf16[3,768,384]{2,1,0:T(8,128)(2,1)S(1)} %copy-done.107), channel_id=1, source_target_pairs={{8,0},{9,1},{1,8},{0,9},{24,16},{25,17},{17,24},{16,25},{10,2},{11... | collective-permute-start | bytes 5308424 | tf_op jit(solution)/shard_map/ppermute | solution.py:293
  148.4 72.7 %collective-permute-start.24 = (bf16[384,768]{1,0:T(8,128)(2,1)S(1)}, bf16[384,768]{1,0:T(8,128)(2,1)S(1)}, u32[]{:S(2)}, u32[]{:S(2)}) collective-permute-start(bf16[384,768]{1,0:T(8,128)(2,1)S(1)} %copy-done.109), channel_id=1, source_target_pairs={{8,0},{9,1},{1,8},{0,9},{24,16},{25,17},{17,24},{16,25},{10,2},{11... | collective-permute-start | bytes 1769480 | tf_op jit(solution)/shard_map/ppermute | solution.py:293
  221.1 82.9 %collective-permute-start.33 = (bf16[384,768]{1,0:T(8,128)(2,1)S(1)}, bf16[384,768]{1,0:T(8,128)(2,1)S(1)}, u32[]{:S(2)}, u32[]{:S(2)}) collective-permute-start(bf16[384,768]{1,0:T(8,128)(2,1)S(1)} %copy-done.110), channel_id=1, source_target_pairs={{8,0},{9,1},{1,8},{0,9},{24,16},{25,17},{17,24},{16,25},{10,2},{11... | collective-permute-start | bytes 1769480 | tf_op jit(solution)/shard_map/ppermute | solution.py:293
  222.3 85.9 %collective-permute-start.35 = (bf16[768,1536]{1,0:T(8,128)(2,1)}, bf16[768,1536]{1,0:T(8,128)(2,1)}, u32[]{:S(2)}, u32[]{:S(2)}) collective-permute-start(bf16[768,1536]{1,0:T(8,128)(2,1)} %param.46), channel_id=1, source_target_pairs={{8,0},{9,1},{1,8},{0,9},{24,16},{25,17},{17,24},{16,25},{10,2},{11... | collective-permute-start | bytes 7077896 | tf_op jit(solution)/shard_map/ppermute | solution.py:293
  305.9 39.9 %collective-permute-start.15 = (bf16[512,768]{1,0:T(8,128)(2,1)S(1)}, bf16[512,768]{1,0:T(8,128)(2,1)}, u32[]{:S(2)}, u32[]{:S(2)}) collective-permute-start(bf16[512,768]{1,0:T(8,128)(2,1)S(1)} %get-tuple-element.186), channel_id=1, source_target_pairs={{0,1},{9,8},{16,17},{25,24},{2,3},{11,10},{18,19},{27,26},{4,5},{1... | collective-permute-start | bytes 2359304 | tf_op jit(solution)/shard_map/ppermute | solution.py:293
  365.0 53.4 %collective-permute-start.38 = (bf16[512,768]{1,0:T(8,128)(2,1)}, bf16[512,768]{1,0:T(8,128)(2,1)}, u32[]{:S(2)}, u32[]{:S(2)}) collective-permute-start(bf16[512,768]{1,0:T(8,128)(2,1)} %get-tuple-element.211), channel_id=1, source_target_pairs={{0,1},{9,8},{16,17},{25,24},{2,3},{11,10},{18,19},{27,26},{4,5},{1... | collective-permute-start | bytes 2359304 | tf_op jit(solution)/shard_map/ppermute | solution.py:293
  411.1 59.8 %collective-permute-start.92 = (bf16[1,2,4,48,1536]{4,3,2,1,0:T(8,128)(2,1)}, bf16[1,2,4,48,1536]{4,3,2,1,0:T(8,128)(2,1)}, u32[]{:S(2)}, u32[]{:S(2)}) collective-permute-start(bf16[1,2,4,48,1536]{4,3,2,1,0:T(8,128)(2,1)} %dynamic-slice_bitcast_fusion.3), channel_id=1, source_target_pairs={{0,16},{8,24},{16,0},{24,8},{1,17},{9,25},{17,1},{25,9},{2,18},{10... | collective-permute-start | bytes 3538952 | tf_op jit(solution)/shard_map/ppermute | solution.py:275
  420.7 40.3 %collective-permute-start.48 = (bf16[256,768]{1,0:T(8,128)(2,1)}, bf16[256,768]{1,0:T(8,128)(2,1)}, u32[]{:S(2)}, u32[]{:S(2)}) collective-permute-start(bf16[256,768]{1,0:T(8,128)(2,1)} %dynamic-slice_convert_fusion.2), channel_id=1, source_target_pairs={{0,8},{8,0},{16,24},{24,16},{1,9},{9,1},{17,25},{25,17},{2,10},{10... | collective-permute-start | bytes 1179656 | tf_op jit(solution)/shard_map/ppermute | solution.py:269
  422.1 39.5 %collective-permute-start.43 = (bf16[256,768]{1,0:T(8,128)(2,1)}, bf16[256,768]{1,0:T(8,128)(2,1)}, u32[]{:S(2)}, u32[]{:S(2)}) collective-permute-start(bf16[256,768]{1,0:T(8,128)(2,1)} %fusion.48), channel_id=1, source_target_pairs={{0,2},{2,4},{4,6},{6,0},{1,3},{3,5},{5,7},{7,1},{8,10},{10,12},{12... | collective-permute-start | bytes 1179656 | tf_op jit(solution)/shard_map/ppermute | solution.py:284
  422.9 46.0 %collective-permute-start.45 = (bf16[256,768]{1,0:T(8,128)(2,1)}, bf16[256,768]{1,0:T(8,128)(2,1)}, u32[]{:S(2)}, u32[]{:S(2)}) collective-permute-start(bf16[256,768]{1,0:T(8,128)(2,1)} %fusion.47), channel_id=1, source_target_pairs={{0,4},{2,6},{4,0},{6,2},{1,5},{3,7},{5,1},{7,3},{8,12},{10,14},{12... | collective-permute-start | bytes 1179656 | tf_op jit(solution)/shard_map/ppermute | solution.py:284
  424.7 44.3 %collective-permute-start.47 = (bf16[256,768]{1,0:T(8,128)(2,1)}, bf16[256,768]{1,0:T(8,128)(2,1)}, u32[]{:S(2)}, u32[]{:S(2)}) collective-permute-start(bf16[256,768]{1,0:T(8,128)(2,1)} %fusion.46), channel_id=1, source_target_pairs={{0,6},{2,0},{4,2},{6,4},{1,7},{3,1},{5,3},{7,5},{8,14},{10,8},{12,... | collective-permute-start | bytes 1179656 | tf_op jit(solution)/shard_map/ppermute | solution.py:284
  461.6 39.2 %collective-permute-start.97 = (bf16[2,4,48,3072]{3,2,1,0:T(8,128)(2,1)S(1)}, bf16[2,4,48,3072]{3,2,1,0:T(8,128)(2,1)S(1)}, u32[]{:S(2)}, u32[]{:S(2)}) collective-permute-start(bf16[2,4,48,3072]{3,2,1,0:T(8,128)(2,1)S(1)} %copy-done.45), channel_id=1, source_target_pairs={{9,8},{8,9},{25,24},{24,25},{11,10},{10,11},{27,26},{26,27},{13,12... | collective-permute-start | bytes 7077896 | tf_op jit(solution)/shard_map/ppermute | solution.py:293
  469.0 51.0 %collective-permute-start.98 = (bf16[2,4,48,3072]{3,2,1,0:T(8,128)(2,1)S(1)}, bf16[2,4,48,3072]{3,2,1,0:T(8,128)(2,1)S(1)}, u32[]{:S(2)}, u32[]{:S(2)}) collective-permute-start(bf16[2,4,48,3072]{3,2,1,0:T(8,128)(2,1)S(1)} %copy-done.54), channel_id=1, source_target_pairs={{9,0},{8,1},{0,8},{1,9},{25,16},{24,17},{16,24},{17,25},{11,2},{10... | collective-permute-start | bytes 7077896 | tf_op jit(solution)/shard_map/ppermute | solution.py:293
  469.1 82.2 %collective-permute-start.87 = (bf16[1,2,4,48,1536]{4,3,2,1,0:T(8,128)(2,1)}, bf16[1,2,4,48,1536]{4,3,2,1,0:T(8,128)(2,1)}, u32[]{:S(2)}, u32[]{:S(2)}) collective-permute-start(bf16[1,2,4,48,1536]{4,3,2,1,0:T(8,128)(2,1)} %dynamic-slice_bitcast_fusion.4), channel_id=1, source_target_pairs={{0,16},{8,24},{16,0},{24,8},{1,17},{9,25},{17,1},{25,9},{2,18},{10... | collective-permute-start | bytes 3538952 | tf_op jit(solution)/shard_map/ppermute | solution.py:275
  477.6 57.2 %collective-permute-start.67 = (bf16[256,768]{1,0:T(8,128)(2,1)}, bf16[256,768]{1,0:T(8,128)(2,1)}, u32[]{:S(2)}, u32[]{:S(2)}) collective-permute-start(bf16[256,768]{1,0:T(8,128)(2,1)} %dynamic-slice_convert_fusion), channel_id=1, source_target_pairs={{0,8},{8,0},{16,24},{24,16},{1,9},{9,1},{17,25},{25,17},{2,10},{10... | collective-permute-start | bytes 1179656 | tf_op jit(solution)/shard_map/ppermute | solution.py:269
  480.6 56.4 %collective-permute-start.62 = (bf16[256,768]{1,0:T(8,128)(2,1)}, bf16[256,768]{1,0:T(8,128)(2,1)}, u32[]{:S(2)}, u32[]{:S(2)}) collective-permute-start(bf16[256,768]{1,0:T(8,128)(2,1)} %fusion.42), channel_id=1, source_target_pairs={{0,2},{2,4},{4,6},{6,0},{1,3},{3,5},{5,7},{7,1},{8,10},{10,12},{12... | collective-permute-start | bytes 1179656 | tf_op jit(solution)/shard_map/ppermute | solution.py:284
  500.9 38.7 %collective-permute-start.64 = (bf16[256,768]{1,0:T(8,128)(2,1)S(1)}, bf16[256,768]{1,0:T(8,128)(2,1)S(1)}, u32[]{:S(2)}, u32[]{:S(2)}) collective-permute-start(bf16[256,768]{1,0:T(8,128)(2,1)S(1)} %copy-done.95), channel_id=1, source_target_pairs={{0,4},{2,6},{4,0},{6,2},{1,5},{3,7},{5,1},{7,3},{8,12},{10,14},{12... | collective-permute-start | bytes 1179656 | tf_op jit(solution)/shard_map/ppermute | solution.py:284
  540.8 143.3 %collective-permute-start.99 = (bf16[1,4,48,3072]{3,2,1,0:T(8,128)(2,1)}, bf16[1,4,48,3072]{3,2,1,0:T(8,128)(2,1)}, u32[]{:S(2)}, u32[]{:S(2)}) collective-permute-start(bf16[1,4,48,3072]{3,2,1,0:T(8,128)(2,1)} %constant_dynamic-slice_fusion.1), channel_id=1, source_target_pairs={{0,16},{8,24},{16,0},{24,8},{1,17},{9,25},{17,1},{25,9},{2,18},{10... | collective-permute-start | bytes 3538952 | tf_op jit(solution)/shard_map/ppermute | solution.py:275
  545.7 87.6 %collective-permute-start.68 = (bf16[256,768]{1,0:T(8,128)(2,1)}, bf16[256,768]{1,0:T(8,128)(2,1)}, u32[]{:S(2)}, u32[]{:S(2)}) collective-permute-start(bf16[256,768]{1,0:T(8,128)(2,1)} %get-tuple-element.168), channel_id=1, source_target_pairs={{0,8},{8,0},{16,24},{24,16},{1,9},{9,1},{17,25},{25,17},{2,10},{10... | collective-permute-start | bytes 1179656 | tf_op jit(solution)/shard_map/ppermute | solution.py:269
  551.2 93.3 %collective-permute-start.95 = (bf16[2,48,1536]{2,1,0:T(8,128)(2,1)}, bf16[2,48,1536]{2,1,0:T(8,128)(2,1)}, u32[]{:S(2)}, u32[]{:S(2)}) collective-permute-start(bf16[2,48,1536]{2,1,0:T(8,128)(2,1)} %dynamic-slice_bitcast_fusion.15), channel_id=1, source_target_pairs={{0,2},{2,0},{4,6},{6,4},{1,3},{3,1},{5,7},{7,5},{8,10},{10,8},{12,... | collective-permute-start | bytes 884744 | tf_op jit(solution)/shard_map/ppermute | solution.py:278
  554.0 127.7 %collective-permute-start.88 = (bf16[4,48,1536]{2,1,0:T(8,128)(2,1)}, bf16[4,48,1536]{2,1,0:T(8,128)(2,1)}, u32[]{:S(2)}, u32[]{:S(2)}) collective-permute-start(bf16[4,48,1536]{2,1,0:T(8,128)(2,1)} %get-tuple-element.214), channel_id=1, source_target_pairs={{9,8},{8,9},{25,24},{24,25},{11,10},{10,11},{27,26},{26,27},{13,12... | collective-permute-start | bytes 1769480 | tf_op jit(solution)/shard_map/ppermute | solution.py:293
  557.3 125.3 %collective-permute-start.89 = (bf16[4,48,1536]{2,1,0:T(8,128)(2,1)}, bf16[4,48,1536]{2,1,0:T(8,128)(2,1)}, u32[]{:S(2)}, u32[]{:S(2)}) collective-permute-start(bf16[4,48,1536]{2,1,0:T(8,128)(2,1)} %get-tuple-element.215), channel_id=1, source_target_pairs={{9,0},{8,1},{0,8},{1,9},{25,16},{24,17},{16,24},{17,25},{11,2},{10... | collective-permute-start | bytes 1769480 | tf_op jit(solution)/shard_map/ppermute | solution.py:293
  676.8 71.0 %collective-permute-start.70 = (bf16[2,4,48,1536]{3,2,1,0:T(8,128)(2,1)S(1)}, bf16[2,4,48,1536]{3,2,1,0:T(8,128)(2,1)}, u32[]{:S(2)}, u32[]{:S(2)}) collective-permute-start(bf16[2,4,48,1536]{3,2,1,0:T(8,128)(2,1)S(1)} %copy-done.50), channel_id=1, source_target_pairs={{9,8},{8,9},{25,24},{24,25},{11,10},{10,11},{27,26},{26,27},{13,12... | collective-permute-start | bytes 3538952 | tf_op jit(solution)/shard_map/ppermute | solution.py:293
  719.9 53.5 %collective-permute-start.80 = (bf16[1,2,4,48,3072]{4,3,2,1,0:T(8,128)(2,1)}, bf16[1,2,4,48,3072]{4,3,2,1,0:T(8,128)(2,1)}, u32[]{:S(2)}, u32[]{:S(2)}) collective-permute-start(bf16[1,2,4,48,3072]{4,3,2,1,0:T(8,128)(2,1)} %dynamic-slice_bitcast_fusion.2), channel_id=1, source_target_pairs={{0,16},{8,24},{16,0},{24,8},{1,17},{9,25},{17,1},{25,9},{2,18},{10... | collective-permute-start | bytes 7077896 | tf_op jit(solution)/shard_map/ppermute | solution.py:275
  (191 other events, 3217.2 us)

commit v2 on v1

--- a/solution.py
+++ b/solution.py
@@ -15,6 +15,7 @@
 NT = (((1,), (1,)), ((), ()))
 TN = (((0,), (0,)), ((), ()))
 KEY_BLOCK = 512
+DOCS = 4
 
 
 def dot_plain(left, right):
@@ -66,17 +67,40 @@
     return lanes >= HEAD_DIM if head % 2 else lanes < HEAD_DIM
 
 
-def allowed_in(index, block, base, low_ref, high_ref, count):
-    part = block // 2
-    place = lax.broadcasted_iota(jnp.int32, (block, count), 0)
-    place = place + jnp.where(place < part, base[2 * index], base[2 * index + 1] - part)
-    return (place >= low_ref[...]) & (place < high_ref[...])
-
-
-def over_blocks(flags, length, block, body, skipped):
+class Mask:
+    def __init__(self, causal, starts, segments, first_row):
+        self.causal, self.starts, self.first_row = causal, starts, first_row
+        segments = segments[...]
+        low = high = jnp.zeros_like(segments)
+        for number in range(DOCS):
+            low = jnp.where(segments == number, starts[number], low)
+            high = jnp.where(segments == number, starts[number + 1], high)
+        self.count = segments.shape[1]
+        if causal:
+            place = first_row + lax.broadcasted_iota(jnp.int32, segments.shape, 1)
+            high = jnp.minimum(high, place + 1)
+        self.low, self.high = low, high
+
+    def allowed(self, index, block):
+        place = lax.broadcasted_iota(jnp.int32, (block, self.count), 0) + index * block
+        return (place >= self.low) & (place < self.high)
+
+    def flag(self, index, block, ends):
+        start, stop = index * block, (index + 1) * block
+        low, low_last = self.starts[ends[0]], self.starts[ends[1]]
+        high_first, high = self.starts[ends[0] + 1], self.starts[ends[1] + 1]
+        if self.causal:
+            high = jnp.minimum(high, self.first_row + self.count)
+            high_first = jnp.minimum(high_first, self.first_row + 1)
+        active = (low < stop) & (high > start)
+        full = (low_last <= start) & (high_first >= stop)
+        return jnp.where(active, jnp.where(full, 2, 1), 0)
+
+
+def over_blocks(mask, ends, length, block, body, skipped):
     @pl.loop(0, length // block)
     def _(index):
-        flag = flags[index]
+        flag = mask.flag(index, block, ends)
         rows = pl.ds(pl.multiple_of(index * block, block), block)
 
         @pl.when(flag == 0)
@@ -92,68 +116,60 @@
             body(index, rows, False)
 
 
-def forward_kernel(
-    block, flags, base, q_ref, kv_ref, low_ref, high_ref, out_ref, lse_ref, masked_q, acc, top
-):
-    count, width = q_ref.shape
-    heads = width // HEAD_DIM
+def forward_start(q_ref, masked_q, acc, top):
+    heads = q_ref.shape[1] // HEAD_DIM
     for head in range(heads):
         pair = q_ref[:, head_columns(head)]
         masked_q[head] = jnp.where(own_lanes(pair.shape, head), pair, jnp.zeros_like(pair))
     acc[...] = jnp.zeros_like(acc)
     top[...] = jnp.full_like(top, NEG)
 
-    def body(index, rows, partial):
+
+def forward_block(index, rows, partial, block, kv_ref, mask, masked_q, acc, top):
+    heads, count = masked_q.shape[:2]
+    width = heads * HEAD_DIM
+    if partial:
+        allowed = mask.allowed(index, block)
+    for head in range(heads):
+        cols = head_columns(head)
+        scores = lax.dot_general(kv_ref[rows, cols], masked_q[head], NT, preferred_element_type=F32)
         if partial:
-            allowed = allowed_in(index, block, base, low_ref, high_ref, count)
-        for head in range(heads):
-            cols = head_columns(head)
-            scores = lax.dot_general(
-                kv_ref[rows, cols], masked_q[head], NT, preferred_element_type=F32
-            )
-            if partial:
-                scores = jnp.where(allowed, scores, NEG)
-            old = top[head : head + 1, :]
-            new = jnp.maximum(old, jnp.max(scores, axis=0, keepdims=True))
-            weights = jnp.exp(scores - new).astype(BF16)
-            vals = kv_ref[rows, width + cols.start : width + cols.stop]
-            vals = jnp.where(own_lanes(vals.shape, head), vals, jnp.ones_like(vals))
-            acc[head] = acc[head] * jnp.exp(old - new) + lax.dot_general(
-                vals, weights, TN, preferred_element_type=F32
-            )
-            top[head : head + 1, :] = new
-
-    over_blocks(flags, kv_ref.shape[0], block, body, lambda rows: None)
+            scores = jnp.where(allowed, scores, NEG)
+        old = top[head : head + 1, :]
+        new = jnp.maximum(old, jnp.max(scores, axis=0, keepdims=True))
+        weights = jnp.exp(scores - new).astype(BF16)
+        vals = kv_ref[rows, width + cols.start : width + cols.stop]
+        vals = jnp.where(own_lanes(vals.shape, head), vals, jnp.ones_like(vals))
+        acc[head] = acc[head] * jnp.exp(old - new) + lax.dot_general(
+            vals, weights, TN, preferred_element_type=F32
+        )
+        top[head : head + 1, :] = new
+
+
+def forward_end(out_ref, lse_ref, acc, top):
     lse_ref[...] = jnp.zeros_like(lse_ref)
-    for head in range(heads):
+    for head in range(acc.shape[0]):
         first = head % 2 * HEAD_DIM
         total = acc[head, HEAD_DIM - first : HEAD_DIM - first + 1, :]
         out_ref[head_rows(head), :] = acc[head, first : first + HEAD_DIM, :] / total
         lse_ref[head : head + 1, :] = top[head : head + 1, :] + jnp.log(total)
 
 
-def backward_kernel(
-    block,
-    flags,
-    base,
-    q_ref,
-    kv_ref,
-    do_ref,
-    dot_ref,
-    out_ref,
-    lse_ref,
-    low_ref,
-    high_ref,
-    dq_ref,
-    dkv_ref,
-    masked_q,
-    masked_do,
-    delta,
-    dq,
+def forward_kernel(
+    block, causal, starts, ends, segments, q_ref, kv_ref, out_ref, lse_ref, masked_q, acc, top
 ):
-    count, width = q_ref.shape
-    heads = width // HEAD_DIM
-    for head in range(heads):
+    mask = Mask(causal, starts, segments, ends[2])
+    forward_start(q_ref, masked_q, acc, top)
+
+    def body(index, rows, partial):
+        forward_block(index, rows, partial, block, kv_ref, mask, masked_q, acc, top)
+
+    over_blocks(mask, ends, kv_ref.shape[0], block, body, lambda rows: None)
+    forward_end(out_ref, lse_ref, acc, top)
+
+
+def backward_start(q_ref, do_ref, dot_ref, out_ref, masked_q, masked_do, delta, dq):
+    for head in range(masked_q.shape[0]):
         pair = q_ref[:, head_columns(head)]
         keep = own_lanes(pair.shape, head)
         masked_q[head] = jnp.where(keep, pair, jnp.zeros_like(pair))
@@ -165,97 +181,656 @@
         )
     dq[...] = jnp.zeros_like(dq)
 
+
+def backward_block(
+    index, rows, partial, block, mask, kv_ref, lse_ref, dkv_ref, masked_q, masked_do, delta, dq
+):
+    heads = masked_q.shape[0]
+    width = heads * HEAD_DIM
+    if partial:
+        allowed = mask.allowed(index, block)
+    for pair in range(heads // 2):
+        cols = head_columns(2 * pair)
+        later = slice(width + cols.start, width + cols.stop)
+        keys, vals = kv_ref[rows, cols], kv_ref[rows, later]
+        dk = dv = 0.0
+        for head in (2 * pair, 2 * pair + 1):
+            scores = lax.dot_general(keys, masked_q[head], NT, preferred_element_type=F32)
+            probs = jnp.exp(scores - lse_ref[head : head + 1, :])
+            if partial:
+                probs = jnp.where(allowed, probs, 0.0)
+            dprobs = lax.dot_general(vals, masked_do[head], NT, preferred_element_type=F32)
+            draw = (probs * (dprobs - delta[head : head + 1, :])).astype(BF16)
+            probs = probs.astype(BF16)
+            dv = dv + jnp.dot(probs, masked_do[head], preferred_element_type=F32)
+            dk = dk + jnp.dot(draw, masked_q[head], preferred_element_type=F32)
+            first = head % 2 * HEAD_DIM
+            both = lax.dot_general(keys, draw, TN, preferred_element_type=F32)
+            dq[head_rows(head), :] += both[first : first + HEAD_DIM]
+        dkv_ref[rows, cols] = dk.astype(BF16)
+        dkv_ref[rows, later] = dv.astype(BF16)
+
+
+def backward_end(dq_ref, dq):
+    dq_ref[...] = (dq[...] * HEAD_DIM ** (-0.5)).astype(BF16)
+
+
+def backward_kernel(
+    block,
+    causal,
+    tokens,
+    starts,
+    ends,
+    segments,
+    q_ref,
+    kv_ref,
+    do_ref,
+    dot_ref,
+    out_ref,
+    lse_ref,
+    *refs,
+):
+    dq_ref, dkv_ref, masked_q, masked_do, delta, dq = refs[tokens:]
+    mask = Mask(causal, starts, segments, ends[2])
+    backward_start(q_ref, do_ref, dot_ref, out_ref, masked_q, masked_do, delta, dq)
+
     def body(index, rows, partial):
-        if partial:
-            allowed = allowed_in(index, block, base, low_ref, high_ref, count)
-        for pair in range(heads // 2):
-            cols = head_columns(2 * pair)
-            later = slice(width + cols.start, width + cols.stop)
-            keys, vals = kv_ref[rows, cols], kv_ref[rows, later]
-            dk = dv = 0.0
-            for head in (2 * pair, 2 * pair + 1):
-                scores = lax.dot_general(keys, masked_q[head], NT, preferred_element_type=F32)
-                probs = jnp.exp(scores - lse_ref[head : head + 1, :])
-                if partial:
-                    probs = jnp.where(allowed, probs, 0.0)
-                dprobs = lax.dot_general(vals, masked_do[head], NT, preferred_element_type=F32)
-                draw = (probs * (dprobs - delta[head : head + 1, :])).astype(BF16)
-                probs = probs.astype(BF16)
-                dv = dv + jnp.dot(probs, masked_do[head], preferred_element_type=F32)
-                dk = dk + jnp.dot(draw, masked_q[head], preferred_element_type=F32)
-                first = head % 2 * HEAD_DIM
-                both = lax.dot_general(keys, draw, TN, preferred_element_type=F32)
-                dq[head_rows(head), :] += both[first : first + HEAD_DIM]
-            dkv_ref[rows, cols] = dk.astype(BF16)
-            dkv_ref[rows, later] = dv.astype(BF16)
+        backward_block(
+            index, rows, partial, block, mask, kv_ref, lse_ref, dkv_ref, masked_q, masked_do, delta, dq
+        )
 
     def skipped(rows):
-        dkv_ref[rows, :] = jnp.zeros((block, 2 * width), BF16)
-
-    over_blocks(flags, kv_ref.shape[0], block, body, skipped)
-    dq_ref[...] = (dq[...] * HEAD_DIM ** (-0.5)).astype(BF16)
+        dkv_ref[rows, :] = jnp.zeros((block, dkv_ref.shape[1]), BF16)
+
+    over_blocks(mask, ends, kv_ref.shape[0], block, body, skipped)
+    backward_end(dq_ref, dq)
 
 
 SCALARS = pl.BlockSpec(memory_space=pltpu.SMEM)
 VECTORS = pl.BlockSpec(memory_space=pltpu.VMEM)
 
 
-def kernel_call(kernel, inputs, scalars, shapes, scratch, work, limit):
-    length, count, width = work
-    product = 2 * length * count * width
-    return pl.pallas_call(
-        kernel,
-        out_shape=shapes,
-        in_specs=[SCALARS] * scalars + [VECTORS] * (len(inputs) - scalars),
-        out_specs=(VECTORS,) * len(shapes),
-        scratch_shapes=scratch,
-        compiler_params=pltpu.CompilerParams(vmem_limit_bytes=limit),
-        cost_estimate=pl.CostEstimate(
-            flops=5 * product, bytes_accessed=8 * length * width, transcendentals=0
-        ),
-    )(*inputs)
+ANYWHERE = pl.BlockSpec(memory_space=pl.ANY)
+
+
+def cost_of(kv, count, width, products):
+    flops = 2 * products * kv.shape[0] * count * width
+    return pl.CostEstimate(flops=flops, bytes_accessed=flops // 512, transcendentals=0)
+
+
+def forward_scratch(count, width):
+    heads = width // HEAD_DIM
+    return [
+        pltpu.VMEM((heads, count, 128), BF16),
+        pltpu.VMEM((heads, 128, count), F32),
+        pltpu.VMEM((8, count), F32),
+    ]
+
+
+def backward_scratch(count, width):
+    heads = width // HEAD_DIM
+    return [
+        pltpu.VMEM((heads, count, 128), BF16),
+        pltpu.VMEM((heads, count, 128), BF16),
+        pltpu.VMEM((8, count), F32),
+        pltpu.VMEM((width, count), F32),
+    ]
 
 
 def attend(queries, kv, mask):
     count, width = queries.shape
-    heads = width // HEAD_DIM
-    flags, base, low, high = mask
-    return kernel_call(
-        functools.partial(forward_kernel, KEY_BLOCK),
-        (flags, base, queries, kv, low, high),
-        2,
-        (jax.ShapeDtypeStruct((width, count), F32), jax.ShapeDtypeStruct((8, count), F32)),
-        [
-            pltpu.VMEM((heads, count, 128), BF16),
-            pltpu.VMEM((heads, 128, count), F32),
-            pltpu.VMEM((8, count), F32),
-        ],
-        (kv.shape[0], count, width),
-        40 << 20,
-    )
-
-
-def attend_back(queries, kv, grad_out, grad_out_t, output, lse, mask):
+    causal, starts, ends, segments = mask
+    return pl.pallas_call(
+        functools.partial(forward_kernel, KEY_BLOCK, causal),
+        out_shape=(
+            jax.ShapeDtypeStruct((width, count), F32),
+            jax.ShapeDtypeStruct((8, count), F32),
+        ),
+        in_specs=[SCALARS] * 2 + [VECTORS] * 3,
+        out_specs=(VECTORS,) * 2,
+        scratch_shapes=forward_scratch(count, width),
+        compiler_params=pltpu.CompilerParams(vmem_limit_bytes=40 << 20),
+        cost_estimate=cost_of(kv, count, width, 2),
+    )(starts, ends, segments, queries, kv)
+
+
+def attend_back(queries, kv, grad_out, grad_out_t, output, lse, mask, tokens=()):
     count, width = queries.shape
-    heads = width // HEAD_DIM
-    flags, base, low, high = mask
-    return kernel_call(
-        functools.partial(backward_kernel, KEY_BLOCK),
-        (flags, base, queries, kv, grad_out, grad_out_t, output, lse, low, high),
-        2,
-        (
+    causal, starts, ends, segments = mask
+    return pl.pallas_call(
+        functools.partial(backward_kernel, KEY_BLOCK, causal, len(tokens)),
+        out_shape=(
             jax.ShapeDtypeStruct((width, count), BF16),
             jax.ShapeDtypeStruct(kv.shape, BF16),
         ),
-        [
-            pltpu.VMEM((heads, count, 128), BF16),
-            pltpu.VMEM((heads, count, 128), BF16),
-            pltpu.VMEM((8, count), F32),
-            pltpu.VMEM((width, count), F32),
-        ],
-        (kv.shape[0], count, width),
-        48 << 20,
-    )
+        in_specs=[SCALARS] * 2 + [VECTORS] * 7 + [ANYWHERE] * len(tokens),
+        out_specs=(VECTORS,) * 2,
+        scratch_shapes=backward_scratch(count, width),
+        compiler_params=pltpu.CompilerParams(vmem_limit_bytes=48 << 20),
+        cost_estimate=cost_of(kv, count, width, 5),
+    )(starts, ends, segments, queries, kv, grad_out, grad_out_t, output, lse, *tokens)
+
+
+MESH = pl.DeviceIdType.MESH
+DMA = pltpu.SemaphoreType.DMA
+
+
+class Here:
+    def __init__(self, ring):
+        self.ring = ring
+        self.d, self.z, self.y = (lax.axis_index(a) for a in ("dp", "seq", "tensor"))
+        self.core, self.x = lax.rem(self.d, 2), lax.div(self.d, 2)
+        self.other_d = self.d + 1 - 2 * self.core
+        self.partner = (self.other_d, self.z, self.y)
+        self.right = (self.d, self.z + 1, self.y)
+        self.left = (self.d, self.z - 1, self.y)
+
+    def meet(self, devices):
+        barrier = pltpu.get_barrier_semaphore()
+        wanted = 0
+        for condition, device in devices:
+
+            @pl.when(condition)
+            def _(device=device):
+                pl.semaphore_signal(barrier, inc=1, device_id=device, device_id_type=MESH)
+
+            wanted = wanted + jnp.where(condition, 1, 0)
+        pl.semaphore_wait(barrier, wanted)
+
+    def neighbours(self):
+        return [
+            (self.core >= 0, self.partner),
+            (self.z + 1 < self.ring, self.right),
+            (self.z > 0, self.left),
+        ]
+
+
+def remote(source, target, sent, received, device):
+    return pltpu.make_async_remote_copy(
+        src_ref=source,
+        dst_ref=target,
+        send_sem=sent,
+        recv_sem=received,
+        device_id=device,
+        device_id_type=MESH,
+    )
+
+
+class Gather:
+    def __init__(self, here, rows_ref, sems):
+        self.here, self.rows_ref = here, rows_ref
+        self.count = rows_ref.shape[0] // here.ring
+        self.sent, self.got, self.core_sent, self.core_got = sems
+
+    def half(self, shard, core):
+        part = self.count // 2
+        start = pl.multiple_of(shard * self.count + core * part, part)
+        return self.rows_ref.at[pl.ds(start, part)]
+
+    def ways(self, step):
+        here = self.here
+        z, ring = here.z, here.ring
+        return [
+            (0, z - step, z >= step, z - step + 1, (z + 1 < ring) & (z + 1 >= step), here.right),
+            (1, z + step, z + step < ring, z + step - 1, (z > 0) & (z + step <= ring), here.left),
+        ]
+
+    def along(self, way, step, shard, device):
+        view = self.half(shard, self.here.core)
+        return remote(view, view, self.sent.at[way, step], self.got.at[way, step], device)
+
+    def across(self, way, step, shard, core):
+        view = self.half(shard, core)
+        return remote(
+            view, view, self.core_sent.at[way, step], self.core_got.at[way, step], self.here.partner
+        )
+
+    def start(self, step):
+        for way, _, _, shard, sends, device in self.ways(step):
+
+            @pl.when(sends)
+            def _(way=way, shard=shard, device=device):
+                self.along(way, step, shard, device).start()
+
+    def arrive(self, step):
+        for way, shard, comes, _, _, device in self.ways(step):
+
+            @pl.when(comes)
+            def _(way=way, shard=shard, device=device):
+                self.along(way, step, shard, self.here.partner).wait_recv()
+                self.across(way, step, shard, self.here.core).start()
+
+    def finish(self, step):
+        for way, shard, comes, out, sends, device in self.ways(step):
+
+            @pl.when(sends)
+            def _(way=way, out=out, device=device):
+                self.along(way, step, out, device).wait_send()
+
+            @pl.when(comes)
+            def _(way=way, shard=shard):
+                self.across(way, step, shard, self.here.core).wait_send()
+                self.across(way, step, shard, 1 - self.here.core).wait_recv()
+
+
+class Fetch:
+    def __init__(self, here, inputs, outputs, sems):
+        self.here, self.inputs, self.outputs = here, inputs, outputs
+        self.y_sent, self.y_got, self.x_sent, self.x_got, self.core_sent, self.core_got = sems
+        self.x_partner = (here.d + 2 - 4 * lax.rem(here.x, 2), here.z, here.y)
+        self.y_partner = (here.other_d, here.z, 1 - here.y)
+
+    def devices(self):
+        here = self.here
+        return [(here.core >= 0, self.y_partner), (here.core == 1, self.x_partner)]
+
+    def part(self, ref, which):
+        rows = ref.shape[0] // 2
+        return ref.at[pl.ds(pl.multiple_of(which * rows, rows), rows)]
+
+    def over_y(self, k):
+        which = lax.rem(self.here.x, 2)
+        return remote(
+            self.part(self.inputs[k], which),
+            self.part(self.outputs[k], which),
+            self.y_sent.at[k],
+            self.y_got.at[k],
+            self.y_partner,
+        )
+
+    def over_x(self, k, which):
+        view = self.part(self.outputs[k], which)
+        return remote(view, view, self.x_sent.at[k], self.x_got.at[k], self.x_partner)
+
+    def across(self, k):
+        return remote(
+            self.inputs[k], self.outputs[k], self.core_sent.at[k], self.core_got.at[k], self.here.partner
+        )
+
+    def begin(self):
+        @pl.when(self.here.core == 0)
+        def _():
+            for k in range(min(2, len(self.inputs))):
+                self.over_y(k).start()
+
+        @pl.when(self.here.core == 1)
+        def _():
+            for k in range(len(self.inputs)):
+                self.across(k).start()
+
+    def advance(self, k):
+        @pl.when(self.here.core == 0)
+        def _():
+            self.over_y(k).wait_send()
+            if k + 2 < len(self.inputs):
+                self.over_y(k + 2).start()
+
+        @pl.when(self.here.core == 1)
+        def _():
+            self.over_y(k).wait_recv()
+            self.over_x(k, lax.rem(self.here.x, 2)).start()
+
+    def end(self):
+        @pl.when(self.here.core == 0)
+        def _():
+            for k in range(len(self.inputs)):
+                self.across(k).wait_recv()
+
+        @pl.when(self.here.core == 1)
+        def _():
+            for k in range(len(self.inputs)):
+                self.over_x(k, lax.rem(self.here.x, 2)).wait_send()
+                self.over_x(k, 1 - lax.rem(self.here.x, 2)).wait_recv()
+                self.across(k).wait_send()
+
+
+def gather_sems(ring):
+    return [DMA((2, ring))] * 4
+
+
+def fetch_sems(number):
+    return [DMA((number,))] * 6
+
+
+def opening_kernel(ring, number, *refs):
+    inputs, outputs, sems = refs[: 4 + number], refs[4 + number : 8 + 2 * number], refs[8 + 2 * number :]
+    source, target, segments, vectors = inputs[:4]
+    source_all, target_all, segments_out, vectors_out = outputs[:4]
+    shard_sems, vector_sems = sems[:3], sems[3:6]
+    here = Here(ring)
+    fetch = Fetch(here, inputs[4:], outputs[4:], sems[14:])
+    here.meet(here.neighbours() + fetch.devices())
+    count = source.shape[0]
+    own = pl.ds(pl.multiple_of(here.z * count, count), count)
+    moves = [
+        (source, source_all.at[own]),
+        (target, target_all.at[own]),
+        (segments, segments_out),
+    ]
+    owner = here.core == here.y
+
+    def shard_copy(k):
+        start, end = moves[k]
+        sent, got, copied = shard_sems
+        return (
+            remote(start, end, sent.at[k], got.at[k], here.partner),
+            pltpu.make_async_copy(start, end, copied.at[k]),
+        )
+
+    def vector_copy():
+        sent, got, copied = vector_sems
+        return (
+            remote(vectors, vectors_out, sent, got, fetch.y_partner),
+            pltpu.make_async_copy(vectors, vectors_out, copied),
+        )
+
+    def wait_shard(k):
+        across, local = shard_copy(k)
+
+        @pl.when(owner)
+        def _():
+            across.wait_send()
+            local.wait()
+
+        @pl.when(jnp.logical_not(owner))
+        def _():
+            across.wait_recv()
+
+    @pl.when(owner)
+    def _():
+        for k in range(3):
+            across, local = shard_copy(k)
+            across.start()
+            local.start()
+
+    @pl.when(here.core == 0)
+    def _():
+        across, local = vector_copy()
+        across.start()
+        local.start()
+
+    fetch.begin()
+    gathers = [Gather(here, source_all, sems[6:10]), Gather(here, target_all, sems[10:14])]
+    slots = 2 * (ring - 1)
+    done = 0
+    for k, gather in enumerate(gathers):
+        wait_shard(k)
+        for step in range(1, ring):
+            gather.start(step)
+            slot = k * (ring - 1) + step
+            while done < number * slot // slots:
+                fetch.advance(done)
+                done += 1
+            gather.arrive(step)
+    for gather in gathers:
+        for step in range(1, ring):
+            gather.finish(step)
+    wait_shard(2)
+    fetch.end()
+    across, local = vector_copy()
+
+    @pl.when(here.core == 0)
+    def _():
+        across.wait_send()
+        local.wait()
+
+    @pl.when(here.core == 1)
+    def _():
+        across.wait_recv()
+
+
+def opening(ring, source, target, segments, vectors, weights):
+    inputs = (source, target, segments, vectors) + tuple(weights)
+    count, model = source.shape
+    rows = jax.ShapeDtypeStruct((ring * count, model), BF16)
+    shapes = (rows, rows) + tuple(jax.ShapeDtypeStruct(v.shape, v.dtype) for v in inputs[2:])
+    number = len(weights)
+    return pl.pallas_call(
+        functools.partial(opening_kernel, ring, number),
+        out_shape=shapes,
+        in_specs=[VECTORS] * 4 + [ANYWHERE] * number,
+        out_specs=(ANYWHERE,) * 2 + (VECTORS,) * 2 + (ANYWHERE,) * number,
+        scratch_shapes=[DMA((3,))] * 3 + [DMA] * 3 + gather_sems(ring) * 2 + fetch_sems(number),
+        compiler_params=pltpu.CompilerParams(collective_id=1, has_side_effects=True),
+    )(*inputs)
+
+
+def gather_attend_kernel(block, causal, ring, tokens, starts, segments, q_ref, kv_ref, own_ref, *refs):
+    out_ref, lse_ref, all_ref, masked_q, acc, top, copied = refs[tokens : tokens + 7]
+    here = Here(ring)
+    gather = Gather(here, all_ref, refs[tokens + 7 :])
+    here.meet(here.neighbours())
+    count = own_ref.shape[0]
+    first_row = pl.multiple_of(here.z * count, count)
+    local = pltpu.make_async_copy(own_ref, all_ref.at[pl.ds(first_row, count)], copied)
+    local.start()
+    local.wait()
+    gather.start(1)
+    mask = Mask(causal, starts, segments, first_row)
+    forward_start(q_ref, masked_q, acc, top)
+
+    @pl.loop(0, kv_ref.shape[0] // block)
+    def _(index):
+        rows = pl.ds(pl.multiple_of(index * block, block), block)
+        forward_block(index, rows, True, block, kv_ref, mask, masked_q, acc, top)
+
+        @pl.when((index >= 1) & (index < ring))
+        def _():
+            gather.arrive(index)
+
+        @pl.when((index >= 1) & (index < ring - 1))
+        def _():
+            gather.start(index + 1)
+
+    forward_end(out_ref, lse_ref, acc, top)
+
+    @pl.loop(1, ring)
+    def _(step):
+        gather.finish(step)
+
+
+def gather_attend(ring, queries, kv, mask, own, tokens):
+    count, width = queries.shape
+    causal, starts, _, segments = mask
+    return pl.pallas_call(
+        functools.partial(gather_attend_kernel, KEY_BLOCK, causal, ring, len(tokens)),
+        out_shape=(
+            jax.ShapeDtypeStruct((width, count), F32),
+            jax.ShapeDtypeStruct((8, count), F32),
+            jax.ShapeDtypeStruct((ring * own.shape[0], own.shape[1]), BF16),
+        ),
+        in_specs=[SCALARS] + [VECTORS] * 4 + [ANYWHERE] * len(tokens),
+        out_specs=(VECTORS, VECTORS, ANYWHERE),
+        scratch_shapes=forward_scratch(count, width) + [DMA] + gather_sems(ring),
+        compiler_params=pltpu.CompilerParams(
+            vmem_limit_bytes=40 << 20, collective_id=2, has_side_effects=True
+        ),
+        cost_estimate=cost_of(kv, count, width, 2),
+    )(starts, segments, queries, kv, own, *tokens)
+
+
+class Return:
+    def __init__(self, here, terms_ref, query_ref, out_ref, refs):
+        self.here, self.terms_ref, self.query_ref, self.out_ref = here, terms_ref, query_ref, out_ref
+        self.mine, self.outgoing, self.from_core, self.arrived, self.total = refs[:5]
+        self.core_sent, self.core_got, self.sent, self.got, self.end_sent, self.end_got = refs[5:]
+        self.count = terms_ref.shape[0] // here.ring
+        self.part = self.count // 2
+        self.order = list(range(1, here.ring)) + [0]
+
+    def devices(self):
+        here = self.here
+        found = [(here.core >= 0, here.partner)]
+        for step in range(1, here.ring):
+            found.append((here.core >= 0, self.to(step)))
+        return found
+
+    def to(self, step):
+        here = self.here
+        return (here.d, lax.rem(here.z + step, here.ring), here.y)
+
+    def half(self, core):
+        return pl.ds(pl.multiple_of(core * self.part, self.part), self.part)
+
+    def rows(self, step, core):
+        start = lax.rem(self.here.z + step, self.here.ring) * self.count + core * self.part
+        return pl.ds(pl.multiple_of(start, self.part), self.part)
+
+    def across(self, step):
+        other = 1 - self.here.core
+        if step == 0 and self.query_ref is not None:
+            source = self.mine.at[self.half(other)]
+        else:
+            source = self.terms_ref.at[self.rows(step, other)]
+        return remote(
+            source,
+            self.from_core.at[step],
+            self.core_sent.at[step],
+            self.core_got.at[step],
+            self.here.partner,
+        )
+
+    def along(self, step):
+        return remote(
+            self.outgoing.at[step], self.arrived.at[step], self.sent.at[step], self.got.at[step], self.to(step)
+        )
+
+    def begin(self):
+        if self.query_ref is not None:
+            start = pl.multiple_of(self.here.z * self.count, self.count)
+            own = self.terms_ref[pl.ds(start, self.count), :].astype(F32)
+            self.mine[...] = (own + self.query_ref[...].astype(F32)).astype(BF16)
+        for step in self.order:
+            self.across(step).start()
+
+    def send(self):
+        for step in self.order:
+            self.across(step).wait_recv()
+            if step == 0 and self.query_ref is not None:
+                local = self.mine[self.half(self.here.core), :]
+            else:
+                local = self.terms_ref[self.rows(step, self.here.core), :]
+            both = local.astype(F32) + self.from_core[step].astype(F32)
+            if step:
+                self.outgoing[step] = both.astype(BF16)
+                self.along(step).start()
+            else:
+                self.total[...] = both
+
+    def end(self):
+        for step in range(1, self.here.ring):
+            self.along(step).wait_recv()
+            self.total[...] += self.arrived[step].astype(F32)
+        own, other = self.half(self.here.core), self.half(1 - self.here.core)
+        self.out_ref[own, :] = self.total[...].astype(BF16)
+        for half, waits in ((own, False), (other, True)):
+            view = self.out_ref.at[half]
+            copy = remote(view, view, self.end_sent, self.end_got, self.here.partner)
+            if waits:
+                copy.wait_recv()
+            else:
+                copy.start()
+                copy.wait_send()
+        for step in self.order:
+            self.across(step).wait_send()
+            if step:
+                self.along(step).wait_send()
+
+
+def return_scratch(ring, count, model):
+    part = count // 2
+    return (
+        [pltpu.VMEM((count, model), BF16)]
+        + [pltpu.VMEM((ring, part, model), BF16)] * 3
+        + [pltpu.VMEM((part, model), F32)]
+        + [DMA((ring,))] * 4
+        + [DMA] * 2
+    )
+
+
+def return_kernel(ring, tokens, terms_ref, query_ref, *refs):
+    returned = Return(Here(ring), terms_ref, query_ref, refs[tokens], refs[tokens + 1 :])
+    returned.here.meet(returned.devices())
+    returned.begin()
+    returned.send()
+    returned.end()
+
+
+def return_rows(ring, number, terms, query, tokens=()):
+    rows, model = terms.shape
+    count = rows // ring
+    return pl.pallas_call(
+        functools.partial(return_kernel, ring, len(tokens)),
+        out_shape=jax.ShapeDtypeStruct((count, model), BF16),
+        in_specs=[VECTORS] * 2 + [ANYWHERE] * len(tokens),
+        out_specs=VECTORS,
+        scratch_shapes=return_scratch(ring, count, model),
+        compiler_params=pltpu.CompilerParams(
+            vmem_limit_bytes=40 << 20, collective_id=number, has_side_effects=True
+        ),
+    )(terms, query, *tokens)
+
+
+def back_return_kernel(
+    block,
+    causal,
+    ring,
+    has_query,
+    tokens,
+    starts,
+    segments,
+    q_ref,
+    kv_ref,
+    do_ref,
+    dot_ref,
+    out_ref,
+    lse_ref,
+    terms_ref,
+    *refs,
+):
+    query_ref, refs = (refs[0], refs[1:]) if has_query else (None, refs)
+    dq_ref, dkv_ref, sum_ref, masked_q, masked_do, delta, dq = refs[tokens : tokens + 7]
+    here = Here(ring)
+    returned = Return(here, terms_ref, query_ref, sum_ref, refs[tokens + 7 :])
+    here.meet(returned.devices())
+    returned.begin()
+    mask = Mask(causal, starts, segments, here.z * q_ref.shape[0])
+    backward_start(q_ref, do_ref, dot_ref, out_ref, masked_q, masked_do, delta, dq)
+    returned.send()
+
+    @pl.loop(0, kv_ref.shape[0] // block)
+    def _(index):
+        rows = pl.ds(pl.multiple_of(index * block, block), block)
+        backward_block(
+            index, rows, True, block, mask, kv_ref, lse_ref, dkv_ref, masked_q, masked_do, delta, dq
+        )
+
+    backward_end(dq_ref, dq)
+    returned.end()
+
+
+def back_return(ring, number, queries, kv, grad_out, grad_out_t, output, lse, mask, terms, query, tokens):
+    count, width = queries.shape
+    model = terms.shape[1]
+    causal, starts, _, segments = mask
+    more = (terms,) if query is None else (terms, query)
+    return pl.pallas_call(
+        functools.partial(
+            back_return_kernel, KEY_BLOCK, causal, ring, query is not None, len(tokens)
+        ),
+        out_shape=(
+            jax.ShapeDtypeStruct((width, count), BF16),
+            jax.ShapeDtypeStruct(kv.shape, BF16),
+            jax.ShapeDtypeStruct((count, model), BF16),
+        ),
+        in_specs=[SCALARS] + [VECTORS] * (7 + len(more)) + [ANYWHERE] * len(tokens),
+        out_specs=(VECTORS,) * 3,
+        scratch_shapes=backward_scratch(count, width) + return_scratch(ring, count, model),
+        compiler_params=pltpu.CompilerParams(
+            vmem_limit_bytes=56 << 20, collective_id=number, has_side_effects=True
+        ),
+        cost_estimate=cost_of(kv, count, width, 5),
+    )(starts, segments, queries, kv, grad_out, grad_out_t, output, lse, *more, *tokens)
 
 
 class Places:
@@ -305,45 +880,6 @@
     def hand_out(self, rows):
         other = self.permute(rows, lambda d, y: (d, 1 - y) if d % 2 != y else None)
         return jnp.where(self.core == self.y, rows, other)
-
-    def gather_rows(self, own):
-        part = own.shape[0] // 2
-        half = lax.dynamic_slice_in_dim(own, self.core * part, part, 0)
-        pieces = [own]
-        for step in range(1, self.ring):
-            mine = self.from_z(half, step)
-            pieces += [mine, self.swap_core(mine)]
-        return jnp.concatenate(pieces, axis=0)
-
-    def bases(self, count):
-        part = count // 2
-        places = [self.z * count, self.z * count + part]
-        for step in range(1, self.ring):
-            shard = (self.z + step) % self.ring * count
-            places += [shard + self.core * part, shard + (1 - self.core) * part]
-        return jnp.stack(places).astype(jnp.int32)
-
-    def return_rows(self, piece_of, count):
-        part = count // 2
-        total = None
-        for step in list(range(1, self.ring)) + [0]:
-            piece = rounded(piece_of(step))
-            if step == 0:
-                mine = lax.dynamic_slice_in_dim(piece, self.core * part, part, 0)
-                others = lax.dynamic_slice_in_dim(piece, (1 - self.core) * part, part, 0)
-            else:
-                mine, others = piece[:part], piece[part:]
-            both = mine + self.swap_core(others.astype(BF16)).astype(F32)
-            if step:
-                both = self.to_z(both.astype(BF16), step).astype(F32)
-            total = both if total is None else total + both
-        total = rounded(total)
-        other = self.swap_core(total.astype(BF16)).astype(F32)
-        return jnp.where(
-            self.core == 0,
-            jnp.concatenate([total, other]),
-            jnp.concatenate([other, total]),
-        )
 
     def scatter(self, grad, x_first):
         rows, columns = grad.shape
@@ -391,44 +927,38 @@
         return whole, halves
 
 
-def mask_of(query_seg, key_seg, first_row, base, causal, count):
-    low = jnp.sum(key_seg[None, :] < query_seg[:, None], axis=1, dtype=jnp.int32)
-    high = jnp.sum(key_seg[None, :] <= query_seg[:, None], axis=1, dtype=jnp.int32)
-    if causal:
-        high = jnp.minimum(high, first_row + jnp.arange(count, dtype=jnp.int32) + 1)
-    part = count // 2
-    active = (jnp.min(low) < base + part) & (jnp.max(high) > base)
-    full = (jnp.max(low) <= base) & (jnp.min(high) >= base + part)
-    per = KEY_BLOCK // part
-    active = jnp.any(active.reshape(-1, per), axis=1)
-    full = jnp.all(full.reshape(-1, per), axis=1)
-    flags = active.astype(jnp.int32) + full.astype(jnp.int32)
-    return (flags, base, low[None], high[None])
-
-
-def attention_forward(place, query_in, key_in, weights, out_weight, out_bias, mask):
+def starts_of(segments):
+    numbers = jnp.arange(8, dtype=jnp.int32)
+    return jnp.sum(segments[None, :] < numbers[:, None], axis=1, dtype=jnp.int32)
+
+
+def mask_of(query_seg, key_starts, first_row, causal):
+    ends = jnp.stack([query_seg[0], query_seg[-1], first_row])
+    return (causal, key_starts, ends, query_seg[None])
+
+
+def projected(query_in, key_in, weights):
     w_q, w_kv, b_q, b_kv = weights
     scale = HEAD_DIM ** (-0.5)
     queries = ((dot_plain(query_in, w_q) + b_q).astype(BF16) * scale).astype(BF16)
-    kv = (dot_plain(key_in, w_kv) + b_kv).astype(BF16)
-    output, lse = attend(queries, kv, mask)
+    return queries, (dot_plain(key_in, w_kv) + b_kv).astype(BF16)
+
+
+def attention_output(place, queries, kv, output, lse, out_weight, out_bias):
     mixed = output.astype(BF16)
     branch = place.core_sum(dot_first(mixed, out_weight)) + out_bias.astype(F32)
     return (branch, (queries, kv, output, lse, mixed))
 
 
-def attention_backward(grad_branch, saved, query_in, key_in, weights, out_weight, mask):
+def attention_backward(grad_branch, saved, query_in, key_in, weights, out_weight, back):
     queries, kv, output, lse, mixed = saved
     w_q, w_kv = weights[:2]
-    count, width = queries.shape
+    width = queries.shape[1]
     grad_mixed = dot_last(grad_branch, out_weight).astype(BF16)
     grad_mixed_t = dot_last(out_weight, grad_branch).astype(BF16)
-    grad_q, grad_kv = attend_back(queries, kv, grad_mixed, grad_mixed_t, output, lse, mask)
+    grad_q, grad_kv, *more = back(queries, kv, grad_mixed, grad_mixed_t, output, lse)
     grad_query_in = dot_general_q(grad_q, w_q)
-
-    def grad_key_in(step):
-        return dot_last(grad_kv[step * count : (step + 1) * count], w_kv)
-
+    grad_key_in = dot_last(grad_kv, w_kv).astype(BF16)
     grad_qkv = jnp.concatenate(
         [
             lax.dot_general(query_in, grad_q, (((0,), (1,)), ((), ())), preferred_element_type=F32),
@@ -442,7 +972,7 @@
     grad_bias = jnp.concatenate(
         [jnp.sum(grad_q.astype(F32), axis=1), column_sum(grad_kv[:, width:])]
     )
-    return (grad_query_in, grad_key_in, grad_qkv, grad_out, grad_bias)
+    return (grad_query_in, grad_key_in, grad_qkv, grad_out, grad_bias, *more)
 
 
 def dot_general_q(grad_q, w_q):
@@ -504,44 +1034,64 @@
     place = Places(lax.axis_size("dp"), lax.axis_size("seq"))
     first_row = place.z * count
 
-    xs = place.own_pair(source[0])
-    x_all = place.gather_rows(xs)
-    enc_qkv = place.fetch_weight(enc_qkv)
-    vectors = place.fetch_weight(
-        jnp.concatenate(
-            [
-                enc_qv_bias.reshape(-1),
-                dec_self_bias.reshape(-1),
-                dec_cross_bias.reshape(-1),
-                enc_ff_in_bias,
-                dec_ff_in_bias,
-            ]
-        )
-    )
-    ts = place.own_pair(target[0])
-    t_all = place.gather_rows(ts)
-    segments = place.own_pair(jnp.concatenate([source_segments, target_segments]))
-    dec_self = place.fetch_weight(dec_self)
-    enc_proj = place.fetch_weight(enc_proj)
-    enc_ff_in = place.fetch_weight(enc_ff_in)
-    enc_ff_out = place.fetch_weight(enc_ff_out)
-    dec_self_proj = place.fetch_weight(dec_self_proj)
-    dec_cross = place.fetch_weight(dec_cross)
-    dec_cross_proj = place.fetch_weight(dec_cross_proj)
+    ring = place.ring
+    width = enc_qkv.shape[2]
+    hidden_units = enc_ff_in.shape[1]
+
+    vectors = jnp.concatenate(
+        [
+            enc_qv_bias.reshape(-1),
+            dec_self_bias.reshape(-1),
+            dec_cross_bias.reshape(-1),
+            enc_ff_in_bias,
+            dec_ff_in_bias,
+        ]
+    ).astype(F32)
+    (
+        x_all,
+        t_all,
+        segments,
+        vectors,
+        enc_qkv,
+        dec_self,
+        enc_proj,
+        dec_self_proj,
+        enc_ff_in,
+        enc_ff_out,
+        dec_cross,
+        dec_cross_proj,
+    ) = opening(
+        ring,
+        source[0],
+        target[0],
+        jnp.concatenate([source_segments, target_segments]),
+        vectors.reshape(-1, 128),
+        (
+            enc_qkv.reshape(-1, width),
+            dec_self.reshape(-1, width),
+            enc_proj,
+            dec_self_proj,
+            enc_ff_in,
+            enc_ff_out,
+            dec_cross.reshape(-1, width),
+            dec_cross_proj,
+        ),
+    )
+    vectors = vectors.reshape(-1)
+    xs = lax.dynamic_slice_in_dim(x_all, first_row, count, 0)
+    ts = lax.dynamic_slice_in_dim(t_all, first_row, count, 0)
     dec_ff_in = place.fetch_weight(dec_ff_in)
     dec_ff_out = place.fetch_weight(dec_ff_out)
     enc_cot = place.own_pair(enc_cotangent[0])
     dec_cot = place.own_pair(dec_cotangent[0])
 
-    width = enc_qkv.shape[2]
-    hidden_units = enc_ff_in.shape[1]
     marks = [0, 2 * width, 4 * width, 6 * width, 6 * width + hidden_units, 6 * width + 2 * hidden_units]
     enc_qv_bias, dec_self_bias, dec_cross_bias, enc_ff_in_bias, dec_ff_in_bias = (
         vectors[a:b] for a, b in zip(marks[:-1], marks[1:])
     )
 
     def prepared(qkv, bias):
-        bias = bias.astype(F32)
+        qkv = qkv.reshape(3, model, width)
         b_kv = jnp.concatenate([jnp.zeros((width,), F32), bias[width:]])
         return (qkv[0], jnp.concatenate([qkv[1], qkv[2]], axis=1), bias[:width], b_kv)
 
@@ -552,12 +1102,14 @@
     source_keys, target_keys = segments[0], segments[1]
     source_own = lax.dynamic_slice_in_dim(source_keys, first_row, count, 0)
     target_own = lax.dynamic_slice_in_dim(target_keys, first_row, count, 0)
-    base = place.bases(count)
-    enc_mask = mask_of(source_own, source_keys, first_row, base, False, count)
-    self_mask = mask_of(target_own, target_keys, first_row, base, True, count)
-    cross_mask = mask_of(target_own, source_keys, first_row, base, False, count)
-
-    branch, enc_attn = attention_forward(place, xs, x_all, enc_w, enc_proj, enc_bias[0], enc_mask)
+    source_starts, target_starts = starts_of(source_keys), starts_of(target_keys)
+    enc_mask = mask_of(source_own, source_starts, first_row, False)
+    self_mask = mask_of(target_own, target_starts, first_row, True)
+    cross_mask = mask_of(target_own, source_starts, first_row, False)
+
+    queries, kv = projected(xs, x_all, enc_w)
+    output, lse = attend(queries, kv, enc_mask)
+    branch, enc_attn = attention_output(place, queries, kv, output, lse, enc_proj, enc_bias[0])
     first, enc_norm_one = norm_forward(xs.astype(F32) + branch, enc_gains[0], enc_shifts[0])
     first_low = first.astype(BF16)
     branch, enc_feed = feed_forward(
@@ -565,15 +1117,20 @@
     )
     encoded, enc_norm_two = norm_forward(first + branch, enc_gains[1], enc_shifts[1])
     encoded_low = encoded.astype(BF16)
-    e_all = place.gather_rows(encoded_low)
-
-    branch, self_attn = attention_forward(
-        place, ts, t_all, self_w, dec_self_proj, dec_bias[0], self_mask
+
+    queries, kv = projected(ts, t_all, self_w)
+    output, lse, e_all = gather_attend(
+        ring, queries, kv, self_mask, encoded_low, (dec_ff_in, dec_ff_out)
+    )
+    branch, self_attn = attention_output(
+        place, queries, kv, output, lse, dec_self_proj, dec_bias[0]
     )
     second, dec_norm_one = norm_forward(ts.astype(F32) + branch, dec_gains[0], dec_shifts[0])
     second_low = second.astype(BF16)
-    branch, cross_attn = attention_forward(
-        place, second_low, e_all, cross_w, dec_cross_proj, dec_bias[1], cross_mask
+    queries, kv = projected(second_low, e_all, cross_w)
+    output, lse = attend(queries, kv, cross_mask)
+    branch, cross_attn = attention_output(
+        place, queries, kv, output, lse, dec_cross_proj, dec_bias[1]
     )
     third, dec_norm_two = norm_forward(second + branch, dec_gains[1], dec_shifts[1])
     third_low = third.astype(BF16)
@@ -595,28 +1152,35 @@
     grad_hidden, dec_gain_two, dec_shift_two = norm_backward(grad_third, dec_norm_two, dec_gains[1])
     grad_branch = grad_hidden.astype(BF16)
     query_part, key_part, cross_qkv, cross_proj, cross_bias = attention_backward(
-        grad_branch, cross_attn, second_low, e_all, cross_w, dec_cross_proj, cross_mask
+        grad_branch,
+        cross_attn,
+        second_low,
+        e_all,
+        cross_w,
+        dec_cross_proj,
+        functools.partial(attend_back, mask=cross_mask),
     )
     cross_grad = place.scatter(jnp.concatenate([cross_qkv, cross_proj], axis=1), True)
     dec_bias_two = column_sum(grad_branch)
-    key_total = place.return_rows(key_part, count)
     grad_second = grad_hidden + place.core_sum(query_part)
     grad_hidden, dec_gain_one, dec_shift_one = norm_backward(
         grad_second, dec_norm_one, dec_gains[0]
     )
     grad_branch = grad_hidden.astype(BF16)
-    query_part, key_part, self_qkv, self_proj, self_bias = attention_backward(
-        grad_branch, self_attn, ts, t_all, self_w, dec_self_proj, self_mask
+    query_part, key_part, self_qkv, self_proj, self_bias, key_total = attention_backward(
+        grad_branch,
+        self_attn,
+        ts,
+        t_all,
+        self_w,
+        dec_self_proj,
+        lambda *parts: back_return(ring, 3, *parts, self_mask, key_part, None, ()),
     )
     self_grad = place.scatter(jnp.concatenate([self_qkv, self_proj], axis=1), True)
     dec_bias_one = column_sum(grad_branch)
-
-    def self_part(step, query_part=query_part, key_part=key_part):
-        return key_part(step) if step else key_part(step) + query_part
-
-    grad_target = grad_hidden + place.return_rows(self_part, count)
+    target_hidden = grad_hidden
     grad_hidden, enc_gain_two, enc_shift_two = norm_backward(
-        enc_cot.astype(F32) + key_total, enc_norm_two, enc_gains[1]
+        enc_cot.astype(F32) + key_total.astype(F32), enc_norm_two, enc_gains[1]
     )
     grad_branch = grad_hidden.astype(BF16)
     feed_in, enc_w_in, enc_b_in, enc_w_out = feed_backward(
@@ -627,16 +1191,27 @@
     grad_first = grad_hidden + feed_in
     grad_hidden, enc_gain_one, enc_shift_one = norm_backward(grad_first, enc_norm_one, enc_gains[0])
     grad_branch = grad_hidden.astype(BF16)
-    query_part, key_part, enc_qkv_grad, enc_proj_grad, enc_bias_grad = attention_backward(
-        grad_branch, enc_attn, xs, x_all, enc_w, enc_proj, enc_mask
-    )
+    target_query, target_key = query_part.astype(BF16), key_part
+    query_part, key_part, enc_qkv_grad, enc_proj_grad, enc_bias_grad, target_total = (
+        attention_backward(
+            grad_branch,
+            enc_attn,
+            xs,
+            x_all,
+            enc_w,
+            enc_proj,
+            lambda *parts: back_return(
+                ring, 4, *parts, enc_mask, target_key, target_query, (dec_ff_grad, cross_grad)
+            ),
+        )
+    )
+    grad_target = target_hidden + target_total.astype(F32)
     enc_grad = place.scatter(jnp.concatenate([enc_qkv_grad, enc_proj_grad], axis=1), False)
     enc_bias_one = column_sum(grad_branch)
-
-    def enc_part(step, query_part=query_part, key_part=key_part):
-        return key_part(step) if step else key_part(step) + query_part
-
-    grad_source = grad_hidden + place.return_rows(enc_part, count)
+    source_total = return_rows(
+        ring, 5, key_part, query_part.astype(BF16), (self_grad, enc_ff_grad)
+    )
+    grad_source = grad_hidden + source_total.astype(F32)
 
     def attention_grads(grad):
         qkv = grad[:, : 3 * width].reshape(-1, 3, width).transpose(1, 0, 2)

time: 848 us -> 765 us (0.902)
  Pallas kernels: 84.3 us -> 265 us
  waiting for transfers between devices: 311 us -> 141 us
  local copies, waits for them, and re-layouts: 111 us -> 65.7 us
  starting transfers between devices: 137 us -> 113 us
  other arithmetic: 88.7 us -> 70.2 us
    pallas_call x6 -> x8, Pallas kernels: 84.3 us -> 265 us  [the longest x1 87.5 us: opening(): pl.pallas_call(functools.partial(opening_kernel, ring, number), out_shape...]
    ppermute x26 -> x17, waiting for transfers between devices: 142 us -> 35.4 us  [permute(): return lax.ppermute(value, ('dp', 'tensor'), moves)]
    ppermute x18 -> x0, waiting for transfers between devices: 74.8 us -> none  [the longest x9 67.4 us: from_z(): lax.ppermute(value, 'seq', [((i + step) % self.ring, i) for i in range(se...]
    ppermute x18 -> x0, starting transfers between devices: 67.1 us -> none  [the longest x9 34.4 us: from_z(): lax.ppermute(value, 'seq', [((i + step) % self.ring, i) for i in range(se...]
    unnamed x286 -> x269, local copies, waits for them, and re-layouts: 55.8 us -> 15.5 us
    ppermute x12, starting transfers between devices: 9.43 us -> 48.1 us  [swap_z(): lax.ppermute(value, 'seq', [(i, i ^ 1 << bit) for i in range(self.ring)])]
    ppermute x6, starting transfers between devices: 2.12 us -> 18.1 us  [swap_x(): lax.ppermute(value, 'dp', [(i, i ^ 2 << bit) for i in range(self.pairs)])]
    ppermute x6, waiting for transfers between devices: 20.6 us -> 35.7 us  [swap_x(): lax.ppermute(value, 'dp', [(i, i ^ 2 << bit) for i in range(self.pairs)])]
  transfers between devices with their start and end apart: 102 -> 48, of which waited for: 32 -> 16; matrix products, arithmetic and copies ran while one was open for 33% -> 26% of each run, Pallas kernels for 10% -> 16%
where the time goes in v2:
time: 765 us; the launch traced here: 754 us
  Pallas kernels  265 us (35%)
  waiting for transfers between devices  141 us (18%)
  starting transfers between devices  113 us (15%)
  matrix products  96.1 us (13%)
  other arithmetic  70.2 us (9%)
  local copies, waits for them, and re-layouts  65.7 us (9%)
    pallas_call x1, Pallas kernels, opening(): pl.pallas_call(functools.partial(opening_kernel, ring, number), out_shape...  87.5 us
    pallas_call x2, Pallas kernels, back_return(): pl.pallas_call(functools.partial(back_return_kernel, KEY_BLOCK, causal, r...  81.7 us
    ppermute x12, waiting for transfers between devices, swap_z(): lax.ppermute(value, 'seq', [(i, i ^ 1 << bit) for i in range(self.ring)])  54.9 us
    ppermute x12, starting transfers between devices, swap_z(): lax.ppermute(value, 'seq', [(i, i ^ 1 << bit) for i in range(self.ring)])  48.1 us
    ppermute x6, waiting for transfers between devices, swap_x(): lax.ppermute(value, 'dp', [(i, i ^ 2 << bit) for i in range(self.pairs)])  35.7 us
    pallas_call x1, Pallas kernels, gather_attend(): pl.pallas_call(functools.partial(gather_attend_kernel, KEY_BLOCK, causal,...  35.6 us
    ppermute x17, waiting for transfers between devices, permute(): return lax.ppermute(value, ('dp', 'tensor'), moves)  35.4 us
    dot_general x10, matrix products, dot_plain(): return jnp.dot(left, right, preferred_element_type=F32)  34.5 us
  transfers between devices with their start and end apart: 48, of which 16 were waited for; matrix products, arithmetic and copies ran while one was open for 26% of the time, Pallas kernels for 16%

profile of v2, /device:TPU:1, one launch (start us, length us, event | category | flops | bytes accessed | tf_op | source)
XLA Modules:
  0.0 754.2 jit_solution(2175897758433524472)
XLA Ops:
  7.0 87.5 %shard_map.450 = (bf16[2048,768]{1,0:T(8,128)(2,1)}, bf16[2048,768]{1,0:T(8,128)(2,1)}, s32[2,2048]{1,0:T(2,128)}, f32[42,128]{1,0:T(8,128)}, bf16[2304,384]{1,0...) custom-call(bf16[512,768]{1,0:T(8,128)(2,1)} %bitcast.226, ...), custom_call_target="tpu_custom_call" | custom-call | tf_op jit(solution)/shard_map/pallas_call | solution.py:588
  104.9 14.8 %shard_map.451 = (f32[384,512]{1,0:T(8,128)S(1)}, f32[8,512]{1,0:T(8,128)S(1)}) custom-call(s32[8]{0:T(128)S(1)} %convert_reduce_fusion.15.starts, s32[3]{0:T(128)S(1)} %add_add_fusion.8.ends, s32[1,512]{1,0:T(1,128)S(1)} %constant_dynamic-slice_fusion.12.segments, bf16[512,384]{1,0:T(8,128)(2,1)S(1)} %fusion.32.q_ref, ...), custom_call_target="tpu_custom_call" | custom-call | flops 1610612736 | bytes 3145728 | tf_op jit(solution)/shard_map/pallas_call | solution.py:283
  127.6 9.3 %multiply_convert_fusion.1 = (bf16[512,1536]{1,0:T(8,128)(2,1)S(1)}, f32[512,1536]{1,0:T(8,128)}, f32[512,1536]{1,0:T(8,128)}) fusion(f32[1536]{0:T(1024)S(1)} %get-tuple-element.235, bf16[768,1536]{1,0:T(8,128)(2,1)S(1)} %copy-done.108, f32[512,768]{1,0:T(8,128)S(1)} %get-tuple-element.195, f32[768]{0:T(1024)S(1)} %get-tuple-element.161, ...), kind=kOutput, calls=%fused_computation.41 | convolution fusion | flops 1261830144 | bytes 11812864 | tf_op jit(solution)/shard_map/dot_general | solution.py:22
  144.3 4.7 collective-permute-done.3.refs_0_
  149.0 25.3 %collective-permute-done.4.refs_1_ = bf16[1536,768]{1,0:T(8,128)(2,1)S(1)} collective-permute-done((bf16[1536,768]{1,0:T(8,128)(2,1)}, bf16[1536,768]{1,0:T(8,128)(2,1)S(1)}, u32[]{:S(2)}, u32[]{:S(2)}) %collective-permute-start.4) | collective-permute-done | bytes 2359328 | tf_op jit(solution)/shard_map/ppermute | solution.py:868
  174.3 35.6 %shard_map.452 = (f32[384,512]{1,0:T(8,128)S(1)}, f32[8,512]{1,0:T(8,128)S(1)}, bf16[2048,768]{1,0:T(8,128)(2,1)S(1)}) custom-call(s32[8]{0:T(128)S(1)} %convert_reduce_fusion.14.starts, s32[1,512]{1,0:T(1,128)S(1)} %constant_dynamic-slice_fusion.11.segments, bf16[512,384]{1,0:T(8,128)(2,1)S(1)} %fusion.31.q_ref, ...), custom_call_target="tpu_custom_call" | custom-call | flops 1610612736 | bytes 3145728 | tf_op jit(solution)/shard_map/pallas_call | solution.py:635
  217.9 4.6 shard_map.453
  226.5 9.4 %multiply_convert_fusion = (bf16[512,1536]{1,0:T(8,128)(2,1)S(1)}, f32[512,1536]{1,0:T(8,128)}, f32[512,1536]{1,0:T(8,128)}) fusion(f32[1536]{0:T(1024)S(1)} %get-tuple-element.234, bf16[768,1536]{1,0:T(8,128)(2,1)S(1)} %collective-permute-done.3.refs_0_, f32[512,768]{1,0:T(8,128)S(1)} %get-tuple-element.187, f32[768]{0:T(1024)S(1)} %get-tuple-element.154, ...), kind=kOutput, calls=%fused_computation.28 | convolution fusion | flops 1261830144 | bytes 11812864 | tf_op jit(solution)/shard_map/dot_general | solution.py:22
  238.8 11.8 %collective-permute-start.7 = (bf16[512,768]{1,0:T(8,128)(2,1)}, bf16[512,768]{1,0:T(8,128)(2,1)}, u32[]{:S(2)}, u32[]{:S(2)}) collective-permute-start(bf16[512,768]{1,0:T(8,128)(2,1)} %get-tuple-element.252), channel_id=1, source_target_pairs={{0,8},{8,0},{16,24},{24,16},{1,9},{9,1},{17,25},{25,17},{2,10},{10... | collective-permute-start | bytes 2359304 | tf_op jit(solution)/shard_map/ppermute | solution.py:844
  283.8 7.7 %shard_map.454 = (bf16[384,512]{1,0:T(8,128)(2,1)S(1)}, bf16[2048,768]{1,0:T(8,128)(2,1)S(1)}) custom-call(s32[8]{0:T(128)S(1)} %convert_reduce_fusion.15.starts, s32[3]{0:T(128)S(1)} %add_add_fusion.9.ends, s32[1,512]{1,0:T(1,128)S(1)} %constant_dynamic-slice_fusion.11.segments, bf16[512,384]{1,0:T(8,128)(2,1)S(1)} %fusion.30.q_ref, ...), custom_call_target="tpu_custom_call" | custom-call | flops 4026531840 | bytes 7864320 | tf_op jit(solution)/shard_map/pallas_call | solution.py:300
  300.0 4.4 copy.66
  307.0 12.9 %collective-permute-start.19 = (bf16[1,2,4,48,1536]{4,3,2,1,0:T(8,128)(2,1)}, bf16[1,2,4,48,1536]{4,3,2,1,0:T(8,128)(2,1)}, u32[]{:S(2)}, u32[]{:S(2)}) collective-permute-start(bf16[1,2,4,48,1536]{4,3,2,1,0:T(8,128)(2,1)} %dynamic-slice_bitcast_fusion.8), channel_id=1, source_target_pairs={{0,16},{8,24},{16,0},{24,8},{1,17},{9,25},{17,1},{25,9},{2,18},{10... | collective-permute-start | bytes 3538952 | tf_op jit(solution)/shard_map/ppermute | solution.py:850
  333.0 39.9 %shard_map.455 = (bf16[384,512]{1,0:T(8,128)(2,1)}, bf16[2048,768]{1,0:T(8,128)(2,1)}, bf16[512,768]{1,0:T(8,128)(2,1)}) custom-call(s32[8]{0:T(128)} %copy-done.14, s32[1,512]{1,0:T(1,128)} %copy-done.13, bf16[512,384]{1,0:T(8,128)(2,1)} %copy-done.12, bf16[2048,768]{1,0:T(8,128)(2,1)} %copy-done, bf16[512,384]{1,0:T(8,128)(2,1)} %convolution_convert_fusion.21.do_ref, ...), custom_call_target="tpu_custom_call" | custom-call | flops 4026531840 | bytes 7864320 | tf_op jit(solution)/shard_map/pallas_call | solution.py:817
  399.2 4.7 copy.68
  437.7 8.6 %collective-permute-start.22 = (bf16[2,48,1536]{2,1,0:T(8,128)(2,1)S(1)}, bf16[2,48,1536]{2,1,0:T(8,128)(2,1)S(1)}, u32[]{:S(2)}, u32[]{:S(2)}) collective-permute-start(bf16[2,48,1536]{2,1,0:T(8,128)(2,1)S(1)} %dynamic-slice_bitcast_fusion.17), channel_id=1, source_target_pairs={{0,2},{2,0},{4,6},{6,4},{1,3},{3,1},{5,7},{7,5},{8,10},{10,8},{12,... | collective-permute-start | bytes 884744 | tf_op jit(solution)/shard_map/ppermute | solution.py:853
  446.6 5.1 collective-permute-done.22
  464.8 4.3 collective-permute-done.25
  472.7 35.7 %collective-permute-done.16 = bf16[1,4,48,3072]{3,2,1,0:T(8,128)(2,1)} collective-permute-done((bf16[1,4,48,3072]{3,2,1,0:T(8,128)(2,1)}, bf16[1,4,48,3072]{3,2,1,0:T(8,128)(2,1)}, u32[]{:S(2)}, u32[]{:S(2)}) %collective-permute-start.16) | collective-permute-done | bytes 1179680 | tf_op jit(solution)/shard_map/ppermute | solution.py:850
  510.3 6.1 collective-permute-start.28
  516.5 4.8 collective-permute-start.17
  526.2 7.1 collective-permute-done.17
  544.6 4.6 collective-permute-done.18
  550.1 41.8 %shard_map.456 = (bf16[384,512]{1,0:T(8,128)(2,1)}, bf16[2048,768]{1,0:T(8,128)(2,1)}, bf16[512,768]{1,0:T(8,128)(2,1)}) custom-call(s32[8]{0:T(128)} %copy-done.16, s32[1,512]{1,0:T(1,128)} %copy-done.15, bf16[512,384]{1,0:T(8,128)(2,1)} %copy-done.20, bf16[2048,768]{1,0:T(8,128)(2,1)} %copy-done.21, bf16[512,384]{1,0:T(8,128)(2,1)} %convolution_convert_fusion.19.do_ref, ...), custom_call_target="tpu_custom_call" | custom-call | flops 4026531840 | bytes 7864320 | tf_op jit(solution)/shard_map/pallas_call | solution.py:817
  591.9 4.7 convolution_convert_fusion.2.terms_ref
  606.2 8.7 %collective-permute-start.42 = (f32[16896]{0:T(1024)S(1)}, f32[16896]{0:T(1024)S(1)}, u32[]{:S(2)}, u32[]{:S(2)}) collective-permute-start(f32[16896]{0:T(1024)S(1)} %add.583), channel_id=1, source_target_pairs={{0,2},{2,0},{4,6},{6,4},{1,3},{3,1},{5,7},{7,5},{8,10},{10,8},{12,... | collective-permute-start | bytes 202760 | tf_op jit(solution)/shard_map/ppermute | solution.py:853
  636.3 14.0 %collective-permute-done.46 = f32[11520]{0:T(1024)S(1)} collective-permute-done((f32[11520]{0:T(1024)S(1)}, f32[11520]{0:T(1024)S(1)}, u32[]{:S(2)}, u32[]{:S(2)}) %collective-permute-start.46) | collective-permute-done | bytes 46112 | tf_op jit(solution)/shard_map/ppermute | solution.py:847
  666.8 8.2 %collective-permute-done.32 = bf16[2,48,3072]{2,1,0:T(8,128)(2,1)} collective-permute-done((bf16[2,48,3072]{2,1,0:T(8,128)(2,1)}, bf16[2,48,3072]{2,1,0:T(8,128)(2,1)}, u32[]{:S(2)}, u32[]{:S(2)}) %collective-permute-start.32) | collective-permute-done | bytes 589856 | tf_op jit(solution)/shard_map/ppermute | solution.py:853
  679.2 13.3 %collective-permute-done.33 = bf16[1,48,3072]{2,1,0:T(8,128)(2,1)S(1)} collective-permute-done((bf16[1,48,3072]{2,1,0:T(8,128)(2,1)S(1)}, bf16[1,48,3072]{2,1,0:T(8,128)(2,1)S(1)}, u32[]{:S(2)}, u32[]{:S(2)}) %collective-permute-start.33) | collective-permute-done | bytes 294944 | tf_op jit(solution)/shard_map/ppermute | solution.py:853
  692.5 33.5 %shard_map.457 = bf16[512,768]{1,0:T(8,128)(2,1)S(1)} custom-call(bf16[2048,768]{1,0:T(8,128)(2,1)S(1)} %convolution_convert_fusion.2.terms_ref, bf16[512,768]{1,0:T(8,128)(2,1)S(1)} %copy-done.5, f32[48,1536]{1,0:T(8,128)S(1)} %add_bitcast_fusion.3.refs_0_, f32[48,3072]{1,0:T(8,128)S(1)} %add_bitcast_fusion.refs_1_), custom_call_target="tpu_custom_call" | custom-call | tf_op jit(solution)/shard_map/pallas_call | solution.py:762
  726.3 8.7 %collective-permute-start.39 = (bf16[2,48,1536]{2,1,0:T(8,128)(2,1)S(1)}, bf16[2,48,1536]{2,1,0:T(8,128)(2,1)S(1)}, u32[]{:S(2)}, u32[]{:S(2)}) collective-permute-start(bf16[2,48,1536]{2,1,0:T(8,128)(2,1)S(1)} %dynamic-slice_bitcast_fusion.15), channel_id=1, source_target_pairs={{0,2},{2,0},{4,6},{6,4},{1,3},{3,1},{5,7},{7,5},{8,10},{10,8},{12,... | collective-permute-start | bytes 884744 | tf_op jit(solution)/shard_map/ppermute | solution.py:853
  736.4 5.8 collective-permute-done.39
  743.9 7.3 collective-permute-done.40
  (547 shorter events, 256.1 us)
Async XLA Ops:
  120.5 28.5 %collective-permute-start.3 = (bf16[768,1536]{1,0:T(8,128)(2,1)}, bf16[768,1536]{1,0:T(8,128)(2,1)S(1)}, u32[]{:S(2)}, u32[]{:S(2)}) collective-permute-start(bf16[768,1536]{1,0:T(8,128)(2,1)} %param.46), channel_id=1, source_target_pairs={{8,0},{9,1},{1,8},{0,9},{24,16},{25,17},{17,24},{16,25},{10,2},{11... | collective-permute-start | bytes 7077896 | tf_op jit(solution)/shard_map/ppermute | solution.py:868
  121.0 53.3 %collective-permute-start.4 = (bf16[1536,768]{1,0:T(8,128)(2,1)}, bf16[1536,768]{1,0:T(8,128)(2,1)S(1)}, u32[]{:S(2)}, u32[]{:S(2)}) collective-permute-start(bf16[1536,768]{1,0:T(8,128)(2,1)} %param.48), channel_id=1, source_target_pairs={{8,0},{9,1},{1,8},{0,9},{24,16},{25,17},{17,24},{16,25},{10,2},{11... | collective-permute-start | bytes 7077896 | tf_op jit(solution)/shard_map/ppermute | solution.py:868
  223.3 27.8 %collective-permute-start.2 = (bf16[512,768]{1,0:T(8,128)(2,1)}, bf16[512,768]{1,0:T(8,128)(2,1)}, u32[]{:S(2)}, u32[]{:S(2)}) collective-permute-start(bf16[512,768]{1,0:T(8,128)(2,1)} %add_convert_fusion.10.own_ref), channel_id=1, source_target_pairs={{0,1},{9,8},{16,17},{25,24},{2,3},{11,10},{18,19},{27,26},{4,5},{1... | collective-permute-start | bytes 2359304 | tf_op jit(solution)/shard_map/ppermute | solution.py:868
  238.8 15.0 %collective-permute-start.7 = (bf16[512,768]{1,0:T(8,128)(2,1)}, bf16[512,768]{1,0:T(8,128)(2,1)}, u32[]{:S(2)}, u32[]{:S(2)}) collective-permute-start(bf16[512,768]{1,0:T(8,128)(2,1)} %get-tuple-element.252), channel_id=1, source_target_pairs={{0,8},{8,0},{16,24},{24,16},{1,9},{9,1},{17,25},{25,17},{2,10},{10... | collective-permute-start | bytes 2359304 | tf_op jit(solution)/shard_map/ppermute | solution.py:844
  250.7 127.2 %collective-permute-start.9 = (bf16[512,768]{1,0:T(8,128)(2,1)}, bf16[512,768]{1,0:T(8,128)(2,1)}, u32[]{:S(2)}, u32[]{:S(2)}) collective-permute-start(bf16[512,768]{1,0:T(8,128)(2,1)} %bitcast.23), channel_id=1, source_target_pairs={{0,8},{8,0},{16,24},{24,16},{1,9},{9,1},{17,25},{25,17},{2,10},{10... | collective-permute-start | bytes 2359304 | tf_op jit(solution)/shard_map/ppermute | solution.py:844
  259.8 47.2 %collective-permute-start.8 = (bf16[512,768]{1,0:T(8,128)(2,1)}, bf16[512,768]{1,0:T(8,128)(2,1)}, u32[]{:S(2)}, u32[]{:S(2)}) collective-permute-start(bf16[512,768]{1,0:T(8,128)(2,1)} %get-tuple-element.208), channel_id=1, source_target_pairs={{0,1},{9,8},{16,17},{25,24},{2,3},{11,10},{18,19},{27,26},{4,5},{1... | collective-permute-start | bytes 2359304 | tf_op jit(solution)/shard_map/ppermute | solution.py:868
  275.3 151.1 %collective-permute-start.15 = (bf16[2,4,48,3072]{3,2,1,0:T(8,128)(2,1)}, bf16[2,4,48,3072]{3,2,1,0:T(8,128)(2,1)}, u32[]{:S(2)}, u32[]{:S(2)}) collective-permute-start(bf16[2,4,48,3072]{3,2,1,0:T(8,128)(2,1)} %get-tuple-element.197), channel_id=1, source_target_pairs={{9,0},{8,1},{0,8},{1,9},{25,16},{24,17},{16,24},{17,25},{11,2},{10... | collective-permute-start | bytes 7077896 | tf_op jit(solution)/shard_map/ppermute | solution.py:868
  277.6 151.6 %collective-permute-start.14 = (bf16[2,4,48,3072]{3,2,1,0:T(8,128)(2,1)}, bf16[2,4,48,3072]{3,2,1,0:T(8,128)(2,1)}, u32[]{:S(2)}, u32[]{:S(2)}) collective-permute-start(bf16[2,4,48,3072]{3,2,1,0:T(8,128)(2,1)} %get-tuple-element.196), channel_id=1, source_target_pairs={{9,8},{8,9},{25,24},{24,25},{11,10},{10,11},{27,26},{26,27},{13,12... | collective-permute-start | bytes 7077896 | tf_op jit(solution)/shard_map/ppermute | solution.py:868
  295.1 31.5 %collective-permute-start.12 = (bf16[512,768]{1,0:T(8,128)(2,1)}, bf16[512,768]{1,0:T(8,128)(2,1)}, u32[]{:S(2)}, u32[]{:S(2)}) collective-permute-start(bf16[512,768]{1,0:T(8,128)(2,1)} %get-tuple-element.256), channel_id=1, source_target_pairs={{0,8},{8,0},{16,24},{24,16},{1,9},{9,1},{17,25},{25,17},{2,10},{10... | collective-permute-start | bytes 2359304 | tf_op jit(solution)/shard_map/ppermute | solution.py:844
  307.0 108.6 %collective-permute-start.19 = (bf16[1,2,4,48,1536]{4,3,2,1,0:T(8,128)(2,1)}, bf16[1,2,4,48,1536]{4,3,2,1,0:T(8,128)(2,1)}, u32[]{:S(2)}, u32[]{:S(2)}) collective-permute-start(bf16[1,2,4,48,1536]{4,3,2,1,0:T(8,128)(2,1)} %dynamic-slice_bitcast_fusion.8), channel_id=1, source_target_pairs={{0,16},{8,24},{16,0},{24,8},{1,17},{9,25},{17,1},{25,9},{2,18},{10... | collective-permute-start | bytes 3538952 | tf_op jit(solution)/shard_map/ppermute | solution.py:850
  394.8 23.3 %collective-permute-start.13 = (bf16[512,768]{1,0:T(8,128)(2,1)}, bf16[512,768]{1,0:T(8,128)(2,1)}, u32[]{:S(2)}, u32[]{:S(2)}) collective-permute-start(bf16[512,768]{1,0:T(8,128)(2,1)} %get-tuple-element.258), channel_id=1, source_target_pairs={{0,8},{8,0},{16,24},{24,16},{1,9},{9,1},{17,25},{25,17},{2,10},{10... | collective-permute-start | bytes 2359304 | tf_op jit(solution)/shard_map/ppermute | solution.py:844
  405.4 40.8 %collective-permute-start.24 = (bf16[1,2,4,48,1536]{4,3,2,1,0:T(8,128)(2,1)S(1)}, bf16[1,2,4,48,1536]{4,3,2,1,0:T(8,128)(2,1)S(1)}, u32[]{:S(2)}, u32[]{:S(2)}) collective-permute-start(bf16[1,2,4,48,1536]{4,3,2,1,0:T(8,128)(2,1)S(1)} %dynamic-slice_bitcast_fusion.7), channel_id=1, source_target_pairs={{0,16},{8,24},{16,0},{24,8},{1,17},{9,25},{17,1},{25,9},{2,18},{10... | collective-permute-start | bytes 3538952 | tf_op jit(solution)/shard_map/ppermute | solution.py:850
  415.7 107.1 %collective-permute-start.29 = (bf16[1,2,4,48,3072]{4,3,2,1,0:T(8,128)(2,1)}, bf16[1,2,4,48,3072]{4,3,2,1,0:T(8,128)(2,1)}, u32[]{:S(2)}, u32[]{:S(2)}) collective-permute-start(bf16[1,2,4,48,3072]{4,3,2,1,0:T(8,128)(2,1)} %dynamic-slice_bitcast_fusion), channel_id=1, source_target_pairs={{0,16},{8,24},{16,0},{24,8},{1,17},{9,25},{17,1},{25,9},{2,18},{10... | collective-permute-start | bytes 7077896 | tf_op jit(solution)/shard_map/ppermute | solution.py:850
  418.0 18.3 %collective-permute-start.21 = (bf16[4,48,1536]{2,1,0:T(8,128)(2,1)S(1)}, bf16[4,48,1536]{2,1,0:T(8,128)(2,1)S(1)}, u32[]{:S(2)}, u32[]{:S(2)}) collective-permute-start(bf16[4,48,1536]{2,1,0:T(8,128)(2,1)S(1)} %get-tuple-element.212), channel_id=1, source_target_pairs={{9,0},{8,1},{0,8},{1,9},{25,16},{24,17},{16,24},{17,25},{11,2},{10... | collective-permute-start | bytes 1769480 | tf_op jit(solution)/shard_map/ppermute | solution.py:868
  426.4 11.0 %collective-permute-start.20 = (bf16[4,48,1536]{2,1,0:T(8,128)(2,1)S(1)}, bf16[4,48,1536]{2,1,0:T(8,128)(2,1)S(1)}, u32[]{:S(2)}, u32[]{:S(2)}) collective-permute-start(bf16[4,48,1536]{2,1,0:T(8,128)(2,1)S(1)} %get-tuple-element.211), channel_id=1, source_target_pairs={{9,8},{8,9},{25,24},{24,25},{11,10},{10,11},{27,26},{26,27},{13,12... | collective-permute-start | bytes 1769480 | tf_op jit(solution)/shard_map/ppermute | solution.py:868
  434.0 74.5 %collective-permute-start.16 = (bf16[1,4,48,3072]{3,2,1,0:T(8,128)(2,1)}, bf16[1,4,48,3072]{3,2,1,0:T(8,128)(2,1)}, u32[]{:S(2)}, u32[]{:S(2)}) collective-permute-start(bf16[1,4,48,3072]{3,2,1,0:T(8,128)(2,1)} %constant_dynamic-slice_fusion.10), channel_id=1, source_target_pairs={{0,16},{8,24},{16,0},{24,8},{1,17},{9,25},{17,1},{25,9},{2,18},{10... | collective-permute-start | bytes 3538952 | tf_op jit(solution)/shard_map/ppermute | solution.py:850
  437.7 14.0 %collective-permute-start.22 = (bf16[2,48,1536]{2,1,0:T(8,128)(2,1)S(1)}, bf16[2,48,1536]{2,1,0:T(8,128)(2,1)S(1)}, u32[]{:S(2)}, u32[]{:S(2)}) collective-permute-start(bf16[2,48,1536]{2,1,0:T(8,128)(2,1)S(1)} %dynamic-slice_bitcast_fusion.17), channel_id=1, source_target_pairs={{0,2},{2,0},{4,6},{6,4},{1,3},{3,1},{5,7},{7,5},{8,10},{10,8},{12,... | collective-permute-start | bytes 884744 | tf_op jit(solution)/shard_map/ppermute | solution.py:853
  454.8 14.4 %collective-permute-start.25 = (bf16[4,48,1536]{2,1,0:T(8,128)(2,1)S(1)}, bf16[4,48,1536]{2,1,0:T(8,128)(2,1)}, u32[]{:S(2)}, u32[]{:S(2)}) collective-permute-start(bf16[4,48,1536]{2,1,0:T(8,128)(2,1)S(1)} %get-tuple-element.209), channel_id=1, source_target_pairs={{9,8},{8,9},{25,24},{24,25},{11,10},{10,11},{27,26},{26,27},{13,12... | collective-permute-start | bytes 1769480 | tf_op jit(solution)/shard_map/ppermute | solution.py:868
  470.7 39.5 %collective-permute-start.27 = (bf16[2,48,1536]{2,1,0:T(8,128)(2,1)S(1)}, bf16[2,48,1536]{2,1,0:T(8,128)(2,1)S(1)}, u32[]{:S(2)}, u32[]{:S(2)}) collective-permute-start(bf16[2,48,1536]{2,1,0:T(8,128)(2,1)S(1)} %dynamic-slice_bitcast_fusion.16), channel_id=1, source_target_pairs={{0,2},{2,0},{4,6},{6,4},{1,3},{3,1},{5,7},{7,5},{8,10},{10,8},{12,... | collective-permute-start | bytes 884744 | tf_op jit(solution)/shard_map/ppermute | solution.py:853
  516.5 16.8 %collective-permute-start.17 = (bf16[2,48,3072]{2,1,0:T(8,128)(2,1)S(1)}, bf16[2,48,3072]{2,1,0:T(8,128)(2,1)S(1)}, u32[]{:S(2)}, u32[]{:S(2)}) collective-permute-start(bf16[2,48,3072]{2,1,0:T(8,128)(2,1)S(1)} %dynamic-slice_bitcast_fusion.14), channel_id=1, source_target_pairs={{0,2},{2,0},{4,6},{6,4},{1,3},{3,1},{5,7},{7,5},{8,10},{10,8},{12,... | collective-permute-start | bytes 1769480 | tf_op jit(solution)/shard_map/ppermute | solution.py:853
  533.5 15.7 %collective-permute-start.18 = (bf16[1,48,3072]{2,1,0:T(8,128)(2,1)S(1)}, bf16[1,48,3072]{2,1,0:T(8,128)(2,1)S(1)}, u32[]{:S(2)}, u32[]{:S(2)}) collective-permute-start(bf16[1,48,3072]{2,1,0:T(8,128)(2,1)S(1)} %constant_dynamic-slice_fusion.9), channel_id=1, source_target_pairs={{0,4},{2,6},{4,0},{6,2},{1,5},{3,7},{5,1},{7,3},{8,12},{10,14},{12... | collective-permute-start | bytes 884744 | tf_op jit(solution)/shard_map/ppermute | solution.py:853
  538.8 117.7 %collective-permute-start.31 = (bf16[4,48,3072]{2,1,0:T(8,128)(2,1)}, bf16[4,48,3072]{2,1,0:T(8,128)(2,1)}, u32[]{:S(2)}, u32[]{:S(2)}) collective-permute-start(bf16[4,48,3072]{2,1,0:T(8,128)(2,1)} %get-tuple-element.201), channel_id=1, source_target_pairs={{9,0},{8,1},{0,8},{1,9},{25,16},{24,17},{16,24},{17,25},{11,2},{10... | collective-permute-start | bytes 3538952 | tf_op jit(solution)/shard_map/ppermute | solution.py:868
  542.7 113.8 %collective-permute-start.30 = (bf16[4,48,3072]{2,1,0:T(8,128)(2,1)}, bf16[4,48,3072]{2,1,0:T(8,128)(2,1)}, u32[]{:S(2)}, u32[]{:S(2)}) collective-permute-start(bf16[4,48,3072]{2,1,0:T(8,128)(2,1)} %get-tuple-element.200), channel_id=1, source_target_pairs={{9,8},{8,9},{25,24},{24,25},{11,10},{10,11},{27,26},{26,27},{13,12... | collective-permute-start | bytes 3538952 | tf_op jit(solution)/shard_map/ppermute | solution.py:868
  615.4 49.0 %collective-permute-start.35 = (bf16[512,768]{1,0:T(8,128)(2,1)}, bf16[512,768]{1,0:T(8,128)(2,1)}, u32[]{:S(2)}, u32[]{:S(2)}) collective-permute-start(bf16[512,768]{1,0:T(8,128)(2,1)} %reduce-precision_convert_fusion), channel_id=1, source_target_pairs={{0,1},{9,8},{16,17},{25,24},{2,3},{11,10},{18,19},{27,26},{4,5},{1... | collective-permute-start | bytes 2359304 | tf_op jit(solution)/shard_map/ppermute | solution.py:868
  635.2 41.3 %collective-permute-start.37 = (bf16[2,4,48,1536]{3,2,1,0:T(8,128)(2,1)}, bf16[2,4,48,1536]{3,2,1,0:T(8,128)(2,1)}, u32[]{:S(2)}, u32[]{:S(2)}) collective-permute-start(bf16[2,4,48,1536]{3,2,1,0:T(8,128)(2,1)} %get-tuple-element.199), channel_id=1, source_target_pairs={{9,0},{8,1},{0,8},{1,9},{25,16},{24,17},{16,24},{17,25},{11,2},{10... | collective-permute-start | bytes 3538952 | tf_op jit(solution)/shard_map/ppermute | solution.py:868
  635.6 14.6 %collective-permute-start.46 = (f32[11520]{0:T(1024)S(1)}, f32[11520]{0:T(1024)S(1)}, u32[]{:S(2)}, u32[]{:S(2)}) collective-permute-start(f32[11520]{0:T(1024)S(1)} %slice.427), channel_id=1, source_target_pairs={{0,1},{1,0},{2,3},{3,2},{4,5},{5,4},{6,7},{7,6},{8,9},{9,8},{10,11... | collective-permute-start | bytes 138248 | tf_op jit(solution)/shard_map/ppermute | solution.py:847
  652.1 24.5 %collective-permute-start.36 = (bf16[2,4,48,1536]{3,2,1,0:T(8,128)(2,1)}, bf16[2,4,48,1536]{3,2,1,0:T(8,128)(2,1)}, u32[]{:S(2)}, u32[]{:S(2)}) collective-permute-start(bf16[2,4,48,1536]{3,2,1,0:T(8,128)(2,1)} %get-tuple-element.198), channel_id=1, source_target_pairs={{9,8},{8,9},{25,24},{24,25},{11,10},{10,11},{27,26},{26,27},{13,12... | collective-permute-start | bytes 3538952 | tf_op jit(solution)/shard_map/ppermute | solution.py:868
  660.7 14.4 %collective-permute-start.32 = (bf16[2,48,3072]{2,1,0:T(8,128)(2,1)}, bf16[2,48,3072]{2,1,0:T(8,128)(2,1)}, u32[]{:S(2)}, u32[]{:S(2)}) collective-permute-start(bf16[2,48,3072]{2,1,0:T(8,128)(2,1)} %dynamic-slice_bitcast_fusion.9), channel_id=1, source_target_pairs={{0,2},{2,0},{4,6},{6,4},{1,3},{3,1},{5,7},{7,5},{8,10},{10,8},{12,... | collective-permute-start | bytes 1769480 | tf_op jit(solution)/shard_map/ppermute | solution.py:853
  676.3 16.1 %collective-permute-start.33 = (bf16[1,48,3072]{2,1,0:T(8,128)(2,1)S(1)}, bf16[1,48,3072]{2,1,0:T(8,128)(2,1)S(1)}, u32[]{:S(2)}, u32[]{:S(2)}) collective-permute-start(bf16[1,48,3072]{2,1,0:T(8,128)(2,1)S(1)} %constant_dynamic-slice_fusion.6), channel_id=1, source_target_pairs={{0,4},{2,6},{4,0},{6,2},{1,5},{3,7},{5,1},{7,3},{8,12},{10,14},{12... | collective-permute-start | bytes 884744 | tf_op jit(solution)/shard_map/ppermute | solution.py:853
  678.7 47.4 %collective-permute-start.38 = (bf16[1,4,48,1536]{3,2,1,0:T(8,128)(2,1)S(1)}, bf16[1,4,48,1536]{3,2,1,0:T(8,128)(2,1)S(1)}, u32[]{:S(2)}, u32[]{:S(2)}) collective-permute-start(bf16[1,4,48,1536]{3,2,1,0:T(8,128)(2,1)S(1)} %constant_dynamic-slice_fusion.5), channel_id=1, source_target_pairs={{0,16},{8,24},{16,0},{24,8},{1,17},{9,25},{17,1},{25,9},{2,18},{10... | collective-permute-start | bytes 1769480 | tf_op jit(solution)/shard_map/ppermute | solution.py:850
  726.3 15.9 %collective-permute-start.39 = (bf16[2,48,1536]{2,1,0:T(8,128)(2,1)S(1)}, bf16[2,48,1536]{2,1,0:T(8,128)(2,1)S(1)}, u32[]{:S(2)}, u32[]{:S(2)}) collective-permute-start(bf16[2,48,1536]{2,1,0:T(8,128)(2,1)S(1)} %dynamic-slice_bitcast_fusion.15), channel_id=1, source_target_pairs={{0,2},{2,0},{4,6},{6,4},{1,3},{3,1},{5,7},{7,5},{8,10},{10,8},{12,... | collective-permute-start | bytes 884744 | tf_op jit(solution)/shard_map/ppermute | solution.py:853
  735.1 17.6 %collective-permute-start.34 = (bf16[512,768]{1,0:T(8,128)(2,1)S(1)}, bf16[512,768]{1,0:T(8,128)(2,1)S(1)}, u32[]{:S(2)}, u32[]{:S(2)}) collective-permute-start(bf16[512,768]{1,0:T(8,128)(2,1)S(1)} %reduce-precision_convert_fusion.1), channel_id=1, source_target_pairs={{0,1},{9,8},{16,17},{25,24},{2,3},{11,10},{18,19},{27,26},{4,5},{1... | collective-permute-start | bytes 2359304 | tf_op jit(solution)/shard_map/ppermute | solution.py:868
  (136 other events, 1605.0 us)

commit v3 on v2

--- a/solution.py
+++ b/solution.py
@@ -211,41 +211,6 @@
         dkv_ref[rows, later] = dv.astype(BF16)
 
 
-def backward_end(dq_ref, dq):
-    dq_ref[...] = (dq[...] * HEAD_DIM ** (-0.5)).astype(BF16)
-
-
-def backward_kernel(
-    block,
-    causal,
-    tokens,
-    starts,
-    ends,
-    segments,
-    q_ref,
-    kv_ref,
-    do_ref,
-    dot_ref,
-    out_ref,
-    lse_ref,
-    *refs,
-):
-    dq_ref, dkv_ref, masked_q, masked_do, delta, dq = refs[tokens:]
-    mask = Mask(causal, starts, segments, ends[2])
-    backward_start(q_ref, do_ref, dot_ref, out_ref, masked_q, masked_do, delta, dq)
-
-    def body(index, rows, partial):
-        backward_block(
-            index, rows, partial, block, mask, kv_ref, lse_ref, dkv_ref, masked_q, masked_do, delta, dq
-        )
-
-    def skipped(rows):
-        dkv_ref[rows, :] = jnp.zeros((block, dkv_ref.shape[1]), BF16)
-
-    over_blocks(mask, ends, kv_ref.shape[0], block, body, skipped)
-    backward_end(dq_ref, dq)
-
-
 SCALARS = pl.BlockSpec(memory_space=pltpu.SMEM)
 VECTORS = pl.BlockSpec(memory_space=pltpu.VMEM)
 
@@ -294,23 +259,6 @@
     )(starts, ends, segments, queries, kv)
 
 
-def attend_back(queries, kv, grad_out, grad_out_t, output, lse, mask, tokens=()):
-    count, width = queries.shape
-    causal, starts, ends, segments = mask
-    return pl.pallas_call(
-        functools.partial(backward_kernel, KEY_BLOCK, causal, len(tokens)),
-        out_shape=(
-            jax.ShapeDtypeStruct((width, count), BF16),
-            jax.ShapeDtypeStruct(kv.shape, BF16),
-        ),
-        in_specs=[SCALARS] * 2 + [VECTORS] * 7 + [ANYWHERE] * len(tokens),
-        out_specs=(VECTORS,) * 2,
-        scratch_shapes=backward_scratch(count, width),
-        compiler_params=pltpu.CompilerParams(vmem_limit_bytes=48 << 20),
-        cost_estimate=cost_of(kv, count, width, 5),
-    )(starts, ends, segments, queries, kv, grad_out, grad_out_t, output, lse, *tokens)
-
-
 MESH = pl.DeviceIdType.MESH
 DMA = pltpu.SemaphoreType.DMA
 
@@ -324,6 +272,9 @@
         self.partner = (self.other_d, self.z, self.y)
         self.right = (self.d, self.z + 1, self.y)
         self.left = (self.d, self.z - 1, self.y)
+        self.over_x = (self.d + 2 - 4 * lax.rem(self.x, 2), self.z, self.y)
+        self.over_y = (self.d, self.z, 1 - self.y)
+        self.diagonal = (self.other_d, self.z, 1 - self.y)
 
     def meet(self, devices):
         barrier = pltpu.get_barrier_semaphore()
@@ -336,6 +287,14 @@
 
             wanted = wanted + jnp.where(condition, 1, 0)
         pl.semaphore_wait(barrier, wanted)
+
+    def along_z(self, step):
+        return (self.d, lax.rem(self.z + step, self.ring), self.y)
+
+    def everyone(self):
+        devices = [self.partner, self.over_x, self.over_y, self.diagonal]
+        devices += [self.along_z(step) for step in range(1, self.ring)]
+        return [(self.core >= 0, device) for device in devices]
 
     def neighbours(self):
         return [
@@ -649,41 +608,199 @@
     )(starts, segments, queries, kv, own, *tokens)
 
 
-class Return:
-    def __init__(self, here, terms_ref, query_ref, out_ref, refs):
-        self.here, self.terms_ref, self.query_ref, self.out_ref = here, terms_ref, query_ref, out_ref
-        self.mine, self.outgoing, self.from_core, self.arrived, self.total = refs[:5]
-        self.core_sent, self.core_got, self.sent, self.got, self.end_sent, self.end_got = refs[5:]
-        self.count = terms_ref.shape[0] // here.ring
+class Part:
+    def __init__(self, inputs, in_specs, out_shapes, scratch, bind):
+        self.inputs, self.in_specs, self.out_shapes = inputs, in_specs, out_shapes
+        self.scratch, self.bind = scratch, bind
+
+
+def run_parts(number, body, parts, cost=None):
+    ring = lax.axis_size("seq")
+    counts = [(len(p.inputs), len(p.out_shapes), len(p.scratch)) for p in parts]
+
+    def kernel(*refs):
+        here = Here(ring)
+        taken, offset = [[] for _ in parts], 0
+        for kind in range(3):
+            for refs_of, count in zip(taken, counts):
+                refs_of.append(refs[offset : offset + count[kind]])
+                offset += count[kind]
+        here.meet(here.everyone())
+        body(here, *(p.bind(here, *refs_of) for p, refs_of in zip(parts, taken)))
+
+    results = pl.pallas_call(
+        kernel,
+        out_shape=[shape for p in parts for shape in p.out_shapes],
+        in_specs=[spec for p in parts for spec in p.in_specs],
+        out_specs=[VECTORS for p in parts for _ in p.out_shapes],
+        scratch_shapes=[shape for p in parts for shape in p.scratch],
+        compiler_params=pltpu.CompilerParams(
+            vmem_limit_bytes=60 << 20, collective_id=number, has_side_effects=True
+        ),
+        cost_estimate=cost,
+    )(*(array for p in parts for array in p.inputs))
+    given = []
+    for _, count, _ in counts:
+        given.append(results[:count])
+        results = results[count:]
+    return given
+
+
+class Stage:
+    def __init__(self, here, kind, source, result, buffers, sems):
+        self.here, self.kind, self.source, self.result = here, kind, source, result
+        self.buffers, (self.sent, self.got) = buffers, sems
+        rows = source.shape[0]
+        if kind == "x":
+            half = rows // 2
+            self.kept = [half * here.x]
+            self.given = [half * (1 - here.x)]
+            self.size, self.to = half, here.over_x
+        elif kind == "y":
+            self.size = 192
+            self.starts = list(range(0, rows, 2 * self.size))
+        elif kind == "v":
+            bit = lax.rem(here.z, 2)
+            self.size = rows // 4
+            self.kept = [self.size * bit, self.size * (bit + 2)]
+            self.given = [self.size * (1 - bit), self.size * (3 - bit)]
+            self.to = (here.d, here.z + 1 - 2 * bit, here.y)
+        else:
+            bit = lax.div(here.z, 2)
+            self.size = rows // 2
+            self.kept, self.given = [self.size * bit], [self.size * (1 - bit)]
+            self.to = (here.d, here.z + 2 - 4 * bit, here.y)
+
+    def rows(self, start):
+        if not isinstance(start, int):
+            start = pl.multiple_of(start, 16)
+        return pl.ds(start, self.size)
+
+    def move(self, start, place, buffer, sem, to):
+        return remote(
+            self.source.at[self.rows(start)],
+            self.buffers[buffer].at[self.rows(place * self.size)],
+            self.sent.at[sem],
+            self.got.at[sem],
+            to,
+        )
+
+    def moves(self):
+        here = self.here
+        if self.kind != "y":
+            both = [
+                (None, self.move(start, k, 0, k, self.to)) for k, start in enumerate(self.given)
+            ]
+            return both, both
+        sends, arrivals = [], []
+        for k, start in enumerate(self.starts):
+            upper = start + self.size
+            sends.append((here.core == 0, self.move(upper, k, 0, 2 * k, here.partner)))
+            sends.append((here.core == 1, self.move(start, k, 0, 2 * k, here.diagonal)))
+            sends.append((here.core == 1, self.move(upper, k, 1, 2 * k + 1, here.over_y)))
+            arrivals.append((None, self.move(upper, k, 0, 2 * k, here.partner)))
+            arrivals.append((here.core == 1, self.move(upper, k, 1, 2 * k + 1, here.over_y)))
+        return sends, arrivals
+
+    @staticmethod
+    def each(moves, act):
+        for condition, copy in moves:
+            if condition is None:
+                act(copy)
+            else:
+                pl.when(condition)(functools.partial(act, copy))
+
+    def begin(self):
+        self.each(self.moves()[0], lambda copy: copy.start())
+
+    def end(self):
+        sends, arrivals = self.moves()
+        self.each(arrivals, lambda copy: copy.wait_recv())
+        kept = self.kept if self.kind != "y" else self.starts
+        for k, start in enumerate(kept):
+            place = self.rows(k * self.size)
+
+            def add(own_ref, own, place=place):
+                both = own_ref[own, :].astype(F32) + self.buffers[0][place, :].astype(F32)
+                self.result[place, :] = both.astype(self.result.dtype)
+
+            if self.kind == "y":
+                pl.when(self.here.core == 0)(functools.partial(add, self.source, self.rows(start)))
+                pl.when(self.here.core == 1)(functools.partial(add, self.buffers[1], place))
+            else:
+                add(self.source, self.rows(start))
+        self.each(sends, lambda copy: copy.wait_send())
+
+
+class Chain:
+    def __init__(self, stages, times):
+        self.stages, self.times = stages, times
+
+    def event(self, time):
+        for k, own in enumerate(self.times):
+            if own == time:
+                if k:
+                    self.stages[k - 1].end()
+                if k < len(self.stages):
+                    self.stages[k].begin()
+
+
+def chain(array, kinds, times):
+    rows, columns = array.shape
+    scratch, shapes = [], []
+    for kind in kinds:
+        rows = rows // 2
+        scratch += [pltpu.VMEM((rows, columns), BF16)] * (2 if kind == "y" else 1)
+        scratch += [DMA((4,))] * 2
+        shapes.append((rows, columns))
+    scratch += [pltpu.VMEM(shape, BF16) for shape in shapes[:-1]]
+    final = jax.ShapeDtypeStruct(shapes[-1], F32 if kinds[-1] == "w" else BF16)
+
+    def bind(here, inputs, outputs, refs):
+        refs = list(refs)
+        results = refs[len(refs) - len(kinds) + 1 :] + [outputs[0]]
+        source, stages = inputs[0], []
+        for kind, result in zip(kinds, results):
+            buffers = [refs.pop(0) for _ in range(2 if kind == "y" else 1)]
+            sems = [refs.pop(0) for _ in range(2)]
+            stages.append(Stage(here, kind, source, result, buffers, sems))
+            source = result
+        return Chain(stages, times)
+
+    return Part((array,), [VECTORS], [final], scratch, bind)
+
+
+def run_chains(number, chains, events):
+    def body(here, *bound):
+        for time in range(events):
+            for one in bound:
+                one.event(time)
+
+    return [given[0] for given in run_parts(number, body, chains)]
+
+
+class Back:
+    def __init__(self, here, causal, apart, inputs, outputs, scratch):
+        self.here, self.causal, self.apart = here, causal, apart
+        self.starts, self.segments, self.q, self.kv, self.do, self.dot, self.out, self.lse = inputs[:8]
+        self.w_q, self.w_kv = inputs[8:]
+        self.dq_out, self.dkv, self.sum = outputs[:3]
+        self.query_sum = outputs[3] if apart else None
+        self.work, scratch = scratch[:4], scratch[4:]
+        self.terms, self.from_core, self.outgoing, self.arrived, self.total = scratch[:5]
+        self.core_sent, self.core_got, self.sent, self.got, self.end_sent, self.end_got = scratch[5:11]
+        if apart:
+            self.query_low, self.query_got, self.query_sems = scratch[11:]
+        self.count = self.q.shape[0]
         self.part = self.count // 2
-        self.order = list(range(1, here.ring)) + [0]
-
-    def devices(self):
-        here = self.here
-        found = [(here.core >= 0, here.partner)]
-        for step in range(1, here.ring):
-            found.append((here.core >= 0, self.to(step)))
-        return found
-
-    def to(self, step):
-        here = self.here
-        return (here.d, lax.rem(here.z + step, here.ring), here.y)
+        self.mask = Mask(causal, self.starts, self.segments, here.z * self.count)
 
     def half(self, core):
         return pl.ds(pl.multiple_of(core * self.part, self.part), self.part)
 
-    def rows(self, step, core):
-        start = lax.rem(self.here.z + step, self.here.ring) * self.count + core * self.part
-        return pl.ds(pl.multiple_of(start, self.part), self.part)
-
     def across(self, step):
-        other = 1 - self.here.core
-        if step == 0 and self.query_ref is not None:
-            source = self.mine.at[self.half(other)]
-        else:
-            source = self.terms_ref.at[self.rows(step, other)]
         return remote(
-            source,
+            self.terms.at[step, self.half(1 - self.here.core)],
             self.from_core.at[step],
             self.core_sent.at[step],
             self.core_got.at[step],
@@ -692,145 +809,138 @@
 
     def along(self, step):
         return remote(
-            self.outgoing.at[step], self.arrived.at[step], self.sent.at[step], self.got.at[step], self.to(step)
+            self.outgoing.at[step],
+            self.arrived.at[step],
+            self.sent.at[step],
+            self.got.at[step],
+            self.here.along_z(step),
         )
 
-    def begin(self):
-        if self.query_ref is not None:
-            start = pl.multiple_of(self.here.z * self.count, self.count)
-            own = self.terms_ref[pl.ds(start, self.count), :].astype(F32)
-            self.mine[...] = (own + self.query_ref[...].astype(F32)).astype(BF16)
-        for step in self.order:
+    def both(self, step):
+        self.across(step).wait_recv()
+        own = self.terms[step, self.half(self.here.core), :].astype(F32)
+        return own + self.from_core[step].astype(F32)
+
+    def forward(self, step):
+        self.outgoing[step] = self.both(step).astype(BF16)
+        self.along(step).start()
+
+    def block(self, step):
+        shard = lax.rem(self.here.z + step, self.here.ring)
+        rows = pl.ds(pl.multiple_of(shard * self.count, self.count), self.count)
+        backward_block(
+            shard, rows, True, self.count, self.mask, self.kv, self.lse, self.dkv, *self.work
+        )
+        return dot_last(self.dkv[rows, :], self.w_kv[...])
+
+    def run(self, event):
+        ring = self.here.ring
+        event(0)
+        backward_start(self.q, self.do, self.dot, self.out, *self.work)
+
+        @pl.loop(1, ring)
+        def _(step):
+            self.terms[step] = self.block(step).astype(BF16)
             self.across(step).start()
 
-    def send(self):
-        for step in self.order:
-            self.across(step).wait_recv()
-            if step == 0 and self.query_ref is not None:
-                local = self.mine[self.half(self.here.core), :]
-            else:
-                local = self.terms_ref[self.rows(step, self.here.core), :]
-            both = local.astype(F32) + self.from_core[step].astype(F32)
-            if step:
-                self.outgoing[step] = both.astype(BF16)
-                self.along(step).start()
-            else:
-                self.total[...] = both
-
-    def end(self):
-        for step in range(1, self.here.ring):
+            @pl.when(step > 1)
+            def _():
+                self.forward(step - 1)
+
+            for time in range(1, ring):
+                pl.when(step == time)(functools.partial(event, time))
+
+        own = self.block(0)
+        self.forward(ring - 1)
+        event(ring)
+        low = (self.work[3][...] * HEAD_DIM ** (-0.5)).T.astype(BF16)
+        self.dq_out[...] = low
+        query = dot_last(low, self.w_q[...])
+        if self.apart:
+            self.query_low[...] = query.astype(BF16)
+            exchange = remote(
+                self.query_low, self.query_got, self.query_sems.at[0], self.query_sems.at[1], self.here.partner
+            )
+            exchange.start()
+        else:
+            own = own + query
+        self.terms[0] = own.astype(BF16)
+        self.across(0).start()
+        if self.apart:
+            exchange.wait()
+            self.query_sum[...] = self.query_low[...].astype(F32) + self.query_got[...].astype(F32)
+        self.total[...] = self.both(0)
+        event(ring + 1)
+        for step in range(1, ring):
             self.along(step).wait_recv()
             self.total[...] += self.arrived[step].astype(F32)
         own, other = self.half(self.here.core), self.half(1 - self.here.core)
-        self.out_ref[own, :] = self.total[...].astype(BF16)
+        self.sum[own, :] = self.total[...].astype(BF16)
         for half, waits in ((own, False), (other, True)):
-            view = self.out_ref.at[half]
+            view = self.sum.at[half]
             copy = remote(view, view, self.end_sent, self.end_got, self.here.partner)
             if waits:
                 copy.wait_recv()
             else:
                 copy.start()
                 copy.wait_send()
-        for step in self.order:
+        for step in range(ring):
             self.across(step).wait_send()
             if step:
                 self.along(step).wait_send()
-
-
-def return_scratch(ring, count, model):
+        event(ring + 2)
+
+
+def attend_back(number, saved, grad_mixed, grad_mixed_t, weights, mask, apart, chains):
+    queries, kv, output, lse, _ = saved
+    causal, starts, segments = mask
+    ring = lax.axis_size("seq")
+    count, width = queries.shape
+    model = weights[0].shape[0]
     part = count // 2
-    return (
-        [pltpu.VMEM((count, model), BF16)]
-        + [pltpu.VMEM((ring, part, model), BF16)] * 3
-        + [pltpu.VMEM((part, model), F32)]
-        + [DMA((ring,))] * 4
-        + [DMA] * 2
-    )
-
-
-def return_kernel(ring, tokens, terms_ref, query_ref, *refs):
-    returned = Return(Here(ring), terms_ref, query_ref, refs[tokens], refs[tokens + 1 :])
-    returned.here.meet(returned.devices())
-    returned.begin()
-    returned.send()
-    returned.end()
-
-
-def return_rows(ring, number, terms, query, tokens=()):
-    rows, model = terms.shape
-    count = rows // ring
-    return pl.pallas_call(
-        functools.partial(return_kernel, ring, len(tokens)),
-        out_shape=jax.ShapeDtypeStruct((count, model), BF16),
-        in_specs=[VECTORS] * 2 + [ANYWHERE] * len(tokens),
-        out_specs=VECTORS,
-        scratch_shapes=return_scratch(ring, count, model),
-        compiler_params=pltpu.CompilerParams(
-            vmem_limit_bytes=40 << 20, collective_id=number, has_side_effects=True
-        ),
-    )(terms, query, *tokens)
-
-
-def back_return_kernel(
-    block,
-    causal,
-    ring,
-    has_query,
-    tokens,
-    starts,
-    segments,
-    q_ref,
-    kv_ref,
-    do_ref,
-    dot_ref,
-    out_ref,
-    lse_ref,
-    terms_ref,
-    *refs,
-):
-    query_ref, refs = (refs[0], refs[1:]) if has_query else (None, refs)
-    dq_ref, dkv_ref, sum_ref, masked_q, masked_do, delta, dq = refs[tokens : tokens + 7]
-    here = Here(ring)
-    returned = Return(here, terms_ref, query_ref, sum_ref, refs[tokens + 7 :])
-    here.meet(returned.devices())
-    returned.begin()
-    mask = Mask(causal, starts, segments, here.z * q_ref.shape[0])
-    backward_start(q_ref, do_ref, dot_ref, out_ref, masked_q, masked_do, delta, dq)
-    returned.send()
-
-    @pl.loop(0, kv_ref.shape[0] // block)
-    def _(index):
-        rows = pl.ds(pl.multiple_of(index * block, block), block)
-        backward_block(
-            index, rows, True, block, mask, kv_ref, lse_ref, dkv_ref, masked_q, masked_do, delta, dq
-        )
-
-    backward_end(dq_ref, dq)
-    returned.end()
-
-
-def back_return(ring, number, queries, kv, grad_out, grad_out_t, output, lse, mask, terms, query, tokens):
-    count, width = queries.shape
-    model = terms.shape[1]
-    causal, starts, _, segments = mask
-    more = (terms,) if query is None else (terms, query)
-    return pl.pallas_call(
-        functools.partial(
-            back_return_kernel, KEY_BLOCK, causal, ring, query is not None, len(tokens)
-        ),
-        out_shape=(
-            jax.ShapeDtypeStruct((width, count), BF16),
-            jax.ShapeDtypeStruct(kv.shape, BF16),
-            jax.ShapeDtypeStruct((count, model), BF16),
-        ),
-        in_specs=[SCALARS] + [VECTORS] * (7 + len(more)) + [ANYWHERE] * len(tokens),
-        out_specs=(VECTORS,) * 3,
-        scratch_shapes=backward_scratch(count, width) + return_scratch(ring, count, model),
-        compiler_params=pltpu.CompilerParams(
-            vmem_limit_bytes=56 << 20, collective_id=number, has_side_effects=True
-        ),
-        cost_estimate=cost_of(kv, count, width, 5),
-    )(starts, segments, queries, kv, grad_out, grad_out_t, output, lse, *more, *tokens)
+    shapes = [
+        jax.ShapeDtypeStruct((count, width), BF16),
+        jax.ShapeDtypeStruct(kv.shape, BF16),
+        jax.ShapeDtypeStruct((count, model), BF16),
+    ]
+    scratch = backward_scratch(count, width) + [
+        pltpu.VMEM((ring, count, model), BF16),
+        *[pltpu.VMEM((ring, part, model), BF16)] * 3,
+        pltpu.VMEM((part, model), F32),
+        *[DMA((ring,))] * 4,
+        *[DMA] * 2,
+    ]
+    if apart:
+        shapes.append(jax.ShapeDtypeStruct((count, model), F32))
+        scratch += [pltpu.VMEM((count, model), BF16)] * 2 + [DMA((2,))]
+    main = Part(
+        (starts, segments, queries, kv, grad_mixed, grad_mixed_t, output, lse, *weights[:2]),
+        [SCALARS] + [VECTORS] * 9,
+        shapes,
+        scratch,
+        lambda here, *refs: Back(here, causal, apart, *refs),
+    )
+
+    def body(here, back, *bound):
+        def event(time):
+            for one in bound:
+                one.event(time)
+
+        back.run(event)
+
+    first, *rest = run_parts(number, body, [main] + list(chains), cost_of(kv, count, width, 7))
+    return first, [given[0] for given in rest]
+
+
+class Plan:
+    def __init__(self, kernels):
+        self.kernels = kernels
+
+    def chains(self, wanted):
+        return [chain(*one) for one in wanted] if self.kernels else []
+
+    def given(self, wanted, results):
+        return results if self.kernels else [one[0] for one in wanted]
 
 
 class Places:
@@ -880,6 +990,9 @@
     def hand_out(self, rows):
         other = self.permute(rows, lambda d, y: (d, 1 - y) if d % 2 != y else None)
         return jnp.where(self.core == self.y, rows, other)
+
+    def plan(self):
+        return Plan(self.pairs == 4 and self.ring == 4)
 
     def scatter(self, grad, x_first):
         rows, columns = grad.shape
@@ -950,33 +1063,25 @@
     return (branch, (queries, kv, output, lse, mixed))
 
 
-def attention_backward(grad_branch, saved, query_in, key_in, weights, out_weight, back):
-    queries, kv, output, lse, mixed = saved
-    w_q, w_kv = weights[:2]
-    width = queries.shape[1]
+def attention_backward(
+    number, grad_branch, saved, query_in, key_in, weights, out_weight, mask, apart, plan, wanted
+):
+    mixed = saved[4]
+    width = saved[0].shape[1]
     grad_mixed = dot_last(grad_branch, out_weight).astype(BF16)
     grad_mixed_t = dot_last(out_weight, grad_branch).astype(BF16)
-    grad_q, grad_kv, *more = back(queries, kv, grad_mixed, grad_mixed_t, output, lse)
-    grad_query_in = dot_general_q(grad_q, w_q)
-    grad_key_in = dot_last(grad_kv, w_kv).astype(BF16)
-    grad_qkv = jnp.concatenate(
-        [
-            lax.dot_general(query_in, grad_q, (((0,), (1,)), ((), ())), preferred_element_type=F32),
-            dot_first(key_in, grad_kv),
-        ],
-        axis=1,
-    ).astype(BF16)
-    grad_out = lax.dot_general(
-        grad_branch, mixed, (((0,), (1,)), ((), ())), preferred_element_type=F32
-    ).astype(BF16)
-    grad_bias = jnp.concatenate(
-        [jnp.sum(grad_q.astype(F32), axis=1), column_sum(grad_kv[:, width:])]
-    )
-    return (grad_query_in, grad_key_in, grad_qkv, grad_out, grad_bias, *more)
-
-
-def dot_general_q(grad_q, w_q):
-    return lax.dot_general(grad_q, w_q, (((0,), (1,)), ((), ())), preferred_element_type=F32)
+    (grad_q, grad_kv, *sums), given = attend_back(
+        number, saved, grad_mixed, grad_mixed_t, weights, mask, apart, plan.chains(wanted)
+    )
+    grads = (
+        dot_first(query_in, grad_q).astype(BF16),
+        lax.dot_general(
+            grad_branch, mixed, (((0,), (1,)), ((), ())), preferred_element_type=F32
+        ).astype(BF16),
+        dot_first(key_in, grad_kv).astype(BF16),
+    )
+    grad_bias = jnp.concatenate([column_sum(grad_q), column_sum(grad_kv[:, width:])])
+    return (sums, grads, grad_bias, plan.given(wanted, given))
 
 
 def feed_forward(place, x_in, w_in, b_in, w_out, b_out):
@@ -1139,6 +1244,9 @@
     )
     decoded, dec_norm_three = norm_forward(third + branch, dec_gains[2], dec_shifts[2])
 
+    def back_mask(mask):
+        return (mask[0], mask[1], mask[3])
+
     grad_hidden, dec_gain_three, dec_shift_three = norm_backward(
         dec_cot.astype(F32), dec_norm_three, dec_gains[2]
     )
@@ -1146,39 +1254,53 @@
     feed_in, dec_w_in, dec_b_in, dec_w_out = feed_backward(
         place, grad_branch, dec_feed, third_low, dec_ff_in, dec_ff_out
     )
-    dec_ff_grad = place.scatter(jnp.concatenate([dec_w_in, dec_w_out], axis=1), False)
     dec_bias_three = column_sum(grad_branch)
     grad_third = grad_hidden + feed_in
     grad_hidden, dec_gain_two, dec_shift_two = norm_backward(grad_third, dec_norm_two, dec_gains[1])
     grad_branch = grad_hidden.astype(BF16)
-    query_part, key_part, cross_qkv, cross_proj, cross_bias = attention_backward(
+    plan = place.plan()
+    (key_total, query_total), cross_grads, cross_bias, (dec_w_in, dec_w_out) = attention_backward(
+        3,
         grad_branch,
         cross_attn,
         second_low,
         e_all,
         cross_w,
         dec_cross_proj,
-        functools.partial(attend_back, mask=cross_mask),
-    )
-    cross_grad = place.scatter(jnp.concatenate([cross_qkv, cross_proj], axis=1), True)
+        back_mask(cross_mask),
+        True,
+        plan,
+        [(dec_w_in, "x", (0, 6)), (dec_w_out, "y", (0, 6))],
+    )
     dec_bias_two = column_sum(grad_branch)
-    grad_second = grad_hidden + place.core_sum(query_part)
+    grad_second = grad_hidden + query_total
     grad_hidden, dec_gain_one, dec_shift_one = norm_backward(
         grad_second, dec_norm_one, dec_gains[0]
     )
     grad_branch = grad_hidden.astype(BF16)
-    query_part, key_part, self_qkv, self_proj, self_bias, key_total = attention_backward(
+    cross_q, cross_proj, cross_kv = cross_grads
+    (target_total,), self_grads, self_bias, given = attention_backward(
+        4,
         grad_branch,
         self_attn,
         ts,
         t_all,
         self_w,
         dec_self_proj,
-        lambda *parts: back_return(ring, 3, *parts, self_mask, key_part, None, ()),
-    )
-    self_grad = place.scatter(jnp.concatenate([self_qkv, self_proj], axis=1), True)
+        back_mask(self_mask),
+        False,
+        plan,
+            [
+                (dec_w_in, "y", (0, 6)),
+                (dec_w_out, "x", (0, 6)),
+                (cross_kv, "x", (0, 6)),
+                (cross_q, "y", (0, 6)),
+                (cross_proj, "y", (0, 6)),
+            ],
+    )
+    dec_w_in, dec_w_out, cross_kv, cross_q, cross_proj = given
     dec_bias_one = column_sum(grad_branch)
-    target_hidden = grad_hidden
+    grad_target = grad_hidden + target_total.astype(F32)
     grad_hidden, enc_gain_two, enc_shift_two = norm_backward(
         enc_cot.astype(F32) + key_total.astype(F32), enc_norm_two, enc_gains[1]
     )
@@ -1186,45 +1308,60 @@
     feed_in, enc_w_in, enc_b_in, enc_w_out = feed_backward(
         place, grad_branch, enc_feed, first_low, enc_ff_in, enc_ff_out
     )
-    enc_ff_grad = place.scatter(jnp.concatenate([enc_w_in, enc_w_out], axis=1), True)
     enc_bias_two = column_sum(grad_branch)
     grad_first = grad_hidden + feed_in
     grad_hidden, enc_gain_one, enc_shift_one = norm_backward(grad_first, enc_norm_one, enc_gains[0])
     grad_branch = grad_hidden.astype(BF16)
-    target_query, target_key = query_part.astype(BF16), key_part
-    query_part, key_part, enc_qkv_grad, enc_proj_grad, enc_bias_grad, target_total = (
-        attention_backward(
-            grad_branch,
-            enc_attn,
-            xs,
-            x_all,
-            enc_w,
-            enc_proj,
-            lambda *parts: back_return(
-                ring, 4, *parts, enc_mask, target_key, target_query, (dec_ff_grad, cross_grad)
-            ),
-        )
-    )
-    grad_target = target_hidden + target_total.astype(F32)
-    enc_grad = place.scatter(jnp.concatenate([enc_qkv_grad, enc_proj_grad], axis=1), False)
+    self_q, self_proj, self_kv = self_grads
+    (source_total,), enc_grads, enc_bias_grad, given = attention_backward(
+        5,
+        grad_branch,
+        enc_attn,
+        xs,
+        x_all,
+        enc_w,
+        enc_proj,
+        back_mask(enc_mask),
+        False,
+        plan,
+            [
+                (cross_kv, "y", (0, 6)),
+                (cross_q, "x", (0, 6)),
+                (cross_proj, "x", (0, 6)),
+                (enc_w_in, "x", (0, 6)),
+                (enc_w_out, "y", (0, 6)),
+                (dec_w_in, "vw", (0, 4, 6)),
+                (dec_w_out, "vw", (0, 4, 6)),
+            ],
+    )
+    cross_kv, cross_q, cross_proj, enc_w_in, enc_w_out, dec_w_in, dec_w_out = given
     enc_bias_one = column_sum(grad_branch)
-    source_total = return_rows(
-        ring, 5, key_part, query_part.astype(BF16), (self_grad, enc_ff_grad)
-    )
     grad_source = grad_hidden + source_total.astype(F32)
-
-    def attention_grads(grad):
-        qkv = grad[:, : 3 * width].reshape(-1, 3, width).transpose(1, 0, 2)
-        return (qkv, grad[:, 3 * width :].T)
-
-    def feed_grads(grad):
-        return (grad[:, :hidden_units], grad[:, hidden_units:].T)
-
-    out_enc_qkv, out_enc_proj = attention_grads(enc_grad)
-    out_self, out_self_proj = attention_grads(self_grad)
-    out_cross, out_cross_proj = attention_grads(cross_grad)
-    out_enc_in, out_enc_out = feed_grads(enc_ff_grad)
-    out_dec_in, out_dec_out = feed_grads(dec_ff_grad)
+    enc_q, enc_proj_grad, enc_kv = enc_grads
+    rest = [
+        (enc_kv, "xyvw", (0, 2, 4, 5, 6)),
+        (enc_q, "yxvw", (0, 2, 4, 5, 6)),
+        (enc_proj_grad, "yxvw", (0, 2, 4, 5, 6)),
+        (self_kv, "xyvw", (0, 1, 3, 4, 5)),
+        (self_q, "yxvw", (0, 1, 3, 4, 5)),
+        (self_proj, "yxvw", (0, 1, 3, 4, 5)),
+        (enc_w_in, "yvw", (0, 2, 3, 4)),
+        (enc_w_out, "xvw", (0, 2, 3, 4)),
+        (cross_kv, "vw", (0, 1, 2)),
+        (cross_q, "vw", (0, 1, 2)),
+        (cross_proj, "vw", (0, 1, 2)),
+    ]
+    if plan.kernels:
+        given = run_chains(6, plan.chains(rest), 7)
+    else:
+        given = [place.scatter(array, True) for array, _, _ in rest]
+        dec_w_in, dec_w_out = (place.scatter(array, True) for array in (dec_w_in, dec_w_out))
+    enc_kv, enc_q, enc_proj_grad, self_kv, self_q, self_proj = given[:6]
+    enc_w_in, enc_w_out, cross_kv, cross_q, cross_proj = given[6:]
+
+    def qkv_grads(of_q, of_kv):
+        return jnp.stack([of_q, of_kv[:, :width], of_kv[:, width:]])
+
     whole, halves = place.all_sum(
         jnp.concatenate(
             [
@@ -1254,24 +1391,24 @@
         place.hand_out(decoded.astype(BF16))[None],
         place.hand_out(rounded(grad_source).astype(BF16)).astype(F32)[None],
         place.hand_out(rounded(grad_target).astype(BF16)).astype(F32)[None],
-        out_enc_qkv,
+        qkv_grads(enc_q, enc_kv),
         small[0].reshape(2, width),
-        out_enc_proj,
-        out_enc_in,
+        enc_proj_grad.T,
+        enc_w_in,
         small[3],
-        out_enc_out,
+        enc_w_out.T,
         whole[0:2],
         whole[2:4],
         whole[4:6],
-        out_self,
+        qkv_grads(self_q, self_kv),
         small[1].reshape(2, width),
-        out_self_proj,
-        out_cross,
+        self_proj.T,
+        qkv_grads(cross_q, cross_kv),
         small[2].reshape(2, width),
-        out_cross_proj,
-        out_dec_in,
+        cross_proj.T,
+        dec_w_in,
         small[4],
-        out_dec_out,
+        dec_w_out.T,
         whole[6:9],
         whole[9:12],
         whole[12:15],

time: 765 us -> 669 us (0.87)
  Pallas kernels: 265 us -> 436 us
  starting transfers between devices: 113 us -> 11.9 us
  waiting for transfers between devices: 141 us -> 41.1 us
  local copies, waits for them, and re-layouts: 65.7 us -> 34.1 us
  other arithmetic: 70.2 us -> 45.2 us
    pallas_call x4, Pallas kernels: 123 us -> 294 us  [run_parts(): pl.pallas_call(kernel, out_shape=[shape for p in parts for shape in p.out...]
    ppermute x12 -> x2, starting transfers between devices: 48.1 us -> 0.14 us  [swap_z(): lax.ppermute(value, 'seq', [(i, i ^ 1 << bit) for i in range(self.ring)])]
    ppermute x12 -> x2, waiting for transfers between devices: 54.9 us -> 8.18 us  [swap_z(): lax.ppermute(value, 'seq', [(i, i ^ 1 << bit) for i in range(self.ring)])]
    ppermute x6 -> x1, waiting for transfers between devices: 35.7 us -> 0.01 us  [swap_x(): lax.ppermute(value, 'dp', [(i, i ^ 2 << bit) for i in range(self.pairs)])]
    ppermute x17 -> x7, starting transfers between devices: 30 us -> 6.73 us  [permute(): return lax.ppermute(value, ('dp', 'tensor'), moves)]
    convert_element_type x15 -> x0, other arithmetic: 18.4 us -> none  [the longest x5 9.65 us: scatter(): grad = (kept.astype(F32) + first.astype(F32)).astype(BF16)]
    ppermute x6 -> x1, starting transfers between devices: 18.1 us -> 0.32 us  [swap_x(): lax.ppermute(value, 'dp', [(i, i ^ 2 << bit) for i in range(self.pairs)])]
    squeeze x20 -> x0, local copies, waits for them, and re-layouts: 16.4 us -> none  [the longest x5 8.45 us: scatter(): kept = lax.dynamic_index_in_dim(grad, self.core, grad.ndim - 4, False)]
  transfers between devices with their start and end apart: 48 -> 22, of which waited for: 16 -> 8; matrix products, arithmetic and copies ran while one was open for 26% -> 18% of each run, Pallas kernels for 16% -> 45%
where the time goes in v3:
time: 669 us; the launch traced here: 660 us
  Pallas kernels  436 us (65%)
  matrix products  89.8 us (13%)
  other arithmetic  45.2 us (7%)
  waiting for transfers between devices  41.1 us (6%)
  local copies, waits for them, and re-layouts  34.1 us (5%)
  starting transfers between devices  11.9 us (2%)
    pallas_call x4, Pallas kernels, run_parts(): pl.pallas_call(kernel, out_shape=[shape for p in parts for shape in p.out...  294 us
    pallas_call x1, Pallas kernels, opening(): pl.pallas_call(functools.partial(opening_kernel, ring, number), out_shape...  87.5 us
    dot_general x10, matrix products, dot_plain(): return jnp.dot(left, right, preferred_element_type=F32)  35.4 us
    dot_general x13, matrix products, dot_first(): return lax.dot_general(left, right, TN, preferred_element_type=F32)  34.9 us
    pallas_call x1, Pallas kernels, gather_attend(): pl.pallas_call(functools.partial(gather_attend_kernel, KEY_BLOCK, causal,...  34.4 us
    ppermute x7, waiting for transfers between devices, permute(): return lax.ppermute(value, ('dp', 'tensor'), moves)  28.6 us
    pallas_call x2, Pallas kernels, attend(): pl.pallas_call(functools.partial(forward_kernel, KEY_BLOCK, causal), out_...  19.6 us
    unnamed x223, local copies, waits for them, and re-layouts  16.4 us
  transfers between devices with their start and end apart: 22, of which 8 were waited for; matrix products, arithmetic and copies ran while one was open for 18% of the time, Pallas kernels for 45%

profile of v3, /device:TPU:1, one launch (start us, length us, event | category | flops | bytes accessed | tf_op | source)
XLA Modules:
  0.0 660.1 jit_solution(5502837572989688308)
XLA Ops:
  7.0 87.5 %shard_map.450 = (bf16[2048,768]{1,0:T(8,128)(2,1)}, bf16[2048,768]{1,0:T(8,128)(2,1)}, s32[2,2048]{1,0:T(2,128)}, f32[42,128]{1,0:T(8,128)}, bf16[2304,384]{1,0...) custom-call(bf16[512,768]{1,0:T(8,128)(2,1)} %bitcast.118, ...), custom_call_target="tpu_custom_call" | custom-call | tf_op jit(solution)/shard_map/pallas_call | solution.py:547
  96.4 2.5 fusion.71
  102.6 2.8 add_convert_fusion.2.kv_ref.refs_3_
  105.5 14.8 %shard_map.451 = (f32[384,512]{1,0:T(8,128)S(1)}, f32[8,512]{1,0:T(8,128)S(1)}) custom-call(s32[8]{0:T(128)S(1)} %convert_reduce_fusion.15.starts.refs_0_, s32[3]{0:T(128)S(1)} %add_add_fusion.7.ends, s32[1,512]{1,0:T(1,128)S(1)} %constant_dynamic-slice_fusion.5.segments.refs_1_, bf16[512,384]{1,0:T(8,128)(2,1)S(1)} %fusion.29.q_ref.refs_2_, ...), custom_call_target="tpu_custom_call" | custom-call | flops 1610612736 | bytes 3145728 | tf_op jit(solution)/shard_map/pallas_call | solution.py:248
  129.8 9.4 %multiply_convert_fusion.1 = (bf16[512,1536]{1,0:T(8,128)(2,1)S(1)}, f32[512,1536]{1,0:T(8,128)}, f32[512,1536]{1,0:T(8,128)}) fusion(f32[1536]{0:T(1024)S(1)} %get-tuple-element.234, bf16[768,1536]{1,0:T(8,128)(2,1)S(1)} %copy-done.83, f32[512,768]{1,0:T(8,128)S(1)} %get-tuple-element.199, f32[768]{0:T(1024)S(1)} %get-tuple-element.165, ...), kind=kOutput, calls=%fused_computation.33 | convolution fusion | flops 1261830144 | bytes 11812864 | tf_op jit(solution)/shard_map/dot_general | solution.py:22
  141.6 2.8 add_convert_fusion.1.kv_ref.refs_3_
  146.7 3.0 collective-permute-done.3.refs_0_
  149.7 25.3 %collective-permute-done.4.refs_1_ = bf16[1536,768]{1,0:T(8,128)(2,1)S(1)} collective-permute-done((bf16[1536,768]{1,0:T(8,128)(2,1)}, bf16[1536,768]{1,0:T(8,128)(2,1)S(1)}, u32[]{:S(2)}, u32[]{:S(2)}) %collective-permute-start.4) | collective-permute-done | bytes 2359328 | tf_op jit(solution)/shard_map/ppermute | solution.py:978
  175.0 34.4 %shard_map.452 = (f32[384,512]{1,0:T(8,128)S(1)}, f32[8,512]{1,0:T(8,128)S(1)}, bf16[2048,768]{1,0:T(8,128)(2,1)S(1)}) custom-call(s32[8]{0:T(128)S(1)} %convert_reduce_fusion.14.starts.refs_0_, s32[1,512]{1,0:T(1,128)S(1)} %constant_dynamic-slice_fusion.4.segments.refs_1_, bf16[512,384]{1,0:T(8,128)(2,1)S(1)} %fusion.28.q_ref.refs_2_, ...), custom_call_target="tpu_custom_call" | custom-call | flops 1610612736 | bytes 3145728 | tf_op jit(solution)/shard_map/pallas_call | solution.py:594
  212.5 2.9 add_convert_fusion.kv_ref.refs_3_
  218.0 4.8 shard_map.453
  227.1 9.3 %multiply_convert_fusion = (bf16[512,1536]{1,0:T(8,128)(2,1)S(1)}, f32[512,1536]{1,0:T(8,128)}, f32[512,1536]{1,0:T(8,128)}) fusion(f32[1536]{0:T(1024)S(1)} %get-tuple-element.233, bf16[768,1536]{1,0:T(8,128)(2,1)S(1)} %collective-permute-done.3.refs_0_, f32[512,768]{1,0:T(8,128)S(1)} %get-tuple-element.191, f32[768]{0:T(1024)S(1)} %get-tuple-element.158, ...), kind=kOutput, calls=%fused_computation.20 | convolution fusion | flops 1261830144 | bytes 11812864 | tf_op jit(solution)/shard_map/dot_general | solution.py:22
  236.4 2.8 fusion.82
  248.6 2.4 fusion.18
  260.4 2.9 convolution_convert_fusion.2.refs_11_
  263.3 3.2 convolution_convert_fusion.3.refs_10_
  271.8 63.9 %shard_map.454 = (bf16[512,384]{1,0:T(8,128)(2,1)}, bf16[2048,768]{1,0:T(8,128)(2,1)}, bf16[512,768]{1,0:T(8,128)(2,1)}, f32[512,768]{1,0:T(8,128)}, bf16[384,15...) custom-call(s32[8]{0:T(128)} %copy-done.17, s32[1,512]{1,0:T(1,128)} %copy-done.14, bf16[512,384]{1,0:T(8,128)(2,1)} %copy-done.22, ...), custom_call_target="tpu_custom_call" | custom-call | flops 5637144576 | bytes 11010048 | tf_op jit(solution)/shard_map/pallas_call | solution.py:631
  335.7 2.7 multiply_reduce_fusion.1
  344.2 3.8 convolution_convert_fusion.6.refs_12_
  349.4 59.3 %shard_map.455 = (bf16[512,384]{1,0:T(8,128)(2,1)}, bf16[2048,768]{1,0:T(8,128)(2,1)}, bf16[512,768]{1,0:T(8,128)(2,1)}, bf16[192,1536]{1,0:T(8,128)(2,1)}, bf16...) custom-call(s32[8]{0:T(128)} %copy-done.15, ...), custom_call_target="tpu_custom_call" | custom-call | flops 5637144576 | bytes 11010048 | tf_op jit(solution)/shard_map/pallas_call | solution.py:631
  411.8 2.5 convolution_convert_fusion.8.refs_4_
  415.8 2.6 multiply_reduce_fusion.2
  426.6 2.8 convolution_convert_fusion.refs_14_
  429.4 3.2 convolution_convert_fusion.1.refs_13_
  434.8 3.8 convolution_convert_fusion.4.refs_3_
  443.2 80.6 %shard_map.456 = (bf16[512,384]{1,0:T(8,128)(2,1)}, bf16[2048,768]{1,0:T(8,128)(2,1)}, bf16[512,768]{1,0:T(8,128)(2,1)}, bf16[192,768]{1,0:T(8,128)(2,1)}, bf16[...) custom-call(s32[8]{0:T(128)} %copy-done.17, ...), custom_call_target="tpu_custom_call" | custom-call | flops 5637144576 | bytes 11010048 | tf_op jit(solution)/shard_map/pallas_call | solution.py:631
  523.8 2.7 convolution_convert_fusion.10.refs_1_
  526.6 6.7 %convolution_convert_fusion.5.refs_0_ = bf16[768,768]{1,0:T(8,128)(2,1)} fusion(bf16[2048,768]{1,0:T(8,128)(2,1)} %get-tuple-element.79, bf16[2048,768]{1,0:T(8,128)(2,1)} %get-tuple-element.111), kind=kOutput, calls=%fused_computation.96 | convolution fusion | flops 2416508928 | bytes 7471104 | tf_op jit(solution)/shard_map/dot_general | solution.py:30
  538.1 90.4 %shard_map.457 = (f32[48,768]{1,0:T(8,128)}, f32[48,384]{1,0:T(8,128)}, f32[48,384]{1,0:T(8,128)}, f32[48,768]{1,0:T(8,128)}, f32[48,384]{1,0:T(8,128)}, /*index...) custom-call(bf16[768,768]{1,0:T(8,128)(2,1)} %convolution_convert_fu, ...), custom_call_target="tpu_custom_call" | custom-call | tf_op jit(solution)/shard_map/pallas_call | solution.py:631
  630.5 2.5 bitcast_convert_fusion
  633.8 3.0 collective-permute-done.16
  637.6 5.2 collective-permute-done.17
  (393 shorter events, 111.2 us)
Async XLA Ops:
  95.5 122.5 %copy-start.17 = (s32[8]{0:T(128)}, s32[8]{0:T(128)S(1)}, u32[]{:S(2)}) copy-start(s32[8]{0:T(128)S(1)} %convert_reduce_fusion.15.starts.refs_0_) | copy-start | bytes 100
  121.2 6.0 collective-permute-start
  121.2 28.5 %collective-permute-start.3 = (bf16[768,1536]{1,0:T(8,128)(2,1)}, bf16[768,1536]{1,0:T(8,128)(2,1)S(1)}, u32[]{:S(2)}, u32[]{:S(2)}) collective-permute-start(bf16[768,1536]{1,0:T(8,128)(2,1)} %param.46), channel_id=1, source_target_pairs={{8,0},{9,1},{1,8},{0,9},{24,16},{25,17},{17,24},{16,25},{10,2},{11... | collective-permute-start | bytes 7077896 | tf_op jit(solution)/shard_map/ppermute | solution.py:978
  121.7 53.3 %collective-permute-start.4 = (bf16[1536,768]{1,0:T(8,128)(2,1)}, bf16[1536,768]{1,0:T(8,128)(2,1)S(1)}, u32[]{:S(2)}, u32[]{:S(2)}) collective-permute-start(bf16[1536,768]{1,0:T(8,128)(2,1)} %param.48), channel_id=1, source_target_pairs={{8,0},{9,1},{1,8},{0,9},{24,16},{25,17},{17,24},{16,25},{10,2},{11... | collective-permute-start | bytes 7077896 | tf_op jit(solution)/shard_map/ppermute | solution.py:978
  122.5 52.4 %copy-start.15 = (s32[8]{0:T(128)}, s32[8]{0:T(128)S(1)}, u32[]{:S(2)}) copy-start(s32[8]{0:T(128)S(1)} %convert_reduce_fusion.14.starts.refs_0_) | copy-start | bytes 100
  124.3 50.7 %copy-start.13 = (bf16[512,384]{1,0:T(8,128)(2,1)}, bf16[512,384]{1,0:T(8,128)(2,1)S(1)}, u32[]{:S(2)}) copy-start(bf16[512,384]{1,0:T(8,128)(2,1)S(1)} %fusion.28.q_ref.refs_2_) | copy-start | bytes 1179652
  127.1 85.4 %copy-start.41 = (bf16[768,384]{1,0:T(8,128)(2,1)}, bf16[768,384]{1,0:T(8,128)(2,1)S(1)}, u32[]{:S(2)}) copy-start(bf16[768,384]{1,0:T(8,128)(2,1)S(1)} %get-tuple-element.207) | copy-start | bytes 1769476
  127.1 85.4 %copy-start.42 = (bf16[768,384]{1,0:T(8,128)(2,1)}, bf16[768,384]{1,0:T(8,128)(2,1)S(1)}, u32[]{:S(2)}) copy-start(bf16[768,384]{1,0:T(8,128)(2,1)S(1)} %get-tuple-element.208) | copy-start | bytes 1769476
  140.6 3.9 collective-permute-start.1
  141.1 76.9 %copy-start.14 = (s32[1,512]{1,0:T(1,128)}, s32[1,512]{1,0:T(1,128)S(1)}, u32[]{:S(2)}) copy-start(s32[1,512]{1,0:T(1,128)S(1)} %constant_dynamic-slice_fusion.4.segments.refs_1_) | copy-start | bytes 6148
  146.7 62.7 %copy-start.7 = (bf16[512,768]{1,0:T(8,128)(2,1)}, bf16[512,768]{1,0:T(8,128)(2,1)S(1)}, u32[]{:S(2)}) copy-start(bf16[512,768]{1,0:T(8,128)(2,1)S(1)} %add_convert_fusion.6.own_ref) | copy-start | bytes 2359300
  146.7 63.3 %copy-start.55 = (bf16[384,768]{1,0:T(8,128)(2,1)S(1)}, bf16[384,768]{1,0:T(8,128)(2,1)}, u32[]{:S(2)}) copy-start(bf16[384,768]{1,0:T(8,128)(2,1)} %get-tuple-element.90) | copy-start | bytes 1769476
  149.7 77.4 %copy-start.9 = (bf16[768,1536]{1,0:T(8,128)(2,1)}, bf16[768,1536]{1,0:T(8,128)(2,1)S(1)}, u32[]{:S(2)}) copy-start(bf16[768,1536]{1,0:T(8,128)(2,1)S(1)} %collective-permute-done.3.refs_0_) | copy-start | bytes 7077892
  175.0 61.4 %copy-start.11 = (bf16[1536,768]{1,0:T(8,128)(2,1)}, bf16[1536,768]{1,0:T(8,128)(2,1)S(1)}, u32[]{:S(2)}) copy-start(bf16[1536,768]{1,0:T(8,128)(2,1)S(1)} %collective-permute-done.4.refs_1_) | copy-start | bytes 7077892
  210.9 4.5 collective-permute-start.5
  223.8 2.3 collective-permute-start.6
  239.2 7.2 %collective-permute-start.7 = (bf16[512,768]{1,0:T(8,128)(2,1)}, bf16[512,768]{1,0:T(8,128)(2,1)}, u32[]{:S(2)}, u32[]{:S(2)}) collective-permute-start(bf16[512,768]{1,0:T(8,128)(2,1)} %get-tuple-element.251), channel_id=1, source_target_pairs={{0,8},{8,0},{16,24},{24,16},{1,9},{9,1},{17,25},{25,17},{2,10},{10... | collective-permute-start | bytes 2359304 | tf_op jit(solution)/shard_map/ppermute | solution.py:954
  239.6 9.0 %collective-permute-start.10 = (bf16[512,768]{1,0:T(8,128)(2,1)}, bf16[512,768]{1,0:T(8,128)(2,1)}, u32[]{:S(2)}, u32[]{:S(2)}) collective-permute-start(bf16[512,768]{1,0:T(8,128)(2,1)} %bitcast.24), channel_id=1, source_target_pairs={{0,8},{8,0},{16,24},{24,16},{1,9},{9,1},{17,25},{25,17},{2,10},{10... | collective-permute-start | bytes 2359304 | tf_op jit(solution)/shard_map/ppermute | solution.py:954
  239.7 176.1 %collective-permute-start.9 = (bf16[512,768]{1,0:T(8,128)(2,1)}, bf16[512,768]{1,0:T(8,128)(2,1)}, u32[]{:S(2)}, u32[]{:S(2)}) collective-permute-start(bf16[512,768]{1,0:T(8,128)(2,1)} %bitcast.23), channel_id=1, source_target_pairs={{0,8},{8,0},{16,24},{24,16},{1,9},{9,1},{17,25},{25,17},{2,10},{10... | collective-permute-start | bytes 2359304 | tf_op jit(solution)/shard_map/ppermute | solution.py:954
  245.1 12.7 %collective-permute-start.2 = (bf16[512,768]{1,0:T(8,128)(2,1)S(1)}, bf16[512,768]{1,0:T(8,128)(2,1)S(1)}, u32[]{:S(2)}, u32[]{:S(2)}) collective-permute-start(bf16[512,768]{1,0:T(8,128)(2,1)S(1)} %copy-done.8), channel_id=1, source_target_pairs={{0,1},{9,8},{16,17},{25,24},{2,3},{11,10},{18,19},{27,26},{4,5},{1... | collective-permute-start | bytes 2359304 | tf_op jit(solution)/shard_map/ppermute | solution.py:978
  256.7 9.8 %collective-permute-start.11 = (bf16[512,768]{1,0:T(8,128)(2,1)S(1)}, bf16[512,768]{1,0:T(8,128)(2,1)S(1)}, u32[]{:S(2)}, u32[]{:S(2)}) collective-permute-start(bf16[512,768]{1,0:T(8,128)(2,1)S(1)} %get-tuple-element.253), channel_id=1, source_target_pairs={{0,8},{8,0},{16,24},{24,16},{1,9},{9,1},{17,25},{25,17},{2,10},{10... | collective-permute-start | bytes 2359304 | tf_op jit(solution)/shard_map/ppermute | solution.py:954
  259.1 173.5 %collective-permute-start.8 = (bf16[512,768]{1,0:T(8,128)(2,1)}, bf16[512,768]{1,0:T(8,128)(2,1)}, u32[]{:S(2)}, u32[]{:S(2)}) collective-permute-start(bf16[512,768]{1,0:T(8,128)(2,1)} %get-tuple-element.209), channel_id=1, source_target_pairs={{0,1},{9,8},{16,17},{25,24},{2,3},{11,10},{18,19},{27,26},{4,5},{1... | collective-permute-start | bytes 2359304 | tf_op jit(solution)/shard_map/ppermute | solution.py:978
  424.0 14.6 %collective-permute-start.12 = (bf16[512,768]{1,0:T(8,128)(2,1)S(1)}, bf16[512,768]{1,0:T(8,128)(2,1)S(1)}, u32[]{:S(2)}, u32[]{:S(2)}) collective-permute-start(bf16[512,768]{1,0:T(8,128)(2,1)S(1)} %get-tuple-element.255), channel_id=1, source_target_pairs={{0,8},{8,0},{16,24},{24,16},{1,9},{9,1},{17,25},{25,17},{2,10},{10... | collective-permute-start | bytes 2359304 | tf_op jit(solution)/shard_map/ppermute | solution.py:954
  424.4 206.1 %collective-permute-start.14 = (bf16[512,768]{1,0:T(8,128)(2,1)S(1)}, bf16[512,768]{1,0:T(8,128)(2,1)}, u32[]{:S(2)}, u32[]{:S(2)}) collective-permute-start(bf16[512,768]{1,0:T(8,128)(2,1)S(1)} %reduce-precision_convert_fusion), channel_id=1, source_target_pairs={{0,1},{9,8},{16,17},{25,24},{2,3},{11,10},{18,19},{27,26},{4,5},{1... | collective-permute-start | bytes 2359304 | tf_op jit(solution)/shard_map/ppermute | solution.py:978
  534.6 119.2 %collective-permute-start.13 = (bf16[512,768]{1,0:T(8,128)(2,1)S(1)}, bf16[512,768]{1,0:T(8,128)(2,1)S(1)}, u32[]{:S(2)}, u32[]{:S(2)}) collective-permute-start(bf16[512,768]{1,0:T(8,128)(2,1)S(1)} %reduce-precision_convert_fusion.1), channel_id=1, source_target_pairs={{0,1},{9,8},{16,17},{25,24},{2,3},{11,10},{18,19},{27,26},{4,5},{1... | collective-permute-start | bytes 2359304 | tf_op jit(solution)/shard_map/ppermute | solution.py:978
  536.4 96.6 %collective-permute-start.15 = (f32[16896]{0:T(1024)S(1)}, f32[16896]{0:T(1024)S(1)}, u32[]{:S(2)}, u32[]{:S(2)}) collective-permute-start(f32[16896]{0:T(1024)S(1)} %constant_dynamic-update-slice_fusion), channel_id=1, source_target_pairs={{0,16},{8,24},{16,0},{24,8},{1,17},{9,25},{17,1},{25,9},{2,18},{10... | collective-permute-start | bytes 202760 | tf_op jit(solution)/shard_map/ppermute | solution.py:960
  633.0 3.8 collective-permute-start.16
  636.8 6.0 collective-permute-start.17
  642.8 2.6 collective-permute-start.19
  642.8 3.3 collective-permute-start.18
  645.4 2.9 collective-permute-start.20
  648.3 1.8 collective-permute-start.21
  (85 other events, 338.8 us)

commit v4 on v3

--- a/solution.py
+++ b/solution.py
@@ -36,6 +36,10 @@
 
 def rounded(value):
     return lax.reduce_precision(value, 8, 7)
+
+
+def after(array):
+    return jnp.minimum(jnp.abs(array[0, 0].astype(F32)), 0.0)
 
 
 def norm_forward(hidden, gain, shift):
@@ -183,13 +187,14 @@
 
 
 def backward_block(
-    index, rows, partial, block, mask, kv_ref, lse_ref, dkv_ref, masked_q, masked_do, delta, dq
+    index, rows, block, mask, kv_ref, lse_ref, dkv_ref, masked_q, masked_do, delta, dq, between
 ):
     heads = masked_q.shape[0]
     width = heads * HEAD_DIM
-    if partial:
-        allowed = mask.allowed(index, block)
+    allowed = mask.allowed(index, block)
     for pair in range(heads // 2):
+        if pair == 1:
+            between()
         cols = head_columns(2 * pair)
         later = slice(width + cols.start, width + cols.stop)
         keys, vals = kv_ref[rows, cols], kv_ref[rows, later]
@@ -197,8 +202,7 @@
         for head in (2 * pair, 2 * pair + 1):
             scores = lax.dot_general(keys, masked_q[head], NT, preferred_element_type=F32)
             probs = jnp.exp(scores - lse_ref[head : head + 1, :])
-            if partial:
-                probs = jnp.where(allowed, probs, 0.0)
+            probs = jnp.where(allowed, probs, 0.0)
             dprobs = lax.dot_general(vals, masked_do[head], NT, preferred_element_type=F32)
             draw = (probs * (dprobs - delta[head : head + 1, :])).astype(BF16)
             probs = probs.astype(BF16)
@@ -372,83 +376,122 @@
                 self.across(way, step, shard, 1 - self.here.core).wait_recv()
 
 
+def pieces_of(weights):
+    found = []
+    for k, weight in enumerate(weights):
+        rows, columns = weight.shape
+        number = 3 if rows == 6 * columns else 1
+        while 2 * rows * columns > 655360 * number and rows % (64 * number) == 0:
+            number *= 2
+        found += [(k, i * (rows // number), rows // number) for i in range(number)]
+    return found
+
+
+def beside(weight, model):
+    rows, columns = weight.shape
+    matrices = 3 if rows == 3 * model else 1
+    return jax.ShapeDtypeStruct((rows // matrices, columns * matrices), weight.dtype)
+
+
 class Fetch:
     def __init__(self, here, inputs, outputs, sems):
         self.here, self.inputs, self.outputs = here, inputs, outputs
         self.y_sent, self.y_got, self.x_sent, self.x_got, self.core_sent, self.core_got = sems
-        self.x_partner = (here.d + 2 - 4 * lax.rem(here.x, 2), here.z, here.y)
-        self.y_partner = (here.other_d, here.z, 1 - here.y)
+        self.pieces = pieces_of(inputs)
+        self.matrices = [
+            (k, matrix)
+            for k, (given, out) in enumerate(zip(inputs, outputs))
+            for matrix in range(given.shape[0] // out.shape[0])
+        ]
+        self.number = len(self.pieces)
+        self.own = lax.rem(here.x, 2)
 
     def devices(self):
         here = self.here
-        return [(here.core >= 0, self.y_partner), (here.core == 1, self.x_partner)]
-
-    def part(self, ref, which):
-        rows = ref.shape[0] // 2
-        return ref.at[pl.ds(pl.multiple_of(which * rows, rows), rows)]
-
-    def over_y(self, k):
-        which = lax.rem(self.here.x, 2)
+        return [(here.core >= 0, here.diagonal), (here.core == 1, here.over_x)]
+
+    def part(self, p, which):
+        k, start, rows = self.pieces[p]
+        first = pl.multiple_of(start + which * (rows // 2), 16)
+        return self.inputs[k].at[pl.ds(first, rows // 2)]
+
+    def place(self, p, which):
+        k, start, rows = self.pieces[p]
+        out = self.outputs[k]
+        matrix, start = divmod(start, out.shape[0])
+        columns = self.inputs[k].shape[1]
+        first = pl.multiple_of(start + which * (rows // 2), 16)
+        return out.at[pl.ds(first, rows // 2), pl.ds(matrix * columns, columns)]
+
+    def over_y(self, p):
         return remote(
-            self.part(self.inputs[k], which),
-            self.part(self.outputs[k], which),
-            self.y_sent.at[k],
-            self.y_got.at[k],
-            self.y_partner,
+            self.part(p, self.own),
+            self.place(p, self.own),
+            self.y_sent.at[p],
+            self.y_got.at[p],
+            self.here.diagonal,
         )
 
-    def over_x(self, k, which):
-        view = self.part(self.outputs[k], which)
-        return remote(view, view, self.x_sent.at[k], self.x_got.at[k], self.x_partner)
-
-    def across(self, k):
+    def over_x(self, p, which):
+        view = self.place(p, which)
+        return remote(view, view, self.x_sent.at[p], self.x_got.at[p], self.here.over_x)
+
+    def across(self, m):
+        k, matrix = self.matrices[m]
+        rows, columns = self.outputs[k].shape[0], self.inputs[k].shape[1]
         return remote(
-            self.inputs[k], self.outputs[k], self.core_sent.at[k], self.core_got.at[k], self.here.partner
+            self.inputs[k].at[pl.ds(matrix * rows, rows)],
+            self.outputs[k].at[:, pl.ds(matrix * columns, columns)],
+            self.core_sent.at[m],
+            self.core_got.at[m],
+            self.here.partner,
         )
 
     def begin(self):
         @pl.when(self.here.core == 0)
         def _():
-            for k in range(min(2, len(self.inputs))):
-                self.over_y(k).start()
+            for p in range(min(2, self.number)):
+                self.over_y(p).start()
 
         @pl.when(self.here.core == 1)
         def _():
-            for k in range(len(self.inputs)):
-                self.across(k).start()
-
-    def advance(self, k):
+            for m in range(len(self.matrices)):
+                self.across(m).start()
+
+    def advance(self, p):
         @pl.when(self.here.core == 0)
         def _():
-            self.over_y(k).wait_send()
-            if k + 2 < len(self.inputs):
-                self.over_y(k + 2).start()
+            self.over_y(p).wait_send()
+            if p + 2 < self.number:
+                self.over_y(p + 2).start()
 
         @pl.when(self.here.core == 1)
         def _():
-            self.over_y(k).wait_recv()
-            self.over_x(k, lax.rem(self.here.x, 2)).start()
+            self.over_y(p).wait_recv()
+            self.over_x(p, self.own).start()
 
     def end(self):
         @pl.when(self.here.core == 0)
         def _():
-            for k in range(len(self.inputs)):
-                self.across(k).wait_recv()
+            for m in range(len(self.matrices)):
+                self.across(m).wait_recv()
 
         @pl.when(self.here.core == 1)
         def _():
-            for k in range(len(self.inputs)):
-                self.over_x(k, lax.rem(self.here.x, 2)).wait_send()
-                self.over_x(k, 1 - lax.rem(self.here.x, 2)).wait_recv()
-                self.across(k).wait_send()
+            for p in range(self.number):
+                self.over_x(p, self.own).wait_send()
+                self.over_x(p, 1 - self.own).wait_recv()
+            for m in range(len(self.matrices)):
+                self.across(m).wait_send()
 
 
 def gather_sems(ring):
     return [DMA((2, ring))] * 4
 
 
-def fetch_sems(number):
-    return [DMA((number,))] * 6
+def fetch_sems(weights):
+    number = len(pieces_of(weights))
+    return [DMA((number,))] * 4 + [DMA((3 * len(weights),))] * 2
 
 
 def opening_kernel(ring, number, *refs):
@@ -479,7 +522,7 @@
     def vector_copy():
         sent, got, copied = vector_sems
         return (
-            remote(vectors, vectors_out, sent, got, fetch.y_partner),
+            remote(vectors, vectors_out, sent, got, here.diagonal),
             pltpu.make_async_copy(vectors, vectors_out, copied),
         )
 
@@ -517,7 +560,7 @@
         for step in range(1, ring):
             gather.start(step)
             slot = k * (ring - 1) + step
-            while done < number * slot // slots:
+            while done < fetch.number * slot // slots:
                 fetch.advance(done)
                 done += 1
             gather.arrive(step)
@@ -542,33 +585,42 @@
     inputs = (source, target, segments, vectors) + tuple(weights)
     count, model = source.shape
     rows = jax.ShapeDtypeStruct((ring * count, model), BF16)
-    shapes = (rows, rows) + tuple(jax.ShapeDtypeStruct(v.shape, v.dtype) for v in inputs[2:])
+    shapes = (rows, rows) + tuple(jax.ShapeDtypeStruct(v.shape, v.dtype) for v in inputs[2:4])
+    shapes += tuple(beside(weight, model) for weight in weights)
     number = len(weights)
     return pl.pallas_call(
         functools.partial(opening_kernel, ring, number),
         out_shape=shapes,
         in_specs=[VECTORS] * 4 + [ANYWHERE] * number,
         out_specs=(ANYWHERE,) * 2 + (VECTORS,) * 2 + (ANYWHERE,) * number,
-        scratch_shapes=[DMA((3,))] * 3 + [DMA] * 3 + gather_sems(ring) * 2 + fetch_sems(number),
+        scratch_shapes=[DMA((3,))] * 3 + [DMA] * 3 + gather_sems(ring) * 2 + fetch_sems(weights),
         compiler_params=pltpu.CompilerParams(collective_id=1, has_side_effects=True),
     )(*inputs)
 
 
-def gather_attend_kernel(block, causal, ring, tokens, starts, segments, q_ref, kv_ref, own_ref, *refs):
-    out_ref, lse_ref, all_ref, masked_q, acc, top, copied = refs[tokens : tokens + 7]
+def gather_attend_kernel(
+    block, causal, ring, number, tokens, starts, segments, q_ref, kv_ref, own_ref, *refs
+):
+    weights, refs = refs[:number], refs[number + tokens :]
+    out_ref, lse_ref, all_ref = refs[:3]
+    fetched, refs = refs[3 : 3 + number], refs[3 + number :]
+    masked_q, acc, top, copied = refs[:4]
     here = Here(ring)
-    gather = Gather(here, all_ref, refs[tokens + 7 :])
-    here.meet(here.neighbours())
+    gather = Gather(here, all_ref, refs[4:8])
+    fetch = Fetch(here, weights, fetched, refs[8:])
+    here.meet(here.neighbours() + fetch.devices())
     count = own_ref.shape[0]
     first_row = pl.multiple_of(here.z * count, count)
     local = pltpu.make_async_copy(own_ref, all_ref.at[pl.ds(first_row, count)], copied)
     local.start()
+    fetch.begin()
     local.wait()
     gather.start(1)
     mask = Mask(causal, starts, segments, first_row)
     forward_start(q_ref, masked_q, acc, top)
-
-    @pl.loop(0, kv_ref.shape[0] // block)
+    blocks = kv_ref.shape[0] // block
+
+    @pl.loop(0, blocks)
     def _(index):
         rows = pl.ds(pl.multiple_of(index * block, block), block)
         forward_block(index, rows, True, block, kv_ref, mask, masked_q, acc, top)
@@ -581,31 +633,43 @@
         def _():
             gather.start(index + 1)
 
+        for p in range(min(fetch.number, blocks - 1)):
+            pl.when(index == p + 1)(functools.partial(fetch.advance, p))
+
     forward_end(out_ref, lse_ref, acc, top)
+    for p in range(min(fetch.number, blocks - 1), fetch.number):
+        fetch.advance(p)
 
     @pl.loop(1, ring)
     def _(step):
         gather.finish(step)
 
-
-def gather_attend(ring, queries, kv, mask, own, tokens):
+    fetch.end()
+
+
+def gather_attend(ring, queries, kv, mask, own, weights, tokens):
     count, width = queries.shape
     causal, starts, _, segments = mask
+    number = len(weights)
     return pl.pallas_call(
-        functools.partial(gather_attend_kernel, KEY_BLOCK, causal, ring, len(tokens)),
+        functools.partial(gather_attend_kernel, KEY_BLOCK, causal, ring, number, len(tokens)),
         out_shape=(
             jax.ShapeDtypeStruct((width, count), F32),
             jax.ShapeDtypeStruct((8, count), F32),
             jax.ShapeDtypeStruct((ring * own.shape[0], own.shape[1]), BF16),
-        ),
-        in_specs=[SCALARS] + [VECTORS] * 4 + [ANYWHERE] * len(tokens),
-        out_specs=(VECTORS, VECTORS, ANYWHERE),
-        scratch_shapes=forward_scratch(count, width) + [DMA] + gather_sems(ring),
+        )
+        + tuple(beside(weight, own.shape[1]) for weight in weights),
+        in_specs=[SCALARS] + [VECTORS] * 4 + [ANYWHERE] * (number + len(tokens)),
+        out_specs=(VECTORS, VECTORS) + (ANYWHERE,) * (1 + number),
+        scratch_shapes=forward_scratch(count, width)
+        + [DMA]
+        + gather_sems(ring)
+        + fetch_sems(weights),
         compiler_params=pltpu.CompilerParams(
             vmem_limit_bytes=40 << 20, collective_id=2, has_side_effects=True
         ),
         cost_estimate=cost_of(kv, count, width, 2),
-    )(starts, segments, queries, kv, own, *tokens)
+    )(starts, segments, queries, kv, own, *weights, *tokens)
 
 
 class Part:
@@ -770,6 +834,85 @@
     return Part((array,), [VECTORS], [final], scratch, bind)
 
 
+class Small:
+    def __init__(self, here, rows, held_rows, given, result, refs, times):
+        self.here, self.given, self.result, self.times = here, given, result, times
+        self.rows, self.held_rows = rows, held_rows
+        self.arrived, self.sent, self.got = refs
+        self.bits = [lax.rem(here.z, 2), lax.div(here.z, 2)]
+
+    def copies(self, stage):
+        here = self.here
+        low, high = self.bits
+
+        def to(device, slot, source=self.result, target=None):
+            target = self.arrived.at[slot] if target is None else target
+            return remote(source, target, self.sent.at[slot], self.got.at[slot], device)
+
+        if stage < 3:
+            device = (
+                here.over_x,
+                (here.d, here.z + 1 - 2 * low, here.y),
+                (here.d, here.z + 2 - 4 * high, here.y),
+            )[stage]
+            both = [(None, to(device, stage))]
+            return both, both
+        if stage == 3:
+            sends = [
+                (None, to(here.over_y, 3)),
+                (here.core == 0, to(here.partner, 4)),
+                (here.core == 1, to(here.diagonal, 4)),
+            ]
+            return sends, sends[:1] + [(None, to(here.partner, 4))]
+        return [(here.core == 0, to(here.partner, 5))], [(here.core == 1, to(here.partner, 5))]
+
+    def end(self, stage):
+        sends, arrivals = self.copies(stage)
+        Stage.each(arrivals, lambda copy: copy.wait_recv())
+        Stage.each(sends, lambda copy: copy.wait_send())
+        core = self.here.core
+        if stage < 3:
+            self.result[...] += self.arrived[stage]
+        elif stage == 3:
+            whole, halves = slice(0, self.held_rows), slice(self.held_rows, self.rows)
+            self.result[whole, :] += self.arrived[3, whole, :]
+            own = jnp.where(core == 0, self.result[halves, :], self.arrived[3, halves, :])
+            self.result[halves, :] = own + self.arrived[4, halves, :]
+        else:
+            whole = slice(0, self.held_rows)
+
+            @pl.when(core == 1)
+            def _():
+                self.result[whole, :] = self.arrived[5, whole, :]
+
+    def event(self, time):
+        for k, own in enumerate(self.times):
+            if own == time:
+                if k == 0:
+                    self.result[...] = self.given[...]
+                else:
+                    self.end(k - 1)
+                if k < 5:
+                    Stage.each(self.copies(k)[0], lambda copy: copy.start())
+
+
+def small_sums(whole, halves, times):
+    both = jnp.concatenate([whole, halves])
+    rows, columns = both.shape
+    shape = jax.ShapeDtypeStruct(both.shape, F32)
+    part = Part(
+        (both,),
+        [VECTORS],
+        [shape],
+        [pltpu.VMEM((6, rows, columns), F32), DMA((6,)), DMA((6,))],
+        lambda here, inputs, outputs, refs: Small(
+            here, rows, whole.shape[0], inputs[0], outputs[0], refs, times
+        ),
+    )
+    part.rows, part.vectors = whole.shape[0], (whole.reshape(-1), halves.reshape(-1))
+    return part
+
+
 def run_chains(number, chains, events):
     def body(here, *bound):
         for time in range(events):
@@ -783,7 +926,7 @@
     def __init__(self, here, causal, apart, inputs, outputs, scratch):
         self.here, self.causal, self.apart = here, causal, apart
         self.starts, self.segments, self.q, self.kv, self.do, self.dot, self.out, self.lse = inputs[:8]
-        self.w_q, self.w_kv = inputs[8:]
+        self.weights = inputs[8]
         self.dq_out, self.dkv, self.sum = outputs[:3]
         self.query_sum = outputs[3] if apart else None
         self.work, scratch = scratch[:4], scratch[4:]
@@ -791,103 +934,146 @@
         self.core_sent, self.core_got, self.sent, self.got, self.end_sent, self.end_got = scratch[5:11]
         if apart:
             self.query_low, self.query_got, self.query_sems = scratch[11:]
-        self.count = self.q.shape[0]
+        self.count, self.width = self.q.shape
         self.part = self.count // 2
         self.mask = Mask(causal, self.starts, self.segments, here.z * self.count)
 
     def half(self, core):
         return pl.ds(pl.multiple_of(core * self.part, self.part), self.part)
 
-    def across(self, step):
+    def shard_at(self, turn):
+        ring, z, shard = self.here.ring, self.here.z, 0
+        for device in range(ring):
+            others = [t for t in range(ring) if t != device]
+            others.sort(key=lambda t: (ring - t + device) if t > device else (t + ring - device))
+            for k, other in enumerate(others):
+                shard = jnp.where((z == device) & (turn == k + 1), other, shard)
+        return shard
+
+    def across(self, shard):
         return remote(
-            self.terms.at[step, self.half(1 - self.here.core)],
-            self.from_core.at[step],
-            self.core_sent.at[step],
-            self.core_got.at[step],
+            self.terms.at[shard, self.half(1 - self.here.core)],
+            self.from_core.at[shard],
+            self.core_sent.at[shard],
+            self.core_got.at[shard],
             self.here.partner,
         )
 
-    def along(self, step):
+    def along(self, way, shard, device):
         return remote(
-            self.outgoing.at[step],
-            self.arrived.at[step],
-            self.sent.at[step],
-            self.got.at[step],
-            self.here.along_z(step),
+            self.outgoing.at[shard],
+            self.arrived.at[way, shard],
+            self.sent.at[shard],
+            self.got.at[way, shard],
+            device,
         )
 
-    def both(self, step):
-        self.across(step).wait_recv()
-        own = self.terms[step, self.half(self.here.core), :].astype(F32)
-        return own + self.from_core[step].astype(F32)
-
-    def forward(self, step):
-        self.outgoing[step] = self.both(step).astype(BF16)
-        self.along(step).start()
-
-    def block(self, step):
-        shard = lax.rem(self.here.z + step, self.here.ring)
+    def both(self, shard):
+        self.across(shard).wait_recv()
+        own = self.terms[shard, self.half(self.here.core), :].astype(F32)
+        return own + self.from_core[shard].astype(F32)
+
+    def forward(self, shard):
+        here = self.here
+        self.total[...] = self.both(shard)
+        for way, mine, comes, device in (
+            (0, shard > here.z, here.z > 0, here.right),
+            (1, shard < here.z, here.z + 1 < here.ring, here.left),
+        ):
+
+            @pl.when(mine & comes)
+            def _(way=way):
+                self.along(way, shard, here.partner).wait_recv()
+                self.total[...] += self.arrived[way, shard].astype(F32)
+
+        self.outgoing[shard] = self.total[...].astype(BF16)
+        for way, mine, device in ((0, shard > here.z, here.right), (1, shard < here.z, here.left)):
+
+            @pl.when(mine)
+            def _(way=way, device=device):
+                self.along(way, shard, device).start()
+
+    def block(self, shard, between):
         rows = pl.ds(pl.multiple_of(shard * self.count, self.count), self.count)
         backward_block(
-            shard, rows, True, self.count, self.mask, self.kv, self.lse, self.dkv, *self.work
+            shard, rows, self.count, self.mask, self.kv, self.lse, self.dkv, *self.work, between
         )
-        return dot_last(self.dkv[rows, :], self.w_kv[...])
+        return dot_last(self.dkv[rows, :], self.weights[:, self.width :])
 
     def run(self, event):
-        ring = self.here.ring
+        here, ring = self.here, self.here.ring
+        at_end = (here.z == 0) | (here.z == ring - 1)
         event(0)
         backward_start(self.q, self.do, self.dot, self.out, *self.work)
 
         @pl.loop(1, ring)
-        def _(step):
-            self.terms[step] = self.block(step).astype(BF16)
-            self.across(step).start()
-
-            @pl.when(step > 1)
-            def _():
-                self.forward(step - 1)
-
+        def _(turn):
+            shard = self.shard_at(turn)
+
+            def between():
+                @pl.when((turn > 1) & at_end)
+                def _():
+                    self.forward(self.shard_at(turn - 1))
+
+            self.terms[shard] = self.block(shard, between).astype(BF16)
+            self.across(shard).start()
             for time in range(1, ring):
-                pl.when(step == time)(functools.partial(event, time))
-
-        own = self.block(0)
-        self.forward(ring - 1)
+                pl.when(turn == time)(functools.partial(event, time))
+
+        def between():
+            self.forward(self.shard_at(jnp.where(at_end, ring - 1, 1)))
+
+        own = self.block(here.z, between)
         event(ring)
         low = (self.work[3][...] * HEAD_DIM ** (-0.5)).T.astype(BF16)
         self.dq_out[...] = low
-        query = dot_last(low, self.w_q[...])
+        query = dot_last(low, self.weights[:, : self.width])
         if self.apart:
             self.query_low[...] = query.astype(BF16)
             exchange = remote(
-                self.query_low, self.query_got, self.query_sems.at[0], self.query_sems.at[1], self.here.partner
+                self.query_low, self.query_got, self.query_sems.at[0], self.query_sems.at[1], here.partner
             )
             exchange.start()
         else:
             own = own + query
-        self.terms[0] = own.astype(BF16)
-        self.across(0).start()
+        self.terms[here.z] = own.astype(BF16)
+        self.across(here.z).start()
         if self.apart:
             exchange.wait()
             self.query_sum[...] = self.query_low[...].astype(F32) + self.query_got[...].astype(F32)
-        self.total[...] = self.both(0)
+
+        @pl.when(jnp.logical_not(at_end))
+        def _():
+            @pl.loop(2, ring)
+            def _(turn):
+                self.forward(self.shard_at(turn))
+
         event(ring + 1)
-        for step in range(1, ring):
-            self.along(step).wait_recv()
-            self.total[...] += self.arrived[step].astype(F32)
-        own, other = self.half(self.here.core), self.half(1 - self.here.core)
+        self.total[...] = self.both(here.z)
+        for way, comes in ((0, here.z > 0), (1, here.z + 1 < ring)):
+
+            @pl.when(comes)
+            def _(way=way):
+                self.along(way, here.z, here.partner).wait_recv()
+                self.total[...] += self.arrived[way, here.z].astype(F32)
+
+        own, other = self.half(here.core), self.half(1 - here.core)
         self.sum[own, :] = self.total[...].astype(BF16)
         for half, waits in ((own, False), (other, True)):
             view = self.sum.at[half]
-            copy = remote(view, view, self.end_sent, self.end_got, self.here.partner)
+            copy = remote(view, view, self.end_sent, self.end_got, here.partner)
             if waits:
                 copy.wait_recv()
             else:
                 copy.start()
                 copy.wait_send()
-        for step in range(ring):
-            self.across(step).wait_send()
-            if step:
-                self.along(step).wait_send()
+        for shard in range(ring):
+            self.across(shard).wait_send()
+
+            @pl.when(here.z != shard)
+            def _(shard=shard):
+                self.along(0, shard, here.partner).wait_send()
+
         event(ring + 2)
 
 
@@ -905,17 +1091,19 @@
     ]
     scratch = backward_scratch(count, width) + [
         pltpu.VMEM((ring, count, model), BF16),
-        *[pltpu.VMEM((ring, part, model), BF16)] * 3,
+        *[pltpu.VMEM((ring, part, model), BF16)] * 2,
+        pltpu.VMEM((2, ring, part, model), BF16),
         pltpu.VMEM((part, model), F32),
-        *[DMA((ring,))] * 4,
+        *[DMA((ring,))] * 3,
+        DMA((2, ring)),
         *[DMA] * 2,
     ]
     if apart:
         shapes.append(jax.ShapeDtypeStruct((count, model), F32))
         scratch += [pltpu.VMEM((count, model), BF16)] * 2 + [DMA((2,))]
     main = Part(
-        (starts, segments, queries, kv, grad_mixed, grad_mixed_t, output, lse, *weights[:2]),
-        [SCALARS] + [VECTORS] * 9,
+        (starts, segments, queries, kv, grad_mixed, grad_mixed_t, output, lse, weights[0]),
+        [SCALARS] + [VECTORS] * 8,
         shapes,
         scratch,
         lambda here, *refs: Back(here, causal, apart, *refs),
@@ -1051,10 +1239,11 @@
 
 
 def projected(query_in, key_in, weights):
-    w_q, w_kv, b_q, b_kv = weights
+    w_all, b_q, b_kv = weights
+    width = b_q.shape[0]
     scale = HEAD_DIM ** (-0.5)
-    queries = ((dot_plain(query_in, w_q) + b_q).astype(BF16) * scale).astype(BF16)
-    return queries, (dot_plain(key_in, w_kv) + b_kv).astype(BF16)
+    queries = ((dot_plain(query_in, w_all[:, :width]) + b_q).astype(BF16) * scale).astype(BF16)
+    return queries, (dot_plain(key_in, w_all[:, width:]) + b_kv).astype(BF16)
 
 
 def attention_output(place, queries, kv, output, lse, out_weight, out_bias):
@@ -1163,8 +1352,6 @@
         dec_self_proj,
         enc_ff_in,
         enc_ff_out,
-        dec_cross,
-        dec_cross_proj,
     ) = opening(
         ring,
         source[0],
@@ -1178,8 +1365,6 @@
             dec_self_proj,
             enc_ff_in,
             enc_ff_out,
-            dec_cross.reshape(-1, width),
-            dec_cross_proj,
         ),
     )
     vectors = vectors.reshape(-1)
@@ -1196,13 +1381,11 @@
     )
 
     def prepared(qkv, bias):
-        qkv = qkv.reshape(3, model, width)
         b_kv = jnp.concatenate([jnp.zeros((width,), F32), bias[width:]])
-        return (qkv[0], jnp.concatenate([qkv[1], qkv[2]], axis=1), bias[:width], b_kv)
+        return (qkv, bias[:width], b_kv)
 
     enc_w = prepared(enc_qkv, enc_qv_bias)
     self_w = prepared(dec_self, dec_self_bias)
-    cross_w = prepared(dec_cross, dec_cross_bias)
 
     source_keys, target_keys = segments[0], segments[1]
     source_own = lax.dynamic_slice_in_dim(source_keys, first_row, count, 0)
@@ -1217,6 +1400,7 @@
     branch, enc_attn = attention_output(place, queries, kv, output, lse, enc_proj, enc_bias[0])
     first, enc_norm_one = norm_forward(xs.astype(F32) + branch, enc_gains[0], enc_shifts[0])
     first_low = first.astype(BF16)
+    enc_ff_in_bias = enc_ff_in_bias + after(dec_ff_in)
     branch, enc_feed = feed_forward(
         place, first_low, enc_ff_in, enc_ff_in_bias, enc_ff_out, enc_bias[1]
     )
@@ -1224,9 +1408,16 @@
     encoded_low = encoded.astype(BF16)
 
     queries, kv = projected(ts, t_all, self_w)
-    output, lse, e_all = gather_attend(
-        ring, queries, kv, self_mask, encoded_low, (dec_ff_in, dec_ff_out)
-    )
+    output, lse, e_all, dec_cross, dec_cross_proj = gather_attend(
+        ring,
+        queries,
+        kv,
+        self_mask,
+        encoded_low,
+        (dec_cross.reshape(-1, width), dec_cross_proj),
+        (dec_ff_out,),
+    )
+    cross_w = prepared(dec_cross, dec_cross_bias)
     branch, self_attn = attention_output(
         place, queries, kv, output, lse, dec_self_proj, dec_bias[0]
     )
@@ -1291,11 +1482,11 @@
         False,
         plan,
             [
-                (dec_w_in, "y", (0, 6)),
-                (dec_w_out, "x", (0, 6)),
-                (cross_kv, "x", (0, 6)),
-                (cross_q, "y", (0, 6)),
-                (cross_proj, "y", (0, 6)),
+                (dec_w_in, "yvw", (0, 3, 5, 6)),
+                (dec_w_out, "xvw", (0, 3, 5, 6)),
+                (cross_kv, "x", (1, 6)),
+                (cross_q, "y", (1, 6)),
+                (cross_proj, "y", (1, 6)),
             ],
     )
     dec_w_in, dec_w_out, cross_kv, cross_q, cross_proj = given
@@ -1325,44 +1516,31 @@
         False,
         plan,
             [
-                (cross_kv, "y", (0, 6)),
-                (cross_q, "x", (0, 6)),
-                (cross_proj, "x", (0, 6)),
+                (cross_kv, "yvw", (0, 3, 5, 6)),
+                (cross_q, "xvw", (0, 3, 5, 6)),
+                (cross_proj, "xvw", (0, 3, 5, 6)),
                 (enc_w_in, "x", (0, 6)),
                 (enc_w_out, "y", (0, 6)),
-                (dec_w_in, "vw", (0, 4, 6)),
-                (dec_w_out, "vw", (0, 4, 6)),
+                (self_kv, "x", (2, 6)),
+                (self_q, "y", (2, 6)),
+                (self_proj, "y", (2, 6)),
             ],
     )
-    cross_kv, cross_q, cross_proj, enc_w_in, enc_w_out, dec_w_in, dec_w_out = given
+    cross_kv, cross_q, cross_proj, enc_w_in, enc_w_out, self_kv, self_q, self_proj = given
     enc_bias_one = column_sum(grad_branch)
     grad_source = grad_hidden + source_total.astype(F32)
     enc_q, enc_proj_grad, enc_kv = enc_grads
     rest = [
-        (enc_kv, "xyvw", (0, 2, 4, 5, 6)),
-        (enc_q, "yxvw", (0, 2, 4, 5, 6)),
-        (enc_proj_grad, "yxvw", (0, 2, 4, 5, 6)),
-        (self_kv, "xyvw", (0, 1, 3, 4, 5)),
-        (self_q, "yxvw", (0, 1, 3, 4, 5)),
-        (self_proj, "yxvw", (0, 1, 3, 4, 5)),
-        (enc_w_in, "yvw", (0, 2, 3, 4)),
-        (enc_w_out, "xvw", (0, 2, 3, 4)),
-        (cross_kv, "vw", (0, 1, 2)),
-        (cross_q, "vw", (0, 1, 2)),
-        (cross_proj, "vw", (0, 1, 2)),
+        (enc_w_in, "yvw", (0, 1, 2, 4)),
+        (enc_w_out, "xvw", (0, 1, 2, 4)),
+        (self_kv, "yvw", (0, 1, 2, 4)),
+        (self_q, "xvw", (0, 1, 2, 4)),
+        (self_proj, "xvw", (0, 1, 2, 4)),
+        (enc_kv, "xyvw", (1, 3, 4, 5, 6)),
+        (enc_q, "yxvw", (1, 3, 4, 5, 6)),
+        (enc_proj_grad, "yxvw", (1, 3, 4, 5, 6)),
     ]
-    if plan.kernels:
-        given = run_chains(6, plan.chains(rest), 7)
-    else:
-        given = [place.scatter(array, True) for array, _, _ in rest]
-        dec_w_in, dec_w_out = (place.scatter(array, True) for array in (dec_w_in, dec_w_out))
-    enc_kv, enc_q, enc_proj_grad, self_kv, self_q, self_proj = given[:6]
-    enc_w_in, enc_w_out, cross_kv, cross_q, cross_proj = given[6:]
-
-    def qkv_grads(of_q, of_kv):
-        return jnp.stack([of_q, of_kv[:, :width], of_kv[:, width:]])
-
-    whole, halves = place.all_sum(
+    small = small_sums(
         jnp.concatenate(
             [
                 enc_bias_one,
@@ -1381,10 +1559,26 @@
                 dec_shift_two,
                 dec_shift_three,
             ]
-        ),
-        jnp.concatenate([enc_bias_grad, self_bias, cross_bias, enc_b_in, dec_b_in]),
-    )
-    whole = whole.reshape(15, model)
+        ).reshape(15, model),
+        jnp.concatenate([enc_bias_grad, self_bias, cross_bias, enc_b_in, dec_b_in]).reshape(-1, model),
+        (0, 1, 2, 3, 4, 5),
+    )
+    if plan.kernels:
+        vectors, *given = run_chains(6, [small] + plan.chains(rest), 7)
+        whole, halves = vectors[: small.rows], vectors[small.rows :]
+    else:
+        whole, halves = place.all_sum(*small.vectors)
+        given = [place.scatter(array, True) for array, _, _ in rest]
+        dec_w_in, dec_w_out, cross_kv, cross_q, cross_proj = (
+            place.scatter(array, True)
+            for array in (dec_w_in, dec_w_out, cross_kv, cross_q, cross_proj)
+        )
+    enc_w_in, enc_w_out, self_kv, self_q, self_proj, enc_kv, enc_q, enc_proj_grad = given
+
+    def qkv_grads(of_q, of_kv):
+        return jnp.stack([of_q, of_kv[:, :width], of_kv[:, width:]])
+
+    whole, halves = whole.reshape(-1, model), halves.reshape(-1)
     small = [halves[a:b] for a, b in zip(marks[:-1], marks[1:])]
     return (
         place.hand_out(encoded_low)[None],

time: 669 us -> 606 us (0.906)
  Pallas kernels: 436 us -> 397 us
  waiting for transfers between devices: 41.1 us -> 7.97 us
  starting transfers between devices: 11.9 us -> 21.7 us
  local copies, waits for them, and re-layouts: 34.1 us -> 26.1 us
    pallas_call x4, Pallas kernels: 294 us -> 251 us  [run_parts(): pl.pallas_call(kernel, out_shape=[shape for p in parts for shape in p.out...]
    ppermute x7 -> x6, waiting for transfers between devices: 28.6 us -> 5.48 us  [permute(): return lax.ppermute(value, ('dp', 'tensor'), moves)]
    ppermute x10 -> x9, starting transfers between devices: 2.87 us -> 15.3 us  [swap_core(): return lax.ppermute(value, 'dp', [(i, i ^ 1) for i in range(self.pairs)])]
    ppermute x5 -> x0, waiting for transfers between devices: 10.5 us -> none  [the longest x2 8.18 us: swap_z(): lax.ppermute(value, 'seq', [(i, i ^ 1 << bit) for i in range(self.ring)])]
    unnamed x223 -> x198, local copies, waits for them, and re-layouts: 16.4 us -> 11.6 us
  transfers between devices with their start and end apart: 22 -> 15, of which waited for: 8 -> 4; matrix products, arithmetic and copies ran while one was open for 18% -> 23% of each run, Pallas kernels for 45% -> 59%
where the time goes in v4:
time: 606 us; the launch traced here: 596 us
  Pallas kernels  397 us (66%)
  matrix products  95.5 us (16%)
  other arithmetic  44.3 us (7%)
  local copies, waits for them, and re-layouts  26.1 us (4%)
  starting transfers between devices  21.7 us (4%)
  waiting for transfers between devices  7.97 us (1%)
    pallas_call x4, Pallas kernels, run_parts(): pl.pallas_call(kernel, out_shape=[shape for p in parts for shape in p.out...  251 us
    pallas_call x1, Pallas kernels, opening(): pl.pallas_call(functools.partial(opening_kernel, ring, number), out_shape...  86.4 us
    pallas_call x1, Pallas kernels, gather_attend(): pl.pallas_call(functools.partial(gather_attend_kernel, KEY_BLOCK, causal,...  40.3 us
    dot_general x10, matrix products, dot_plain(): return jnp.dot(left, right, preferred_element_type=F32)  39.4 us
    dot_general x13, matrix products, dot_first(): return lax.dot_general(left, right, TN, preferred_element_type=F32)  34.7 us
    pallas_call x2, Pallas kernels, attend(): pl.pallas_call(functools.partial(forward_kernel, KEY_BLOCK, causal), out_...  19.4 us
    dot_general x10, matrix products, dot_last(): return lax.dot_general(left, right, NT, preferred_element_type=F32)  17 us
    ppermute x9, starting transfers between devices, swap_core(): return lax.ppermute(value, 'dp', [(i, i ^ 1) for i in range(self.pairs)])  15.3 us
  transfers between devices with their start and end apart: 15, of which 4 were waited for; matrix products, arithmetic and copies ran while one was open for 23% of the time, Pallas kernels for 59%

profile of v4, /device:TPU:1, one launch (start us, length us, event | category | flops | bytes accessed | tf_op | source)
XLA Modules:
  0.0 595.7 jit_solution(14933868110858390722)
XLA Ops:
  7.1 86.4 %shard_map.450 = (bf16[2048,768]{1,0:T(8,128)(2,1)}, bf16[2048,768]{1,0:T(8,128)(2,1)}, s32[2,2048]{1,0:T(2,128)}, f32[42,128]{1,0:T(8,128)}, bf16[768,1152]{1,0...) custom-call(bf16[512,768]{1,0:T(8,128)(2,1)} %bitcast.119, ...), custom_call_target="tpu_custom_call" | custom-call | tf_op jit(solution)/shard_map/pallas_call | solution.py:591
  97.3 4.7 add_convert_fusion.2.kv_ref.refs_3_
  104.2 14.6 %shard_map.451 = (f32[384,512]{1,0:T(8,128)S(1)}, f32[8,512]{1,0:T(8,128)S(1)}) custom-call(s32[8]{0:T(128)S(1)} %convert_reduce_fusion.15.starts.refs_0_, s32[3]{0:T(128)S(1)} %add_add_fusion.7.ends, s32[1,512]{1,0:T(1,128)S(1)} %constant_dynamic-slice_fusion.5.segments.refs_1_, bf16[512,384]{1,0:T(8,128)(2,1)S(1)} %fusion.29.q_ref.refs_2_, ...), custom_call_target="tpu_custom_call" | custom-call | flops 1610612736 | bytes 3145728 | tf_op jit(solution)/shard_map/pallas_call | solution.py:252
  125.9 9.3 %multiply_convert_fusion.1 = (bf16[512,1536]{1,0:T(8,128)(2,1)S(1)}, f32[512,1536]{1,0:T(8,128)}, f32[512,1536]{1,0:T(8,128)}) fusion(f32[1536]{0:T(1024)S(1)} %get-tuple-element.223, bf16[768,1536]{1,0:T(8,128)(2,1)S(1)} %copy-done.69, f32[512,768]{1,0:T(8,128)S(1)} %get-tuple-element.200, f32[768]{0:T(1024)S(1)} %get-tuple-element.166, ...), kind=kOutput, calls=%fused_computation.33 | convolution fusion | flops 1261830144 | bytes 11812864 | tf_op jit(solution)/shard_map/dot_general | solution.py:22
  136.8 4.0 add_convert_fusion.1.kv_ref.refs_3_
  142.7 5.5 collective-permute-done.4.refs_2_
  148.2 40.3 %shard_map.452 = (f32[384,512]{1,0:T(8,128)S(1)}, f32[8,512]{1,0:T(8,128)S(1)}, bf16[2048,768]{1,0:T(8,128)(2,1)S(1)}, bf16[768,1152]{1,0:T(8,128)(2,1)S(1)}, bf16[384,768]{1,0:T(8,128)(2,1)S(1)}) custom-call(s32[8]{0:T(128)S(1)} %convert_reduce_fusion.14.starts.refs_0_, s32[1,512]{1,0:T(1,128)S(1)} %constant_dynamic-slice_fusion.4.segments.refs_1_, ...), custom_call_target="tpu_custom_call" | custom-call | flops 1610612736 | bytes 3145728 | tf_op jit(solution)/shard_map/pallas_call | solution.py:654
  191.4 2.8 add_convert_fusion.kv_ref.refs_3_
  196.0 4.8 shard_map.453
  205.1 11.4 %multiply_convert_fusion = (bf16[512,1536]{1,0:T(8,128)(2,1)S(1)}, f32[512,1536]{1,0:T(8,128)}, f32[512,1536]{1,0:T(8,128)}) fusion(f32[1536]{0:T(1024)S(1)} %get-tuple-element.222, bf16[768,1536]{1,0:T(8,128)(2,1)} %collective-permute-done.1, f32[512,768]{1,0:T(8,128)S(1)} %get-tuple-element.192, f32[768]{0:T(1024)S(1)} %get-tuple-element.159, ...), kind=kOutput, calls=%fused_computation.20 | convolution fusion | flops 1261830144 | bytes 11812864 | tf_op jit(solution)/shard_map/dot_general | solution.py:22
  216.5 2.8 fusion.80
  224.5 2.4 fusion.18
  228.8 2.3 convert_reduce_fusion
  231.1 3.2 fusion.81
  234.4 13.1 %collective-permute-start.11 = (bf16[512,768]{1,0:T(8,128)(2,1)S(1)}, bf16[512,768]{1,0:T(8,128)(2,1)S(1)}, u32[]{:S(2)}, u32[]{:S(2)}) collective-permute-start(bf16[512,768]{1,0:T(8,128)(2,1)S(1)} %get-tuple-element.242), channel_id=1, source_target_pairs={{0,8},{8,0},{16,24},{24,16},{1,9},{9,1},{17,25},{25,17},{2,10},{10... | collective-permute-start | bytes 2359304 | tf_op jit(solution)/shard_map/ppermute | solution.py:1142
  250.1 2.9 convolution_convert_fusion.2.refs_10_
  253.0 3.2 convolution_convert_fusion.3.refs_9_
  261.4 50.5 %shard_map.454 = (bf16[512,384]{1,0:T(8,128)(2,1)}, bf16[2048,768]{1,0:T(8,128)(2,1)}, bf16[512,768]{1,0:T(8,128)(2,1)}, f32[512,768]{1,0:T(8,128)}, bf16[384,15...) custom-call(s32[8]{0:T(128)} %copy-done.14, s32[1,512]{1,0:T(1,128)} %copy-done.11, bf16[512,384]{1,0:T(8,128)(2,1)} %copy-done.20, ...), custom_call_target="tpu_custom_call" | custom-call | flops 5637144576 | bytes 11010048 | tf_op jit(solution)/shard_map/pallas_call | solution.py:695
  311.9 2.3 multiply_reduce_fusion.1
  319.3 3.8 convolution_convert_fusion.6.refs_11_
  324.5 65.5 %shard_map.455 = (bf16[512,384]{1,0:T(8,128)(2,1)}, bf16[2048,768]{1,0:T(8,128)(2,1)}, bf16[512,768]{1,0:T(8,128)(2,1)}, f32[48,1536]{1,0:T(8,128)}, f32[48,1536...) custom-call(s32[8]{0:T(128)} %copy-done.12, s32[1,512]{1,0:T(1,128)} %copy-done.11, ...), custom_call_target="tpu_custom_call" | custom-call | flops 5637144576 | bytes 11010048 | tf_op jit(solution)/shard_map/pallas_call | solution.py:695
  393.0 2.6 convolution_convert_fusion.10.refs_15_
  397.1 2.6 multiply_reduce_fusion.2
  401.6 2.3 convert_reduce_fusion.1
  408.5 2.8 convolution_convert_fusion.refs_13_
  411.3 3.2 convolution_convert_fusion.1.refs_12_
  416.7 3.8 convolution_convert_fusion.5.refs_14_
  425.1 60.9 %shard_map.456 = (bf16[512,384]{1,0:T(8,128)(2,1)}, bf16[2048,768]{1,0:T(8,128)(2,1)}, bf16[512,768]{1,0:T(8,128)(2,1)}, f32[48,768]{1,0:T(8,128)}, f32[48,384]{...) custom-call(s32[8]{0:T(128)} %copy-done.14, ...), custom_call_target="tpu_custom_call" | custom-call | flops 5637144576 | bytes 11010048 | tf_op jit(solution)/shard_map/pallas_call | solution.py:695
  487.8 6.6 %convolution_convert_fusion.4.refs_6_ = bf16[768,768]{1,0:T(8,128)(2,1)} fusion(bf16[2048,768]{1,0:T(8,128)(2,1)} %get-tuple-element.78, bf16[2048,768]{1,0:T(8,128)(2,1)} %get-tuple-element.111), kind=kOutput, calls=%fused_computation.95 | convolution fusion | flops 2416508928 | bytes 7471104 | tf_op jit(solution)/shard_map/dot_general | solution.py:30
  494.4 2.6 convolution_convert_fusion.8.refs_7_
  501.0 74.3 %shard_map.457 = (f32[22,768]{1,0:T(8,128)}, f32[48,1536]{1,0:T(8,128)}, f32[48,1536]{1,0:T(8,128)}, f32[48,768]{1,0:T(8,128)}, f32[48,384]{1,0:T(8,128)}, /*ind...) custom-call(f32[22,768]{1,0:T(8,128)} %pad_maximum_fusion.3.refs_0_, ...), custom_call_target="tpu_custom_call" | custom-call | tf_op jit(solution)/shard_map/pallas_call | solution.py:695
  587.0 2.4 bitcast_convert_fusion
  (341 shorter events, 93.1 us)
Async XLA Ops:
  0.7 123.3 %collective-permute-start.1 = (bf16[768,1536]{1,0:T(8,128)(2,1)}, bf16[768,1536]{1,0:T(8,128)(2,1)}, u32[]{:S(2)}, u32[]{:S(2)}) collective-permute-start(bf16[768,1536]{1,0:T(8,128)(2,1)} %param.46), channel_id=1, source_target_pairs={{8,0},{9,1},{1,8},{0,9},{24,16},{25,17},{17,24},{16,25},{10,2},{11... | collective-permute-start | bytes 7077896 | tf_op jit(solution)/shard_map/ppermute | solution.py:1166
  94.6 101.3 %copy-start.14 = (s32[8]{0:T(128)}, s32[8]{0:T(128)S(1)}, u32[]{:S(2)}) copy-start(s32[8]{0:T(128)S(1)} %convert_reduce_fusion.15.starts.refs_0_) | copy-start | bytes 100
  102.0 16.7 %copy-start.21 = (bf16[2048,768]{1,0:T(8,128)(2,1)}, bf16[2048,768]{1,0:T(8,128)(2,1)S(1)}, u32[]{:S(2)}) copy-start(bf16[2048,768]{1,0:T(8,128)(2,1)S(1)} %add_convert_fusion.2.kv_ref.refs_3_) | copy-start | bytes 9437188
  104.1 14.6 %copy-start.42 = (bf16[384,768]{1,0:T(8,128)(2,1)S(1)}, bf16[384,768]{1,0:T(8,128)(2,1)}, u32[]{:S(2)}) copy-start(bf16[384,768]{1,0:T(8,128)(2,1)} %get-tuple-element.83) | copy-start | bytes 1769476
  104.1 15.5 %copy-start.68 = (bf16[1536,768]{1,0:T(8,128)(2,1)S(1)}, bf16[1536,768]{1,0:T(8,128)(2,1)}, u32[]{:S(2)}) copy-start(bf16[1536,768]{1,0:T(8,128)(2,1)} %param.48) | copy-start | bytes 7077892
  104.2 16.5 %copy-start.74 = (bf16[768,1152]{1,0:T(8,128)(2,1)S(1)}, bf16[768,1152]{1,0:T(8,128)(2,1)}, u32[]{:S(2)}) copy-start(bf16[768,1152]{1,0:T(8,128)(2,1)} %get-tuple-element.87.refs_8_) | copy-start | bytes 5308420
  119.6 2.3 collective-permute-start
  119.6 28.5 %collective-permute-start.4 = (bf16[1536,768]{1,0:T(8,128)(2,1)S(1)}, bf16[1536,768]{1,0:T(8,128)(2,1)S(1)}, u32[]{:S(2)}, u32[]{:S(2)}) collective-permute-start(bf16[1536,768]{1,0:T(8,128)(2,1)S(1)} %copy-done.68), channel_id=1, source_target_pairs={{8,0},{9,1},{1,8},{0,9},{24,16},{25,17},{17,24},{16,25},{10,2},{11... | collective-permute-start | bytes 7077896 | tf_op jit(solution)/shard_map/ppermute | solution.py:1166
  120.5 27.6 %copy-start.12 = (s32[8]{0:T(128)}, s32[8]{0:T(128)S(1)}, u32[]{:S(2)}) copy-start(s32[8]{0:T(128)S(1)} %convert_reduce_fusion.14.starts.refs_0_) | copy-start | bytes 100
  121.6 26.5 %copy-start.10 = (bf16[512,384]{1,0:T(8,128)(2,1)}, bf16[512,384]{1,0:T(8,128)(2,1)S(1)}, u32[]{:S(2)}) copy-start(bf16[512,384]{1,0:T(8,128)(2,1)S(1)} %fusion.28.q_ref.refs_2_) | copy-start | bytes 1179652
  123.6 17.2 %copy-start.30 = (f32[512,768]{1,0:T(8,128)}, f32[512,768]{1,0:T(8,128)S(1)}, u32[]{:S(2)}) copy-start(f32[512,768]{1,0:T(8,128)S(1)} %get-tuple-element.200) | copy-start | bytes 4718596
  136.6 4.2 collective-permute-start.2
  136.8 59.1 %copy-start.11 = (s32[1,512]{1,0:T(1,128)}, s32[1,512]{1,0:T(1,128)S(1)}, u32[]{:S(2)}) copy-start(s32[1,512]{1,0:T(1,128)S(1)} %constant_dynamic-slice_fusion.4.segments.refs_1_) | copy-start | bytes 6148
  148.1 68.3 %copy-start.6 = (bf16[1536,768]{1,0:T(8,128)(2,1)}, bf16[1536,768]{1,0:T(8,128)(2,1)S(1)}, u32[]{:S(2)}) copy-start(bf16[1536,768]{1,0:T(8,128)(2,1)S(1)} %collective-permute-done.4.refs_2_) | copy-start | bytes 7077892
  148.1 40.9 %copy-start.44 = (bf16[384,768]{1,0:T(8,128)(2,1)S(1)}, bf16[384,768]{1,0:T(8,128)(2,1)}, u32[]{:S(2)}) copy-start(bf16[384,768]{1,0:T(8,128)(2,1)} %get-tuple-element.89) | copy-start | bytes 1769476
  189.9 4.3 collective-permute-start.5
  201.7 2.3 collective-permute-start.6
  219.3 2.6 collective-permute-start.7
  219.6 4.8 collective-permute-start.10
  219.8 177.4 %collective-permute-start.9 = (bf16[512,768]{1,0:T(8,128)(2,1)}, bf16[512,768]{1,0:T(8,128)(2,1)}, u32[]{:S(2)}, u32[]{:S(2)}) collective-permute-start(bf16[512,768]{1,0:T(8,128)(2,1)} %bitcast.24), channel_id=1, source_target_pairs={{0,8},{8,0},{16,24},{24,16},{1,9},{9,1},{17,25},{25,17},{2,10},{10... | collective-permute-start | bytes 2359304 | tf_op jit(solution)/shard_map/ppermute | solution.py:1142
  220.1 27.4 %collective-permute-start.3 = (bf16[512,768]{1,0:T(8,128)(2,1)S(1)}, bf16[512,768]{1,0:T(8,128)(2,1)S(1)}, u32[]{:S(2)}, u32[]{:S(2)}) collective-permute-start(bf16[512,768]{1,0:T(8,128)(2,1)S(1)} %add_convert_fusion.6.own_ref), channel_id=1, source_target_pairs={{0,1},{9,8},{16,17},{25,24},{2,3},{11,10},{18,19},{27,26},{4,5},{1... | collective-permute-start | bytes 2359304 | tf_op jit(solution)/shard_map/ppermute | solution.py:1166
  231.1 16.4 %copy-start.26 = (f32[512,768]{1,0:T(8,128)S(1)}, f32[512,768]{1,0:T(8,128)}, u32[]{:S(2)}) copy-start(f32[512,768]{1,0:T(8,128)} %copy-done.25) | copy-start | bytes 4718596
  234.3 15.7 %copy-start.78 = (bf16[512,1536]{1,0:T(8,128)(2,1)S(1)}, bf16[512,1536]{1,0:T(8,128)(2,1)}, u32[]{:S(2)}) copy-start(bf16[512,1536]{1,0:T(8,128)(2,1)} %copy-done.77) | copy-start | bytes 4718596
  234.4 21.8 %collective-permute-start.11 = (bf16[512,768]{1,0:T(8,128)(2,1)S(1)}, bf16[512,768]{1,0:T(8,128)(2,1)S(1)}, u32[]{:S(2)}, u32[]{:S(2)}) collective-permute-start(bf16[512,768]{1,0:T(8,128)(2,1)S(1)} %get-tuple-element.242), channel_id=1, source_target_pairs={{0,8},{8,0},{16,24},{24,16},{1,9},{9,1},{17,25},{25,17},{2,10},{10... | collective-permute-start | bytes 2359304 | tf_op jit(solution)/shard_map/ppermute | solution.py:1142
  248.8 165.7 %collective-permute-start.8 = (bf16[512,768]{1,0:T(8,128)(2,1)}, bf16[512,768]{1,0:T(8,128)(2,1)}, u32[]{:S(2)}, u32[]{:S(2)}) collective-permute-start(bf16[512,768]{1,0:T(8,128)(2,1)} %get-tuple-element.201), channel_id=1, source_target_pairs={{0,1},{9,8},{16,17},{25,24},{2,3},{11,10},{18,19},{27,26},{4,5},{1... | collective-permute-start | bytes 2359304 | tf_op jit(solution)/shard_map/ppermute | solution.py:1166
  261.4 50.5 %copy-start.29 = (f32[512,768]{1,0:T(8,128)S(1)}, f32[512,768]{1,0:T(8,128)}, u32[]{:S(2)}) copy-start(f32[512,768]{1,0:T(8,128)} %copy-done.28) | copy-start | bytes 4718596
  261.4 50.5 %copy-start.32 = (f32[512,768]{1,0:T(8,128)S(1)}, f32[512,768]{1,0:T(8,128)}, u32[]{:S(2)}) copy-start(f32[512,768]{1,0:T(8,128)} %get-tuple-element.173) | copy-start | bytes 4718596
  405.3 15.1 %collective-permute-start.12 = (bf16[512,768]{1,0:T(8,128)(2,1)S(1)}, bf16[512,768]{1,0:T(8,128)(2,1)S(1)}, u32[]{:S(2)}, u32[]{:S(2)}) collective-permute-start(bf16[512,768]{1,0:T(8,128)(2,1)S(1)} %get-tuple-element.244), channel_id=1, source_target_pairs={{0,8},{8,0},{16,24},{24,16},{1,9},{9,1},{17,25},{25,17},{2,10},{10... | collective-permute-start | bytes 2359304 | tf_op jit(solution)/shard_map/ppermute | solution.py:1142
  406.3 180.8 %collective-permute-start.14 = (bf16[512,768]{1,0:T(8,128)(2,1)S(1)}, bf16[512,768]{1,0:T(8,128)(2,1)}, u32[]{:S(2)}, u32[]{:S(2)}) collective-permute-start(bf16[512,768]{1,0:T(8,128)(2,1)S(1)} %reduce-precision_convert_fusion), channel_id=1, source_target_pairs={{0,1},{9,8},{16,17},{25,24},{2,3},{11,10},{18,19},{27,26},{4,5},{1... | collective-permute-start | bytes 2359304 | tf_op jit(solution)/shard_map/ppermute | solution.py:1166
  498.7 90.8 %collective-permute-start.13 = (bf16[512,768]{1,0:T(8,128)(2,1)S(1)}, bf16[512,768]{1,0:T(8,128)(2,1)S(1)}, u32[]{:S(2)}, u32[]{:S(2)}) collective-permute-start(bf16[512,768]{1,0:T(8,128)(2,1)S(1)} %reduce-precision_convert_fusion.1), channel_id=1, source_target_pairs={{0,1},{9,8},{16,17},{25,24},{2,3},{11,10},{18,19},{27,26},{4,5},{1... | collective-permute-start | bytes 2359304 | tf_op jit(solution)/shard_map/ppermute | solution.py:1166
  501.0 76.3 %copy-start.55 = (f32[48,768]{1,0:T(8,128)S(1)}, f32[48,768]{1,0:T(8,128)}, u32[]{:S(2)}) copy-start(f32[48,768]{1,0:T(8,128)} %get-tuple-element.127) | copy-start | bytes 442372
  575.3 11.1 %copy-start.56 = (f32[22,768]{1,0:T(8,128)S(1)}, f32[22,768]{1,0:T(8,128)}, u32[]{:S(2)}) copy-start(f32[22,768]{1,0:T(8,128)} %get-tuple-element.119) | copy-start | bytes 202756
  (66 other events, 219.1 us)

commit v5 on v4

--- a/solution.py
+++ b/solution.py
@@ -1,4 +1,5 @@
 import functools
+import math
 
 import jax
 import jax.numpy as jnp
@@ -15,6 +16,7 @@
 NT = (((1,), (1,)), ((), ()))
 TN = (((0,), (0,)), ((), ()))
 KEY_BLOCK = 512
+CHUNKS = 2
 DOCS = 4
 
 
@@ -300,6 +302,12 @@
         devices += [self.along_z(step) for step in range(1, self.ring)]
         return [(self.core >= 0, device) for device in devices]
 
+    def crosswise(self):
+        return [
+            (self.z + 1 < self.ring, (self.other_d, self.z + 1, self.y)),
+            (self.z > 0, (self.other_d, self.z - 1, self.y)),
+        ]
+
     def neighbours(self):
         return [
             (self.core >= 0, self.partner),
@@ -320,15 +328,15 @@
 
 
 class Gather:
-    def __init__(self, here, rows_ref, sems):
-        self.here, self.rows_ref = here, rows_ref
+    def __init__(self, here, rows_ref, sems, source=None, owner=None):
+        self.here, self.rows_ref, self.source, self.owner = here, rows_ref, source, owner
         self.count = rows_ref.shape[0] // here.ring
+        self.size = self.count // (2 * CHUNKS)
         self.sent, self.got, self.core_sent, self.core_got = sems
 
-    def half(self, shard, core):
-        part = self.count // 2
-        start = pl.multiple_of(shard * self.count + core * part, part)
-        return self.rows_ref.at[pl.ds(start, part)]
+    def chunk(self, shard, core, chunk):
+        start = shard * self.count + core * (self.count // 2) + chunk * self.size
+        return self.rows_ref.at[pl.ds(pl.multiple_of(start, self.size), self.size)]
 
     def ways(self, step):
         here = self.here
@@ -338,49 +346,86 @@
             (1, z + step, z + step < ring, z + step - 1, (z > 0) & (z + step <= ring), here.left),
         ]
 
-    def along(self, way, step, shard, device):
-        view = self.half(shard, self.here.core)
-        return remote(view, view, self.sent.at[way, step], self.got.at[way, step], device)
-
-    def across(self, way, step, shard, core):
-        view = self.half(shard, core)
+    def along(self, way, step, shard, chunk, device):
+        view = self.chunk(shard, self.here.core, chunk)
+        k = way * CHUNKS + chunk
+        return remote(view, view, self.sent.at[k, step], self.got.at[k, step], device)
+
+    def across(self, way, step, shard, core, chunk):
+        view = self.chunk(shard, core, chunk)
+        k = way * CHUNKS + chunk
         return remote(
-            view, view, self.core_sent.at[way, step], self.core_got.at[way, step], self.here.partner
+            view, view, self.core_sent.at[k, step], self.core_got.at[k, step], self.here.partner
         )
 
-    def start(self, step):
-        for way, _, _, shard, sends, device in self.ways(step):
-
-            @pl.when(sends)
-            def _(way=way, shard=shard, device=device):
-                self.along(way, step, shard, device).start()
-
-    def arrive(self, step):
-        for way, shard, comes, _, _, device in self.ways(step):
-
-            @pl.when(comes)
-            def _(way=way, shard=shard, device=device):
-                self.along(way, step, shard, self.here.partner).wait_recv()
-                self.across(way, step, shard, self.here.core).start()
-
-    def finish(self, step):
-        for way, shard, comes, out, sends, device in self.ways(step):
-
-            @pl.when(sends)
-            def _(way=way, out=out, device=device):
-                self.along(way, step, out, device).wait_send()
-
-            @pl.when(comes)
-            def _(way=way, shard=shard):
-                self.across(way, step, shard, self.here.core).wait_send()
-                self.across(way, step, shard, 1 - self.here.core).wait_recv()
+    def firsts(self):
+        found = []
+        for chunk in range(CHUNKS):
+            for way, _, _, shard, sends, device in self.ways(1):
+                if self.source is None:
+                    found.append((sends, self.along(way, 1, shard, chunk, device)))
+                    continue
+                for core in range(2):
+                    k = way * CHUNKS + chunk
+                    start = core * (self.count // 2) + chunk * self.size
+                    to = (self.here.d - self.here.core + core, *device[1:])
+                    copy = remote(
+                        self.source.at[pl.ds(start, self.size)],
+                        self.chunk(shard, core, chunk),
+                        self.sent.at[k, core],
+                        self.got.at[k, 1],
+                        to,
+                    )
+                    found.append((sends & self.owner, copy))
+        return found
+
+    def begin(self):
+        for condition, copy in self.firsts():
+            pl.when(condition)(copy.start)
+
+    def advance(self, step):
+        for chunk in range(CHUNKS):
+            for way, shard, comes, _, _, _ in self.ways(step):
+
+                @pl.when(comes)
+                def _(way=way, shard=shard, chunk=chunk):
+                    self.along(way, step, shard, chunk, self.here.partner).wait_recv()
+
+                _, _, _, _, sends, device = self.ways(step + 1)[way]
+
+                @pl.when(sends)
+                def _(way=way, shard=shard, chunk=chunk, device=device):
+                    self.along(way, step + 1, shard, chunk, device).start()
+
+                @pl.when(comes)
+                def _(way=way, shard=shard, chunk=chunk):
+                    self.across(way, step, shard, self.here.core, chunk).start()
+
+    def finish(self):
+        for condition, copy in self.firsts():
+            pl.when(condition)(copy.wait_send)
+
+        @pl.loop(1, self.here.ring)
+        def _(step):
+            for chunk in range(CHUNKS):
+                for way, shard, comes, out, sends, device in self.ways(step):
+
+                    @pl.when(sends & (step > 1))
+                    def _(way=way, out=out, device=device, chunk=chunk):
+                        self.along(way, step, out, chunk, device).wait_send()
+
+                    @pl.when(comes)
+                    def _(way=way, shard=shard, chunk=chunk):
+                        core = self.here.core
+                        self.across(way, step, shard, core, chunk).wait_send()
+                        self.across(way, step, shard, 1 - core, chunk).wait_recv()
 
 
 def pieces_of(weights):
     found = []
     for k, weight in enumerate(weights):
         rows, columns = weight.shape
-        number = 3 if rows == 6 * columns else 1
+        number = 1 if rows % 3 else 3
         while 2 * rows * columns > 655360 * number and rows % (64 * number) == 0:
             number *= 2
         found += [(k, i * (rows // number), rows // number) for i in range(number)]
@@ -391,6 +436,9 @@
     rows, columns = weight.shape
     matrices = 3 if rows == 3 * model else 1
     return jax.ShapeDtypeStruct((rows // matrices, columns * matrices), weight.dtype)
+
+
+AHEAD = 4
 
 
 class Fetch:
@@ -450,7 +498,7 @@
     def begin(self):
         @pl.when(self.here.core == 0)
         def _():
-            for p in range(min(2, self.number)):
+            for p in range(min(AHEAD, self.number)):
                 self.over_y(p).start()
 
         @pl.when(self.here.core == 1)
@@ -462,8 +510,8 @@
         @pl.when(self.here.core == 0)
         def _():
             self.over_y(p).wait_send()
-            if p + 2 < self.number:
-                self.over_y(p + 2).start()
+            if p + AHEAD < self.number:
+                self.over_y(p + AHEAD).start()
 
         @pl.when(self.here.core == 1)
         def _():
@@ -486,7 +534,7 @@
 
 
 def gather_sems(ring):
-    return [DMA((2, ring))] * 4
+    return [DMA((2 * CHUNKS, ring))] * 4
 
 
 def fetch_sems(weights):
@@ -497,16 +545,16 @@
 def opening_kernel(ring, number, *refs):
     inputs, outputs, sems = refs[: 4 + number], refs[4 + number : 8 + 2 * number], refs[8 + 2 * number :]
     source, target, segments, vectors = inputs[:4]
-    source_all, target_all, segments_out, vectors_out = outputs[:4]
+    source_all, target_out, segments_out, vectors_out = outputs[:4]
     shard_sems, vector_sems = sems[:3], sems[3:6]
     here = Here(ring)
-    fetch = Fetch(here, inputs[4:], outputs[4:], sems[14:])
-    here.meet(here.neighbours() + fetch.devices())
+    fetch = Fetch(here, inputs[4:], outputs[4:], sems[10:])
+    here.meet(here.neighbours() + here.crosswise() + fetch.devices())
     count = source.shape[0]
     own = pl.ds(pl.multiple_of(here.z * count, count), count)
     moves = [
         (source, source_all.at[own]),
-        (target, target_all.at[own]),
+        (target, target_out),
         (segments, segments_out),
     ]
     owner = here.core == here.y
@@ -551,22 +599,21 @@
         across.start()
         local.start()
 
+    gather = Gather(here, source_all, sems[6:10], source, owner)
+    gather.begin()
     fetch.begin()
-    gathers = [Gather(here, source_all, sems[6:10]), Gather(here, target_all, sems[10:14])]
-    slots = 2 * (ring - 1)
     done = 0
-    for k, gather in enumerate(gathers):
-        wait_shard(k)
-        for step in range(1, ring):
-            gather.start(step)
-            slot = k * (ring - 1) + step
-            while done < fetch.number * slot // slots:
-                fetch.advance(done)
-                done += 1
-            gather.arrive(step)
-    for gather in gathers:
-        for step in range(1, ring):
-            gather.finish(step)
+    for step in range(1, ring):
+        while done < fetch.number * (2 * step - 1) // (2 * ring - 2):
+            fetch.advance(done)
+            done += 1
+        gather.advance(step)
+    while done < fetch.number:
+        fetch.advance(done)
+        done += 1
+    gather.finish()
+    wait_shard(0)
+    wait_shard(1)
     wait_shard(2)
     fetch.end()
     across, local = vector_copy()
@@ -585,15 +632,15 @@
     inputs = (source, target, segments, vectors) + tuple(weights)
     count, model = source.shape
     rows = jax.ShapeDtypeStruct((ring * count, model), BF16)
-    shapes = (rows, rows) + tuple(jax.ShapeDtypeStruct(v.shape, v.dtype) for v in inputs[2:4])
+    shapes = (rows, jax.ShapeDtypeStruct(target.shape, BF16)) + tuple(jax.ShapeDtypeStruct(v.shape, v.dtype) for v in inputs[2:4])
     shapes += tuple(beside(weight, model) for weight in weights)
     number = len(weights)
     return pl.pallas_call(
         functools.partial(opening_kernel, ring, number),
         out_shape=shapes,
         in_specs=[VECTORS] * 4 + [ANYWHERE] * number,
-        out_specs=(ANYWHERE,) * 2 + (VECTORS,) * 2 + (ANYWHERE,) * number,
-        scratch_shapes=[DMA((3,))] * 3 + [DMA] * 3 + gather_sems(ring) * 2 + fetch_sems(weights),
+        out_specs=(ANYWHERE,) + (VECTORS,) * 3 + (ANYWHERE,) * number,
+        scratch_shapes=[DMA((3,))] * 3 + [DMA] * 3 + gather_sems(ring) + fetch_sems(weights),
         compiler_params=pltpu.CompilerParams(collective_id=1, has_side_effects=True),
     )(*inputs)
 
@@ -615,7 +662,7 @@
     local.start()
     fetch.begin()
     local.wait()
-    gather.start(1)
+    gather.begin()
     mask = Mask(causal, starts, segments, first_row)
     forward_start(q_ref, masked_q, acc, top)
     blocks = kv_ref.shape[0] // block
@@ -627,46 +674,39 @@
 
         @pl.when((index >= 1) & (index < ring))
         def _():
-            gather.arrive(index)
-
-        @pl.when((index >= 1) & (index < ring - 1))
-        def _():
-            gather.start(index + 1)
-
-        for p in range(min(fetch.number, blocks - 1)):
-            pl.when(index == p + 1)(functools.partial(fetch.advance, p))
+            gather.advance(index)
+
+        for p in range(fetch.number):
+            pl.when(index == 1 + p * (blocks - 1) // fetch.number)(
+                functools.partial(fetch.advance, p)
+            )
 
     forward_end(out_ref, lse_ref, acc, top)
-    for p in range(min(fetch.number, blocks - 1), fetch.number):
-        fetch.advance(p)
-
-    @pl.loop(1, ring)
-    def _(step):
-        gather.finish(step)
-
+
+    gather.finish()
     fetch.end()
 
 
-def gather_attend(ring, queries, kv, mask, own, weights, tokens):
+def gather_attend(number, ring, queries, kv, mask, own, weights, tokens=()):
     count, width = queries.shape
     causal, starts, _, segments = mask
-    number = len(weights)
+    fetched = len(weights)
     return pl.pallas_call(
-        functools.partial(gather_attend_kernel, KEY_BLOCK, causal, ring, number, len(tokens)),
+        functools.partial(gather_attend_kernel, KEY_BLOCK, causal, ring, fetched, len(tokens)),
         out_shape=(
             jax.ShapeDtypeStruct((width, count), F32),
             jax.ShapeDtypeStruct((8, count), F32),
             jax.ShapeDtypeStruct((ring * own.shape[0], own.shape[1]), BF16),
         )
         + tuple(beside(weight, own.shape[1]) for weight in weights),
-        in_specs=[SCALARS] + [VECTORS] * 4 + [ANYWHERE] * (number + len(tokens)),
-        out_specs=(VECTORS, VECTORS) + (ANYWHERE,) * (1 + number),
+        in_specs=[SCALARS] + [VECTORS] * 4 + [ANYWHERE] * (fetched + len(tokens)),
+        out_specs=(VECTORS, VECTORS) + (ANYWHERE,) * (1 + fetched),
         scratch_shapes=forward_scratch(count, width)
         + [DMA]
         + gather_sems(ring)
         + fetch_sems(weights),
         compiler_params=pltpu.CompilerParams(
-            vmem_limit_bytes=40 << 20, collective_id=2, has_side_effects=True
+            vmem_limit_bytes=40 << 20, collective_id=number, has_side_effects=True
         ),
         cost_estimate=cost_of(kv, count, width, 2),
     )(starts, segments, queries, kv, own, *weights, *tokens)
@@ -699,7 +739,7 @@
         out_specs=[VECTORS for p in parts for _ in p.out_shapes],
         scratch_shapes=[shape for p in parts for shape in p.scratch],
         compiler_params=pltpu.CompilerParams(
-            vmem_limit_bytes=60 << 20, collective_id=number, has_side_effects=True
+            vmem_limit_bytes=62 << 20, collective_id=number, has_side_effects=True
         ),
         cost_estimate=cost,
     )(*(array for p in parts for array in p.inputs))
@@ -1077,7 +1117,133 @@
         event(ring + 2)
 
 
-def attend_back(number, saved, grad_mixed, grad_mixed_t, weights, mask, apart, chains):
+class Products:
+    def __init__(self, back, inputs, outputs, scratch, time):
+        self.back, self.time = back, time
+        self.block, self.copied = scratch
+        self.query_in, self.key_in, self.grad_branch, self.mixed = inputs
+        self.of_q, self.of_out, self.of_kv, self.of_bias = outputs
+
+    def event(self, time):
+        if time != self.time:
+            return
+        dq, dkv = self.back.dq_out, self.back.dkv
+        width = dq.shape[1]
+        self.of_q[...] = dot_first(self.query_in[...], dq[...]).astype(BF16)
+        self.of_out[...] = dot_first(self.grad_branch[...], self.mixed[...].T).astype(BF16)
+        self.of_bias[0:1, :] = jnp.sum(dq[...].astype(F32), axis=0, keepdims=True)
+        self.of_bias[1:2, :] = jnp.sum(dkv[:, width:].astype(F32), axis=0, keepdims=True)
+
+        @pl.loop(0, self.of_kv.shape[0] // 256)
+        def _(index):
+            part = pl.ds(pl.multiple_of(index * 256, 256), 256)
+            copy = pltpu.make_async_copy(self.key_in.at[:, part], self.block, self.copied)
+            copy.start()
+            copy.wait()
+            self.of_kv[part, :] = dot_first(self.block[...], dkv[...]).astype(BF16)
+
+
+def products(box, query_in, key_in, grad_branch, mixed, time):
+    model, width = query_in.shape[1], mixed.shape[0]
+    return Part(
+        (query_in, key_in, grad_branch, mixed),
+        [VECTORS, ANYWHERE, VECTORS, VECTORS],
+        [
+            jax.ShapeDtypeStruct((model, width), BF16),
+            jax.ShapeDtypeStruct((model, width), BF16),
+            jax.ShapeDtypeStruct((model, 2 * width), BF16),
+            jax.ShapeDtypeStruct((2, width), F32),
+        ],
+        [pltpu.VMEM((key_in.shape[0], 256), BF16), DMA],
+        lambda here, inputs, outputs, refs: Products(box["back"], inputs, outputs, refs, time),
+    )
+
+
+class FeedBack:
+    def __init__(self, here, inputs, outputs, scratch, time):
+        self.here, self.time = here, time
+        self.grad, self.x_in = inputs[:2]
+        self.streamed = inputs[2:]
+        self.sum, self.of_bias, self.of_in, self.of_out = outputs
+        self.blocks, (self.low, self.got, self.copied, self.sems) = scratch[:4], scratch[4:]
+
+    def event(self, time):
+        if time != self.time:
+            return
+        span = self.blocks[0].shape[2]
+        number = self.of_in.shape[1] // span
+        self.sum[...] = jnp.zeros_like(self.sum)
+
+        def columns(index):
+            return pl.ds(pl.multiple_of(index * span, span), span)
+
+        def copies(index):
+            slot, part = lax.rem(index, 2), columns(index)
+            return [
+                pltpu.make_async_copy(
+                    ref.at[part] if k == 3 else ref.at[:, part],
+                    self.blocks[k].at[slot],
+                    self.copied.at[k, slot],
+                )
+                for k, ref in enumerate(self.streamed)
+            ]
+
+        for copy in copies(0):
+            copy.start()
+
+        @pl.loop(0, number)
+        def _(index):
+            part = columns(index)
+
+            @pl.when(index + 1 < number)
+            def _():
+                for copy in copies(index + 1):
+                    copy.start()
+
+            for copy in copies(index):
+                copy.wait()
+            slope, active, w_in, w_out = (block.at[lax.rem(index, 2)] for block in self.blocks)
+            hidden = (slope[...] * dot_last(self.grad[...], w_out[...])).astype(BF16)
+            self.of_bias[:, part] = jnp.sum(hidden.astype(F32), axis=0, keepdims=True)
+            self.sum[...] += dot_last(hidden, w_in[...])
+            self.of_in[:, part] = dot_first(self.x_in[...], hidden).astype(BF16)
+            self.of_out[:, part] = dot_first(self.grad[...], active[...]).astype(BF16)
+
+        self.low[...] = self.sum[...].astype(BF16)
+        exchange = remote(self.low, self.got, self.sems.at[0], self.sems.at[1], self.here.partner)
+        exchange.start()
+        exchange.wait()
+        self.sum[...] = self.low[...].astype(F32) + self.got[...].astype(F32)
+
+
+def feed_back(grad_branch, slope, w_in, w_out, x_in, active, time):
+    count, model = x_in.shape
+    units = w_in.shape[1]
+    span = 256
+    return Part(
+        (grad_branch, x_in, slope, active, w_in, w_out),
+        [VECTORS] * 2 + [ANYWHERE] * 4,
+        [
+            jax.ShapeDtypeStruct((count, model), F32),
+            jax.ShapeDtypeStruct((1, units), F32),
+            jax.ShapeDtypeStruct((model, units), BF16),
+            jax.ShapeDtypeStruct((model, units), BF16),
+        ],
+        [
+            pltpu.VMEM((2, count, span), slope.dtype),
+            pltpu.VMEM((2, count, span), BF16),
+            pltpu.VMEM((2, model, span), BF16),
+            pltpu.VMEM((2, span, model), BF16),
+            pltpu.VMEM((count, model), BF16),
+            pltpu.VMEM((count, model), BF16),
+            DMA((4, 2)),
+            DMA((2,)),
+        ],
+        lambda here, *refs: FeedBack(here, *refs, time),
+    )
+
+
+def attend_back(number, saved, grad_mixed, grad_mixed_t, weights, mask, apart, more, box):
     queries, kv, output, lse, _ = saved
     causal, starts, segments = mask
     ring = lax.axis_size("seq")
@@ -1106,7 +1272,7 @@
         [SCALARS] + [VECTORS] * 8,
         shapes,
         scratch,
-        lambda here, *refs: Back(here, causal, apart, *refs),
+        lambda here, *refs: box.setdefault("back", Back(here, causal, apart, *refs)),
     )
 
     def body(here, back, *bound):
@@ -1116,8 +1282,7 @@
 
         back.run(event)
 
-    first, *rest = run_parts(number, body, [main] + list(chains), cost_of(kv, count, width, 7))
-    return first, [given[0] for given in rest]
+    return run_parts(number, body, [main] + list(more), cost_of(kv, count, width, 7))
 
 
 class Plan:
@@ -1253,38 +1418,45 @@
 
 
 def attention_backward(
-    number, grad_branch, saved, query_in, key_in, weights, out_weight, mask, apart, plan, wanted
+    number, grad_branch, saved, query_in, key_in, weights, out_weight, mask, apart, plan, wanted, inside=()
 ):
     mixed = saved[4]
-    width = saved[0].shape[1]
     grad_mixed = dot_last(grad_branch, out_weight).astype(BF16)
     grad_mixed_t = dot_last(out_weight, grad_branch).astype(BF16)
-    (grad_q, grad_kv, *sums), given = attend_back(
-        number, saved, grad_mixed, grad_mixed_t, weights, mask, apart, plan.chains(wanted)
-    )
-    grads = (
-        dot_first(query_in, grad_q).astype(BF16),
-        lax.dot_general(
-            grad_branch, mixed, (((0,), (1,)), ((), ())), preferred_element_type=F32
-        ).astype(BF16),
-        dot_first(key_in, grad_kv).astype(BF16),
-    )
-    grad_bias = jnp.concatenate([column_sum(grad_q), column_sum(grad_kv[:, width:])])
-    return (sums, grads, grad_bias, plan.given(wanted, given))
+    box = {}
+    more = []
+    if plan.kernels:
+        made = products(box, query_in, key_in, grad_branch, mixed, 5)
+        more = [made, *plan.chains(wanted), *inside]
+    (grad_q, grad_kv, *sums), *rest = attend_back(
+        number, saved, grad_mixed, grad_mixed_t, weights, mask, apart, more, box
+    )
+    if plan.kernels:
+        *grads, grad_bias = rest.pop(0)
+    else:
+        grads = (
+            dot_first(query_in, grad_q).astype(BF16),
+            dot_first(grad_branch, mixed.T).astype(BF16),
+            dot_first(key_in, grad_kv).astype(BF16),
+        )
+        grad_bias = jnp.stack([column_sum(grad_q), column_sum(grad_kv[:, grad_q.shape[1] :])])
+    given = [results[0] for results in rest[: len(rest) - len(inside)]]
+    rest = rest[len(rest) - len(inside) :]
+    return (sums, grads, grad_bias.reshape(-1), plan.given(wanted, given), rest)
 
 
 def feed_forward(place, x_in, w_in, b_in, w_out, b_out):
     hidden = dot_plain(x_in, w_in) + b_in.astype(F32)
-    active = jax.nn.gelu(hidden, approximate=False).astype(BF16)
+    spread = 0.5 * (1.0 + lax.erf(hidden * 0.5**0.5))
+    active = (hidden * spread).astype(BF16)
+    slope = spread + hidden * jnp.exp(-0.5 * hidden * hidden) * (2.0 * math.pi) ** (-0.5)
     branch = place.core_sum(dot_plain(active, w_out)) + b_out.astype(F32)
-    return (branch, (hidden, active))
+    return (branch, (slope, active))
 
 
 def feed_backward(place, grad_branch, saved, x_in, w_in, w_out):
-    hidden, active = saved
-    grad_active = dot_last(grad_branch, w_out)
-    slope = jax.vjp(lambda value: jax.nn.gelu(value, approximate=False), hidden)[1](grad_active)[0]
-    grad_hidden = slope.astype(BF16)
+    slope, active = saved
+    grad_hidden = (slope * dot_last(grad_branch, w_out)).astype(BF16)
     grad_in = place.core_sum(dot_last(grad_hidden, w_in))
     return (
         grad_in,
@@ -1343,15 +1515,13 @@
     ).astype(F32)
     (
         x_all,
-        t_all,
+        ts,
         segments,
         vectors,
         enc_qkv,
+        enc_proj,
         dec_self,
-        enc_proj,
         dec_self_proj,
-        enc_ff_in,
-        enc_ff_out,
     ) = opening(
         ring,
         source[0],
@@ -1360,16 +1530,13 @@
         vectors.reshape(-1, 128),
         (
             enc_qkv.reshape(-1, width),
+            enc_proj,
             dec_self.reshape(-1, width),
-            enc_proj,
             dec_self_proj,
-            enc_ff_in,
-            enc_ff_out,
         ),
     )
     vectors = vectors.reshape(-1)
     xs = lax.dynamic_slice_in_dim(x_all, first_row, count, 0)
-    ts = lax.dynamic_slice_in_dim(t_all, first_row, count, 0)
     dec_ff_in = place.fetch_weight(dec_ff_in)
     dec_ff_out = place.fetch_weight(dec_ff_out)
     enc_cot = place.own_pair(enc_cotangent[0])
@@ -1396,7 +1563,9 @@
     cross_mask = mask_of(target_own, source_starts, first_row, False)
 
     queries, kv = projected(xs, x_all, enc_w)
-    output, lse = attend(queries, kv, enc_mask)
+    output, lse, t_all, enc_ff_in, enc_ff_out = gather_attend(
+        7, ring, queries, kv, enc_mask, ts, (enc_ff_in, enc_ff_out)
+    )
     branch, enc_attn = attention_output(place, queries, kv, output, lse, enc_proj, enc_bias[0])
     first, enc_norm_one = norm_forward(xs.astype(F32) + branch, enc_gains[0], enc_shifts[0])
     first_low = first.astype(BF16)
@@ -1409,6 +1578,7 @@
 
     queries, kv = projected(ts, t_all, self_w)
     output, lse, e_all, dec_cross, dec_cross_proj = gather_attend(
+        2,
         ring,
         queries,
         kv,
@@ -1450,7 +1620,7 @@
     grad_hidden, dec_gain_two, dec_shift_two = norm_backward(grad_third, dec_norm_two, dec_gains[1])
     grad_branch = grad_hidden.astype(BF16)
     plan = place.plan()
-    (key_total, query_total), cross_grads, cross_bias, (dec_w_in, dec_w_out) = attention_backward(
+    (key_total, query_total), cross_grads, cross_bias, (dec_w_in, dec_w_out), _ = attention_backward(
         3,
         grad_branch,
         cross_attn,
@@ -1470,9 +1640,16 @@
     )
     grad_branch = grad_hidden.astype(BF16)
     cross_q, cross_proj, cross_kv = cross_grads
-    (target_total,), self_grads, self_bias, given = attention_backward(
+    target_hidden, target_branch = grad_hidden, grad_branch
+    grad_hidden, enc_gain_two, enc_shift_two = norm_backward(
+        enc_cot.astype(F32) + key_total.astype(F32), enc_norm_two, enc_gains[1]
+    )
+    grad_branch = grad_hidden.astype(BF16)
+    enc_bias_two = column_sum(grad_branch)
+    slope, active = enc_feed
+    (target_total,), self_grads, self_bias, given, inside = attention_backward(
         4,
-        grad_branch,
+        target_branch,
         self_attn,
         ts,
         t_all,
@@ -1488,23 +1665,25 @@
                 (cross_q, "y", (1, 6)),
                 (cross_proj, "y", (1, 6)),
             ],
+        [feed_back(grad_branch, slope, enc_ff_in, enc_ff_out, first_low, active, 5)]
+        if plan.kernels
+        else (),
     )
     dec_w_in, dec_w_out, cross_kv, cross_q, cross_proj = given
-    dec_bias_one = column_sum(grad_branch)
-    grad_target = grad_hidden + target_total.astype(F32)
-    grad_hidden, enc_gain_two, enc_shift_two = norm_backward(
-        enc_cot.astype(F32) + key_total.astype(F32), enc_norm_two, enc_gains[1]
-    )
-    grad_branch = grad_hidden.astype(BF16)
-    feed_in, enc_w_in, enc_b_in, enc_w_out = feed_backward(
-        place, grad_branch, enc_feed, first_low, enc_ff_in, enc_ff_out
-    )
-    enc_bias_two = column_sum(grad_branch)
+    if plan.kernels:
+        feed_in, enc_b_in, enc_w_in, enc_w_out = inside[0]
+        enc_b_in = enc_b_in.reshape(-1)
+    else:
+        feed_in, enc_w_in, enc_b_in, enc_w_out = feed_backward(
+            place, grad_branch, enc_feed, first_low, enc_ff_in, enc_ff_out
+        )
+    dec_bias_one = column_sum(target_branch)
+    grad_target = target_hidden + target_total.astype(F32)
     grad_first = grad_hidden + feed_in
     grad_hidden, enc_gain_one, enc_shift_one = norm_backward(grad_first, enc_norm_one, enc_gains[0])
     grad_branch = grad_hidden.astype(BF16)
     self_q, self_proj, self_kv = self_grads
-    (source_total,), enc_grads, enc_bias_grad, given = attention_backward(
+    (source_total,), enc_grads, enc_bias_grad, given, _ = attention_backward(
         5,
         grad_branch,
         enc_attn,

time: 606 us -> 574 us (0.947)
  matrix products: 95.5 us -> 55.1 us
    pallas_call x1 -> x2, Pallas kernels: 40.3 us -> 75 us  [gather_attend(): pl.pallas_call(functools.partial(gather_attend_kernel, KEY_BLOCK, causal,...]
    pallas_call x1, Pallas kernels: 86.4 us -> 58.3 us  [opening(): pl.pallas_call(functools.partial(opening_kernel, ring, number), out_shape...]
    dot_general x13 -> x5, matrix products: 34.7 us -> 9.04 us  [dot_first(): return lax.dot_general(left, right, TN, preferred_element_type=F32)]
    pallas_call x2 -> x1, Pallas kernels: 19.4 us -> 4.82 us  [attend(): pl.pallas_call(functools.partial(forward_kernel, KEY_BLOCK, causal), out_...]
    pallas_call x4, Pallas kernels: 251 us -> 260 us  [run_parts(): pl.pallas_call(kernel, out_shape=[shape for p in parts for shape in p.out...]
    dot_general x10, matrix products: 39.4 us -> 31.3 us  [dot_plain(): return jnp.dot(left, right, preferred_element_type=F32)]
    unnamed x198 -> x191, local copies, waits for them, and re-layouts: 11.6 us -> 15.9 us
    ppermute x9 -> x8, starting transfers between devices: 15.3 us -> 12.9 us  [swap_core(): return lax.ppermute(value, 'dp', [(i, i ^ 1) for i in range(self.pairs)])]
  transfers between devices with their start and end apart: 15 -> 14, of which waited for: 4 -> 4; matrix products, arithmetic and copies ran while one was open for 23% -> 18% of each run, Pallas kernels for 59% -> 64%
where the time goes in v5:
time: 574 us; the launch traced here: 565 us
  Pallas kernels  398 us (69%)
  matrix products  55.1 us (10%)
  other arithmetic  45.7 us (8%)
  local copies, waits for them, and re-layouts  31.2 us (5%)
  starting transfers between devices  19 us (3%)
  waiting for transfers between devices  12.3 us (2%)
    pallas_call x4, Pallas kernels, run_parts(): pl.pallas_call(kernel, out_shape=[shape for p in parts for shape in p.out...  260 us
    pallas_call x2, Pallas kernels, gather_attend(): pl.pallas_call(functools.partial(gather_attend_kernel, KEY_BLOCK, causal,...  75 us
    pallas_call x1, Pallas kernels, opening(): pl.pallas_call(functools.partial(opening_kernel, ring, number), out_shape...  58.3 us
    dot_general x10, matrix products, dot_plain(): return jnp.dot(left, right, preferred_element_type=F32)  31.3 us
    unnamed x191, local copies, waits for them, and re-layouts  15.9 us
    dot_general x8, matrix products, dot_last(): return lax.dot_general(left, right, NT, preferred_element_type=F32)  14.7 us
    ppermute x8, starting transfers between devices, swap_core(): return lax.ppermute(value, 'dp', [(i, i ^ 1) for i in range(self.pairs)])  12.9 us
  transfers between devices with their start and end apart: 14, of which 4 were waited for; matrix products, arithmetic and copies ran while one was open for 18% of the time, Pallas kernels for 64%

profile of v5, /device:TPU:1, one launch (start us, length us, event | category | flops | bytes accessed | tf_op | source)
XLA Modules:
  0.0 564.7 jit_solution(8423017316243501456)
XLA Ops:
  7.1 58.3 %shard_map.450 = (bf16[2048,768]{1,0:T(8,128)(2,1)}, bf16[512,768]{1,0:T(8,128)(2,1)}, s32[2,2048]{1,0:T(2,128)}, f32[42,128]{1,0:T(8,128)}, bf16[768,1152]{1,0:...) custom-call(bf16[512,768]{1,0:T(8,128)(2,1)} %bitcast.105, ...), custom_call_target="tpu_custom_call" | custom-call | tf_op jit(solution)/shard_map/pallas_call | solution.py:638
  67.7 6.8 %add_convert_fusion.2.kv_ref.refs_3_ = bf16[2048,768]{1,0:T(8,128)(2,1)} fusion(bf16[2048,768]{1,0:T(8,128)(2,1)} %get-tuple-element.89.refs_10_, f32[768]{0:T(1024)S(1)} %concatenate.26, bf16[768,1152]{1,0:T(8,128)(2,1)} %get-tuple-element.91.refs_8_), kind=kOutput, calls=%fused_computation.2 | convolution fusion | flops 2419064832 | bytes 7474176 | tf_op jit(solution)/shard_map/dot_general | solution.py:24
  76.3 41.6 %shard_map.451 = (f32[384,512]{1,0:T(8,128)S(1)}, f32[8,512]{1,0:T(8,128)S(1)}, bf16[2048,768]{1,0:T(8,128)(2,1)S(1)}, bf16[768,1536]{1,0:T(8,128)(2,1)S(1)}, bf16[1536,768]{1,0:T(8,128)(2,1)S(1)}) custom-call(s32[8]{0:T(128)S(1)} %convert_reduce_fusion.8.starts.refs_0_, s32[1,512]{1,0:T(1,128)S(1)} %constant_dynamic-slice_fusion.3.segments.refs_1_, ...), custom_call_target="tpu_custom_call" | custom-call | flops 1610612736 | bytes 3145728 | tf_op jit(solution)/shard_map/pallas_call | solution.py:694
  122.3 2.0 fusion.51
  129.2 1.9 slice.270
  131.7 3.6 fusion.9
  137.8 3.9 add_convert_fusion.1.kv_ref.refs_3_
  143.6 9.6 %collective-permute-done.4.refs_2_ = bf16[1536,768]{1,0:T(8,128)(2,1)} collective-permute-done((bf16[1536,768]{1,0:T(8,128)(2,1)}, bf16[1536,768]{1,0:T(8,128)(2,1)}, u32[]{:S(2)}, u32[]{:S(2)}) %collective-permute-start.4) | collective-permute-done | bytes 2359328 | tf_op jit(solution)/shard_map/ppermute | solution.py:1331
  153.2 33.4 %shard_map.452 = (f32[384,512]{1,0:T(8,128)S(1)}, f32[8,512]{1,0:T(8,128)S(1)}, bf16[2048,768]{1,0:T(8,128)(2,1)S(1)}, bf16[768,1152]{1,0:T(8,128)(2,1)S(1)}, bf16[384,768]{1,0:T(8,128)(2,1)S(1)}) custom-call(s32[8]{0:T(128)S(1)} %convert_reduce_fusion.7.starts.refs_0_, s32[1,512]{1,0:T(1,128)S(1)} %constant_dynamic-slice_fusion.2.segments.refs_1_, ...), custom_call_target="tpu_custom_call" | custom-call | flops 1610612736 | bytes 3145728 | tf_op jit(solution)/shard_map/pallas_call | solution.py:694
  190.3 2.8 add_convert_fusion.kv_ref.refs_3_
  196.2 4.8 shard_map.453
  202.5 1.9 collective-permute-done.6
  205.4 4.8 multiply_convert_fusion
  210.2 5.0 fusion.55
  217.8 2.2 fusion.43
  220.4 2.1 fusion.16
  224.7 3.7 convert_reduce_fusion
  228.5 3.2 fusion.56
  231.7 11.2 %collective-permute-start.11 = (bf16[512,768]{1,0:T(8,128)(2,1)S(1)}, bf16[512,768]{1,0:T(8,128)(2,1)S(1)}, u32[]{:S(2)}, u32[]{:S(2)}) collective-permute-start(bf16[512,768]{1,0:T(8,128)(2,1)S(1)} %get-tuple-element.261), channel_id=1, source_target_pairs={{0,8},{8,0},{16,24},{24,16},{1,9},{9,1},{17,25},{25,17},{2,10},{10... | collective-permute-start | bytes 2359304 | tf_op jit(solution)/shard_map/ppermute | solution.py:1307
  245.7 2.8 convolution_convert_fusion.refs_14_
  248.5 3.0 convolution_convert_fusion.1.refs_13_
  256.7 53.3 %shard_map.454 = (bf16[512,384]{1,0:T(8,128)(2,1)}, bf16[2048,768]{1,0:T(8,128)(2,1)}, bf16[512,768]{1,0:T(8,128)(2,1)}, f32[512,768]{1,0:T(8,128)}, bf16[768,38...) custom-call(s32[8]{0:T(128)} %copy-done.22, ...), custom_call_target="tpu_custom_call" | custom-call | flops 5637144576 | bytes 11010048 | tf_op jit(solution)/shard_map/pallas_call | solution.py:735
  310.0 2.7 multiply_reduce_fusion.1
  317.1 2.4 multiply_reduce_fusion.2
  319.6 2.0 convert_reduce_fusion.5
  321.6 67.8 %shard_map.455 = (bf16[512,384]{1,0:T(8,128)(2,1)}, bf16[2048,768]{1,0:T(8,128)(2,1)}, bf16[512,768]{1,0:T(8,128)(2,1)}, bf16[768,384]{1,0:T(8,128)(2,1)}, bf16[...) custom-call(s32[8]{0:T(128)} %copy-done.21, ...), custom_call_target="tpu_custom_call" | custom-call | flops 5637144576 | bytes 11010048 | tf_op jit(solution)/shard_map/pallas_call | solution.py:735
  389.4 2.7 multiply_reduce_fusion.3
  396.5 62.6 %shard_map.456 = (bf16[512,384]{1,0:T(8,128)(2,1)}, bf16[2048,768]{1,0:T(8,128)(2,1)}, bf16[512,768]{1,0:T(8,128)(2,1)}, bf16[768,384]{1,0:T(8,128)(2,1)}, bf16[...) custom-call(s32[8]{0:T(128)} %copy-done.22, ...), custom_call_target="tpu_custom_call" | custom-call | flops 5637144576 | bytes 11010048 | tf_op jit(solution)/shard_map/pallas_call | solution.py:735
  459.1 2.3 reduce-precision_convert_fusion.1
  465.2 76.7 %shard_map.457 = (f32[22,768]{1,0:T(8,128)}, f32[48,1536]{1,0:T(8,128)}, f32[48,1536]{1,0:T(8,128)}, f32[48,768]{1,0:T(8,128)}, f32[48,384]{1,0:T(8,128)}, /*ind...) custom-call(f32[22,768]{1,0:T(8,128)} %pad_maximum_fusion.3.refs_0_, ...), custom_call_target="tpu_custom_call" | custom-call | tf_op jit(solution)/shard_map/pallas_call | solution.py:735
  553.7 2.1 select_bitcast_fusion
  557.0 2.5 bitcast_convert_fusion
  (321 shorter events, 75.6 us)
Async XLA Ops:
  0.7 128.5 %collective-permute-start.1 = (bf16[768,1536]{1,0:T(8,128)(2,1)}, bf16[768,1536]{1,0:T(8,128)(2,1)}, u32[]{:S(2)}, u32[]{:S(2)}) collective-permute-start(bf16[768,1536]{1,0:T(8,128)(2,1)} %param.46), channel_id=1, source_target_pairs={{8,0},{9,1},{1,8},{0,9},{24,16},{25,17},{17,24},{16,25},{10,2},{11... | collective-permute-start | bytes 7077896 | tf_op jit(solution)/shard_map/ppermute | solution.py:1331
  66.4 129.8 %copy-start.22 = (s32[8]{0:T(128)}, s32[8]{0:T(128)S(1)}, u32[]{:S(2)}) copy-start(s32[8]{0:T(128)S(1)} %convert_reduce_fusion.8.starts.refs_0_) | copy-start | bytes 100
  76.2 41.7 %copy-start.17 = (bf16[512,384]{1,0:T(8,128)(2,1)}, bf16[512,384]{1,0:T(8,128)(2,1)S(1)}, u32[]{:S(2)}) copy-start(bf16[512,384]{1,0:T(8,128)(2,1)S(1)} %fusion.27.q_ref.refs_2_) | copy-start | bytes 1179652
  124.3 2.6 collective-permute-start
  124.4 28.8 %collective-permute-start.4 = (bf16[1536,768]{1,0:T(8,128)(2,1)}, bf16[1536,768]{1,0:T(8,128)(2,1)}, u32[]{:S(2)}, u32[]{:S(2)}) collective-permute-start(bf16[1536,768]{1,0:T(8,128)(2,1)} %param.48), channel_id=1, source_target_pairs={{8,0},{9,1},{1,8},{0,9},{24,16},{25,17},{17,24},{16,25},{10,2},{11... | collective-permute-start | bytes 7077896 | tf_op jit(solution)/shard_map/ppermute | solution.py:1331
  125.9 27.3 %copy-start.21 = (s32[8]{0:T(128)}, s32[8]{0:T(128)S(1)}, u32[]{:S(2)}) copy-start(s32[8]{0:T(128)S(1)} %convert_reduce_fusion.7.starts.refs_0_) | copy-start | bytes 100
  126.6 26.6 %copy-start.11 = (bf16[512,384]{1,0:T(8,128)(2,1)}, bf16[512,384]{1,0:T(8,128)(2,1)S(1)}, u32[]{:S(2)}) copy-start(bf16[512,384]{1,0:T(8,128)(2,1)S(1)} %fusion.26.q_ref.refs_2_) | copy-start | bytes 1179652
  128.5 13.3 %copy-start.31 = (f32[512,768]{1,0:T(8,128)}, f32[512,768]{1,0:T(8,128)S(1)}, u32[]{:S(2)}) copy-start(f32[512,768]{1,0:T(8,128)S(1)} %get-tuple-element.219) | copy-start | bytes 4718596
  136.8 5.0 collective-permute-start.2
  137.0 59.2 %copy-start.18 = (s32[1,512]{1,0:T(1,128)}, s32[1,512]{1,0:T(1,128)S(1)}, u32[]{:S(2)}) copy-start(s32[1,512]{1,0:T(1,128)S(1)} %constant_dynamic-slice_fusion.2.segments.refs_1_) | copy-start | bytes 6148
  142.8 10.5 %copy-start.10 = (bf16[3,768,384]{2,1,0:T(8,128)(2,1)S(1)}, bf16[3,768,384]{2,1,0:T(8,128)(2,1)}, u32[]{:S(2)}) copy-start(bf16[3,768,384]{2,1,0:T(8,128)(2,1)} %param.43) | copy-start | bytes 5308420
  142.8 10.5 %copy-start.14 = (bf16[384,768]{1,0:T(8,128)(2,1)S(1)}, bf16[384,768]{1,0:T(8,128)(2,1)}, u32[]{:S(2)}) copy-start(bf16[384,768]{1,0:T(8,128)(2,1)} %refs_1_.3) | copy-start | bytes 1769476
  186.7 14.4 %copy-start.15 = (bf16[384,768]{1,0:T(8,128)(2,1)}, bf16[384,768]{1,0:T(8,128)(2,1)S(1)}, u32[]{:S(2)}) copy-start(bf16[384,768]{1,0:T(8,128)(2,1)S(1)} %get-tuple-element.105) | copy-start | bytes 1769476
  188.8 4.3 collective-permute-start.5
  193.6 10.8 %copy-start.29 = (f32[512,768]{1,0:T(8,128)}, f32[512,768]{1,0:T(8,128)S(1)}, u32[]{:S(2)}) copy-start(f32[512,768]{1,0:T(8,128)S(1)} %get-tuple-element.215) | copy-start | bytes 4718596
  202.0 2.4 collective-permute-start.6
  215.2 2.6 collective-permute-start.7
  215.6 4.8 collective-permute-start.10
  215.7 101.4 %collective-permute-start.9 = (bf16[512,768]{1,0:T(8,128)(2,1)}, bf16[512,768]{1,0:T(8,128)(2,1)}, u32[]{:S(2)}, u32[]{:S(2)}) collective-permute-start(bf16[512,768]{1,0:T(8,128)(2,1)} %bitcast.22), channel_id=1, source_target_pairs={{0,8},{8,0},{16,24},{24,16},{1,9},{9,1},{17,25},{25,17},{2,10},{10... | collective-permute-start | bytes 2359304 | tf_op jit(solution)/shard_map/ppermute | solution.py:1307
  216.1 26.8 %collective-permute-start.3 = (bf16[512,768]{1,0:T(8,128)(2,1)S(1)}, bf16[512,768]{1,0:T(8,128)(2,1)S(1)}, u32[]{:S(2)}, u32[]{:S(2)}) collective-permute-start(bf16[512,768]{1,0:T(8,128)(2,1)S(1)} %add_convert_fusion.4.own_ref), channel_id=1, source_target_pairs={{0,1},{9,8},{16,17},{25,24},{2,3},{11,10},{18,19},{27,26},{4,5},{1... | collective-permute-start | bytes 2359304 | tf_op jit(solution)/shard_map/ppermute | solution.py:1331
  228.4 14.4 %copy-start.34 = (f32[512,768]{1,0:T(8,128)S(1)}, f32[512,768]{1,0:T(8,128)}, u32[]{:S(2)}) copy-start(f32[512,768]{1,0:T(8,128)} %copy-done.33) | copy-start | bytes 4718596
  231.7 14.0 %copy-start.79 = (bf16[512,1536]{1,0:T(8,128)(2,1)S(1)}, bf16[512,1536]{1,0:T(8,128)(2,1)}, u32[]{:S(2)}) copy-start(bf16[512,1536]{1,0:T(8,128)(2,1)} %copy-done.78) | copy-start | bytes 4718596
  231.7 19.8 %collective-permute-start.11 = (bf16[512,768]{1,0:T(8,128)(2,1)S(1)}, bf16[512,768]{1,0:T(8,128)(2,1)S(1)}, u32[]{:S(2)}, u32[]{:S(2)}) collective-permute-start(bf16[512,768]{1,0:T(8,128)(2,1)S(1)} %get-tuple-element.261), channel_id=1, source_target_pairs={{0,8},{8,0},{16,24},{24,16},{1,9},{9,1},{17,25},{25,17},{2,10},{10... | collective-permute-start | bytes 2359304 | tf_op jit(solution)/shard_map/ppermute | solution.py:1307
  244.2 309.5 %collective-permute-start.8 = (bf16[512,768]{1,0:T(8,128)(2,1)}, bf16[512,768]{1,0:T(8,128)(2,1)}, u32[]{:S(2)}, u32[]{:S(2)}) collective-permute-start(bf16[512,768]{1,0:T(8,128)(2,1)} %get-tuple-element.222), channel_id=1, source_target_pairs={{0,1},{9,8},{16,17},{25,24},{2,3},{11,10},{18,19},{27,26},{4,5},{1... | collective-permute-start | bytes 2359304 | tf_op jit(solution)/shard_map/ppermute | solution.py:1331
  256.7 53.3 %copy-start.30 = (f32[512,768]{1,0:T(8,128)S(1)}, f32[512,768]{1,0:T(8,128)}, u32[]{:S(2)}) copy-start(f32[512,768]{1,0:T(8,128)} %copy-done.29) | copy-start | bytes 4718596
  321.6 67.8 %copy-start.32 = (f32[512,768]{1,0:T(8,128)S(1)}, f32[512,768]{1,0:T(8,128)}, u32[]{:S(2)}) copy-start(f32[512,768]{1,0:T(8,128)} %copy-done.31) | copy-start | bytes 4718596
  396.5 62.6 %copy-start.37 = (f32[512,768]{1,0:T(8,128)S(1)}, f32[512,768]{1,0:T(8,128)}, u32[]{:S(2)}) copy-start(f32[512,768]{1,0:T(8,128)} %get-tuple-element.204) | copy-start | bytes 4718596
  461.4 94.4 %collective-permute-start.12 = (bf16[512,768]{1,0:T(8,128)(2,1)}, bf16[512,768]{1,0:T(8,128)(2,1)S(1)}, u32[]{:S(2)}, u32[]{:S(2)}) collective-permute-start(bf16[512,768]{1,0:T(8,128)(2,1)} %reduce-precision_convert_fusion.1), channel_id=1, source_target_pairs={{0,1},{9,8},{16,17},{25,24},{2,3},{11,10},{18,19},{27,26},{4,5},{1... | collective-permute-start | bytes 2359304 | tf_op jit(solution)/shard_map/ppermute | solution.py:1331
  462.9 94.1 %collective-permute-start.13 = (bf16[512,768]{1,0:T(8,128)(2,1)S(1)}, bf16[512,768]{1,0:T(8,128)(2,1)}, u32[]{:S(2)}, u32[]{:S(2)}) collective-permute-start(bf16[512,768]{1,0:T(8,128)(2,1)S(1)} %reduce-precision_convert_fusion), channel_id=1, source_target_pairs={{0,1},{9,8},{16,17},{25,24},{2,3},{11,10},{18,19},{27,26},{4,5},{1... | collective-permute-start | bytes 2359304 | tf_op jit(solution)/shard_map/ppermute | solution.py:1331
  465.2 78.6 %copy-start.61 = (f32[48,768]{1,0:T(8,128)S(1)}, f32[48,768]{1,0:T(8,128)}, u32[]{:S(2)}) copy-start(f32[48,768]{1,0:T(8,128)} %get-tuple-element.149) | copy-start | bytes 442372
  541.9 10.4 %copy-start.63 = (f32[48,384]{1,0:T(8,128)S(1)}, f32[48,384]{1,0:T(8,128)}, u32[]{:S(2)}) copy-start(f32[48,384]{1,0:T(8,128)} %get-tuple-element.148) | copy-start | bytes 221188
  541.9 11.1 %copy-start.62 = (f32[22,768]{1,0:T(8,128)S(1)}, f32[22,768]{1,0:T(8,128)}, u32[]{:S(2)}) copy-start(f32[22,768]{1,0:T(8,128)} %get-tuple-element.141) | copy-start | bytes 202756
  (63 other events, 207.3 us)

commit v6 on v5

--- a/solution.py
+++ b/solution.py
@@ -161,9 +161,8 @@
         lse_ref[head : head + 1, :] = top[head : head + 1, :] + jnp.log(total)
 
 
-def forward_kernel(
-    block, causal, starts, ends, segments, q_ref, kv_ref, out_ref, lse_ref, masked_q, acc, top
-):
+def forward_kernel(block, causal, tokens, starts, ends, segments, q_ref, kv_ref, *refs):
+    out_ref, lse_ref, masked_q, acc, top = refs[tokens:]
     mask = Mask(causal, starts, segments, ends[2])
     forward_start(q_ref, masked_q, acc, top)
 
@@ -248,21 +247,21 @@
     ]
 
 
-def attend(queries, kv, mask):
+def attend(queries, kv, mask, tokens):
     count, width = queries.shape
     causal, starts, ends, segments = mask
     return pl.pallas_call(
-        functools.partial(forward_kernel, KEY_BLOCK, causal),
+        functools.partial(forward_kernel, KEY_BLOCK, causal, len(tokens)),
         out_shape=(
             jax.ShapeDtypeStruct((width, count), F32),
             jax.ShapeDtypeStruct((8, count), F32),
         ),
-        in_specs=[SCALARS] * 2 + [VECTORS] * 3,
+        in_specs=[SCALARS] * 2 + [VECTORS] * 3 + [ANYWHERE] * len(tokens),
         out_specs=(VECTORS,) * 2,
         scratch_shapes=forward_scratch(count, width),
         compiler_params=pltpu.CompilerParams(vmem_limit_bytes=40 << 20),
         cost_estimate=cost_of(kv, count, width, 2),
-    )(starts, ends, segments, queries, kv)
+    )(starts, ends, segments, queries, kv, *tokens)
 
 
 MESH = pl.DeviceIdType.MESH
@@ -424,18 +423,22 @@
 def pieces_of(weights):
     found = []
     for k, weight in enumerate(weights):
-        rows, columns = weight.shape
+        rows, columns = weight.shape[-2:]
         number = 1 if rows % 3 else 3
         while 2 * rows * columns > 655360 * number and rows % (64 * number) == 0:
             number *= 2
-        found += [(k, i * (rows // number), rows // number) for i in range(number)]
+        for matrix in range(matrices_of(weight)):
+            found += [(k, matrix, i * (rows // number), rows // number) for i in range(number)]
     return found
 
 
-def beside(weight, model):
-    rows, columns = weight.shape
-    matrices = 3 if rows == 3 * model else 1
-    return jax.ShapeDtypeStruct((rows // matrices, columns * matrices), weight.dtype)
+def matrices_of(weight):
+    return weight.shape[0] if len(weight.shape) == 3 else 1
+
+
+def beside(weight):
+    rows, columns = weight.shape[-2:]
+    return jax.ShapeDtypeStruct((rows, columns * matrices_of(weight)), weight.dtype)
 
 
 AHEAD = 4
@@ -448,8 +451,8 @@
         self.pieces = pieces_of(inputs)
         self.matrices = [
             (k, matrix)
-            for k, (given, out) in enumerate(zip(inputs, outputs))
-            for matrix in range(given.shape[0] // out.shape[0])
+            for k, given in enumerate(inputs)
+            for matrix in range(matrices_of(given))
         ]
         self.number = len(self.pieces)
         self.own = lax.rem(here.x, 2)
@@ -458,18 +461,20 @@
         here = self.here
         return [(here.core >= 0, here.diagonal), (here.core == 1, here.over_x)]
 
+    def matrix(self, k, matrix):
+        given = self.inputs[k]
+        return given.at[matrix] if len(given.shape) == 3 else given
+
     def part(self, p, which):
-        k, start, rows = self.pieces[p]
+        k, matrix, start, rows = self.pieces[p]
         first = pl.multiple_of(start + which * (rows // 2), 16)
-        return self.inputs[k].at[pl.ds(first, rows // 2)]
+        return self.matrix(k, matrix).at[pl.ds(first, rows // 2)]
 
     def place(self, p, which):
-        k, start, rows = self.pieces[p]
-        out = self.outputs[k]
-        matrix, start = divmod(start, out.shape[0])
-        columns = self.inputs[k].shape[1]
+        k, matrix, start, rows = self.pieces[p]
+        columns = self.inputs[k].shape[-1]
         first = pl.multiple_of(start + which * (rows // 2), 16)
-        return out.at[pl.ds(first, rows // 2), pl.ds(matrix * columns, columns)]
+        return self.outputs[k].at[pl.ds(first, rows // 2), pl.ds(matrix * columns, columns)]
 
     def over_y(self, p):
         return remote(
@@ -486,9 +491,9 @@
 
     def across(self, m):
         k, matrix = self.matrices[m]
-        rows, columns = self.outputs[k].shape[0], self.inputs[k].shape[1]
+        columns = self.inputs[k].shape[-1]
         return remote(
-            self.inputs[k].at[pl.ds(matrix * rows, rows)],
+            self.matrix(k, matrix),
             self.outputs[k].at[:, pl.ds(matrix * columns, columns)],
             self.core_sent.at[m],
             self.core_got.at[m],
@@ -543,19 +548,21 @@
 
 
 def opening_kernel(ring, number, *refs):
-    inputs, outputs, sems = refs[: 4 + number], refs[4 + number : 8 + 2 * number], refs[8 + 2 * number :]
-    source, target, segments, vectors = inputs[:4]
-    source_all, target_out, segments_out, vectors_out = outputs[:4]
+    inputs, refs = refs[: 9 + number], refs[9 + number :]
+    outputs, (vectors, *sems) = refs[: 5 + number], refs[5 + number :]
+    source, target, source_seg, target_seg = inputs[:4]
+    source_all, target_out, source_seg_out, target_seg_out, vectors_out = outputs[:5]
     shard_sems, vector_sems = sems[:3], sems[3:6]
     here = Here(ring)
-    fetch = Fetch(here, inputs[4:], outputs[4:], sems[10:])
+    fetch = Fetch(here, inputs[9:], outputs[5:], sems[10:])
     here.meet(here.neighbours() + here.crosswise() + fetch.devices())
     count = source.shape[0]
     own = pl.ds(pl.multiple_of(here.z * count, count), count)
     moves = [
         (source, source_all.at[own]),
         (target, target_out),
-        (segments, segments_out),
+        (source_seg, source_seg_out),
+        (target_seg, target_seg_out),
     ]
     owner = here.core == here.y
 
@@ -586,12 +593,26 @@
         def _():
             across.wait_recv()
 
+    gather = Gather(here, source_all, sems[6:10], source, owner)
+    gather.begin()
+
     @pl.when(owner)
     def _():
-        for k in range(3):
+        for k in range(len(moves)):
             across, local = shard_copy(k)
             across.start()
             local.start()
+
+    fetch.begin()
+
+    vectors[...] = jnp.zeros_like(vectors)
+    for row, bias in enumerate(inputs[4:7]):
+        width = bias.shape[1]
+        for part in range(2):
+            value = bias[part : part + 1, :].astype(F32)
+            vectors[row : row + 1, 2 * part * width : (2 * part + 1) * width] = value
+    for row, bias in enumerate(inputs[7:9]):
+        vectors[3 + row : 4 + row, :] = bias[...].astype(F32).reshape(1, -1)
 
     @pl.when(here.core == 0)
     def _():
@@ -599,9 +620,6 @@
         across.start()
         local.start()
 
-    gather = Gather(here, source_all, sems[6:10], source, owner)
-    gather.begin()
-    fetch.begin()
     done = 0
     for step in range(1, ring):
         while done < fetch.number * (2 * step - 1) // (2 * ring - 2):
@@ -612,9 +630,8 @@
         fetch.advance(done)
         done += 1
     gather.finish()
-    wait_shard(0)
-    wait_shard(1)
-    wait_shard(2)
+    for k in range(len(moves)):
+        wait_shard(k)
     fetch.end()
     across, local = vector_copy()
 
@@ -628,48 +645,73 @@
         across.wait_recv()
 
 
-def opening(ring, source, target, segments, vectors, weights):
-    inputs = (source, target, segments, vectors) + tuple(weights)
+def opening(ring, source, target, source_seg, target_seg, biases, weights):
+    inputs = (source, target, source_seg, target_seg, *biases, *weights)
     count, model = source.shape
-    rows = jax.ShapeDtypeStruct((ring * count, model), BF16)
-    shapes = (rows, jax.ShapeDtypeStruct(target.shape, BF16)) + tuple(jax.ShapeDtypeStruct(v.shape, v.dtype) for v in inputs[2:4])
-    shapes += tuple(beside(weight, model) for weight in weights)
     number = len(weights)
+    units = biases[-1].shape[0]
+    shapes = (
+        jax.ShapeDtypeStruct((ring * count, model), BF16),
+        jax.ShapeDtypeStruct(target.shape, BF16),
+        jax.ShapeDtypeStruct(source_seg.shape, jnp.int32),
+        jax.ShapeDtypeStruct(target_seg.shape, jnp.int32),
+        jax.ShapeDtypeStruct((8, units), F32),
+    ) + tuple(beside(weight) for weight in weights)
     return pl.pallas_call(
         functools.partial(opening_kernel, ring, number),
         out_shape=shapes,
-        in_specs=[VECTORS] * 4 + [ANYWHERE] * number,
-        out_specs=(ANYWHERE,) + (VECTORS,) * 3 + (ANYWHERE,) * number,
-        scratch_shapes=[DMA((3,))] * 3 + [DMA] * 3 + gather_sems(ring) + fetch_sems(weights),
+        in_specs=[VECTORS] * 9 + [ANYWHERE] * number,
+        out_specs=(ANYWHERE,) + (VECTORS,) * 4 + (ANYWHERE,) * number,
+        scratch_shapes=[pltpu.VMEM((8, units), F32)]
+        + [DMA((4,))] * 3
+        + [DMA] * 3
+        + gather_sems(ring)
+        + fetch_sems(weights),
         compiler_params=pltpu.CompilerParams(collective_id=1, has_side_effects=True),
     )(*inputs)
 
 
 def gather_attend_kernel(
-    block, causal, ring, number, tokens, starts, segments, q_ref, kv_ref, own_ref, *refs
+    block, causal, ring, number, tokens, starts, segments, bias_ref, own_ref, rows_ref, proj_ref, *refs
 ):
     weights, refs = refs[:number], refs[number + tokens :]
-    out_ref, lse_ref, all_ref = refs[:3]
-    fetched, refs = refs[3 : 3 + number], refs[3 + number :]
-    masked_q, acc, top, copied = refs[:4]
+    q_ref, kv_ref, out_ref, lse_ref, all_ref = refs[:5]
+    fetched, refs = refs[5 : 5 + number], refs[5 + number :]
+    masked_q, acc, top, rows_in, proj, copied, rows_copied, proj_copied = refs[:8]
     here = Here(ring)
-    gather = Gather(here, all_ref, refs[4:8])
-    fetch = Fetch(here, weights, fetched, refs[8:])
+    gather = Gather(here, all_ref, refs[8:12])
+    fetch = Fetch(here, weights, fetched, refs[12:])
+    count, width = q_ref.shape
+    first_row = pl.multiple_of(here.z * count, count)
+
+    def rows_copy(shard):
+        rows = pl.ds(pl.multiple_of(shard * count, count), count)
+        return pltpu.make_async_copy(rows_ref.at[rows], rows_in.at[rows], rows_copied.at[shard])
+
+    proj_copy = pltpu.make_async_copy(proj_ref, proj, proj_copied)
+    proj_copy.start()
+    for shard in range(ring):
+        rows_copy(shard).start()
     here.meet(here.neighbours() + fetch.devices())
-    count = own_ref.shape[0]
-    first_row = pl.multiple_of(here.z * count, count)
     local = pltpu.make_async_copy(own_ref, all_ref.at[pl.ds(first_row, count)], copied)
     local.start()
     fetch.begin()
     local.wait()
     gather.begin()
     mask = Mask(causal, starts, segments, first_row)
+    proj_copy.wait()
+    for shard in range(ring):
+        rows_copy(shard).wait()
+    queries = dot_plain(rows_in[pl.ds(first_row, count), :], proj[:, :width]) + bias_ref[:, :width]
+    q_ref[...] = (queries.astype(BF16).astype(F32) * HEAD_DIM ** (-0.5)).astype(BF16)
     forward_start(q_ref, masked_q, acc, top)
     blocks = kv_ref.shape[0] // block
 
     @pl.loop(0, blocks)
     def _(index):
         rows = pl.ds(pl.multiple_of(index * block, block), block)
+        both = dot_plain(rows_in[rows, :], proj[:, width:]) + bias_ref[:, width:]
+        kv_ref[rows, :] = both.astype(BF16)
         forward_block(index, rows, True, block, kv_ref, mask, masked_q, acc, top)
 
         @pl.when((index >= 1) & (index < ring))
@@ -682,34 +724,43 @@
             )
 
     forward_end(out_ref, lse_ref, acc, top)
-
     gather.finish()
     fetch.end()
 
 
-def gather_attend(number, ring, queries, kv, mask, own, weights, tokens=()):
-    count, width = queries.shape
+def gather_attend(number, ring, rows, proj, bias, mask, own, weights, tokens=()):
+    length, model = rows.shape
+    count, width = length // ring, proj.shape[1] // 3
     causal, starts, _, segments = mask
     fetched = len(weights)
+    kv = jax.ShapeDtypeStruct((length, 2 * width), BF16)
     return pl.pallas_call(
         functools.partial(gather_attend_kernel, KEY_BLOCK, causal, ring, fetched, len(tokens)),
         out_shape=(
+            jax.ShapeDtypeStruct((count, width), BF16),
+            kv,
             jax.ShapeDtypeStruct((width, count), F32),
             jax.ShapeDtypeStruct((8, count), F32),
             jax.ShapeDtypeStruct((ring * own.shape[0], own.shape[1]), BF16),
         )
-        + tuple(beside(weight, own.shape[1]) for weight in weights),
-        in_specs=[SCALARS] + [VECTORS] * 4 + [ANYWHERE] * (fetched + len(tokens)),
-        out_specs=(VECTORS, VECTORS) + (ANYWHERE,) * (1 + fetched),
+        + tuple(beside(weight) for weight in weights),
+        in_specs=[SCALARS] + [VECTORS] * 3 + [ANYWHERE] * (2 + fetched + len(tokens)),
+        out_specs=(VECTORS,) * 4 + (ANYWHERE,) * (1 + fetched),
         scratch_shapes=forward_scratch(count, width)
-        + [DMA]
+        + [
+            pltpu.VMEM((length, model), BF16),
+            pltpu.VMEM(proj.shape, BF16),
+            DMA,
+            DMA((ring,)),
+            DMA,
+        ]
         + gather_sems(ring)
         + fetch_sems(weights),
         compiler_params=pltpu.CompilerParams(
-            vmem_limit_bytes=40 << 20, collective_id=number, has_side_effects=True
+            vmem_limit_bytes=50 << 20, collective_id=number, has_side_effects=True
         ),
-        cost_estimate=cost_of(kv, count, width, 2),
-    )(starts, segments, queries, kv, own, *weights, *tokens)
+        cost_estimate=cost_of(kv, count, width, 4),
+    )(starts, segments, bias, own, rows, proj, *weights, *tokens)
 
 
 class Part:
@@ -849,8 +900,8 @@
                     self.stages[k].begin()
 
 
-def chain(array, kinds, times):
-    rows, columns = array.shape
+def chain(array, kinds, times, made=None):
+    rows, columns = made[2] if made else array.shape
     scratch, shapes = [], []
     for kind in kinds:
         rows = rows // 2
@@ -863,7 +914,7 @@
     def bind(here, inputs, outputs, refs):
         refs = list(refs)
         results = refs[len(refs) - len(kinds) + 1 :] + [outputs[0]]
-        source, stages = inputs[0], []
+        source, stages = made[0][made[1]] if made else inputs[0], []
         for kind, result in zip(kinds, results):
             buffers = [refs.pop(0) for _ in range(2 if kind == "y" else 1)]
             sems = [refs.pop(0) for _ in range(2)]
@@ -871,7 +922,62 @@
             source = result
         return Chain(stages, times)
 
-    return Part((array,), [VECTORS], [final], scratch, bind)
+    inputs = () if made else (array,)
+    return Part(inputs, [VECTORS] * len(inputs), [final], scratch, bind)
+
+
+def closing_kernel(flag, *refs):
+    own_source, other_source, own_target, other_target, vectors = refs[:5]
+    grads, outputs = refs[5:18], refs[18:]
+    keeps = flag[0] == 1
+    for own, other, out in (
+        (own_source, other_source, outputs[0]),
+        (own_target, other_target, outputs[1]),
+    ):
+        out[...] = jnp.where(keeps, own[...], other[...]).astype(F32)
+    for k in range(3):
+        of_q, of_out, of_kv = grads[3 * k : 3 * k + 3]
+        qkv, out = outputs[2 + 2 * k : 4 + 2 * k]
+        width = of_q.shape[1]
+        qkv[0] = of_q[...]
+        qkv[1] = of_kv[:, :width]
+        qkv[2] = of_kv[:, width:]
+        out[...] = of_out[...].T
+    for k in range(2):
+        of_in, of_out = grads[9 + 2 * k : 11 + 2 * k]
+        outputs[8 + 2 * k][...] = of_in[...]
+        outputs[9 + 2 * k][...] = of_out[...].T
+    row = 0
+    for out in outputs[12:18]:
+        out[...] = vectors[row : row + out.shape[0], :]
+        row += out.shape[0]
+    for out in outputs[18:21]:
+        width = out.shape[1]
+        out[0:1, :] = vectors[row : row + 1, :width]
+        out[1:2, :] = vectors[row : row + 1, width:]
+        row += 1
+    for out in outputs[21:]:
+        for part in range(out.shape[1] // vectors.shape[1]):
+            span = slice(part * vectors.shape[1], (part + 1) * vectors.shape[1])
+            out[:, span] = vectors[row : row + 1, :]
+            row += 1
+
+
+def closing(flag, rows, vectors, grads, sizes):
+    part, width = grads[0].shape
+    units = grads[9].shape[1]
+    model = vectors.shape[1]
+    shapes = [rows[0].shape] * 2
+    shapes += [(3, part, width), (width, part)] * 3 + [(part, units), (units, part)] * 2
+    shapes += [(size, model) for size in sizes] + [(2, width)] * 3 + [(1, units)] * 2
+    inputs = (flag, *rows, vectors, *grads)
+    return pl.pallas_call(
+        closing_kernel,
+        out_shape=[jax.ShapeDtypeStruct(shape, F32) for shape in shapes],
+        in_specs=[SCALARS] + [VECTORS] * (len(inputs) - 1),
+        out_specs=[VECTORS] * len(shapes),
+        compiler_params=pltpu.CompilerParams(vmem_limit_bytes=50 << 20),
+    )(*inputs)
 
 
 class Small:
@@ -990,28 +1096,40 @@
                 shard = jnp.where((z == device) & (turn == k + 1), other, shard)
         return shard
 
-    def across(self, shard):
+    def across(self, turn, shard):
         return remote(
-            self.terms.at[shard, self.half(1 - self.here.core)],
+            self.terms.at[lax.rem(turn, 2), self.half(1 - self.here.core)],
             self.from_core.at[shard],
             self.core_sent.at[shard],
             self.core_got.at[shard],
             self.here.partner,
         )
 
+    def slot(self, way, shard, z):
+        return jnp.where((way == 1) & (shard == z), self.here.ring, shard)
+
     def along(self, way, shard, device):
         return remote(
             self.outgoing.at[shard],
-            self.arrived.at[way, shard],
+            self.arrived.at[self.slot(way, shard, device[1])],
             self.sent.at[shard],
             self.got.at[way, shard],
             device,
         )
 
+    def put(self, turn, shard, terms):
+        @pl.when(turn > 2)
+        def _():
+            self.across(turn - 2, self.shard_at(turn - 2)).wait_send()
+
+        slot = lax.rem(turn, 2)
+        self.terms[slot] = terms.astype(BF16)
+        self.across(turn, shard).start()
+        self.outgoing[shard] = self.terms[slot, self.half(self.here.core), :]
+
     def both(self, shard):
-        self.across(shard).wait_recv()
-        own = self.terms[shard, self.half(self.here.core), :].astype(F32)
-        return own + self.from_core[shard].astype(F32)
+        self.across(0, shard).wait_recv()
+        return self.outgoing[shard].astype(F32) + self.from_core[shard].astype(F32)
 
     def forward(self, shard):
         here = self.here
@@ -1024,7 +1142,7 @@
             @pl.when(mine & comes)
             def _(way=way):
                 self.along(way, shard, here.partner).wait_recv()
-                self.total[...] += self.arrived[way, shard].astype(F32)
+                self.total[...] += self.arrived[self.slot(way, shard, here.z)].astype(F32)
 
         self.outgoing[shard] = self.total[...].astype(BF16)
         for way, mine, device in ((0, shard > here.z, here.right), (1, shard < here.z, here.left)):
@@ -1055,8 +1173,7 @@
                 def _():
                     self.forward(self.shard_at(turn - 1))
 
-            self.terms[shard] = self.block(shard, between).astype(BF16)
-            self.across(shard).start()
+            self.put(turn, shard, self.block(shard, between))
             for time in range(1, ring):
                 pl.when(turn == time)(functools.partial(event, time))
 
@@ -1076,8 +1193,7 @@
             exchange.start()
         else:
             own = own + query
-        self.terms[here.z] = own.astype(BF16)
-        self.across(here.z).start()
+        self.put(jnp.int32(ring), here.z, own)
         if self.apart:
             exchange.wait()
             self.query_sum[...] = self.query_low[...].astype(F32) + self.query_got[...].astype(F32)
@@ -1095,7 +1211,7 @@
             @pl.when(comes)
             def _(way=way):
                 self.along(way, here.z, here.partner).wait_recv()
-                self.total[...] += self.arrived[way, here.z].astype(F32)
+                self.total[...] += self.arrived[self.slot(way, here.z, here.z)].astype(F32)
 
         own, other = self.half(here.core), self.half(1 - here.core)
         self.sum[own, :] = self.total[...].astype(BF16)
@@ -1107,8 +1223,9 @@
             else:
                 copy.start()
                 copy.wait_send()
+        self.across(ring - 1, self.shard_at(ring - 1)).wait_send()
+        self.across(ring, here.z).wait_send()
         for shard in range(ring):
-            self.across(shard).wait_send()
 
             @pl.when(here.z != shard)
             def _(shard=shard):
@@ -1118,45 +1235,71 @@
 
 
 class Products:
-    def __init__(self, back, inputs, outputs, scratch, time):
+    def __init__(self, back, inputs, of_bias, made, scratch, time):
         self.back, self.time = back, time
-        self.block, self.copied = scratch
         self.query_in, self.key_in, self.grad_branch, self.mixed = inputs
-        self.of_q, self.of_out, self.of_kv, self.of_bias = outputs
+        self.of_bias = of_bias
+        self.of_q, self.of_out, self.of_kv = made
+        self.blocks, self.copied = scratch
+
+    def copy(self, index):
+        part = pl.ds(pl.multiple_of(index * 256, 256), 256)
+        slot = lax.rem(index, 2)
+        return pltpu.make_async_copy(
+            self.key_in.at[:, part], self.blocks.at[slot], self.copied.at[slot]
+        )
 
     def event(self, time):
+        if time == 0:
+            self.copy(0).start()
         if time != self.time:
             return
         dq, dkv = self.back.dq_out, self.back.dkv
         width = dq.shape[1]
+        number = self.of_kv.shape[0] // 256
+
+        @pl.loop(0, number)
+        def _(index):
+            @pl.when(index + 1 < number)
+            def _():
+                self.copy(index + 1).start()
+
+            self.copy(index).wait()
+            part = pl.ds(pl.multiple_of(index * 256, 256), 256)
+            block = self.blocks[lax.rem(index, 2)]
+            self.of_kv[part, :] = dot_first(block, dkv[...]).astype(BF16)
+
         self.of_q[...] = dot_first(self.query_in[...], dq[...]).astype(BF16)
         self.of_out[...] = dot_first(self.grad_branch[...], self.mixed[...].T).astype(BF16)
         self.of_bias[0:1, :] = jnp.sum(dq[...].astype(F32), axis=0, keepdims=True)
         self.of_bias[1:2, :] = jnp.sum(dkv[:, width:].astype(F32), axis=0, keepdims=True)
 
-        @pl.loop(0, self.of_kv.shape[0] // 256)
-        def _(index):
-            part = pl.ds(pl.multiple_of(index * 256, 256), 256)
-            copy = pltpu.make_async_copy(self.key_in.at[:, part], self.block, self.copied)
-            copy.start()
-            copy.wait()
-            self.of_kv[part, :] = dot_first(self.block[...], dkv[...]).astype(BF16)
-
-
-def products(box, query_in, key_in, grad_branch, mixed, time):
+
+def products(box, query_in, key_in, grad_branch, mixed, time, begins):
     model, width = query_in.shape[1], mixed.shape[0]
-    return Part(
+    shapes = ((model, width), (model, width), (model, 2 * width))
+
+    def bind(here, inputs, outputs, refs):
+        made = refs[2:] if begins else outputs[1:]
+        for k in range(3):
+            box[k] = made[k]
+        return Products(box["back"], inputs, outputs[0], made, refs[:2], time)
+
+    part = Part(
         (query_in, key_in, grad_branch, mixed),
         [VECTORS, ANYWHERE, VECTORS, VECTORS],
-        [
-            jax.ShapeDtypeStruct((model, width), BF16),
-            jax.ShapeDtypeStruct((model, width), BF16),
-            jax.ShapeDtypeStruct((model, 2 * width), BF16),
-            jax.ShapeDtypeStruct((2, width), F32),
-        ],
-        [pltpu.VMEM((key_in.shape[0], 256), BF16), DMA],
-        lambda here, inputs, outputs, refs: Products(box["back"], inputs, outputs, refs, time),
-    )
+        [jax.ShapeDtypeStruct((2, width), F32)]
+        + ([] if begins else [jax.ShapeDtypeStruct(shape, BF16) for shape in shapes]),
+        [pltpu.VMEM((2, key_in.shape[0], 256), BF16), DMA((2,))]
+        + ([pltpu.VMEM(shape, BF16) for shape in shapes] if begins else []),
+        bind,
+    )
+    if not begins:
+        return [part]
+    firsts = [
+        chain(None, kind, (time, 6), (box, k, shape)) for k, (kind, shape) in enumerate(zip("yyx", shapes))
+    ]
+    return [part, *firsts]
 
 
 class FeedBack:
@@ -1248,7 +1391,7 @@
     causal, starts, segments = mask
     ring = lax.axis_size("seq")
     count, width = queries.shape
-    model = weights[0].shape[0]
+    model = weights.shape[0]
     part = count // 2
     shapes = [
         jax.ShapeDtypeStruct((count, width), BF16),
@@ -1256,9 +1399,9 @@
         jax.ShapeDtypeStruct((count, model), BF16),
     ]
     scratch = backward_scratch(count, width) + [
-        pltpu.VMEM((ring, count, model), BF16),
+        pltpu.VMEM((2, count, model), BF16),
         *[pltpu.VMEM((ring, part, model), BF16)] * 2,
-        pltpu.VMEM((2, ring, part, model), BF16),
+        pltpu.VMEM((ring + 1, part, model), BF16),
         pltpu.VMEM((part, model), F32),
         *[DMA((ring,))] * 3,
         DMA((2, ring)),
@@ -1268,7 +1411,7 @@
         shapes.append(jax.ShapeDtypeStruct((count, model), F32))
         scratch += [pltpu.VMEM((count, model), BF16)] * 2 + [DMA((2,))]
     main = Part(
-        (starts, segments, queries, kv, grad_mixed, grad_mixed_t, output, lse, weights[0]),
+        (starts, segments, queries, kv, grad_mixed, grad_mixed_t, output, lse, weights),
         [SCALARS] + [VECTORS] * 8,
         shapes,
         scratch,
@@ -1341,8 +1484,10 @@
         return jnp.where(self.core == self.y, rows, self.swap_core(rows))
 
     def hand_out(self, rows):
-        other = self.permute(rows, lambda d, y: (d, 1 - y) if d % 2 != y else None)
-        return jnp.where(self.core == self.y, rows, other)
+        return jnp.where(self.core == self.y, rows, self.others(rows))
+
+    def others(self, rows):
+        return self.permute(rows, lambda d, y: (d, 1 - y) if d % 2 != y else None)
 
     def plan(self):
         return Plan(self.pairs == 4 and self.ring == 4)
@@ -1403,12 +1548,11 @@
     return (causal, key_starts, ends, query_seg[None])
 
 
-def projected(query_in, key_in, weights):
-    w_all, b_q, b_kv = weights
-    width = b_q.shape[0]
-    scale = HEAD_DIM ** (-0.5)
-    queries = ((dot_plain(query_in, w_all[:, :width]) + b_q).astype(BF16) * scale).astype(BF16)
-    return queries, (dot_plain(key_in, w_all[:, width:]) + b_kv).astype(BF16)
+def projected(query_in, key_in, weights, bias):
+    width = bias.shape[1] // 3
+    queries = (dot_plain(query_in, weights[:, :width]) + bias[:, :width]).astype(BF16)
+    kv = (dot_plain(key_in, weights[:, width:]) + bias[:, width:]).astype(BF16)
+    return (queries * HEAD_DIM ** (-0.5)).astype(BF16), kv
 
 
 def attention_output(place, queries, kv, output, lse, out_weight, out_bias):
@@ -1418,7 +1562,19 @@
 
 
 def attention_backward(
-    number, grad_branch, saved, query_in, key_in, weights, out_weight, mask, apart, plan, wanted, inside=()
+    number,
+    grad_branch,
+    saved,
+    query_in,
+    key_in,
+    weights,
+    out_weight,
+    mask,
+    apart,
+    plan,
+    wanted,
+    inside=(),
+    begins=False,
 ):
     mixed = saved[4]
     grad_mixed = dot_last(grad_branch, out_weight).astype(BF16)
@@ -1426,13 +1582,15 @@
     box = {}
     more = []
     if plan.kernels:
-        made = products(box, query_in, key_in, grad_branch, mixed, 5)
-        more = [made, *plan.chains(wanted), *inside]
+        made = products(box, query_in, key_in, grad_branch, mixed, 5, begins)
+        more = [*made, *plan.chains(wanted), *inside]
     (grad_q, grad_kv, *sums), *rest = attend_back(
         number, saved, grad_mixed, grad_mixed_t, weights, mask, apart, more, box
     )
     if plan.kernels:
-        *grads, grad_bias = rest.pop(0)
+        (grad_bias, *grads), *rest = rest
+        if begins:
+            grads, rest = [first[0] for first in rest[:3]], rest[3:]
     else:
         grads = (
             dot_first(query_in, grad_q).astype(BF16),
@@ -1504,57 +1662,27 @@
     width = enc_qkv.shape[2]
     hidden_units = enc_ff_in.shape[1]
 
-    vectors = jnp.concatenate(
-        [
-            enc_qv_bias.reshape(-1),
-            dec_self_bias.reshape(-1),
-            dec_cross_bias.reshape(-1),
-            enc_ff_in_bias,
-            dec_ff_in_bias,
-        ]
-    ).astype(F32)
-    (
-        x_all,
-        ts,
-        segments,
-        vectors,
-        enc_qkv,
-        enc_proj,
-        dec_self,
-        dec_self_proj,
-    ) = opening(
+    x_all, ts, source_keys, target_keys, vectors, enc_qkv, enc_proj, dec_self = opening(
         ring,
         source[0],
         target[0],
-        jnp.concatenate([source_segments, target_segments]),
-        vectors.reshape(-1, 128),
+        source_segments,
+        target_segments,
         (
-            enc_qkv.reshape(-1, width),
-            enc_proj,
-            dec_self.reshape(-1, width),
-            dec_self_proj,
+            enc_qv_bias,
+            dec_self_bias,
+            dec_cross_bias,
+            enc_ff_in_bias,
+            dec_ff_in_bias,
         ),
-    )
-    vectors = vectors.reshape(-1)
+        (enc_qkv, enc_proj, dec_self),
+    )
+    source_keys, target_keys = source_keys[0], target_keys[0]
     xs = lax.dynamic_slice_in_dim(x_all, first_row, count, 0)
-    dec_ff_in = place.fetch_weight(dec_ff_in)
-    dec_ff_out = place.fetch_weight(dec_ff_out)
     enc_cot = place.own_pair(enc_cotangent[0])
     dec_cot = place.own_pair(dec_cotangent[0])
-
-    marks = [0, 2 * width, 4 * width, 6 * width, 6 * width + hidden_units, 6 * width + 2 * hidden_units]
-    enc_qv_bias, dec_self_bias, dec_cross_bias, enc_ff_in_bias, dec_ff_in_bias = (
-        vectors[a:b] for a, b in zip(marks[:-1], marks[1:])
-    )
-
-    def prepared(qkv, bias):
-        b_kv = jnp.concatenate([jnp.zeros((width,), F32), bias[width:]])
-        return (qkv, bias[:width], b_kv)
-
-    enc_w = prepared(enc_qkv, enc_qv_bias)
-    self_w = prepared(dec_self, dec_self_bias)
-
-    source_keys, target_keys = segments[0], segments[1]
+    enc_b, self_b, cross_b = (vectors[k : k + 1, : 3 * width] for k in range(3))
+    enc_ff_in_bias, dec_ff_in_bias = vectors[3], vectors[4]
     source_own = lax.dynamic_slice_in_dim(source_keys, first_row, count, 0)
     target_own = lax.dynamic_slice_in_dim(target_keys, first_row, count, 0)
     source_starts, target_starts = starts_of(source_keys), starts_of(target_keys)
@@ -1562,39 +1690,46 @@
     self_mask = mask_of(target_own, target_starts, first_row, True)
     cross_mask = mask_of(target_own, source_starts, first_row, False)
 
-    queries, kv = projected(xs, x_all, enc_w)
-    output, lse, t_all, enc_ff_in, enc_ff_out = gather_attend(
-        7, ring, queries, kv, enc_mask, ts, (enc_ff_in, enc_ff_out)
-    )
+    queries, kv, output, lse, t_all, enc_ff_in, enc_ff_out = gather_attend(
+        7, ring, x_all, enc_qkv, enc_b, enc_mask, ts, (enc_ff_in, enc_ff_out)
+    )
+    dec_ff_in = place.fetch_weight(dec_ff_in + after(lse).astype(BF16))
     branch, enc_attn = attention_output(place, queries, kv, output, lse, enc_proj, enc_bias[0])
     first, enc_norm_one = norm_forward(xs.astype(F32) + branch, enc_gains[0], enc_shifts[0])
     first_low = first.astype(BF16)
-    enc_ff_in_bias = enc_ff_in_bias + after(dec_ff_in)
     branch, enc_feed = feed_forward(
         place, first_low, enc_ff_in, enc_ff_in_bias, enc_ff_out, enc_bias[1]
     )
     encoded, enc_norm_two = norm_forward(first + branch, enc_gains[1], enc_shifts[1])
     encoded_low = encoded.astype(BF16)
 
-    queries, kv = projected(ts, t_all, self_w)
-    output, lse, e_all, dec_cross, dec_cross_proj = gather_attend(
+    (
+        queries,
+        kv,
+        output,
+        lse,
+        e_all,
+        dec_self_proj,
+        dec_cross,
+        dec_cross_proj,
+    ) = gather_attend(
         2,
         ring,
-        queries,
-        kv,
+        t_all,
+        dec_self,
+        self_b,
         self_mask,
         encoded_low,
-        (dec_cross.reshape(-1, width), dec_cross_proj),
-        (dec_ff_out,),
-    )
-    cross_w = prepared(dec_cross, dec_cross_bias)
+        (dec_self_proj, dec_cross, dec_cross_proj),
+    )
+    dec_ff_out = place.fetch_weight(dec_ff_out + after(lse).astype(BF16))
     branch, self_attn = attention_output(
         place, queries, kv, output, lse, dec_self_proj, dec_bias[0]
     )
     second, dec_norm_one = norm_forward(ts.astype(F32) + branch, dec_gains[0], dec_shifts[0])
     second_low = second.astype(BF16)
-    queries, kv = projected(second_low, e_all, cross_w)
-    output, lse = attend(queries, kv, cross_mask)
+    queries, kv = projected(second_low, e_all, dec_cross, cross_b)
+    output, lse = attend(queries, kv, cross_mask, (dec_ff_in,))
     branch, cross_attn = attention_output(
         place, queries, kv, output, lse, dec_cross_proj, dec_bias[1]
     )
@@ -1626,7 +1761,7 @@
         cross_attn,
         second_low,
         e_all,
-        cross_w,
+        dec_cross,
         dec_cross_proj,
         back_mask(cross_mask),
         True,
@@ -1653,7 +1788,7 @@
         self_attn,
         ts,
         t_all,
-        self_w,
+        dec_self,
         dec_self_proj,
         back_mask(self_mask),
         False,
@@ -1661,13 +1796,14 @@
             [
                 (dec_w_in, "yvw", (0, 3, 5, 6)),
                 (dec_w_out, "xvw", (0, 3, 5, 6)),
-                (cross_kv, "x", (1, 6)),
-                (cross_q, "y", (1, 6)),
-                (cross_proj, "y", (1, 6)),
+                (cross_kv, "x", (3, 6)),
+                (cross_q, "y", (3, 6)),
+                (cross_proj, "y", (3, 6)),
             ],
         [feed_back(grad_branch, slope, enc_ff_in, enc_ff_out, first_low, active, 5)]
         if plan.kernels
         else (),
+        begins=True,
     )
     dec_w_in, dec_w_out, cross_kv, cross_q, cross_proj = given
     if plan.kernels:
@@ -1689,20 +1825,20 @@
         enc_attn,
         xs,
         x_all,
-        enc_w,
+        enc_qkv,
         enc_proj,
         back_mask(enc_mask),
         False,
         plan,
             [
-                (cross_kv, "yvw", (0, 3, 5, 6)),
-                (cross_q, "xvw", (0, 3, 5, 6)),
-                (cross_proj, "xvw", (0, 3, 5, 6)),
-                (enc_w_in, "x", (0, 6)),
-                (enc_w_out, "y", (0, 6)),
-                (self_kv, "x", (2, 6)),
-                (self_q, "y", (2, 6)),
-                (self_proj, "y", (2, 6)),
+                (cross_kv, "yvw", (0, 1, 3, 6)),
+                (cross_q, "xvw", (0, 1, 3, 6)),
+                (cross_proj, "xvw", (0, 1, 3, 6)),
+                (enc_w_in, "x", (1, 6)),
+                (enc_w_out, "y", (1, 6)),
+                (self_kv, "y", (4, 6)),
+                (self_q, "x", (4, 6)),
+                (self_proj, "x", (4, 6)),
             ],
     )
     cross_kv, cross_q, cross_proj, enc_w_in, enc_w_out, self_kv, self_q, self_proj = given
@@ -1710,15 +1846,18 @@
     grad_source = grad_hidden + source_total.astype(F32)
     enc_q, enc_proj_grad, enc_kv = enc_grads
     rest = [
-        (enc_w_in, "yvw", (0, 1, 2, 4)),
-        (enc_w_out, "xvw", (0, 1, 2, 4)),
-        (self_kv, "yvw", (0, 1, 2, 4)),
-        (self_q, "xvw", (0, 1, 2, 4)),
-        (self_proj, "xvw", (0, 1, 2, 4)),
-        (enc_kv, "xyvw", (1, 3, 4, 5, 6)),
-        (enc_q, "yxvw", (1, 3, 4, 5, 6)),
-        (enc_proj_grad, "yxvw", (1, 3, 4, 5, 6)),
+        (self_kv, "vw", (0, 1, 2)),
+        (self_q, "vw", (0, 1, 2)),
+        (self_proj, "vw", (0, 1, 2)),
+        (enc_w_in, "yvw", (0, 2, 4, 7)),
+        (enc_w_out, "xvw", (0, 2, 4, 7)),
+        (enc_kv, "xyvw", (2, 3, 5, 6, 7)),
+        (enc_q, "yxvw", (2, 3, 5, 6, 7)),
+        (enc_proj_grad, "yxvw", (2, 3, 5, 6, 7)),
     ]
+    source_low = rounded(grad_source).astype(BF16)
+    target_low = rounded(grad_target).astype(BF16)
+    rows = (source_low, place.others(source_low), target_low, place.others(target_low))
     small = small_sums(
         jnp.concatenate(
             [
@@ -1743,48 +1882,44 @@
         (0, 1, 2, 3, 4, 5),
     )
     if plan.kernels:
-        vectors, *given = run_chains(6, [small] + plan.chains(rest), 7)
-        whole, halves = vectors[: small.rows], vectors[small.rows :]
+        vectors, *given = run_chains(6, [small] + plan.chains(rest), 8)
     else:
-        whole, halves = place.all_sum(*small.vectors)
+        vectors = jnp.concatenate(place.all_sum(*small.vectors)).reshape(-1, model)
         given = [place.scatter(array, True) for array, _, _ in rest]
         dec_w_in, dec_w_out, cross_kv, cross_q, cross_proj = (
             place.scatter(array, True)
             for array in (dec_w_in, dec_w_out, cross_kv, cross_q, cross_proj)
         )
-    enc_w_in, enc_w_out, self_kv, self_q, self_proj, enc_kv, enc_q, enc_proj_grad = given
-
-    def qkv_grads(of_q, of_kv):
-        return jnp.stack([of_q, of_kv[:, :width], of_kv[:, width:]])
-
-    whole, halves = whole.reshape(-1, model), halves.reshape(-1)
-    small = [halves[a:b] for a, b in zip(marks[:-1], marks[1:])]
+    self_kv, self_q, self_proj, enc_w_in, enc_w_out, enc_kv, enc_q, enc_proj_grad = given
+
+    grads = (enc_q, enc_proj_grad, enc_kv, self_q, self_proj, self_kv, cross_q, cross_proj, cross_kv)
+    grads += (enc_w_in, enc_w_out, dec_w_in, dec_w_out)
+    flag = jnp.where(place.core == place.y, 1, 0).astype(jnp.int32).reshape(1)
+    results = closing(flag, rows, vectors, grads, (2, 2, 2, 3, 3, 3))
+    of_source, of_target, *of_matrices = results[:12]
+    of_whole, of_halves = results[12:18], results[18:]
     return (
         place.hand_out(encoded_low)[None],
         place.hand_out(decoded.astype(BF16))[None],
-        place.hand_out(rounded(grad_source).astype(BF16)).astype(F32)[None],
-        place.hand_out(rounded(grad_target).astype(BF16)).astype(F32)[None],
-        qkv_grads(enc_q, enc_kv),
-        small[0].reshape(2, width),
-        enc_proj_grad.T,
-        enc_w_in,
-        small[3],
-        enc_w_out.T,
-        whole[0:2],
-        whole[2:4],
-        whole[4:6],
-        qkv_grads(self_q, self_kv),
-        small[1].reshape(2, width),
-        self_proj.T,
-        qkv_grads(cross_q, cross_kv),
-        small[2].reshape(2, width),
-        cross_proj.T,
-        dec_w_in,
-        small[4],
-        dec_w_out.T,
-        whole[6:9],
-        whole[9:12],
-        whole[12:15],
+        of_source[None],
+        of_target[None],
+        of_matrices[0],
+        of_halves[0],
+        of_matrices[1],
+        of_matrices[6],
+        of_halves[3].reshape(-1),
+        of_matrices[7],
+        *of_whole[:3],
+        of_matrices[2],
+        of_halves[1],
+        of_matrices[3],
+        of_matrices[4],
+        of_halves[2],
+        of_matrices[5],
+        of_matrices[8],
+        of_halves[4].reshape(-1),
+        of_matrices[9],
+        *of_whole[3:],
     )
 
 

time: 574 us -> 529 us (0.922)
  matrix products: 55.1 us -> 38.1 us
  local copies, waits for them, and re-layouts: 31.2 us -> 20.5 us
  waiting for transfers between devices: 12.3 us -> 2.6 us
  starting transfers between devices: 19 us -> 10.7 us
  Pallas kernels: 398 us -> 405 us
    pallas_call x1, Pallas kernels: 58.3 us -> 41.7 us  [opening(): pl.pallas_call(functools.partial(opening_kernel, ring, number), out_shape...]
    dot_general x10 -> x6, matrix products: 31.3 us -> 16 us  [dot_plain(): return jnp.dot(left, right, preferred_element_type=F32)]
    pallas_call x1 -> x2, Pallas kernels: 4.82 us -> 19.5 us  [the longest x1 14.6 us: attend(): pl.pallas_call(functools.partial(forward_kernel, KEY_BLOCK, causal, len(t...]
    ppermute x6, waiting for transfers between devices: 9.65 us -> 0.02 us  [permute(): return lax.ppermute(value, ('dp', 'tensor'), moves)]
    pallas_call x2, Pallas kernels: 75 us -> 84.3 us  [gather_attend(): pl.pallas_call(functools.partial(gather_attend_kernel, KEY_BLOCK, causal,...]
    ppermute x8, starting transfers between devices: 12.9 us -> 4.22 us  [swap_core(): return lax.ppermute(value, 'dp', [(i, i ^ 1) for i in range(self.pairs)])]
    unnamed x191 -> x189, local copies, waits for them, and re-layouts: 15.9 us -> 14.9 us
  transfers between devices with their start and end apart: 14 -> 14, of which waited for: 4 -> 2; matrix products, arithmetic and copies ran while one was open for 18% -> 15% of each run, Pallas kernels for 64% -> 60%
where the time goes in v6:
time: 529 us; the launch traced here: 522 us
  Pallas kernels  405 us (77%)
  other arithmetic  41.7 us (8%)
  matrix products  38.1 us (7%)
  local copies, waits for them, and re-layouts  20.5 us (4%)
  starting transfers between devices  10.7 us (2%)
    pallas_call x4, Pallas kernels, run_parts(): pl.pallas_call(kernel, out_shape=[shape for p in parts for shape in p.out...  259 us
    pallas_call x2, Pallas kernels, gather_attend(): pl.pallas_call(functools.partial(gather_attend_kernel, KEY_BLOCK, causal,...  84.3 us
    pallas_call x1, Pallas kernels, opening(): pl.pallas_call(functools.partial(opening_kernel, ring, number), out_shape...  41.7 us
    dot_general x6, matrix products, dot_plain(): return jnp.dot(left, right, preferred_element_type=F32)  16 us
    unnamed x189, local copies, waits for them, and re-layouts  14.9 us
    pallas_call x1, Pallas kernels, attend(): pl.pallas_call(functools.partial(forward_kernel, KEY_BLOCK, causal, len(t...  14.6 us
    dot_general x8, matrix products, dot_last(): return lax.dot_general(left, right, NT, preferred_element_type=F32)  13.6 us
    reduce_sum x5, other arithmetic, norm_backward(): return (grad_hidden, jnp.sum(grad * normed, axis=0), jnp.sum(grad, axis=0))  11 us
  transfers between devices with their start and end apart: 14, of which 2 were waited for; matrix products, arithmetic and copies ran while one was open for 15% of the time, Pallas kernels for 60%

profile of v6, /device:TPU:1, one launch (start us, length us, event | category | flops | bytes accessed | tf_op | source)
XLA Modules:
  0.0 522.5 jit_solution(1341371832328041052)
XLA Ops:
  0.7 41.7 %shard_map.450 = (bf16[2048,768]{1,0:T(8,128)(2,1)}, bf16[512,768]{1,0:T(8,128)(2,1)}, s32[1,2048]{1,0:T(1,128)}, s32[1,2048]{1,0:T(1,128)}, f32[8,1536]{1,0:T(8...) custom-call(bf16[512,768]{1,0:T(8,128)(2,1)} %bitcast.54, ...), custom_call_target="tpu_custom_call" | custom-call | tf_op jit(solution)/shard_map/pallas_call | solution.py:660
  47.4 42.6 %shard_map.451 = (bf16[512,384]{1,0:T(8,128)(2,1)S(1)}, bf16[2048,768]{1,0:T(8,128)(2,1)}, f32[384,512]{1,0:T(8,128)S(1)}, f32[8,512]{1,0:T(8,128)S(1)}, bf16[20...) custom-call(s32[8]{0:T(128)S(1)} %convert_reduce_fusion.8.starts.refs_0_, ...), custom_call_target="tpu_custom_call" | custom-call | flops 3221225472 | bytes 6291456 | tf_op jit(solution)/shard_map/pallas_call | solution.py:737
  98.2 2.3 fusion.39
  101.2 1.8 copy-done.51
  103.0 3.6 fusion.9
  108.0 3.4 collective-permute-start.1
  117.4 41.7 %shard_map.452 = (bf16[512,384]{1,0:T(8,128)(2,1)S(1)}, bf16[2048,768]{1,0:T(8,128)(2,1)}, f32[384,512]{1,0:T(8,128)S(1)}, f32[8,512]{1,0:T(8,128)S(1)}, bf16[20...) custom-call(s32[8]{0:T(128)S(1)} %convert_reduce_fusion.7.starts.ref, ...), custom_call_target="tpu_custom_call" | custom-call | flops 3221225472 | bytes 6291456 | tf_op jit(solution)/shard_map/pallas_call | solution.py:737
  163.8 2.8 add_convert_fusion.kv_ref.refs_3_
  169.2 14.6 %shard_map.453 = (f32[384,512]{1,0:T(8,128)S(1)}, f32[8,512]{1,0:T(8,128)S(1)}) custom-call(s32[8]{0:T(128)S(1)} %convert_reduce_fusion.8.starts.refs_0_, s32[3]{0:T(128)S(1)} %pad_add_fusion.ends, s32[1,512]{1,0:T(1,128)S(1)} %constant_dynamic-slice_fusion.2.segments.refs_1_, bf16[512,384]{1,0:T(8,128)(2,1)S(1)} %fusion.23.q_ref.refs_2_, ...), custom_call_target="tpu_custom_call" | custom-call | flops 1610612736 | bytes 3145728 | tf_op jit(solution)/shard_map/pallas_call | solution.py:253
  184.8 2.3 collective-permute-done.5
  188.0 4.8 multiply_convert_fusion
  192.8 2.8 fusion.45
  198.2 2.2 fusion.35
  200.8 2.2 fusion.16
  204.8 2.6 convert_reduce_fusion
  207.4 3.2 fusion.46
  213.3 2.8 convolution_convert_fusion.refs_14_
  216.2 3.0 convolution_convert_fusion.1.refs_13_
  220.1 1.7 convert_reduce_fusion.3
  224.4 52.6 %shard_map.454 = (bf16[512,384]{1,0:T(8,128)(2,1)}, bf16[2048,768]{1,0:T(8,128)(2,1)}, bf16[512,768]{1,0:T(8,128)(2,1)}, f32[512,768]{1,0:T(8,128)}, f32[2,384]{...) custom-call(s32[8]{0:T(128)} %copy-done.26, ...), custom_call_target="tpu_custom_call" | custom-call | flops 5637144576 | bytes 11010048 | tf_op jit(solution)/shard_map/pallas_call | solution.py:786
  277.0 2.7 multiply_reduce_fusion.1
  279.8 1.7 convert_reduce_fusion.4
  284.1 2.4 multiply_reduce_fusion.2
  286.5 2.1 convert_reduce_fusion.5
  288.6 68.8 %shard_map.455 = (bf16[512,384]{1,0:T(8,128)(2,1)}, bf16[2048,768]{1,0:T(8,128)(2,1)}, bf16[512,768]{1,0:T(8,128)(2,1)}, f32[2,384]{1,0:T(2,128)}, bf16[384,384]...) custom-call(s32[8]{0:T(128)} %copy-done.24, ...), custom_call_target="tpu_custom_call" | custom-call | flops 5637144576 | bytes 11010048 | tf_op jit(solution)/shard_map/pallas_call | solution.py:786
  357.4 2.7 multiply_reduce_fusion.3
  360.1 1.7 convert_reduce_fusion.6
  364.4 61.1 %shard_map.456 = (bf16[512,384]{1,0:T(8,128)(2,1)}, bf16[2048,768]{1,0:T(8,128)(2,1)}, bf16[512,768]{1,0:T(8,128)(2,1)}, f32[2,384]{1,0:T(2,128)}, bf16[768,384]...) custom-call(s32[8]{0:T(128)} %copy-done.26, ...), custom_call_target="tpu_custom_call" | custom-call | flops 5637144576 | bytes 11010048 | tf_op jit(solution)/shard_map/pallas_call | solution.py:786
  425.6 2.3 reduce-precision_convert_fusion.1.refs_0_
  431.8 76.6 %shard_map.457 = (f32[22,768]{1,0:T(8,128)}, f32[48,768]{1,0:T(8,128)}, f32[48,384]{1,0:T(8,128)}, f32[48,384]{1,0:T(8,128)}, f32[48,1536]{1,0:T(8,128)}, /*inde...) custom-call(f32[22,768]{1,0:T(8,128)} %pad_maximum_fusion.refs_0_, ...), custom_call_target="tpu_custom_call" | custom-call | tf_op jit(solution)/shard_map/pallas_call | solution.py:786
  508.6 2.2 select_bitcast_fusion
  511.8 5.0 shard_map.458
  (295 shorter events, 54.0 us)
Async XLA Ops:
  43.2 126.0 %copy-start.26 = (s32[8]{0:T(128)}, s32[8]{0:T(128)S(1)}, u32[]{:S(2)}) copy-start(s32[8]{0:T(128)S(1)} %convert_reduce_fusion.8.starts.refs_0_) | copy-start | bytes 100
  43.9 46.1 %copy-start.25 = (s32[1,512]{1,0:T(1,128)}, s32[1,512]{1,0:T(1,128)S(1)}, u32[]{:S(2)}) copy-start(s32[1,512]{1,0:T(1,128)S(1)} %constant_dynamic-slice_fusion.3.segments.refs_1_) | copy-start | bytes 6148
  93.0 5.2 collective-permute-start
  95.9 73.3 %collective-permute-start.4 = (bf16[768,1536]{1,0:T(8,128)(2,1)}, bf16[768,1536]{1,0:T(8,128)(2,1)}, u32[]{:S(2)}, u32[]{:S(2)}) collective-permute-start(bf16[768,1536]{1,0:T(8,128)(2,1)} %broadcast_add_fusion.1), channel_id=1, source_target_pairs={{8,0},{9,1},{1,8},{0,9},{24,16},{25,17},{17,24},{16,25},{10,2},{11... | collective-permute-start | bytes 7077896 | tf_op jit(solution)/shard_map/ppermute | solution.py:1474
  100.5 14.1 %copy-start.37 = (f32[512,768]{1,0:T(8,128)}, f32[512,768]{1,0:T(8,128)S(1)}, u32[]{:S(2)}) copy-start(f32[512,768]{1,0:T(8,128)S(1)} %get-tuple-element.324) | copy-start | bytes 4718596
  101.2 5.4 %copy-start.45 = (bf16[512,768]{1,0:T(8,128)(2,1)}, bf16[512,768]{1,0:T(8,128)(2,1)S(1)}, u32[]{:S(2)}) copy-start(bf16[512,768]{1,0:T(8,128)(2,1)S(1)} %fusion.17.refs_19_) | copy-start | bytes 2359300
  106.6 7.9 %copy-start.66 = (bf16[3,768]{1,0:T(4,128)(2,1)S(1)}, bf16[3,768]{1,0:T(4,128)(2,1)}, u32[]{:S(2)}) copy-start(bf16[3,768]{1,0:T(4,128)(2,1)} %param.49) | copy-start | bytes 13828
  106.6 7.9 %copy-start.67 = (bf16[3,768]{1,0:T(4,128)(2,1)S(1)}, bf16[3,768]{1,0:T(4,128)(2,1)}, u32[]{:S(2)}) copy-start(bf16[3,768]{1,0:T(4,128)(2,1)} %param.51) | copy-start | bytes 13828
  106.6 7.9 %copy-start.68 = (bf16[3,768]{1,0:T(4,128)(2,1)S(1)}, bf16[3,768]{1,0:T(4,128)(2,1)}, u32[]{:S(2)}) copy-start(bf16[3,768]{1,0:T(4,128)(2,1)} %param.50) | copy-start | bytes 13828
  108.0 6.6 %collective-permute-start.1 = (bf16[512,768]{1,0:T(8,128)(2,1)S(1)}, bf16[512,768]{1,0:T(8,128)(2,1)S(1)}, u32[]{:S(2)}, u32[]{:S(2)}) collective-permute-start(bf16[512,768]{1,0:T(8,128)(2,1)S(1)} %get-tuple-element.335), channel_id=1, source_target_pairs={{0,8},{8,0},{16,24},{24,16},{1,9},{9,1},{17,25},{25,17},{2,10},{10... | collective-permute-start | bytes 2359304 | tf_op jit(solution)/shard_map/ppermute | solution.py:1450
  112.9 56.3 %copy-start.23 = (s32[1,512]{1,0:T(1,128)}, s32[1,512]{1,0:T(1,128)S(1)}, u32[]{:S(2)}) copy-start(s32[1,512]{1,0:T(1,128)S(1)} %constant_dynamic-slice_fusion.2.segments.refs_1_) | copy-start | bytes 6148
  160.5 6.2 %collective-permute-start.3 = (bf16[512,768]{1,0:T(8,128)(2,1)S(1)}, bf16[512,768]{1,0:T(8,128)(2,1)S(1)}, u32[]{:S(2)}, u32[]{:S(2)}) collective-permute-start(bf16[512,768]{1,0:T(8,128)(2,1)S(1)} %get-tuple-element.337), channel_id=1, source_target_pairs={{0,8},{8,0},{16,24},{24,16},{1,9},{9,1},{17,25},{25,17},{2,10},{10... | collective-permute-start | bytes 2359304 | tf_op jit(solution)/shard_map/ppermute | solution.py:1450
  162.4 30.4 %collective-permute-start.6 = (bf16[1536,768]{1,0:T(8,128)(2,1)S(1)}, bf16[1536,768]{1,0:T(8,128)(2,1)S(1)}, u32[]{:S(2)}, u32[]{:S(2)}) collective-permute-start(bf16[1536,768]{1,0:T(8,128)(2,1)S(1)} %broadcast_add_fusion), channel_id=1, source_target_pairs={{8,0},{9,1},{1,8},{0,9},{24,16},{25,17},{17,24},{16,25},{10,2},{11... | collective-permute-start | bytes 7077896 | tf_op jit(solution)/shard_map/ppermute | solution.py:1474
  167.0 20.0 %copy-start.35 = (f32[512,768]{1,0:T(8,128)}, f32[512,768]{1,0:T(8,128)S(1)}, u32[]{:S(2)}) copy-start(f32[512,768]{1,0:T(8,128)S(1)} %get-tuple-element.320) | copy-start | bytes 4718596
  169.2 14.6 %copy-start.32 = (bf16[512,384]{1,0:T(8,128)(2,1)}, bf16[512,384]{1,0:T(8,128)(2,1)S(1)}, u32[]{:S(2)}) copy-start(bf16[512,384]{1,0:T(8,128)(2,1)S(1)} %fusion.23.q_ref.refs_2_) | copy-start | bytes 1179652
  184.8 2.3 collective-permute-start.5
  195.6 2.6 collective-permute-start.7
  195.8 5.1 collective-permute-start.10
  196.1 87.9 %collective-permute-start.9 = (bf16[512,768]{1,0:T(8,128)(2,1)}, bf16[512,768]{1,0:T(8,128)(2,1)}, u32[]{:S(2)}, u32[]{:S(2)}) collective-permute-start(bf16[512,768]{1,0:T(8,128)(2,1)} %bitcast.12), channel_id=1, source_target_pairs={{0,8},{8,0},{16,24},{24,16},{1,9},{9,1},{17,25},{25,17},{2,10},{10... | collective-permute-start | bytes 2359304 | tf_op jit(solution)/shard_map/ppermute | solution.py:1450
  196.3 14.5 %collective-permute-start.2 = (bf16[512,768]{1,0:T(8,128)(2,1)}, bf16[512,768]{1,0:T(8,128)(2,1)S(1)}, u32[]{:S(2)}, u32[]{:S(2)}) collective-permute-start(bf16[512,768]{1,0:T(8,128)(2,1)} %add_convert_fusion.2.own_ref), channel_id=1, source_target_pairs={{0,1},{9,8},{16,17},{25,24},{2,3},{11,10},{18,19},{27,26},{4,5},{1... | collective-permute-start | bytes 2359304 | tf_op jit(solution)/shard_map/ppermute | solution.py:1474
  200.8 3.8 copy-start.81
  210.6 8.5 %collective-permute-start.11 = (bf16[512,768]{1,0:T(8,128)(2,1)S(1)}, bf16[512,768]{1,0:T(8,128)(2,1)S(1)}, u32[]{:S(2)}, u32[]{:S(2)}) collective-permute-start(bf16[512,768]{1,0:T(8,128)(2,1)S(1)} %get-tuple-element.345), channel_id=1, source_target_pairs={{0,8},{8,0},{16,24},{24,16},{1,9},{9,1},{17,25},{25,17},{2,10},{10... | collective-permute-start | bytes 2359304 | tf_op jit(solution)/shard_map/ppermute | solution.py:1450
  212.0 296.5 %collective-permute-start.8 = (bf16[512,768]{1,0:T(8,128)(2,1)}, bf16[512,768]{1,0:T(8,128)(2,1)}, u32[]{:S(2)}, u32[]{:S(2)}) collective-permute-start(bf16[512,768]{1,0:T(8,128)(2,1)} %get-tuple-element.328), channel_id=1, source_target_pairs={{0,1},{9,8},{16,17},{25,24},{2,3},{11,10},{18,19},{27,26},{4,5},{1... | collective-permute-start | bytes 2359304 | tf_op jit(solution)/shard_map/ppermute | solution.py:1474
  224.4 52.6 %copy-start.36 = (f32[512,768]{1,0:T(8,128)S(1)}, f32[512,768]{1,0:T(8,128)}, u32[]{:S(2)}) copy-start(f32[512,768]{1,0:T(8,128)} %copy-done.35) | copy-start | bytes 4718596
  288.6 68.8 %copy-start.38 = (f32[512,768]{1,0:T(8,128)S(1)}, f32[512,768]{1,0:T(8,128)}, u32[]{:S(2)}) copy-start(f32[512,768]{1,0:T(8,128)} %copy-done.37) | copy-start | bytes 4718596
  364.4 61.2 %copy-start.43 = (f32[512,768]{1,0:T(8,128)S(1)}, f32[512,768]{1,0:T(8,128)}, u32[]{:S(2)}) copy-start(f32[512,768]{1,0:T(8,128)} %get-tuple-element.309) | copy-start | bytes 4718596
  425.6 3.6 copy-start.42
  425.6 3.6 copy-start.59
  427.9 82.9 %collective-permute-start.12 = (bf16[512,768]{1,0:T(8,128)(2,1)}, bf16[512,768]{1,0:T(8,128)(2,1)S(1)}, u32[]{:S(2)}, u32[]{:S(2)}) collective-permute-start(bf16[512,768]{1,0:T(8,128)(2,1)} %reduce-precision_convert_fusion.1.refs_0_), channel_id=1, source_target_pairs={{0,1},{9,8},{16,17},{25,24},{2,3},{11,10},{18,19},{27,26},{4,5},{1... | collective-permute-start | bytes 2359304 | tf_op jit(solution)/shard_map/ppermute | solution.py:1474
  429.5 79.0 %copy-start.47 = (bf16[512,768]{1,0:T(8,128)(2,1)}, bf16[512,768]{1,0:T(8,128)(2,1)S(1)}, u32[]{:S(2)}) copy-start(bf16[512,768]{1,0:T(8,128)(2,1)S(1)} %reduce-precision_convert_fusion.refs_2_) | copy-start | bytes 2359300
  429.5 81.4 %collective-permute-start.13 = (bf16[512,768]{1,0:T(8,128)(2,1)S(1)}, bf16[512,768]{1,0:T(8,128)(2,1)}, u32[]{:S(2)}, u32[]{:S(2)}) collective-permute-start(bf16[512,768]{1,0:T(8,128)(2,1)S(1)} %reduce-precision_convert_fusion.refs_2_), channel_id=1, source_target_pairs={{0,1},{9,8},{16,17},{25,24},{2,3},{11,10},{18,19},{27,26},{4,5},{1... | collective-permute-start | bytes 2359304 | tf_op jit(solution)/shard_map/ppermute | solution.py:1474
  516.8 4.4 copy-start.57
  (65 other events, 154.4 us)

commit v7 on v6

--- a/solution.py
+++ b/solution.py
@@ -927,39 +927,46 @@
 
 
 def closing_kernel(flag, *refs):
-    own_source, other_source, own_target, other_target, vectors = refs[:5]
-    grads, outputs = refs[5:18], refs[18:]
+    given, outputs, held, copied = refs[:22], refs[22:47], refs[47:69], refs[69]
+    copies = [
+        pltpu.make_async_copy(start, end, copied.at[k])
+        for k, (start, end) in enumerate(zip(given, held))
+    ]
+    for copy in copies:
+        copy.start()
+    for copy in copies:
+        copy.wait()
+    rows, vectors, grads = held[:8], held[8], held[9:22]
     keeps = flag[0] == 1
-    for own, other, out in (
-        (own_source, other_source, outputs[0]),
-        (own_target, other_target, outputs[1]),
-    ):
-        out[...] = jnp.where(keeps, own[...], other[...]).astype(F32)
+    for k in range(4):
+        own, other = rows[2 * k][...], rows[2 * k + 1][...]
+        outputs[k][...] = jnp.where(keeps, own, other).astype(outputs[k].dtype)
     for k in range(3):
-        of_q, of_out, of_kv = grads[3 * k : 3 * k + 3]
-        qkv, out = outputs[2 + 2 * k : 4 + 2 * k]
+        of_q, of_kv = grads[3 * k], grads[3 * k + 2]
+        qkv = outputs[4 + k]
         width = of_q.shape[1]
         qkv[0] = of_q[...]
         qkv[1] = of_kv[:, :width]
         qkv[2] = of_kv[:, width:]
-        out[...] = of_out[...].T
+    outputs[7][...] = grads[9][...]
+    outputs[8][...] = grads[11][...]
+    for k in range(3):
+        outputs[9 + k][...] = grads[3 * k + 1][...]
     for k in range(2):
-        of_in, of_out = grads[9 + 2 * k : 11 + 2 * k]
-        outputs[8 + 2 * k][...] = of_in[...]
-        outputs[9 + 2 * k][...] = of_out[...].T
+        outputs[12 + k][...] = grads[10 + 2 * k][...]
     row = 0
-    for out in outputs[12:18]:
+    for out in outputs[14:20]:
         out[...] = vectors[row : row + out.shape[0], :]
         row += out.shape[0]
-    for out in outputs[18:21]:
+    for out in outputs[20:23]:
         width = out.shape[1]
         out[0:1, :] = vectors[row : row + 1, :width]
         out[1:2, :] = vectors[row : row + 1, width:]
         row += 1
-    for out in outputs[21:]:
-        for part in range(out.shape[1] // vectors.shape[1]):
-            span = slice(part * vectors.shape[1], (part + 1) * vectors.shape[1])
-            out[:, span] = vectors[row : row + 1, :]
+    columns = vectors.shape[1]
+    for out in outputs[23:]:
+        for part in range(out.shape[0] // columns):
+            out[part * columns : (part + 1) * columns] = vectors[row, :]
             row += 1
 
 
@@ -967,17 +974,50 @@
     part, width = grads[0].shape
     units = grads[9].shape[1]
     model = vectors.shape[1]
-    shapes = [rows[0].shape] * 2
-    shapes += [(3, part, width), (width, part)] * 3 + [(part, units), (units, part)] * 2
-    shapes += [(size, model) for size in sizes] + [(2, width)] * 3 + [(1, units)] * 2
+    shapes = [(rows[0].shape, BF16)] * 2 + [(rows[0].shape, F32)] * 2
+    matrices = [(3, part, width)] * 3 + [(part, units)] * 2 + [(part, width)] * 3 + [(part, units)] * 2
+    matrices += [(size, model) for size in sizes] + [(2, width)] * 3 + [(units,)] * 2
+    shapes += [(shape, F32) for shape in matrices]
     inputs = (flag, *rows, vectors, *grads)
     return pl.pallas_call(
         closing_kernel,
-        out_shape=[jax.ShapeDtypeStruct(shape, F32) for shape in shapes],
-        in_specs=[SCALARS] + [VECTORS] * (len(inputs) - 1),
+        out_shape=[jax.ShapeDtypeStruct(*shape) for shape in shapes],
+        in_specs=[SCALARS] + [ANYWHERE] * (len(inputs) - 1),
         out_specs=[VECTORS] * len(shapes),
-        compiler_params=pltpu.CompilerParams(vmem_limit_bytes=50 << 20),
+        scratch_shapes=[pltpu.VMEM(value.shape, value.dtype) for value in inputs[1:]]
+        + [DMA((len(inputs) - 1,))],
+        compiler_params=pltpu.CompilerParams(vmem_limit_bytes=62 << 20),
     )(*inputs)
+
+
+class HandOut:
+    def __init__(self, here, inputs, outputs, scratch, times):
+        self.here, self.times = here, times
+        self.sent, self.got = scratch
+        self.copies = [
+            remote(given, taken, self.sent.at[k], self.got.at[k], here.over_y)
+            for k, (given, taken) in enumerate(zip(inputs, outputs))
+        ]
+
+    def event(self, time):
+        owns = self.here.core == self.here.y
+        for copy in self.copies:
+            if time == self.times[0]:
+                pl.when(owns)(copy.start)
+            if time == self.times[1]:
+                pl.when(owns)(copy.wait_send)
+                pl.when(jnp.logical_not(owns))(copy.wait_recv)
+
+
+def hand_out(rows, times):
+    number = len(rows)
+    return Part(
+        tuple(rows),
+        [VECTORS] * number,
+        [jax.ShapeDtypeStruct(value.shape, value.dtype) for value in rows],
+        [DMA((number,))] * 2,
+        lambda here, *refs: HandOut(here, *refs, times),
+    )
 
 
 class Small:
@@ -1065,7 +1105,7 @@
             for one in bound:
                 one.event(time)
 
-    return [given[0] for given in run_parts(number, body, chains)]
+    return run_parts(number, body, chains)
 
 
 class Back:
@@ -1482,9 +1522,6 @@
 
     def own_pair(self, rows):
         return jnp.where(self.core == self.y, rows, self.swap_core(rows))
-
-    def hand_out(self, rows):
-        return jnp.where(self.core == self.y, rows, self.others(rows))
 
     def others(self, rows):
         return self.permute(rows, lambda d, y: (d, 1 - y) if d % 2 != y else None)
@@ -1857,7 +1894,7 @@
     ]
     source_low = rounded(grad_source).astype(BF16)
     target_low = rounded(grad_target).astype(BF16)
-    rows = (source_low, place.others(source_low), target_low, place.others(target_low))
+    decoded_low = decoded.astype(BF16)
     small = small_sums(
         jnp.concatenate(
             [
@@ -1882,9 +1919,13 @@
         (0, 1, 2, 3, 4, 5),
     )
     if plan.kernels:
-        vectors, *given = run_chains(6, [small] + plan.chains(rest), 8)
+        (vectors,), (source_other, target_other), *given = run_chains(
+            6, [small, hand_out((source_low, target_low), (4, 7))] + plan.chains(rest), 8
+        )
+        given = [results[0] for results in given]
     else:
         vectors = jnp.concatenate(place.all_sum(*small.vectors)).reshape(-1, model)
+        source_other, target_other = place.others(source_low), place.others(target_low)
         given = [place.scatter(array, True) for array, _, _ in rest]
         dec_w_in, dec_w_out, cross_kv, cross_q, cross_proj = (
             place.scatter(array, True)
@@ -1895,30 +1936,38 @@
     grads = (enc_q, enc_proj_grad, enc_kv, self_q, self_proj, self_kv, cross_q, cross_proj, cross_kv)
     grads += (enc_w_in, enc_w_out, dec_w_in, dec_w_out)
     flag = jnp.where(place.core == place.y, 1, 0).astype(jnp.int32).reshape(1)
+    rows = (
+        encoded_low,
+        place.others(encoded_low),
+        decoded_low,
+        place.others(decoded_low),
+        source_low,
+        source_other,
+        target_low,
+        target_other,
+    )
     results = closing(flag, rows, vectors, grads, (2, 2, 2, 3, 3, 3))
-    of_source, of_target, *of_matrices = results[:12]
-    of_whole, of_halves = results[12:18], results[18:]
+    of_rows, of_qkv, of_in = [value[None] for value in results[:4]], results[4:7], results[7:9]
+    of_out, of_ff_out = [value.T for value in results[9:12]], [value.T for value in results[12:14]]
+    of_whole, of_qv_bias, of_in_bias = results[14:20], results[20:23], results[23:]
     return (
-        place.hand_out(encoded_low)[None],
-        place.hand_out(decoded.astype(BF16))[None],
-        of_source[None],
-        of_target[None],
-        of_matrices[0],
-        of_halves[0],
-        of_matrices[1],
-        of_matrices[6],
-        of_halves[3].reshape(-1),
-        of_matrices[7],
+        *of_rows,
+        of_qkv[0],
+        of_qv_bias[0],
+        of_out[0],
+        of_in[0],
+        of_in_bias[0],
+        of_ff_out[0],
         *of_whole[:3],
-        of_matrices[2],
-        of_halves[1],
-        of_matrices[3],
-        of_matrices[4],
-        of_halves[2],
-        of_matrices[5],
-        of_matrices[8],
-        of_halves[4].reshape(-1),
-        of_matrices[9],
+        of_qkv[1],
+        of_qv_bias[1],
+        of_out[1],
+        of_qkv[2],
+        of_qv_bias[2],
+        of_out[2],
+        of_in[1],
+        of_in_bias[1],
+        of_ff_out[1],
         *of_whole[3:],
     )
 

time: 529 us -> 516 us (0.975)
  Pallas kernels: 405 us -> 388 us
  waiting for transfers between devices: 2.6 us -> 13.1 us
    pallas_call x1, Pallas kernels: 14.6 us -> 4.35 us  [attend(): pl.pallas_call(functools.partial(forward_kernel, KEY_BLOCK, causal, len(t...]
    ppermute x6 -> x4, waiting for transfers between devices: 0.02 us -> 8.59 us  [permute(): return lax.ppermute(value, ('dp', 'tensor'), moves)]
    pallas_call x4, Pallas kernels: 259 us -> 251 us  [run_parts(): pl.pallas_call(kernel, out_shape=[shape for p in parts for shape in p.out...]
    unnamed x189 -> x154, local copies, waits for them, and re-layouts: 14.9 us -> 9.34 us
  transfers between devices with their start and end apart: 14 -> 12, of which waited for: 2 -> 3; matrix products, arithmetic and copies ran while one was open for 15% -> 13% of each run, Pallas kernels for 60% -> 58%
where the time goes in v7:
time: 516 us; the launch traced here: 509 us
  Pallas kernels  388 us (75%)
  matrix products  42 us (8%)
  other arithmetic  37.9 us (7%)
  local copies, waits for them, and re-layouts  15.6 us (3%)
  waiting for transfers between devices  13.1 us (3%)
  starting transfers between devices  8.85 us (2%)
    pallas_call x4, Pallas kernels, run_parts(): pl.pallas_call(kernel, out_shape=[shape for p in parts for shape in p.out...  251 us
    pallas_call x2, Pallas kernels, gather_attend(): pl.pallas_call(functools.partial(gather_attend_kernel, KEY_BLOCK, causal,...  84.2 us
    pallas_call x1, Pallas kernels, opening(): pl.pallas_call(functools.partial(opening_kernel, ring, number), out_shape...  41.7 us
    dot_general x6, matrix products, dot_plain(): return jnp.dot(left, right, preferred_element_type=F32)  16.1 us
    dot_general x8, matrix products, dot_last(): return lax.dot_general(left, right, NT, preferred_element_type=F32)  15.5 us
    reduce_sum x5, other arithmetic, norm_backward(): return (grad_hidden, jnp.sum(grad * normed, axis=0), jnp.sum(grad, axis=0))  11 us
    dot_general x5, matrix products, dot_first(): return lax.dot_general(left, right, TN, preferred_element_type=F32)  10.4 us
  transfers between devices with their start and end apart: 12, of which 3 were waited for; matrix products, arithmetic and copies ran while one was open for 13% of the time, Pallas kernels for 58%

profile of v7, /device:TPU:1, one launch (start us, length us, event | category | flops | bytes accessed | tf_op | source)
XLA Modules:
  0.0 509.2 jit_solution(8636667855318922457)
XLA Ops:
  0.7 41.7 %shard_map.450 = (bf16[2048,768]{1,0:T(8,128)(2,1)}, bf16[512,768]{1,0:T(8,128)(2,1)}, s32[1,2048]{1,0:T(1,128)}, s32[1,2048]{1,0:T(1,128)}, f32[8,1536]{1,0:T(8...) custom-call(bf16[512,768]{1,0:T(8,128)(2,1)} %bitcast.57, ...), custom_call_target="tpu_custom_call" | custom-call | tf_op jit(solution)/shard_map/pallas_call | solution.py:660
  47.4 42.6 %shard_map.451 = (bf16[512,384]{1,0:T(8,128)(2,1)S(1)}, bf16[2048,768]{1,0:T(8,128)(2,1)}, f32[384,512]{1,0:T(8,128)S(1)}, f32[8,512]{1,0:T(8,128)S(1)}, bf16[20...) custom-call(s32[8]{0:T(128)S(1)} %convert_reduce_fusion.8.starts.refs_0_, ...), custom_call_target="tpu_custom_call" | custom-call | flops 3221225472 | bytes 6291456 | tf_op jit(solution)/shard_map/pallas_call | solution.py:737
  98.3 2.3 fusion.39
  101.3 1.8 copy-done.37
  103.2 3.6 fusion.9
  108.2 3.5 collective-permute-start.1
  117.6 41.6 %shard_map.452 = (bf16[512,384]{1,0:T(8,128)(2,1)S(1)}, bf16[2048,768]{1,0:T(8,128)(2,1)}, f32[384,512]{1,0:T(8,128)S(1)}, f32[8,512]{1,0:T(8,128)S(1)}, bf16[20...) custom-call(s32[8]{0:T(128)S(1)} %convert_reduce_fusion.7.starts.ref, ...), custom_call_target="tpu_custom_call" | custom-call | flops 3221225472 | bytes 6291456 | tf_op jit(solution)/shard_map/pallas_call | solution.py:737
  163.9 2.9 add_convert_fusion.kv_ref.refs_3_
  169.2 4.3 shard_map.453
  174.8 2.0 collective-permute-done.5
  177.8 4.9 multiply_convert_fusion
  182.8 8.6 %collective-permute-done.6 = bf16[1536,768]{1,0:T(8,128)(2,1)S(1)} collective-permute-done((bf16[1536,768]{1,0:T(8,128)(2,1)S(1)}, bf16[1536,768]{1,0:T(8,128)(2,1)S(1)}, u32[]{:S(2)}, u32[]{:S(2)}) %collective-permute-start.6) | collective-permute-done | bytes 2359328 | tf_op jit(solution)/shard_map/ppermute | solution.py:1514
  191.4 2.8 fusion.45
  194.7 2.4 collective-permute-done.7
  197.1 2.2 fusion.35
  199.7 2.2 fusion.16
  203.6 2.6 convert_reduce_fusion
  206.3 5.1 fusion.46
  214.6 4.7 convolution_convert_fusion.refs_14_
  219.3 3.1 convolution_convert_fusion.1.refs_13_
  227.6 54.9 %shard_map.454 = (bf16[512,384]{1,0:T(8,128)(2,1)}, bf16[2048,768]{1,0:T(8,128)(2,1)}, bf16[512,768]{1,0:T(8,128)(2,1)}, f32[512,768]{1,0:T(8,128)}, f32[2,384]{...) custom-call(s32[8]{0:T(128)} %copy-done.12, ...), custom_call_target="tpu_custom_call" | custom-call | flops 5637144576 | bytes 11010048 | tf_op jit(solution)/shard_map/pallas_call | solution.py:786
  282.5 2.7 multiply_reduce_fusion.1
  285.3 1.7 convert_reduce_fusion.4
  289.6 2.4 multiply_reduce_fusion.2
  292.1 2.0 convert_reduce_fusion.5
  294.1 67.6 %shard_map.455 = (bf16[512,384]{1,0:T(8,128)(2,1)}, bf16[2048,768]{1,0:T(8,128)(2,1)}, bf16[512,768]{1,0:T(8,128)(2,1)}, f32[2,384]{1,0:T(2,128)}, bf16[384,384]...) custom-call(s32[8]{0:T(128)} %copy-done.10, ...), custom_call_target="tpu_custom_call" | custom-call | flops 5637144576 | bytes 11010048 | tf_op jit(solution)/shard_map/pallas_call | solution.py:786
  361.8 2.7 multiply_reduce_fusion.3
  364.5 1.7 convert_reduce_fusion.6
  369.1 62.4 %shard_map.456 = (bf16[512,384]{1,0:T(8,128)(2,1)}, bf16[2048,768]{1,0:T(8,128)(2,1)}, bf16[512,768]{1,0:T(8,128)(2,1)}, f32[2,384]{1,0:T(2,128)}, bf16[768,384]...) custom-call(s32[8]{0:T(128)} %copy-done.12, ...), custom_call_target="tpu_custom_call" | custom-call | flops 5637144576 | bytes 11010048 | tf_op jit(solution)/shard_map/pallas_call | solution.py:786
  433.0 2.3 reduce-precision_convert_fusion.refs_2_.refs_6_
  436.4 66.1 %shard_map.457 = (f32[22,768]{1,0:T(8,128)}, bf16[512,768]{1,0:T(8,128)(2,1)}, bf16[512,768]{1,0:T(8,128)(2,1)}, f32[48,768]{1,0:T(8,128)}, f32[48,384]{1,0:T(8,...) custom-call(f32[22,768]{1,0:T(8,128)} %pad_maximum_fusion.refs_0_, ...), custom_call_target="tpu_custom_call" | custom-call | tf_op jit(solution)/shard_map/pallas_call | solution.py:786
  502.5 6.5 %shard_map.458 = (bf16[512,768]{1,0:T(8,128)(2,1)}, bf16[512,768]{1,0:T(8,128)(2,1)}, f32[512,768]{1,0:T(8,128)}, f32[512,768]{1,0:T(8,128)}, f32[3,48,384]{2,1,...) custom-call(s32[1]{0:T(128)} %bitcast.flag, ...), custom_call_target="tpu_custom_call" | custom-call | tf_op jit(solution)/shard_map/pallas_call | solution.py:982
  (252 shorter events, 47.1 us)
Async XLA Ops:
  43.9 46.0 %copy-start.11 = (s32[1,512]{1,0:T(1,128)}, s32[1,512]{1,0:T(1,128)S(1)}, u32[]{:S(2)}) copy-start(s32[1,512]{1,0:T(1,128)S(1)} %constant_dynamic-slice_fusion.3.segments.refs_1_) | copy-start | bytes 6148
  44.8 124.4 %copy-start.12 = (s32[8]{0:T(128)}, s32[8]{0:T(128)S(1)}, u32[]{:S(2)}) copy-start(s32[8]{0:T(128)S(1)} %convert_reduce_fusion.8.starts.refs_0_) | copy-start | bytes 100
  93.0 5.3 %collective-permute-start = (bf16[512,768]{1,0:T(8,128)(2,1)}, bf16[512,768]{1,0:T(8,128)(2,1)S(1)}, u32[]{:S(2)}, u32[]{:S(2)}) collective-permute-start(bf16[512,768]{1,0:T(8,128)(2,1)} %get-tuple-element.291), channel_id=1, source_target_pairs={{0,8},{8,0},{16,24},{24,16},{1,9},{9,1},{17,25},{25,17},{2,10},{10... | collective-permute-start | bytes 2359304 | tf_op jit(solution)/shard_map/ppermute | solution.py:1490
  95.9 73.2 %collective-permute-start.4 = (bf16[768,1536]{1,0:T(8,128)(2,1)}, bf16[768,1536]{1,0:T(8,128)(2,1)}, u32[]{:S(2)}, u32[]{:S(2)}) collective-permute-start(bf16[768,1536]{1,0:T(8,128)(2,1)} %broadcast_add_fusion.1), channel_id=1, source_target_pairs={{8,0},{9,1},{1,8},{0,9},{24,16},{25,17},{17,24},{16,25},{10,2},{11... | collective-permute-start | bytes 7077896 | tf_op jit(solution)/shard_map/ppermute | solution.py:1514
  100.7 14.1 %copy-start.23 = (f32[512,768]{1,0:T(8,128)}, f32[512,768]{1,0:T(8,128)S(1)}, u32[]{:S(2)}) copy-start(f32[512,768]{1,0:T(8,128)S(1)} %get-tuple-element.282) | copy-start | bytes 4718596
  101.3 5.4 %copy-start.32 = (bf16[512,768]{1,0:T(8,128)(2,1)}, bf16[512,768]{1,0:T(8,128)(2,1)S(1)}, u32[]{:S(2)}) copy-start(bf16[512,768]{1,0:T(8,128)(2,1)S(1)} %fusion.17.refs_19_) | copy-start | bytes 2359300
  106.8 7.9 %copy-start.51 = (bf16[3,768]{1,0:T(4,128)(2,1)S(1)}, bf16[3,768]{1,0:T(4,128)(2,1)}, u32[]{:S(2)}) copy-start(bf16[3,768]{1,0:T(4,128)(2,1)} %param.49) | copy-start | bytes 13828
  106.8 7.9 %copy-start.52 = (bf16[3,768]{1,0:T(4,128)(2,1)S(1)}, bf16[3,768]{1,0:T(4,128)(2,1)}, u32[]{:S(2)}) copy-start(bf16[3,768]{1,0:T(4,128)(2,1)} %param.51) | copy-start | bytes 13828
  106.8 7.9 %copy-start.53 = (bf16[3,768]{1,0:T(4,128)(2,1)S(1)}, bf16[3,768]{1,0:T(4,128)(2,1)}, u32[]{:S(2)}) copy-start(bf16[3,768]{1,0:T(4,128)(2,1)} %param.50) | copy-start | bytes 13828
  108.2 6.6 %collective-permute-start.1 = (bf16[512,768]{1,0:T(8,128)(2,1)S(1)}, bf16[512,768]{1,0:T(8,128)(2,1)S(1)}, u32[]{:S(2)}, u32[]{:S(2)}) collective-permute-start(bf16[512,768]{1,0:T(8,128)(2,1)S(1)} %get-tuple-element.293), channel_id=1, source_target_pairs={{0,8},{8,0},{16,24},{24,16},{1,9},{9,1},{17,25},{25,17},{2,10},{10... | collective-permute-start | bytes 2359304 | tf_op jit(solution)/shard_map/ppermute | solution.py:1490
  113.0 56.1 %copy-start.9 = (s32[1,512]{1,0:T(1,128)}, s32[1,512]{1,0:T(1,128)S(1)}, u32[]{:S(2)}) copy-start(s32[1,512]{1,0:T(1,128)S(1)} %constant_dynamic-slice_fusion.2.segments.refs_1_) | copy-start | bytes 6148
  160.6 6.2 %collective-permute-start.3 = (bf16[512,768]{1,0:T(8,128)(2,1)S(1)}, bf16[512,768]{1,0:T(8,128)(2,1)S(1)}, u32[]{:S(2)}, u32[]{:S(2)}) collective-permute-start(bf16[512,768]{1,0:T(8,128)(2,1)S(1)} %get-tuple-element.295), channel_id=1, source_target_pairs={{0,8},{8,0},{16,24},{24,16},{1,9},{9,1},{17,25},{25,17},{2,10},{10... | collective-permute-start | bytes 2359304 | tf_op jit(solution)/shard_map/ppermute | solution.py:1490
  162.5 28.8 %collective-permute-start.6 = (bf16[1536,768]{1,0:T(8,128)(2,1)S(1)}, bf16[1536,768]{1,0:T(8,128)(2,1)S(1)}, u32[]{:S(2)}, u32[]{:S(2)}) collective-permute-start(bf16[1536,768]{1,0:T(8,128)(2,1)S(1)} %broadcast_add_fusion), channel_id=1, source_target_pairs={{8,0},{9,1},{1,8},{0,9},{24,16},{25,17},{17,24},{16,25},{10,2},{11... | collective-permute-start | bytes 7077896 | tf_op jit(solution)/shard_map/ppermute | solution.py:1514
  167.2 9.7 %copy-start.21 = (f32[512,768]{1,0:T(8,128)}, f32[512,768]{1,0:T(8,128)S(1)}, u32[]{:S(2)}) copy-start(f32[512,768]{1,0:T(8,128)S(1)} %get-tuple-element.278) | copy-start | bytes 4718596
  169.1 4.4 copy-start.18
  174.6 2.3 collective-permute-start.5
  182.8 11.4 %copy-start.63 = (bf16[512,1536]{1,0:T(8,128)(2,1)}, bf16[512,1536]{1,0:T(8,128)(2,1)S(1)}, u32[]{:S(2)}) copy-start(bf16[512,1536]{1,0:T(8,128)(2,1)S(1)} %get-tuple-element.299) | copy-start | bytes 4718596
  194.2 2.9 collective-permute-start.7
  194.2 5.5 %collective-permute-start.10 = (bf16[512,768]{1,0:T(8,128)(2,1)S(1)}, bf16[512,768]{1,0:T(8,128)(2,1)}, u32[]{:S(2)}, u32[]{:S(2)}) collective-permute-start(bf16[512,768]{1,0:T(8,128)(2,1)S(1)} %bitcast.59), channel_id=1, source_target_pairs={{0,8},{8,0},{16,24},{24,16},{1,9},{9,1},{17,25},{25,17},{2,10},{10... | collective-permute-start | bytes 2359304 | tf_op jit(solution)/shard_map/ppermute | solution.py:1490
  199.7 3.8 copy-start.64
  206.3 5.1 copy-start.66
  211.3 11.0 %collective-permute-start.11 = (bf16[512,768]{1,0:T(8,128)(2,1)}, bf16[512,768]{1,0:T(8,128)(2,1)S(1)}, u32[]{:S(2)}, u32[]{:S(2)}) collective-permute-start(bf16[512,768]{1,0:T(8,128)(2,1)} %get-tuple-element.303), channel_id=1, source_target_pairs={{0,8},{8,0},{16,24},{24,16},{1,9},{9,1},{17,25},{25,17},{2,10},{10... | collective-permute-start | bytes 2359304 | tf_op jit(solution)/shard_map/ppermute | solution.py:1490
  211.3 78.3 %collective-permute-start.9 = (bf16[512,768]{1,0:T(8,128)(2,1)}, bf16[512,768]{1,0:T(8,128)(2,1)}, u32[]{:S(2)}, u32[]{:S(2)}) collective-permute-start(bf16[512,768]{1,0:T(8,128)(2,1)} %bitcast.10), channel_id=1, source_target_pairs={{0,8},{8,0},{16,24},{24,16},{1,9},{9,1},{17,25},{25,17},{2,10},{10... | collective-permute-start | bytes 2359304 | tf_op jit(solution)/shard_map/ppermute | solution.py:1490
  211.8 290.6 %collective-permute-start.2 = (bf16[512,768]{1,0:T(8,128)(2,1)}, bf16[512,768]{1,0:T(8,128)(2,1)}, u32[]{:S(2)}, u32[]{:S(2)}) collective-permute-start(bf16[512,768]{1,0:T(8,128)(2,1)} %add_convert_fusion.2.own_ref.refs_0_), channel_id=1, source_target_pairs={{0,1},{9,8},{16,17},{25,24},{2,3},{11,10},{18,19},{27,26},{4,5},{1... | collective-permute-start | bytes 2359304 | tf_op jit(solution)/shard_map/ppermute | solution.py:1514
  213.1 6.1 %copy-start.67 = (bf16[512,1536]{1,0:T(8,128)(2,1)S(1)}, bf16[512,1536]{1,0:T(8,128)(2,1)}, u32[]{:S(2)}) copy-start(bf16[512,1536]{1,0:T(8,128)(2,1)} %copy-done.66) | copy-start | bytes 4718596
  213.1 289.3 %collective-permute-start.8 = (bf16[512,768]{1,0:T(8,128)(2,1)}, bf16[512,768]{1,0:T(8,128)(2,1)}, u32[]{:S(2)}, u32[]{:S(2)}) collective-permute-start(bf16[512,768]{1,0:T(8,128)(2,1)} %get-tuple-element.286.refs_2_), channel_id=1, source_target_pairs={{0,1},{9,8},{16,17},{25,24},{2,3},{11,10},{18,19},{27,26},{4,5},{1... | collective-permute-start | bytes 2359304 | tf_op jit(solution)/shard_map/ppermute | solution.py:1514
  227.6 54.9 %copy-start.22 = (f32[512,768]{1,0:T(8,128)S(1)}, f32[512,768]{1,0:T(8,128)}, u32[]{:S(2)}) copy-start(f32[512,768]{1,0:T(8,128)} %copy-done.21) | copy-start | bytes 4718596
  294.1 67.6 %copy-start.24 = (f32[512,768]{1,0:T(8,128)S(1)}, f32[512,768]{1,0:T(8,128)}, u32[]{:S(2)}) copy-start(f32[512,768]{1,0:T(8,128)} %copy-done.23) | copy-start | bytes 4718596
  369.0 63.1 %copy-start.59 = (f32[2,384]{1,0:T(2,128)S(1)}, f32[2,384]{1,0:T(2,128)}, u32[]{:S(2)}) copy-start(f32[2,384]{1,0:T(2,128)} %get-tuple-element.164) | copy-start | bytes 9220
  369.0 63.1 %copy-start.58 = (f32[2,384]{1,0:T(2,128)S(1)}, f32[2,384]{1,0:T(2,128)}, u32[]{:S(2)}) copy-start(f32[2,384]{1,0:T(2,128)} %get-tuple-element.165) | copy-start | bytes 9220
  369.0 63.2 %copy-start.57 = (f32[1,1536]{1,0:T(1,128)S(1)}, f32[1,1536]{1,0:T(1,128)}, u32[]{:S(2)}) copy-start(f32[1,1536]{1,0:T(1,128)} %get-tuple-element.166) | copy-start | bytes 18436
  369.1 63.9 %copy-start.27 = (f32[512,768]{1,0:T(8,128)S(1)}, f32[512,768]{1,0:T(8,128)}, u32[]{:S(2)}) copy-start(f32[512,768]{1,0:T(8,128)} %get-tuple-element.261) | copy-start | bytes 4718596
  (48 other events, 106.7 us)

commit v8 on v7

--- a/solution.py
+++ b/solution.py
@@ -1148,12 +1148,17 @@
     def slot(self, way, shard, z):
         return jnp.where((way == 1) & (shard == z), self.here.ring, shard)
 
-    def along(self, way, shard, device):
+    def chunk(self, chunk):
+        size = self.part // CHUNKS
+        return pl.ds(chunk * size, size)
+
+    def along(self, way, shard, chunk, device):
+        rows = self.chunk(chunk)
         return remote(
-            self.outgoing.at[shard],
-            self.arrived.at[self.slot(way, shard, device[1])],
-            self.sent.at[shard],
-            self.got.at[way, shard],
+            self.outgoing.at[shard, rows],
+            self.arrived.at[self.slot(way, shard, device[1]), rows],
+            self.sent.at[chunk, shard],
+            self.got.at[way * CHUNKS + chunk, shard],
             device,
         )
 
@@ -1171,25 +1176,29 @@
         self.across(0, shard).wait_recv()
         return self.outgoing[shard].astype(F32) + self.from_core[shard].astype(F32)
 
+    def take(self, way, shard, chunk):
+        rows = self.chunk(chunk)
+        self.along(way, shard, chunk, self.here.partner).wait_recv()
+        slot = self.slot(way, shard, self.here.z)
+        self.total[rows, :] += self.arrived[slot, rows, :].astype(F32)
+
     def forward(self, shard):
         here = self.here
         self.total[...] = self.both(shard)
-        for way, mine, comes, device in (
+        ways = (
             (0, shard > here.z, here.z > 0, here.right),
             (1, shard < here.z, here.z + 1 < here.ring, here.left),
-        ):
-
-            @pl.when(mine & comes)
-            def _(way=way):
-                self.along(way, shard, here.partner).wait_recv()
-                self.total[...] += self.arrived[self.slot(way, shard, here.z)].astype(F32)
-
-        self.outgoing[shard] = self.total[...].astype(BF16)
-        for way, mine, device in ((0, shard > here.z, here.right), (1, shard < here.z, here.left)):
-
-            @pl.when(mine)
-            def _(way=way, device=device):
-                self.along(way, shard, device).start()
+        )
+        for chunk in range(CHUNKS):
+            rows = self.chunk(chunk)
+            for way, mine, comes, _ in ways:
+                pl.when(mine & comes)(functools.partial(self.take, way, shard, chunk))
+            self.outgoing[shard, rows, :] = self.total[rows, :].astype(BF16)
+            for way, mine, _, device in ways:
+
+                @pl.when(mine)
+                def _(way=way, device=device, chunk=chunk):
+                    self.along(way, shard, chunk, device).start()
 
     def block(self, shard, between):
         rows = pl.ds(pl.multiple_of(shard * self.count, self.count), self.count)
@@ -1246,12 +1255,9 @@
 
         event(ring + 1)
         self.total[...] = self.both(here.z)
-        for way, comes in ((0, here.z > 0), (1, here.z + 1 < ring)):
-
-            @pl.when(comes)
-            def _(way=way):
-                self.along(way, here.z, here.partner).wait_recv()
-                self.total[...] += self.arrived[self.slot(way, here.z, here.z)].astype(F32)
+        for chunk in range(CHUNKS):
+            for way, comes in ((0, here.z > 0), (1, here.z + 1 < ring)):
+                pl.when(comes)(functools.partial(self.take, way, here.z, chunk))
 
         own, other = self.half(here.core), self.half(1 - here.core)
         self.sum[own, :] = self.total[...].astype(BF16)
@@ -1269,7 +1275,8 @@
 
             @pl.when(here.z != shard)
             def _(shard=shard):
-                self.along(0, shard, here.partner).wait_send()
+                for chunk in range(CHUNKS):
+                    self.along(0, shard, chunk, here.partner).wait_send()
 
         event(ring + 2)
 
@@ -1283,7 +1290,7 @@
         self.blocks, self.copied = scratch
 
     def copy(self, index):
-        part = pl.ds(pl.multiple_of(index * 256, 256), 256)
+        part = pl.ds(pl.multiple_of(index * 128, 128), 128)
         slot = lax.rem(index, 2)
         return pltpu.make_async_copy(
             self.key_in.at[:, part], self.blocks.at[slot], self.copied.at[slot]
@@ -1296,7 +1303,7 @@
             return
         dq, dkv = self.back.dq_out, self.back.dkv
         width = dq.shape[1]
-        number = self.of_kv.shape[0] // 256
+        number = self.of_kv.shape[0] // 128
 
         @pl.loop(0, number)
         def _(index):
@@ -1305,7 +1312,7 @@
                 self.copy(index + 1).start()
 
             self.copy(index).wait()
-            part = pl.ds(pl.multiple_of(index * 256, 256), 256)
+            part = pl.ds(pl.multiple_of(index * 128, 128), 128)
             block = self.blocks[lax.rem(index, 2)]
             self.of_kv[part, :] = dot_first(block, dkv[...]).astype(BF16)
 
@@ -1330,7 +1337,7 @@
         [VECTORS, ANYWHERE, VECTORS, VECTORS],
         [jax.ShapeDtypeStruct((2, width), F32)]
         + ([] if begins else [jax.ShapeDtypeStruct(shape, BF16) for shape in shapes]),
-        [pltpu.VMEM((2, key_in.shape[0], 256), BF16), DMA((2,))]
+        [pltpu.VMEM((2, key_in.shape[0], 128), BF16), DMA((2,))]
         + ([pltpu.VMEM(shape, BF16) for shape in shapes] if begins else []),
         bind,
     )
@@ -1348,7 +1355,8 @@
         self.grad, self.x_in = inputs[:2]
         self.streamed = inputs[2:]
         self.sum, self.of_bias, self.of_in, self.of_out = outputs
-        self.blocks, (self.low, self.got, self.copied, self.sems) = scratch[:4], scratch[4:]
+        self.blocks, scratch = scratch[:4], scratch[4:]
+        self.x_turned, self.grad_turned, self.low, self.got, self.copied, self.sems = scratch
 
     def event(self, time):
         if time != self.time:
@@ -1374,6 +1382,12 @@
         for copy in copies(0):
             copy.start()
 
+        @pl.loop(0, self.x_turned.shape[0] // span)
+        def _(index):
+            part = columns(index)
+            self.x_turned[part, :] = self.x_in[:, part].T
+            self.grad_turned[part, :] = self.grad[:, part].T
+
         @pl.loop(0, number)
         def _(index):
             part = columns(index)
@@ -1389,8 +1403,8 @@
             hidden = (slope[...] * dot_last(self.grad[...], w_out[...])).astype(BF16)
             self.of_bias[:, part] = jnp.sum(hidden.astype(F32), axis=0, keepdims=True)
             self.sum[...] += dot_last(hidden, w_in[...])
-            self.of_in[:, part] = dot_first(self.x_in[...], hidden).astype(BF16)
-            self.of_out[:, part] = dot_first(self.grad[...], active[...]).astype(BF16)
+            self.of_in[:, part] = dot_plain(self.x_turned[...], hidden).astype(BF16)
+            self.of_out[:, part] = dot_plain(self.grad_turned[...], active[...]).astype(BF16)
 
         self.low[...] = self.sum[...].astype(BF16)
         exchange = remote(self.low, self.got, self.sems.at[0], self.sems.at[1], self.here.partner)
@@ -1417,6 +1431,8 @@
             pltpu.VMEM((2, count, span), BF16),
             pltpu.VMEM((2, model, span), BF16),
             pltpu.VMEM((2, span, model), BF16),
+            pltpu.VMEM((model, count), BF16),
+            pltpu.VMEM((model, count), BF16),
             pltpu.VMEM((count, model), BF16),
             pltpu.VMEM((count, model), BF16),
             DMA((4, 2)),
@@ -1443,8 +1459,9 @@
         *[pltpu.VMEM((ring, part, model), BF16)] * 2,
         pltpu.VMEM((ring + 1, part, model), BF16),
         pltpu.VMEM((part, model), F32),
-        *[DMA((ring,))] * 3,
-        DMA((2, ring)),
+        *[DMA((ring,))] * 2,
+        DMA((CHUNKS, ring)),
+        DMA((2 * CHUNKS, ring)),
         *[DMA] * 2,
     ]
     if apart:

time: 516 us -> 514 us (level)
  waiting for transfers between devices: 13.1 us -> 4.16 us
  Pallas kernels: 388 us -> 394 us
    pallas_call x1, Pallas kernels: 4.35 us -> 14.6 us  [attend(): pl.pallas_call(functools.partial(forward_kernel, KEY_BLOCK, causal, len(t...]
    ppermute x4, waiting for transfers between devices: 8.59 us -> 0.01 us  [permute(): return lax.ppermute(value, ('dp', 'tensor'), moves)]
  transfers between devices with their start and end apart: 12 -> 12, of which waited for: 3 -> 2; matrix products, arithmetic and copies ran while one was open for 13% -> 13% of each run, Pallas kernels for 58% -> 60%
where the time goes in v8:
time: 514 us; the launch traced here: 507 us
  Pallas kernels  394 us (77%)
  matrix products  42.1 us (8%)
  other arithmetic  37.9 us (7%)
  local copies, waits for them, and re-layouts  15.6 us (3%)
  starting transfers between devices  8.86 us (2%)
    pallas_call x4, Pallas kernels, run_parts(): pl.pallas_call(kernel, out_shape=[shape for p in parts for shape in p.out...  247 us
    pallas_call x2, Pallas kernels, gather_attend(): pl.pallas_call(functools.partial(gather_attend_kernel, KEY_BLOCK, causal,...  84.2 us
    pallas_call x1, Pallas kernels, opening(): pl.pallas_call(functools.partial(opening_kernel, ring, number), out_shape...  41.7 us
    dot_general x6, matrix products, dot_plain(): return jnp.dot(left, right, preferred_element_type=F32)  16.1 us
    dot_general x8, matrix products, dot_last(): return lax.dot_general(left, right, NT, preferred_element_type=F32)  15.5 us
    pallas_call x1, Pallas kernels, attend(): pl.pallas_call(functools.partial(forward_kernel, KEY_BLOCK, causal, len(t...  14.6 us
    reduce_sum x5, other arithmetic, norm_backward(): return (grad_hidden, jnp.sum(grad * normed, axis=0), jnp.sum(grad, axis=0))  11 us
    dot_general x5, matrix products, dot_first(): return lax.dot_general(left, right, TN, preferred_element_type=F32)  10.4 us
  transfers between devices with their start and end apart: 12, of which 2 were waited for; matrix products, arithmetic and copies ran while one was open for 13% of the time, Pallas kernels for 60%

profile of v8, /device:TPU:1, one launch (start us, length us, event | category | flops | bytes accessed | tf_op | source)
XLA Modules:
  0.0 506.5 jit_solution(271408981028026200)
XLA Ops:
  0.7 41.7 %shard_map.450 = (bf16[2048,768]{1,0:T(8,128)(2,1)}, bf16[512,768]{1,0:T(8,128)(2,1)}, s32[1,2048]{1,0:T(1,128)}, s32[1,2048]{1,0:T(1,128)}, f32[8,1536]{1,0:T(8...) custom-call(bf16[512,768]{1,0:T(8,128)(2,1)} %bitcast.57, ...), custom_call_target="tpu_custom_call" | custom-call | tf_op jit(solution)/shard_map/pallas_call | solution.py:660
  47.4 42.6 %shard_map.451 = (bf16[512,384]{1,0:T(8,128)(2,1)S(1)}, bf16[2048,768]{1,0:T(8,128)(2,1)}, f32[384,512]{1,0:T(8,128)S(1)}, f32[8,512]{1,0:T(8,128)S(1)}, bf16[20...) custom-call(s32[8]{0:T(128)S(1)} %convert_reduce_fusion.8.starts.refs_0_, ...), custom_call_target="tpu_custom_call" | custom-call | flops 3221225472 | bytes 6291456 | tf_op jit(solution)/shard_map/pallas_call | solution.py:737
  98.3 2.3 fusion.39
  101.3 1.8 copy-done.37
  103.2 3.6 fusion.9
  108.2 3.5 collective-permute-start.1
  117.6 41.6 %shard_map.452 = (bf16[512,384]{1,0:T(8,128)(2,1)S(1)}, bf16[2048,768]{1,0:T(8,128)(2,1)}, f32[384,512]{1,0:T(8,128)S(1)}, f32[8,512]{1,0:T(8,128)S(1)}, bf16[20...) custom-call(s32[8]{0:T(128)S(1)} %convert_reduce_fusion.7.starts.ref, ...), custom_call_target="tpu_custom_call" | custom-call | flops 3221225472 | bytes 6291456 | tf_op jit(solution)/shard_map/pallas_call | solution.py:737
  163.9 2.9 add_convert_fusion.kv_ref.refs_3_
  169.2 14.6 %shard_map.453 = (f32[384,512]{1,0:T(8,128)S(1)}, f32[8,512]{1,0:T(8,128)S(1)}) custom-call(s32[8]{0:T(128)S(1)} %convert_reduce_fusion.8.starts.refs_0_, s32[3]{0:T(128)S(1)} %pad_add_fusion.ends, s32[1,512]{1,0:T(1,128)S(1)} %constant_dynamic-slice_fusion.2.segments.refs_1_, bf16[512,384]{1,0:T(8,128)(2,1)S(1)} %fusion.23.q_ref.refs_2_, ...), custom_call_target="tpu_custom_call" | custom-call | flops 1610612736 | bytes 3145728 | tf_op jit(solution)/shard_map/pallas_call | solution.py:253
  185.0 2.0 collective-permute-done.5
  188.0 4.9 multiply_convert_fusion
  193.0 2.8 fusion.45
  196.3 2.1 collective-permute-done.7
  198.4 2.2 fusion.35
  201.0 2.2 fusion.16
  205.0 2.7 convert_reduce_fusion
  207.6 5.0 fusion.46
  215.9 4.7 convolution_convert_fusion.refs_14_
  220.6 3.1 convolution_convert_fusion.1.refs_13_
  224.7 1.7 convert_reduce_fusion.3
  229.0 53.8 %shard_map.454 = (bf16[512,384]{1,0:T(8,128)(2,1)}, bf16[2048,768]{1,0:T(8,128)(2,1)}, bf16[512,768]{1,0:T(8,128)(2,1)}, f32[512,768]{1,0:T(8,128)}, f32[2,384]{...) custom-call(s32[8]{0:T(128)} %copy-done.12, ...), custom_call_target="tpu_custom_call" | custom-call | flops 5637144576 | bytes 11010048 | tf_op jit(solution)/shard_map/pallas_call | solution.py:786
  282.8 2.7 multiply_reduce_fusion.1
  285.6 1.7 convert_reduce_fusion.4
  289.9 2.4 multiply_reduce_fusion.2
  292.4 2.0 convert_reduce_fusion.5
  294.4 66.7 %shard_map.455 = (bf16[512,384]{1,0:T(8,128)(2,1)}, bf16[2048,768]{1,0:T(8,128)(2,1)}, bf16[512,768]{1,0:T(8,128)(2,1)}, f32[2,384]{1,0:T(2,128)}, bf16[384,384]...) custom-call(s32[8]{0:T(128)} %copy-done.10, ...), custom_call_target="tpu_custom_call" | custom-call | flops 5637144576 | bytes 11010048 | tf_op jit(solution)/shard_map/pallas_call | solution.py:786
  361.1 2.7 multiply_reduce_fusion.3
  363.9 1.7 convert_reduce_fusion.6
  368.4 58.5 %shard_map.456 = (bf16[512,384]{1,0:T(8,128)(2,1)}, bf16[2048,768]{1,0:T(8,128)(2,1)}, bf16[512,768]{1,0:T(8,128)(2,1)}, f32[2,384]{1,0:T(2,128)}, bf16[768,384]...) custom-call(s32[8]{0:T(128)} %copy-done.12, ...), custom_call_target="tpu_custom_call" | custom-call | flops 5637144576 | bytes 11010048 | tf_op jit(solution)/shard_map/pallas_call | solution.py:786
  428.4 2.3 reduce-precision_convert_fusion.refs_2_.refs_6_
  431.8 67.9 %shard_map.457 = (f32[22,768]{1,0:T(8,128)}, bf16[512,768]{1,0:T(8,128)(2,1)}, bf16[512,768]{1,0:T(8,128)(2,1)}, f32[48,768]{1,0:T(8,128)}, f32[48,384]{1,0:T(8,...) custom-call(f32[22,768]{1,0:T(8,128)} %pad_maximum_fusion.refs_0_, ...), custom_call_target="tpu_custom_call" | custom-call | tf_op jit(solution)/shard_map/pallas_call | solution.py:786
  499.7 6.5 %shard_map.458 = (bf16[512,768]{1,0:T(8,128)(2,1)}, bf16[512,768]{1,0:T(8,128)(2,1)}, f32[512,768]{1,0:T(8,128)}, f32[512,768]{1,0:T(8,128)}, f32[3,48,384]{2,1,...) custom-call(s32[1]{0:T(128)} %bitcast.flag, ...), custom_call_target="tpu_custom_call" | custom-call | tf_op jit(solution)/shard_map/pallas_call | solution.py:982
  (252 shorter events, 45.4 us)
Async XLA Ops:
  43.9 46.0 %copy-start.11 = (s32[1,512]{1,0:T(1,128)}, s32[1,512]{1,0:T(1,128)S(1)}, u32[]{:S(2)}) copy-start(s32[1,512]{1,0:T(1,128)S(1)} %constant_dynamic-slice_fusion.3.segments.refs_1_) | copy-start | bytes 6148
  44.8 124.4 %copy-start.12 = (s32[8]{0:T(128)}, s32[8]{0:T(128)S(1)}, u32[]{:S(2)}) copy-start(s32[8]{0:T(128)S(1)} %convert_reduce_fusion.8.starts.refs_0_) | copy-start | bytes 100
  93.0 5.3 %collective-permute-start = (bf16[512,768]{1,0:T(8,128)(2,1)}, bf16[512,768]{1,0:T(8,128)(2,1)S(1)}, u32[]{:S(2)}, u32[]{:S(2)}) collective-permute-start(bf16[512,768]{1,0:T(8,128)(2,1)} %get-tuple-element.291), channel_id=1, source_target_pairs={{0,8},{8,0},{16,24},{24,16},{1,9},{9,1},{17,25},{25,17},{2,10},{10... | collective-permute-start | bytes 2359304 | tf_op jit(solution)/shard_map/ppermute | solution.py:1507
  95.9 73.2 %collective-permute-start.4 = (bf16[768,1536]{1,0:T(8,128)(2,1)}, bf16[768,1536]{1,0:T(8,128)(2,1)}, u32[]{:S(2)}, u32[]{:S(2)}) collective-permute-start(bf16[768,1536]{1,0:T(8,128)(2,1)} %broadcast_add_fusion.1), channel_id=1, source_target_pairs={{8,0},{9,1},{1,8},{0,9},{24,16},{25,17},{17,24},{16,25},{10,2},{11... | collective-permute-start | bytes 7077896 | tf_op jit(solution)/shard_map/ppermute | solution.py:1531
  100.7 14.1 %copy-start.23 = (f32[512,768]{1,0:T(8,128)}, f32[512,768]{1,0:T(8,128)S(1)}, u32[]{:S(2)}) copy-start(f32[512,768]{1,0:T(8,128)S(1)} %get-tuple-element.282) | copy-start | bytes 4718596
  101.3 5.4 %copy-start.32 = (bf16[512,768]{1,0:T(8,128)(2,1)}, bf16[512,768]{1,0:T(8,128)(2,1)S(1)}, u32[]{:S(2)}) copy-start(bf16[512,768]{1,0:T(8,128)(2,1)S(1)} %fusion.17.refs_19_) | copy-start | bytes 2359300
  106.8 7.9 %copy-start.51 = (bf16[3,768]{1,0:T(4,128)(2,1)S(1)}, bf16[3,768]{1,0:T(4,128)(2,1)}, u32[]{:S(2)}) copy-start(bf16[3,768]{1,0:T(4,128)(2,1)} %param.49) | copy-start | bytes 13828
  106.8 7.9 %copy-start.52 = (bf16[3,768]{1,0:T(4,128)(2,1)S(1)}, bf16[3,768]{1,0:T(4,128)(2,1)}, u32[]{:S(2)}) copy-start(bf16[3,768]{1,0:T(4,128)(2,1)} %param.51) | copy-start | bytes 13828
  106.8 7.9 %copy-start.53 = (bf16[3,768]{1,0:T(4,128)(2,1)S(1)}, bf16[3,768]{1,0:T(4,128)(2,1)}, u32[]{:S(2)}) copy-start(bf16[3,768]{1,0:T(4,128)(2,1)} %param.50) | copy-start | bytes 13828
  108.2 6.6 %collective-permute-start.1 = (bf16[512,768]{1,0:T(8,128)(2,1)S(1)}, bf16[512,768]{1,0:T(8,128)(2,1)S(1)}, u32[]{:S(2)}, u32[]{:S(2)}) collective-permute-start(bf16[512,768]{1,0:T(8,128)(2,1)S(1)} %get-tuple-element.293), channel_id=1, source_target_pairs={{0,8},{8,0},{16,24},{24,16},{1,9},{9,1},{17,25},{25,17},{2,10},{10... | collective-permute-start | bytes 2359304 | tf_op jit(solution)/shard_map/ppermute | solution.py:1507
  113.0 56.1 %copy-start.9 = (s32[1,512]{1,0:T(1,128)}, s32[1,512]{1,0:T(1,128)S(1)}, u32[]{:S(2)}) copy-start(s32[1,512]{1,0:T(1,128)S(1)} %constant_dynamic-slice_fusion.2.segments.refs_1_) | copy-start | bytes 6148
  159.3 3.8 copy-start.65
  160.6 6.2 %collective-permute-start.3 = (bf16[512,768]{1,0:T(8,128)(2,1)S(1)}, bf16[512,768]{1,0:T(8,128)(2,1)S(1)}, u32[]{:S(2)}, u32[]{:S(2)}) collective-permute-start(bf16[512,768]{1,0:T(8,128)(2,1)S(1)} %get-tuple-element.295), channel_id=1, source_target_pairs={{0,8},{8,0},{16,24},{24,16},{1,9},{9,1},{17,25},{25,17},{2,10},{10... | collective-permute-start | bytes 2359304 | tf_op jit(solution)/shard_map/ppermute | solution.py:1507
  162.5 30.5 %collective-permute-start.6 = (bf16[1536,768]{1,0:T(8,128)(2,1)S(1)}, bf16[1536,768]{1,0:T(8,128)(2,1)S(1)}, u32[]{:S(2)}, u32[]{:S(2)}) collective-permute-start(bf16[1536,768]{1,0:T(8,128)(2,1)S(1)} %broadcast_add_fusion), channel_id=1, source_target_pairs={{8,0},{9,1},{1,8},{0,9},{24,16},{25,17},{17,24},{16,25},{10,2},{11... | collective-permute-start | bytes 7077896 | tf_op jit(solution)/shard_map/ppermute | solution.py:1531
  167.2 19.9 %copy-start.21 = (f32[512,768]{1,0:T(8,128)}, f32[512,768]{1,0:T(8,128)S(1)}, u32[]{:S(2)}) copy-start(f32[512,768]{1,0:T(8,128)S(1)} %get-tuple-element.278) | copy-start | bytes 4718596
  169.1 14.6 %copy-start.18 = (bf16[512,384]{1,0:T(8,128)(2,1)}, bf16[512,384]{1,0:T(8,128)(2,1)S(1)}, u32[]{:S(2)}) copy-start(bf16[512,384]{1,0:T(8,128)(2,1)S(1)} %fusion.23.q_ref.refs_2_) | copy-start | bytes 1179652
  184.8 2.3 collective-permute-start.5
  195.8 2.6 collective-permute-start.7
  196.1 4.9 collective-permute-start.10
  201.0 3.8 copy-start.64
  207.6 5.1 copy-start.66
  212.7 11.0 %collective-permute-start.11 = (bf16[512,768]{1,0:T(8,128)(2,1)}, bf16[512,768]{1,0:T(8,128)(2,1)S(1)}, u32[]{:S(2)}, u32[]{:S(2)}) collective-permute-start(bf16[512,768]{1,0:T(8,128)(2,1)} %get-tuple-element.303), channel_id=1, source_target_pairs={{0,8},{8,0},{16,24},{24,16},{1,9},{9,1},{17,25},{25,17},{2,10},{10... | collective-permute-start | bytes 2359304 | tf_op jit(solution)/shard_map/ppermute | solution.py:1507
  212.7 77.2 %collective-permute-start.9 = (bf16[512,768]{1,0:T(8,128)(2,1)}, bf16[512,768]{1,0:T(8,128)(2,1)}, u32[]{:S(2)}, u32[]{:S(2)}) collective-permute-start(bf16[512,768]{1,0:T(8,128)(2,1)} %bitcast.10), channel_id=1, source_target_pairs={{0,8},{8,0},{16,24},{24,16},{1,9},{9,1},{17,25},{25,17},{2,10},{10... | collective-permute-start | bytes 2359304 | tf_op jit(solution)/shard_map/ppermute | solution.py:1507
  213.2 286.5 %collective-permute-start.2 = (bf16[512,768]{1,0:T(8,128)(2,1)}, bf16[512,768]{1,0:T(8,128)(2,1)}, u32[]{:S(2)}, u32[]{:S(2)}) collective-permute-start(bf16[512,768]{1,0:T(8,128)(2,1)} %add_convert_fusion.2.own_ref.refs_0_), channel_id=1, source_target_pairs={{0,1},{9,8},{16,17},{25,24},{2,3},{11,10},{18,19},{27,26},{4,5},{1... | collective-permute-start | bytes 2359304 | tf_op jit(solution)/shard_map/ppermute | solution.py:1531
  214.5 6.1 %copy-start.67 = (bf16[512,1536]{1,0:T(8,128)(2,1)S(1)}, bf16[512,1536]{1,0:T(8,128)(2,1)}, u32[]{:S(2)}) copy-start(bf16[512,1536]{1,0:T(8,128)(2,1)} %copy-done.66) | copy-start | bytes 4718596
  214.5 285.2 %collective-permute-start.8 = (bf16[512,768]{1,0:T(8,128)(2,1)}, bf16[512,768]{1,0:T(8,128)(2,1)}, u32[]{:S(2)}, u32[]{:S(2)}) collective-permute-start(bf16[512,768]{1,0:T(8,128)(2,1)} %get-tuple-element.286.refs_2_), channel_id=1, source_target_pairs={{0,1},{9,8},{16,17},{25,24},{2,3},{11,10},{18,19},{27,26},{4,5},{1... | collective-permute-start | bytes 2359304 | tf_op jit(solution)/shard_map/ppermute | solution.py:1531
  229.0 53.8 %copy-start.22 = (f32[512,768]{1,0:T(8,128)S(1)}, f32[512,768]{1,0:T(8,128)}, u32[]{:S(2)}) copy-start(f32[512,768]{1,0:T(8,128)} %copy-done.21) | copy-start | bytes 4718596
  294.4 66.7 %copy-start.24 = (f32[512,768]{1,0:T(8,128)S(1)}, f32[512,768]{1,0:T(8,128)}, u32[]{:S(2)}) copy-start(f32[512,768]{1,0:T(8,128)} %copy-done.23) | copy-start | bytes 4718596
  368.4 59.3 %copy-start.59 = (f32[2,384]{1,0:T(2,128)S(1)}, f32[2,384]{1,0:T(2,128)}, u32[]{:S(2)}) copy-start(f32[2,384]{1,0:T(2,128)} %get-tuple-element.164) | copy-start | bytes 9220
  368.4 59.3 %copy-start.58 = (f32[2,384]{1,0:T(2,128)S(1)}, f32[2,384]{1,0:T(2,128)}, u32[]{:S(2)}) copy-start(f32[2,384]{1,0:T(2,128)} %get-tuple-element.165) | copy-start | bytes 9220
  368.4 59.3 %copy-start.57 = (f32[1,1536]{1,0:T(1,128)S(1)}, f32[1,1536]{1,0:T(1,128)}, u32[]{:S(2)}) copy-start(f32[1,1536]{1,0:T(1,128)} %get-tuple-element.166) | copy-start | bytes 18436
  368.4 60.0 %copy-start.27 = (f32[512,768]{1,0:T(8,128)S(1)}, f32[512,768]{1,0:T(8,128)}, u32[]{:S(2)}) copy-start(f32[512,768]{1,0:T(8,128)} %get-tuple-element.261) | copy-start | bytes 4718596
  (48 other events, 106.1 us)

commit v9 on v8

--- a/solution.py
+++ b/solution.py
@@ -194,7 +194,7 @@
     width = heads * HEAD_DIM
     allowed = mask.allowed(index, block)
     for pair in range(heads // 2):
-        if pair == 1:
+        if pair == 0:
             between()
         cols = head_columns(2 * pair)
         later = slice(width + cols.start, width + cols.stop)

time: 514 us -> 510 us (level)
  transfers between devices with their start and end apart: 12 -> 12, of which waited for: 2 -> 2; matrix products, arithmetic and copies ran while one was open for 13% -> 14% of each run, Pallas kernels for 60% -> 60%
where the time goes in v9:
time: 510 us; the launch traced here: 503 us
  Pallas kernels  390 us (76%)
  matrix products  42 us (8%)
  other arithmetic  37.9 us (7%)
  local copies, waits for them, and re-layouts  15.6 us (3%)
  starting transfers between devices  8.86 us (2%)
    pallas_call x4, Pallas kernels, run_parts(): pl.pallas_call(kernel, out_shape=[shape for p in parts for shape in p.out...  243 us
    pallas_call x2, Pallas kernels, gather_attend(): pl.pallas_call(functools.partial(gather_attend_kernel, KEY_BLOCK, causal,...  84.2 us
    pallas_call x1, Pallas kernels, opening(): pl.pallas_call(functools.partial(opening_kernel, ring, number), out_shape...  41.7 us
    dot_general x6, matrix products, dot_plain(): return jnp.dot(left, right, preferred_element_type=F32)  16.1 us
    dot_general x8, matrix products, dot_last(): return lax.dot_general(left, right, NT, preferred_element_type=F32)  15.5 us
    pallas_call x1, Pallas kernels, attend(): pl.pallas_call(functools.partial(forward_kernel, KEY_BLOCK, causal, len(t...  14.6 us
    reduce_sum x5, other arithmetic, norm_backward(): return (grad_hidden, jnp.sum(grad * normed, axis=0), jnp.sum(grad, axis=0))  11 us
    dot_general x5, matrix products, dot_first(): return lax.dot_general(left, right, TN, preferred_element_type=F32)  10.4 us
  transfers between devices with their start and end apart: 12, of which 2 were waited for; matrix products, arithmetic and copies ran while one was open for 14% of the time, Pallas kernels for 60%

profile of v9, /device:TPU:1, one launch (start us, length us, event | category | flops | bytes accessed | tf_op | source)
XLA Modules:
  0.0 503.0 jit_solution(17599999335822388536)
XLA Ops:
  0.7 41.7 %shard_map.450 = (bf16[2048,768]{1,0:T(8,128)(2,1)}, bf16[512,768]{1,0:T(8,128)(2,1)}, s32[1,2048]{1,0:T(1,128)}, s32[1,2048]{1,0:T(1,128)}, f32[8,1536]{1,0:T(8...) custom-call(bf16[512,768]{1,0:T(8,128)(2,1)} %bitcast.57, ...), custom_call_target="tpu_custom_call" | custom-call | tf_op jit(solution)/shard_map/pallas_call | solution.py:660
  47.4 42.6 %shard_map.451 = (bf16[512,384]{1,0:T(8,128)(2,1)S(1)}, bf16[2048,768]{1,0:T(8,128)(2,1)}, f32[384,512]{1,0:T(8,128)S(1)}, f32[8,512]{1,0:T(8,128)S(1)}, bf16[20...) custom-call(s32[8]{0:T(128)S(1)} %convert_reduce_fusion.8.starts.refs_0_, ...), custom_call_target="tpu_custom_call" | custom-call | flops 3221225472 | bytes 6291456 | tf_op jit(solution)/shard_map/pallas_call | solution.py:737
  98.3 2.3 fusion.39
  101.3 1.8 copy-done.37
  103.2 3.6 fusion.9
  108.2 3.5 collective-permute-start.1
  117.6 41.6 %shard_map.452 = (bf16[512,384]{1,0:T(8,128)(2,1)S(1)}, bf16[2048,768]{1,0:T(8,128)(2,1)}, f32[384,512]{1,0:T(8,128)S(1)}, f32[8,512]{1,0:T(8,128)S(1)}, bf16[20...) custom-call(s32[8]{0:T(128)S(1)} %convert_reduce_fusion.7.starts.ref, ...), custom_call_target="tpu_custom_call" | custom-call | flops 3221225472 | bytes 6291456 | tf_op jit(solution)/shard_map/pallas_call | solution.py:737
  163.9 2.9 add_convert_fusion.kv_ref.refs_3_
  169.2 14.6 %shard_map.453 = (f32[384,512]{1,0:T(8,128)S(1)}, f32[8,512]{1,0:T(8,128)S(1)}) custom-call(s32[8]{0:T(128)S(1)} %convert_reduce_fusion.8.starts.refs_0_, s32[3]{0:T(128)S(1)} %pad_add_fusion.ends, s32[1,512]{1,0:T(1,128)S(1)} %constant_dynamic-slice_fusion.2.segments.refs_1_, bf16[512,384]{1,0:T(8,128)(2,1)S(1)} %fusion.23.q_ref.refs_2_, ...), custom_call_target="tpu_custom_call" | custom-call | flops 1610612736 | bytes 3145728 | tf_op jit(solution)/shard_map/pallas_call | solution.py:253
  185.0 2.0 collective-permute-done.5
  188.0 4.9 multiply_convert_fusion
  193.0 2.8 fusion.45
  196.3 2.1 collective-permute-done.7
  198.4 2.2 fusion.35
  201.0 2.2 fusion.16
  205.0 2.7 convert_reduce_fusion
  207.6 5.0 %fusion.46 = (bf16[512,768]{1,0:T(8,128)(2,1)}, f32[512,768]{1,0:T(8,128)}) fusion(bf16[512,1536]{1,0:T(8,128)(2,1)S(1)} %get-tuple-element.306, bf16[768,1536]{1,0:T(8,128)(2,1)} %collective-permute-done.4.refs_0_), kind=kOutput, calls=%fused_computation.187 | convolution fusion | flops 1208745984 | bytes 6291456 | tf_op jit(solution)/shard_map/dot_general | solution.py:28
  215.9 4.7 convolution_convert_fusion.refs_14_
  220.6 3.1 convolution_convert_fusion.1.refs_13_
  224.7 1.7 convert_reduce_fusion.3
  229.0 52.6 %shard_map.454 = (bf16[512,384]{1,0:T(8,128)(2,1)}, bf16[2048,768]{1,0:T(8,128)(2,1)}, bf16[512,768]{1,0:T(8,128)(2,1)}, f32[512,768]{1,0:T(8,128)}, f32[2,384]{...) custom-call(s32[8]{0:T(128)} %copy-done.12, ...), custom_call_target="tpu_custom_call" | custom-call | flops 5637144576 | bytes 11010048 | tf_op jit(solution)/shard_map/pallas_call | solution.py:786
  281.6 2.7 multiply_reduce_fusion.1
  284.4 1.7 convert_reduce_fusion.4
  288.7 2.4 multiply_reduce_fusion.2
  291.2 2.0 convert_reduce_fusion.5
  293.2 66.8 %shard_map.455 = (bf16[512,384]{1,0:T(8,128)(2,1)}, bf16[2048,768]{1,0:T(8,128)(2,1)}, bf16[512,768]{1,0:T(8,128)(2,1)}, f32[2,384]{1,0:T(2,128)}, bf16[384,384]...) custom-call(s32[8]{0:T(128)} %copy-done.10, ...), custom_call_target="tpu_custom_call" | custom-call | flops 5637144576 | bytes 11010048 | tf_op jit(solution)/shard_map/pallas_call | solution.py:786
  360.0 2.7 multiply_reduce_fusion.3
  362.8 1.7 convert_reduce_fusion.6
  367.3 57.4 %shard_map.456 = (bf16[512,384]{1,0:T(8,128)(2,1)}, bf16[2048,768]{1,0:T(8,128)(2,1)}, bf16[512,768]{1,0:T(8,128)(2,1)}, f32[2,384]{1,0:T(2,128)}, bf16[768,384]...) custom-call(s32[8]{0:T(128)} %copy-done.12, ...), custom_call_target="tpu_custom_call" | custom-call | flops 5637144576 | bytes 11010048 | tf_op jit(solution)/shard_map/pallas_call | solution.py:786
  426.2 2.3 reduce-precision_convert_fusion.refs_2_.refs_6_
  429.6 66.6 %shard_map.457 = (f32[22,768]{1,0:T(8,128)}, bf16[512,768]{1,0:T(8,128)(2,1)}, bf16[512,768]{1,0:T(8,128)(2,1)}, f32[48,768]{1,0:T(8,128)}, f32[48,384]{1,0:T(8,...) custom-call(f32[22,768]{1,0:T(8,128)} %pad_maximum_fusion.refs_0_, ...), custom_call_target="tpu_custom_call" | custom-call | tf_op jit(solution)/shard_map/pallas_call | solution.py:786
  496.3 6.5 %shard_map.458 = (bf16[512,768]{1,0:T(8,128)(2,1)}, bf16[512,768]{1,0:T(8,128)(2,1)}, f32[512,768]{1,0:T(8,128)}, f32[512,768]{1,0:T(8,128)}, f32[3,48,384]{2,1,...) custom-call(s32[1]{0:T(128)} %bitcast.flag, ...), custom_call_target="tpu_custom_call" | custom-call | tf_op jit(solution)/shard_map/pallas_call | solution.py:982
  (252 shorter events, 45.4 us)
Async XLA Ops:
  43.9 46.0 %copy-start.11 = (s32[1,512]{1,0:T(1,128)}, s32[1,512]{1,0:T(1,128)S(1)}, u32[]{:S(2)}) copy-start(s32[1,512]{1,0:T(1,128)S(1)} %constant_dynamic-slice_fusion.3.segments.refs_1_) | copy-start | bytes 6148
  44.8 124.4 %copy-start.12 = (s32[8]{0:T(128)}, s32[8]{0:T(128)S(1)}, u32[]{:S(2)}) copy-start(s32[8]{0:T(128)S(1)} %convert_reduce_fusion.8.starts.refs_0_) | copy-start | bytes 100
  93.0 5.3 %collective-permute-start = (bf16[512,768]{1,0:T(8,128)(2,1)}, bf16[512,768]{1,0:T(8,128)(2,1)S(1)}, u32[]{:S(2)}, u32[]{:S(2)}) collective-permute-start(bf16[512,768]{1,0:T(8,128)(2,1)} %get-tuple-element.291), channel_id=1, source_target_pairs={{0,8},{8,0},{16,24},{24,16},{1,9},{9,1},{17,25},{25,17},{2,10},{10... | collective-permute-start | bytes 2359304 | tf_op jit(solution)/shard_map/ppermute | solution.py:1507
  95.9 73.2 %collective-permute-start.4 = (bf16[768,1536]{1,0:T(8,128)(2,1)}, bf16[768,1536]{1,0:T(8,128)(2,1)}, u32[]{:S(2)}, u32[]{:S(2)}) collective-permute-start(bf16[768,1536]{1,0:T(8,128)(2,1)} %broadcast_add_fusion.1), channel_id=1, source_target_pairs={{8,0},{9,1},{1,8},{0,9},{24,16},{25,17},{17,24},{16,25},{10,2},{11... | collective-permute-start | bytes 7077896 | tf_op jit(solution)/shard_map/ppermute | solution.py:1531
  100.7 14.1 %copy-start.23 = (f32[512,768]{1,0:T(8,128)}, f32[512,768]{1,0:T(8,128)S(1)}, u32[]{:S(2)}) copy-start(f32[512,768]{1,0:T(8,128)S(1)} %get-tuple-element.282) | copy-start | bytes 4718596
  101.3 5.4 %copy-start.32 = (bf16[512,768]{1,0:T(8,128)(2,1)}, bf16[512,768]{1,0:T(8,128)(2,1)S(1)}, u32[]{:S(2)}) copy-start(bf16[512,768]{1,0:T(8,128)(2,1)S(1)} %fusion.17.refs_19_) | copy-start | bytes 2359300
  106.8 7.9 %copy-start.51 = (bf16[3,768]{1,0:T(4,128)(2,1)S(1)}, bf16[3,768]{1,0:T(4,128)(2,1)}, u32[]{:S(2)}) copy-start(bf16[3,768]{1,0:T(4,128)(2,1)} %param.49) | copy-start | bytes 13828
  106.8 7.9 %copy-start.52 = (bf16[3,768]{1,0:T(4,128)(2,1)S(1)}, bf16[3,768]{1,0:T(4,128)(2,1)}, u32[]{:S(2)}) copy-start(bf16[3,768]{1,0:T(4,128)(2,1)} %param.51) | copy-start | bytes 13828
  106.8 7.9 %copy-start.53 = (bf16[3,768]{1,0:T(4,128)(2,1)S(1)}, bf16[3,768]{1,0:T(4,128)(2,1)}, u32[]{:S(2)}) copy-start(bf16[3,768]{1,0:T(4,128)(2,1)} %param.50) | copy-start | bytes 13828
  108.2 6.6 %collective-permute-start.1 = (bf16[512,768]{1,0:T(8,128)(2,1)S(1)}, bf16[512,768]{1,0:T(8,128)(2,1)S(1)}, u32[]{:S(2)}, u32[]{:S(2)}) collective-permute-start(bf16[512,768]{1,0:T(8,128)(2,1)S(1)} %get-tuple-element.293), channel_id=1, source_target_pairs={{0,8},{8,0},{16,24},{24,16},{1,9},{9,1},{17,25},{25,17},{2,10},{10... | collective-permute-start | bytes 2359304 | tf_op jit(solution)/shard_map/ppermute | solution.py:1507
  113.0 56.1 %copy-start.9 = (s32[1,512]{1,0:T(1,128)}, s32[1,512]{1,0:T(1,128)S(1)}, u32[]{:S(2)}) copy-start(s32[1,512]{1,0:T(1,128)S(1)} %constant_dynamic-slice_fusion.2.segments.refs_1_) | copy-start | bytes 6148
  159.3 3.8 copy-start.65
  160.6 6.2 %collective-permute-start.3 = (bf16[512,768]{1,0:T(8,128)(2,1)S(1)}, bf16[512,768]{1,0:T(8,128)(2,1)S(1)}, u32[]{:S(2)}, u32[]{:S(2)}) collective-permute-start(bf16[512,768]{1,0:T(8,128)(2,1)S(1)} %get-tuple-element.295), channel_id=1, source_target_pairs={{0,8},{8,0},{16,24},{24,16},{1,9},{9,1},{17,25},{25,17},{2,10},{10... | collective-permute-start | bytes 2359304 | tf_op jit(solution)/shard_map/ppermute | solution.py:1507
  162.5 30.5 %collective-permute-start.6 = (bf16[1536,768]{1,0:T(8,128)(2,1)S(1)}, bf16[1536,768]{1,0:T(8,128)(2,1)S(1)}, u32[]{:S(2)}, u32[]{:S(2)}) collective-permute-start(bf16[1536,768]{1,0:T(8,128)(2,1)S(1)} %broadcast_add_fusion), channel_id=1, source_target_pairs={{8,0},{9,1},{1,8},{0,9},{24,16},{25,17},{17,24},{16,25},{10,2},{11... | collective-permute-start | bytes 7077896 | tf_op jit(solution)/shard_map/ppermute | solution.py:1531
  167.2 19.9 %copy-start.21 = (f32[512,768]{1,0:T(8,128)}, f32[512,768]{1,0:T(8,128)S(1)}, u32[]{:S(2)}) copy-start(f32[512,768]{1,0:T(8,128)S(1)} %get-tuple-element.278) | copy-start | bytes 4718596
  169.1 14.6 %copy-start.18 = (bf16[512,384]{1,0:T(8,128)(2,1)}, bf16[512,384]{1,0:T(8,128)(2,1)S(1)}, u32[]{:S(2)}) copy-start(bf16[512,384]{1,0:T(8,128)(2,1)S(1)} %fusion.23.q_ref.refs_2_) | copy-start | bytes 1179652
  184.8 2.3 collective-permute-start.5
  195.8 2.6 collective-permute-start.7
  196.1 4.9 collective-permute-start.10
  201.0 3.8 copy-start.64
  207.6 5.1 %copy-start.66 = (bf16[512,1536]{1,0:T(8,128)(2,1)}, bf16[512,1536]{1,0:T(8,128)(2,1)S(1)}, u32[]{:S(2)}) copy-start(bf16[512,1536]{1,0:T(8,128)(2,1)S(1)} %get-tuple-element.306) | copy-start | bytes 4718596
  212.7 11.0 %collective-permute-start.11 = (bf16[512,768]{1,0:T(8,128)(2,1)}, bf16[512,768]{1,0:T(8,128)(2,1)S(1)}, u32[]{:S(2)}, u32[]{:S(2)}) collective-permute-start(bf16[512,768]{1,0:T(8,128)(2,1)} %get-tuple-element.303), channel_id=1, source_target_pairs={{0,8},{8,0},{16,24},{24,16},{1,9},{9,1},{17,25},{25,17},{2,10},{10... | collective-permute-start | bytes 2359304 | tf_op jit(solution)/shard_map/ppermute | solution.py:1507
  212.7 76.0 %collective-permute-start.9 = (bf16[512,768]{1,0:T(8,128)(2,1)}, bf16[512,768]{1,0:T(8,128)(2,1)}, u32[]{:S(2)}, u32[]{:S(2)}) collective-permute-start(bf16[512,768]{1,0:T(8,128)(2,1)} %bitcast.10), channel_id=1, source_target_pairs={{0,8},{8,0},{16,24},{24,16},{1,9},{9,1},{17,25},{25,17},{2,10},{10... | collective-permute-start | bytes 2359304 | tf_op jit(solution)/shard_map/ppermute | solution.py:1507
  213.2 283.0 %collective-permute-start.2 = (bf16[512,768]{1,0:T(8,128)(2,1)}, bf16[512,768]{1,0:T(8,128)(2,1)}, u32[]{:S(2)}, u32[]{:S(2)}) collective-permute-start(bf16[512,768]{1,0:T(8,128)(2,1)} %add_convert_fusion.2.own_ref.refs_0_), channel_id=1, source_target_pairs={{0,1},{9,8},{16,17},{25,24},{2,3},{11,10},{18,19},{27,26},{4,5},{1... | collective-permute-start | bytes 2359304 | tf_op jit(solution)/shard_map/ppermute | solution.py:1531
  214.5 6.1 %copy-start.67 = (bf16[512,1536]{1,0:T(8,128)(2,1)S(1)}, bf16[512,1536]{1,0:T(8,128)(2,1)}, u32[]{:S(2)}) copy-start(bf16[512,1536]{1,0:T(8,128)(2,1)} %copy-done.66) | copy-start | bytes 4718596
  214.5 281.7 %collective-permute-start.8 = (bf16[512,768]{1,0:T(8,128)(2,1)}, bf16[512,768]{1,0:T(8,128)(2,1)}, u32[]{:S(2)}, u32[]{:S(2)}) collective-permute-start(bf16[512,768]{1,0:T(8,128)(2,1)} %get-tuple-element.286.refs_2_), channel_id=1, source_target_pairs={{0,1},{9,8},{16,17},{25,24},{2,3},{11,10},{18,19},{27,26},{4,5},{1... | collective-permute-start | bytes 2359304 | tf_op jit(solution)/shard_map/ppermute | solution.py:1531
  229.0 52.6 %copy-start.22 = (f32[512,768]{1,0:T(8,128)S(1)}, f32[512,768]{1,0:T(8,128)}, u32[]{:S(2)}) copy-start(f32[512,768]{1,0:T(8,128)} %copy-done.21) | copy-start | bytes 4718596
  293.2 66.8 %copy-start.24 = (f32[512,768]{1,0:T(8,128)S(1)}, f32[512,768]{1,0:T(8,128)}, u32[]{:S(2)}) copy-start(f32[512,768]{1,0:T(8,128)} %copy-done.23) | copy-start | bytes 4718596
  367.3 58.1 %copy-start.59 = (f32[2,384]{1,0:T(2,128)S(1)}, f32[2,384]{1,0:T(2,128)}, u32[]{:S(2)}) copy-start(f32[2,384]{1,0:T(2,128)} %get-tuple-element.164) | copy-start | bytes 9220
  367.3 58.1 %copy-start.58 = (f32[2,384]{1,0:T(2,128)S(1)}, f32[2,384]{1,0:T(2,128)}, u32[]{:S(2)}) copy-start(f32[2,384]{1,0:T(2,128)} %get-tuple-element.165) | copy-start | bytes 9220
  367.3 58.2 %copy-start.57 = (f32[1,1536]{1,0:T(1,128)S(1)}, f32[1,1536]{1,0:T(1,128)}, u32[]{:S(2)}) copy-start(f32[1,1536]{1,0:T(1,128)} %get-tuple-element.166) | copy-start | bytes 18436
  367.3 58.9 %copy-start.27 = (f32[512,768]{1,0:T(8,128)S(1)}, f32[512,768]{1,0:T(8,128)}, u32[]{:S(2)}) copy-start(f32[512,768]{1,0:T(8,128)} %get-tuple-element.261) | copy-start | bytes 4718596
  (48 other events, 106.1 us)
